TPU v7x, 32 devices: a whole 2x2x4 slice. The times are simulated.
32 devices in a mesh: rows: 16 (over z, y, x), seq: 2 (over core).
Axes of the slice: x: 2, y: 2, z: 4, core: 2. Of those that a mesh axis runs over, the one named last changes fastest.
Arguments:
- tokens: bfloat16 [32, 1024, 1280], P('rows', 'seq'), may hold values from -6 to 6
- segments: int32 [32, 1024], P('rows'), may hold values from 0 to 4, as said below
- gain_attn: float32 [1280], replicated, may hold values from 0.1 to 1.9
- w_query: bfloat16 [1280, 1280], P('rows', 'seq'), may hold values from -0.15625 to 0.15625
- w_key: bfloat16 [1280, 1280], P('rows', 'seq'), may hold values from -0.15625 to 0.15625
- w_value: bfloat16 [1280, 1280], P('rows', 'seq'), may hold values from -0.15625 to 0.15625
- w_out: bfloat16 [1280, 1280], P('rows', 'seq'), may hold values from -6 to 6
- gain_ffn: float32 [1280], replicated, may hold values from 0.1 to 1.9
- w_up: bfloat16 [1280, 5120], P('rows', 'seq'), may hold values from -0.15625 to 0.15625
- w_down: bfloat16 [5120, 1280], P('rows', 'seq'), may hold values from -0.078125 to 0.078125
- cotangent: bfloat16 [32, 1024, 1280], P('rows', 'seq'), may hold values from -6 to 6
Outputs:
- layer_out: bfloat16 [32, 1024, 1280], P('rows', 'seq')
- token_grad: float32 [32, 1024, 1280], P('rows', 'seq')
- gain_attn_grad: float32 [1280], replicated
- query_grad: float32 [1280, 1280], P('rows', 'seq')
- key_grad: float32 [1280, 1280], P('rows', 'seq')
- value_grad: float32 [1280, 1280], P('rows', 'seq')
- out_grad: float32 [1280, 1280], P('rows', 'seq')
- gain_ffn_grad: float32 [1280], replicated
- up_grad: float32 [1280, 5120], P('rows', 'seq')
- down_grad: float32 [5120, 1280], P('rows', 'seq')
Inputs may be any that keep to these rules, and one draw needn't show every extreme that they name: `segments`: each row holds five contiguous samples numbered 0 to 4 in order; sample 2 begins within the row's first 512 tokens and ends within its last 512 tokens; every other sample is shorter than 512 tokens.
All inputs are finite; a program needn't handle non-finite values.
Results may differ from a plain program's by a relative error of at most 0.012.
Values may be sent and summed in bfloat16 or wider, within the bound.
A program may use at most 576 MiB of HBM per device.

v0:
```python
import jax
import jax.numpy as jnp
from jax import lax
from jax.sharding import PartitionSpec as P

HEADS = 20
HEAD_DIM = 64


epsilon = 1e-05
root_half = 0.7071067811865476


def norm_rows(values, gain_vec):
    row_mean = jnp.mean(values, -1, keepdims=True)
    centred = values - row_mean
    spread = jnp.mean(centred * centred, -1, keepdims=True)
    return centred * lax.rsqrt(spread + epsilon) * gain_vec


def gelu_exact(values):
    return 0.5 * values * (1.0 + lax.erf(values * root_half))


def times_transposed(left_side, right_side):
    return jnp.einsum("te,de->td", left_side, right_side, preferred_element_type=jnp.float32)


def split_heads(rows_in):
    return rows_in.reshape(rows_in.shape[0], rows_in.shape[1], HEADS, HEAD_DIM)


def join_heads(heads_in):
    return heads_in.reshape(heads_in.shape[0], heads_in.shape[1], HEADS * HEAD_DIM)


def masked_scores(query_heads, key_heads, seg_query, seg_key):
    scores = jnp.einsum(
        "rqhd,rkhd->rhqk", query_heads, key_heads, preferred_element_type=jnp.float32
    )
    scores = scores * HEAD_DIM ** (-0.5)
    allowed = (seg_query[:, :, None] == seg_key[:, None, :])[:, None]
    return (allowed, jnp.where(allowed, scores, -1e30))


def attention_forward(query_rows, key_rows, value_rows, seg_query, seg_key):
    allowed, scores = masked_scores(
        split_heads(query_rows), split_heads(key_rows), seg_query, seg_key
    )
    row_top = jnp.max(scores, -1, keepdims=True)
    exponent = jnp.exp(scores - row_top)
    row_total = jnp.sum(exponent, -1, keepdims=True)
    prob_low = (exponent / row_total).astype(jnp.bfloat16)
    mixed_out = jnp.einsum(
        "rhqk,rkhd->rqhd", prob_low, split_heads(value_rows), preferred_element_type=jnp.float32
    )
    return (join_heads(mixed_out).astype(jnp.bfloat16), row_top + jnp.log(row_total))


def grad_pieces(query_heads, key_heads, value_heads, seg_query, seg_key, log_total, grad_heads):
    allowed, scores = masked_scores(query_heads, key_heads, seg_query, seg_key)
    prob_rows = jnp.where(allowed, jnp.exp(scores - log_total), 0.0)
    grad_probs = jnp.einsum(
        "rqhd,rkhd->rhqk", grad_heads, value_heads, preferred_element_type=jnp.float32
    )
    return (prob_rows, grad_probs)


def attention_grads(query_rows, key_rows, value_rows, seg_query, seg_key, log_total, grad_mixed):
    query_heads = split_heads(query_rows)
    key_heads = split_heads(key_rows)
    grad_heads = split_heads(grad_mixed)
    prob_rows, grad_probs = grad_pieces(
        query_heads, key_heads, split_heads(value_rows), seg_query, seg_key, log_total, grad_heads
    )
    value_part = jnp.einsum(
        "rhqk,rqhd->rkhd",
        prob_rows.astype(jnp.bfloat16),
        grad_heads,
        preferred_element_type=jnp.float32,
    )
    row_inner = jnp.sum(grad_probs * prob_rows, -1, keepdims=True)
    score_grad = (prob_rows * (grad_probs - row_inner)).astype(jnp.bfloat16)
    score_scale = HEAD_DIM ** (-0.5)
    query_part = (
        jnp.einsum("rhqk,rkhd->rqhd", score_grad, key_heads, preferred_element_type=jnp.float32)
        * score_scale
    )
    key_part = (
        jnp.einsum("rhqk,rqhd->rkhd", score_grad, query_heads, preferred_element_type=jnp.float32)
        * score_scale
    )
    return (join_heads(query_part), join_heads(key_part), join_heads(value_part))


def process(token_rows, cot_rows, seg_rows, gain_attn, gain_ffn, weights):
    w_query, w_key, w_value, w_out, w_up, w_down = weights
    row_count, query_count, model_width = token_rows.shape
    offset = lax.axis_index("seq") * query_count
    seg_query = lax.dynamic_slice_in_dim(seg_rows, offset, query_count, 1)

    def shaped(flat_rows):
        return flat_rows.reshape(row_count, query_count, model_width)

    flat_tokens = token_rows.reshape(row_count * query_count, model_width).astype(jnp.float32)
    normed, norm_back = jax.vjp(norm_rows, flat_tokens, gain_attn)
    lowered = normed.astype(jnp.bfloat16)
    queries = jnp.dot(lowered, w_query, preferred_element_type=jnp.float32).astype(jnp.bfloat16)
    key_rows = jnp.dot(lowered, w_key, preferred_element_type=jnp.float32).astype(jnp.bfloat16)
    value_rows = jnp.dot(lowered, w_value, preferred_element_type=jnp.float32).astype(jnp.bfloat16)
    key_whole, value_whole = (
        lax.all_gather(shaped(key_rows), "seq", axis=1, tiled=True),
        lax.all_gather(shaped(value_rows), "seq", axis=1, tiled=True),
    )
    mixed_rows, log_total = attention_forward(
        shaped(queries), key_whole, value_whole, seg_query, seg_rows
    )
    mixed_flat = mixed_rows.reshape(row_count * query_count, model_width)
    residual = flat_tokens + jnp.dot(mixed_flat, w_out, preferred_element_type=jnp.float32)
    normed_two, norm_two_back = jax.vjp(norm_rows, residual, gain_ffn)
    lowered_two = normed_two.astype(jnp.bfloat16)
    hidden_pre = jnp.dot(lowered_two, w_up, preferred_element_type=jnp.float32)
    hidden, gelu_back = jax.vjp(gelu_exact, hidden_pre)
    hidden_low = hidden.astype(jnp.bfloat16)
    layer_rows = (
        residual + jnp.dot(hidden_low, w_down, preferred_element_type=jnp.float32)
    ).astype(jnp.bfloat16)
    grad_out = cot_rows.reshape(row_count * query_count, model_width)
    grad_hidden = times_transposed(grad_out, w_down)
    grad_pre = gelu_back(grad_hidden)[0].astype(jnp.bfloat16)
    grad_normed_two = times_transposed(grad_pre, w_up)
    grad_resid_norm, grad_gain_ffn = norm_two_back(grad_normed_two)
    grad_residual = grad_out.astype(jnp.float32) + grad_resid_norm
    grad_attn = grad_residual.astype(jnp.bfloat16)
    grad_mixed = times_transposed(grad_attn, w_out).astype(jnp.bfloat16)
    query_part, key_part, value_part = attention_grads(
        shaped(queries), key_whole, value_whole, seg_query, seg_rows, log_total, shaped(grad_mixed)
    )
    key_own, value_own = (
        lax.psum_scatter(key_part, "seq", scatter_dimension=1, tiled=True),
        lax.psum_scatter(value_part, "seq", scatter_dimension=1, tiled=True),
    )
    grad_queries = query_part.reshape(row_count * query_count, model_width).astype(jnp.bfloat16)
    grad_keys = key_own.reshape(row_count * query_count, model_width).astype(jnp.bfloat16)
    grad_values = value_own.reshape(row_count * query_count, model_width).astype(jnp.bfloat16)
    grad_normed = (
        times_transposed(grad_queries, w_query)
        + times_transposed(grad_keys, w_key)
        + times_transposed(grad_values, w_value)
    )
    grad_token_norm, grad_gain_attn = norm_back(grad_normed)
    grad_tokens = (grad_residual + grad_token_norm).reshape(row_count, query_count, model_width)
    saved = (
        lowered,
        grad_queries,
        grad_keys,
        grad_values,
        mixed_flat,
        grad_attn,
        lowered_two,
        grad_pre,
        hidden_low,
        grad_out,
    )
    return (
        layer_rows.reshape(row_count, query_count, model_width),
        grad_tokens,
        saved,
        grad_gain_attn,
        grad_gain_ffn,
    )


def body(
    tokens, segments, gain_attn, w_query, w_key, w_value, w_out, gain_ffn, w_up, w_down, cotangent
):
    col_query = lax.all_gather(w_query, "seq", axis=1, tiled=True)
    col_key = lax.all_gather(w_key, "seq", axis=1, tiled=True)
    col_value = lax.all_gather(w_value, "seq", axis=1, tiled=True)
    col_out = lax.all_gather(w_out, "seq", axis=1, tiled=True)
    col_up = lax.all_gather(w_up, "seq", axis=1, tiled=True)
    col_down = lax.all_gather(w_down, "seq", axis=1, tiled=True)
    results = [
        process(
            tokens,
            cotangent,
            segments,
            gain_attn,
            gain_ffn,
            (
                lax.all_gather(col_query, "rows", axis=0, tiled=True),
                lax.all_gather(col_key, "rows", axis=0, tiled=True),
                lax.all_gather(col_value, "rows", axis=0, tiled=True),
                lax.all_gather(col_out, "rows", axis=0, tiled=True),
                lax.all_gather(col_up, "rows", axis=0, tiled=True),
                lax.all_gather(col_down, "rows", axis=0, tiled=True),
            ),
        )
    ]
    layer_out = jnp.concatenate([result_set[0] for result_set in results], 0)
    token_grad = jnp.concatenate([result_set[1] for result_set in results], 0)
    saved = [
        jnp.concatenate([result_set[2][member] for result_set in results], 0)
        for member in range(10)
    ]
    attn_gain_part = sum((result_set[3] for result_set in results))
    ffn_gain_part = sum((result_set[4] for result_set in results))
    gain_attn_grad, gain_ffn_grad = lax.psum((attn_gain_part, ffn_gain_part), ("rows", "seq"))
    (
        lowered,
        grad_queries,
        grad_keys,
        grad_values,
        mixed_flat,
        grad_attn,
        lowered_two,
        grad_pre,
        hidden_low,
        grad_out,
    ) = saved
    splits = lax.axis_size("seq")

    def arrange(grad_block):
        return grad_block.reshape(grad_block.shape[0], splits, grad_block.shape[1] // splits)

    def outer_product(left_side, right_side):
        return jnp.einsum("tc,te->ce", left_side, right_side, preferred_element_type=jnp.float32)

    def input_terms(offset, count):
        blocks = [
            outer_product(lowered, grad_queries),
            outer_product(lowered, grad_keys),
            outer_product(lowered, grad_values),
            outer_product(mixed_flat, grad_attn),
            outer_product(lowered_two, grad_pre),
        ]
        return jnp.concatenate([arrange(grad_block) for grad_block in blocks], 2)

    def hidden_terms(offset, count):
        return arrange(outer_product(hidden_low, grad_out))

    def spread_sum(term_of, shard_rows):
        row_part = lax.psum_scatter(
            term_of(jnp.int32(0), shard_rows * lax.axis_size("rows")),
            "rows",
            scatter_dimension=0,
            tiled=True,
        )
        return lax.psum_scatter(row_part, "seq", scatter_dimension=1, tiled=True)[:, 0, :]

    input_grads = spread_sum(input_terms, w_query.shape[0])
    down_grad = spread_sum(hidden_terms, w_down.shape[0])
    column_width = w_query.shape[1]
    query_grad = input_grads[:, :column_width]
    key_grad = input_grads[:, column_width : 2 * column_width]
    value_grad = input_grads[:, 2 * column_width : 3 * column_width]
    out_grad = input_grads[:, 3 * column_width : 4 * column_width]
    up_grad = input_grads[:, 4 * column_width :]
    return (
        layer_out,
        token_grad,
        gain_attn_grad,
        query_grad,
        key_grad,
        value_grad,
        out_grad,
        gain_ffn_grad,
        up_grad,
        down_grad,
    )


def solution(mesh):
    return jax.shard_map(
        body,
        mesh=mesh,
        in_specs=(
            P("rows", "seq", None),
            P("rows", None),
            P(),
            P("rows", "seq"),
            P("rows", "seq"),
            P("rows", "seq"),
            P("rows", "seq"),
            P(),
            P("rows", "seq"),
            P("rows", "seq"),
            P("rows", "seq", None),
        ),
        out_specs=(
            P("rows", "seq", None),
            P("rows", "seq", None),
            P(),
            P("rows", "seq"),
            P("rows", "seq"),
            P("rows", "seq"),
            P("rows", "seq"),
            P(),
            P("rows", "seq"),
            P("rows", "seq"),
        ),
        check_vma=False,
    )
```

profile of v0, /device:TPU:0, one launch (start us, length us, event | category | flops | bytes accessed | tf_op | source)
XLA Modules:
  0.0 2739.3 jit_solution(4152872306389976185)
XLA Ops:
  7.2 4.0 all_gather.47
  11.4 3.6 all_gather.42
  15.1 3.8 all_gather.45
  23.8 2.3 fusion.14
  26.1 57.1 %all-gather.15.cloned.1.call-done = bf16[1280,1280]{1,0:T(8,128)(2,1)} async-done(((bf16[80,1280]{1,0:T(8,128)(2,1)}), bf16[1280,1280]{1,0:T(8,128)(2,1)}) %all-gather.15.cloned.1.call-update) | async-done | bytes 3276816 | tf_op jit(solution)/shard_map/all_gather | solution.py:192
  83.2 7.9 convolution_convert_fusion.1
  91.2 62.5 %all-gather.9.cloned.1.call-done = bf16[1280,1280]{1,0:T(8,128)(2,1)} async-done(((bf16[80,1280]{1,0:T(8,128)(2,1)}), bf16[1280,1280]{1,0:T(8,128)(2,1)}) %all-gather.9.cloned.1.call-update) | async-done | bytes 3276816 | tf_op jit(solution)/shard_map/all_gather | solution.py:193
  153.8 6.7 convolution_convert_fusion.3
  160.6 2.2 all_gather.50
  162.9 2.5 all_gather.52
  165.5 2.5 all_gather.54
  168.8 55.5 %all-gather.13.cloned.1.call-done = bf16[1280,1280]{1,0:T(8,128)(2,1)} async-done(((bf16[80,1280]{1,0:T(8,128)(2,1)}), bf16[1280,1280]{1,0:T(8,128)(2,1)}) %all-gather.13.cloned.1.call-update) | async-done | bytes 3276816 | tf_op jit(solution)/shard_map/all_gather | solution.py:191
  224.3 7.7 convolution_convert_fusion.2
  232.0 4.7 copy.36
  236.7 5.5 reshape_reshape.8
  242.2 8.1 copy.37
  250.3 33.9 %fusion.1 = (f32[2,20,512]{2,1,0:T(8,128)S(1)}, f32[2,20,512,1024]{3,2,1,0:T(8,128)}) fusion(pred[2,512,1024]{2,1,0:T(8,128)(4,1)S(1)} %broadcast_compare_fusion, bf16[2,1024,20,64]{1,3,2,0:T(8,128)(2,1)} %bitcast.135, bf16[2,512,20,64]{1,0,3,2:T(2,128)(2,1)} %reshape_reshape.8), kind=kOutput, calls=%fused_computation.7 | convolution fusion | flops 2747248640 | bytes 92880896 | tf_op jit(solution)/shard_map/rqhd,rkhd->rhqk/dot_general | solution.py:38
  284.3 7.9 copy.35
  292.1 27.0 fusion
  319.1 33.5 %convert_bitcast_fusion = bf16[2,512,20,64]{1,3,2,0:T(8,128)(2,1)S(1)} fusion(bf16[2,1024,20,64]{1,3,2,0:T(8,128)(2,1)} %bitcast.155, f32[2,20,512,1024]{3,2,1,0:T(8,128)} %get-tuple-element.29, f32[2,20,512]{2,1,0:T(8,128)S(1)} %fusion, f32[2,20,512]{2,1,0:T(8,128)S(1)} %get-tuple-element.28, pred[2,512,1024]{2,1,0:T(8,128)(4,1)S(1)} %broadcast_compare_fusion), kind=kOutput, calls=%fused_computation.57 | convolution fusion | flops 2790522880 | bytes 92962816 | tf_op jit(solution)/shard_map/rhqk,rkhd->rqhd/dot_general | solution.py:54
  352.7 2.7 copy.39
  357.6 6.5 fusion.43
  364.2 2.3 copy-done.4
  367.2 122.1 %all-gather.21.cloned.1.call-done = bf16[1280,5120]{1,0:T(8,128)(2,1)} async-done(((bf16[80,5120]{1,0:T(8,128)(2,1)}), bf16[1280,5120]{1,0:T(8,128)(2,1)}) %all-gather.21.cloned.1.call-update) | async-done | bytes 13107216 | tf_op jit(solution)/shard_map/all_gather | solution.py:195
  489.3 22.8 fusion.40
  512.1 135.2 %all-gather.23.cloned.1.call-done = bf16[5120,1280]{1,0:T(8,128)(2,1)} async-done(((bf16[320,1280]{1,0:T(8,128)(2,1)}), bf16[5120,1280]{1,0:T(8,128)(2,1)}) %all-gather.23.cloned.1.call-update) | async-done | bytes 13107216 | tf_op jit(solution)/shard_map/all_gather | solution.py:196
  647.3 27.0 add_convert_fusion
  674.2 23.3 multiply_reduce_fusion.1
  697.6 5.0 fusion.41
  707.0 4.9 convolution_convert_fusion
  711.9 4.6 copy.40
  716.4 5.5 reshape_reshape.9
  722.0 65.9 %multiply_reduce_fusion = (f32[2,20,512]{2,1,0:T(8,128)S(1)}, f32[2,20,512,1024]{3,2,1,0:T(8,128)}) fusion(f32[2,20,512]{2,1,0:T(8,128)S(1)} %log_add_fusion, f32[2,20,512,1024]{3,2,1,0:T(8,128)} %get-tuple-element.29, pred[2,512,1024]{2,1,0:T(8,128)(4,1)S(1)} %copy-done.7, bf16[2,1024,20,64]{1,3,2,0:T(8,128)(2,1)} %bitcast.156, ...), kind=kOutput, calls=%fused_computation.1 | convolution fusion | flops 2810163200 | bytes 176848896 | tf_op jit(solution)/shard_map/rqhd,rkhd->rhqk/dot_general | solution.py:63
  787.8 65.5 %multiply_convert_fusion = bf16[2,20,512,1024]{3,2,1,0:T(8,128)(2,1)} fusion(f32[2,20,512,1024]{3,2,1,0:T(8,128)} %get-tuple-element.34, f32[2,20,512]{2,1,0:T(8,128)S(1)} %get-tuple-element.33, f32[2,20,512]{2,1,0:T(8,128)S(1)} %log_add_fusion, f32[2,20,512,1024]{3,2,1,0:T(8,128)} %get-tuple-element.29, pred[2,512,1024]{2,1,0:T(8,128)(4,1)S(1)} %copy-done.7), kind=kLoop, calls=%fused_computation | loop fusion | flops 146800640 | bytes 210927616 | tf_op jit(solution)/shard_map/convert_element_type | solution.py:83
  853.3 21.8 broadcast_multiply_fusion
  875.1 11.2 copy.44
  886.4 41.3 %fusion.2 = f32[2,20,64,1024]{3,2,1,0:T(8,128)} fusion(f32[2,20,512,1024]{3,2,1,0:T(8,128)} %get-tuple-element.29, f32[2,20,512]{2,1,0:T(8,128)S(1)} %log_add_fusion, pred[2,512,1024]{2,1,0:T(8,128)(4,1)S(1)} %copy-done.7, bf16[2,512,20,64]{1,0,3,2:T(2,128)(2,1)} %reshape_reshape.9), kind=kOutput, calls=%fused_computation.8 | convolution fusion | flops 2789212160 | bytes 98123776 | tf_op jit(solution)/shard_map/rhqk,rqhd->rkhd/dot_general | solution.py:76
  927.7 11.2 copy.46
  940.7 2.3 fusion.18
  943.0 24.0 fusion.21
  967.0 2.7 copy.42
  971.9 4.6 copy.67
  976.5 9.1 convolution_dynamic-update-slice_fusion.3
  985.7 21.8 fusion.39
  1007.4 2.7 convert_element_type.117
  1010.2 3.0 copy.64
  1013.2 2.7 convert_element_type.120
  1015.9 3.0 copy.65
  1018.9 9.0 convolution_dynamic-update-slice_fusion.2
  1028.0 6.6 convolution_dynamic-update-slice_fusion.1
  1034.6 6.3 convolution_dynamic-update-slice_fusion
  1042.8 9.0 bitcast_dynamic-update-slice_fusion
  1053.5 2.6 copy.69
  1056.1 20.7 fusion.5
  1076.9 1038.4 %reduce-scatter.11.cloned.1.call-done = f32[80,2,5120]{2,0,1:T(8,128)} async-done(((f32[1280,2,5120]{2,0,1:T(8,128)}), f32[80,2,5120]{2,0,1:T(8,128)}) %reduce-scatter.11.cloned.1.call-update) | async-done | bytes 3276816 | tf_op jit(solution)/shard_map/reduce_scatter | solution.py:243
  2115.3 7.5 fusion.44
  2122.9 22.0 add_convert_fusion.1
  2144.9 5.3 fusion.45
  2150.2 510.9 %reduce-scatter.15.cloned.1.call-done = f32[320,2,640]{2,0,1:T(8,128)} async-done(((f32[5120,2,640]{2,0,1:T(8,128)}), f32[320,2,640]{2,0,1:T(8,128)}) %reduce-scatter.15.cloned.1.call-update) | async-done | bytes 1638416 | tf_op jit(solution)/shard_map/reduce_scatter | solution.py:243
  2661.2 9.8 fusion.19
  2671.0 2.3 copy-done.10
  2673.4 2.7 fusion.15
  2676.1 44.6 %all-reduce = (f32[1280]{0:T(1024)}, f32[1280]{0:T(1024)}) all-reduce(f32[1280]{0:T(1024)S(1)} %get-tuple-element.12, f32[1280]{0:T(1024)S(1)} %copy-done.46), channel_id=1, replica_groups=mesh['rows'=16,'seq'=2] {'rows','seq'}, use_global_device_ids=true, to_apply=%region_14.15 | all-reduce | flops 2560 | bytes 20480 | tf_op jit(solution)/shard_map/psum | solution.py:208
  2720.7 7.5 add_add_fusion.2
  (171 shorter events, 25.3 us)
Async XLA Ops:
  7.2 14.0 copy-start
  7.2 16.6 copy-start.24
  7.2 76.0 %all-gather.15.cloned.1.call-start = ((), (), s32[]{:S(2)}) async-start(), calls=%async_computation.9 | async-start | bytes 3481600 | tf_op jit(solution)/shard_map/all_gather | solution.py:192
  11.3 142.4 %all-gather.9.cloned.1.call-start = ((), (), s32[]{:S(2)}) async-start(), calls=%async_computation.6 | async-start | bytes 3481600 | tf_op jit(solution)/shard_map/all_gather | solution.py:193
  15.0 209.3 %all-gather.13.cloned.1.call-start = ((), (), s32[]{:S(2)}) async-start(), calls=%async_computation.8 | async-start | bytes 3481600 | tf_op jit(solution)/shard_map/all_gather | solution.py:191
  18.9 223.3 %all-gather.17.cloned.1.call-start = ((), (), s32[]{:S(2)}) async-start(), calls=%async_computation.10 | async-start | bytes 7864320 | tf_op jit(solution)/shard_map/all_gather | solution.py:112
  26.1 127.6 %copy-start.17 = (bf16[1024,1280]{1,0:T(8,128)(2,1)S(1)}, bf16[1024,1280]{1,0:T(8,128)(2,1)}, u32[]{:S(2)}) copy-start(bf16[1024,1280]{1,0:T(8,128)(2,1)} %fusion.14) | copy-start | bytes 7864324
  91.1 69.4 %copy-start.27 = (bf16[80,640]{1,0:T(8,128)(2,1)S(1)}, bf16[80,640]{1,0:T(8,128)(2,1)}, u32[]{:S(2)}) copy-start(bf16[80,640]{1,0:T(8,128)(2,1)} %param.17) | copy-start | bytes 307204
  91.2 71.7 %copy-start.22 = (bf16[80,2560]{1,0:T(8,128)(2,1)S(1)}, bf16[80,2560]{1,0:T(8,128)(2,1)}, u32[]{:S(2)}) copy-start(bf16[80,2560]{1,0:T(8,128)(2,1)} %param.19) | copy-start | bytes 1228804
  91.2 193.1 %all-gather.11.cloned.1.call-start = ((), (), s32[]{:S(2)}) async-start(), calls=%async_computation.7 | async-start | bytes 7864320 | tf_op jit(solution)/shard_map/all_gather | solution.py:113
  160.5 5.0 copy-start.23
  160.5 7.6 copy-start.40
  160.5 197.1 %all-gather.19.cloned.1.call-start = ((), (), s32[]{:S(2)}) async-start(), calls=%async_computation.11 | async-start | bytes 3481600 | tf_op jit(solution)/shard_map/all_gather | solution.py:194
  162.8 326.5 %all-gather.21.cloned.1.call-start = ((), (), s32[]{:S(2)}) async-start(), calls=%async_computation.12 | async-start | bytes 13926400 | tf_op jit(solution)/shard_map/all_gather | solution.py:195
  165.4 481.8 %all-gather.23.cloned.1.call-start = ((), (), s32[]{:S(2)}) async-start(), calls=%async_computation.13 | async-start | bytes 13926400 | tf_op jit(solution)/shard_map/all_gather | solution.py:196
  168.0 839.4 %reduce-scatter.7.cloned.1.call-start = ((), (), s32[]{:S(2)}) async-start(), calls=%async_computation.14 | async-start | bytes 15728640 | tf_op jit(solution)/shard_map/reduce_scatter | solution.py:140
  168.8 150.3 %copy-start.6 = (pred[2,512,1024]{2,1,0:T(8,128)(4,1)}, pred[2,512,1024]{2,1,0:T(8,128)(4,1)S(1)}, u32[]{:S(2)}) copy-start(pred[2,512,1024]{2,1,0:T(8,128)(4,1)S(1)} %broadcast_compare_fusion) | copy-start | bytes 3145732
  352.7 4.9 copy-start.1
  364.1 2.4 copy-start.4
  364.1 125.2 %copy-start.44 = (f32[1280]{0:T(1024)S(1)}, f32[1280]{0:T(1024)}, u32[]{:S(2)}) copy-start(f32[1280]{0:T(1024)} %param.18) | copy-start | bytes 15364
  364.1 333.4 %copy-start.38 = (f32[1024]{0:T(1024)}, f32[1024]{0:T(1024)S(1)}, u32[]{:S(2)}) copy-start(f32[1024]{0:T(1024)S(1)} %broadcast_multiply_fusion.1) | copy-start | bytes 12292
  367.2 330.4 %copy-start.42 = (f32[1024]{0:T(1024)}, f32[1024]{0:T(1024)S(1)}, u32[]{:S(2)}) copy-start(f32[1024]{0:T(1024)S(1)} %fusion.29) | copy-start | bytes 12292
  367.2 280.1 %copy-start.8 = (bf16[2,512,1280]{2,1,0:T(8,128)(2,1)S(1)}, bf16[2,512,1280]{2,1,0:T(8,128)(2,1)}, u32[]{:S(2)}) copy-start(bf16[2,512,1280]{2,1,0:T(8,128)(2,1)} %param.21) | copy-start | bytes 7864324
  702.6 2.7 copy-start.5
  702.6 2.6 copy-start.34
  702.6 4.4 copy-start.16
  711.9 10.1 copy-start.7
  886.4 126.8 %reduce-scatter.9.cloned.1.call-start = ((), (), s32[]{:S(2)}) async-start(), calls=%async_computation.15 | async-start | bytes 15728640 | tf_op jit(solution)/shard_map/reduce_scatter | solution.py:141
  938.9 1.7 copy-start.25
  938.9 1.7 copy-start.33
  938.9 1.7 copy-start.41
  938.9 1176.3 %reduce-scatter.11.cloned.1.call-start = ((), (), s32[]{:S(2)}) async-start(), calls=%async_computation.16 | async-start | bytes 55705600 | tf_op jit(solution)/shard_map/reduce_scatter | solution.py:243
  971.9 13.7 slice-start
  976.5 9.2 slice-start.1
  976.5 9.2 copy-start.39
  976.5 9.2 copy-start.43
  976.5 9.2 copy-start.45
  1010.2 3.0 copy-start.13
  1015.9 12.0 copy-start.12
  1018.9 9.0 copy-start.19
  1018.9 9.0 copy-start.21
  1028.0 6.6 copy-start.11
  1028.0 6.6 copy-start.20
  1028.0 12.9 slice-start.2
  1028.0 12.9 slice-start.3
  1028.0 12.9 slice-start.4
  1028.0 12.9 slice-start.5
  1034.6 6.3 slice-start.6
  1034.6 8.0 slice-start.7
  1034.6 8.2 slice-start.8
  1051.8 1609.3 %reduce-scatter.15.cloned.1.call-start = ((), (), s32[]{:S(2)}) async-start(), calls=%async_computation.18 | async-start | bytes 27852800 | tf_op jit(solution)/shard_map/reduce_scatter | solution.py:243
  1076.8 1038.5 %copy-start.18 = (bf16[160,8,2,512]{3,1,2,0:T(8,128)(2,1)S(1)}, bf16[160,8,2,512]{3,1,2,0:T(8,128)(2,1)}, u32[]{:S(2)}) copy-start(bf16[160,8,2,512]{3,1,2,0:T(8,128)(2,1)} %copy.74) | copy-start | bytes 7864324
  1076.8 1651.3 %reduce-scatter.13.cloned.1.call-start = ((), (), s32[]{:S(2)}) async-start(), calls=%async_computation.17 | async-start | bytes 4915200 | tf_op jit(solution)/shard_map/reduce_scatter | solution.py:249
  2115.3 617.1 %reduce-scatter.17.cloned.1.call-start = ((), (), s32[]{:S(2)}) async-start(), calls=%async_computation.19 | async-start | bytes 2457600 | tf_op jit(solution)/shard_map/reduce_scatter | solution.py:249
  2122.9 22.0 copy-start.14
  2122.9 22.0 copy-start.47
  2144.9 516.3 %copy-start.3 = (bf16[2,512,1280]{2,1,0:T(8,128)(2,1)S(1)}, bf16[2,512,1280]{2,1,0:T(8,128)(2,1)}, u32[]{:S(2)}) copy-start(bf16[2,512,1280]{2,1,0:T(8,128)(2,1)} %param.11) | copy-start | bytes 7864324
  2144.9 516.3 %copy-start.26 = (f32[1280]{0:T(1024)S(1)}, f32[1280]{0:T(1024)}, u32[]{:S(2)}) copy-start(f32[1280]{0:T(1024)} %param.13) | copy-start | bytes 15364
  2144.9 516.3 %copy-start.31 = (f32[1,4,2,128]{3,1,2,0:T(4,128)S(1)}, f32[1,4,2,128]{3,1,2,0:T(4,128)}, u32[]{:S(2)}) copy-start(f32[1,4,2,128]{3,1,2,0:T(4,128)} %copy-done.30) | copy-start | bytes 12292
  2661.1 9.9 copy-start.37
  2661.2 12.2 copy-start.29
  2671.0 2.4 copy-start.10
  2671.0 5.1 copy-start.46
  2671.0 49.7 %copy-start.35 = (f32[1024]{0:T(1024)S(1)}, f32[1024]{0:T(1024)}, u32[]{:S(2)}) copy-start(f32[1024]{0:T(1024)} %copy-done.34) | copy-start | bytes 12292
  (7 other events, 8.3 us)
Sparse Core Ops, SparseCore 0:
  11.4 71.6 all-gather.14
  85.9 67.7 all-gather.8
  156.5 67.7 all-gather.12
  225.7 13.7 all-gather.16
  241.4 16.3 all-gather.10
  260.4 70.4 all-gather.18
  333.7 155.5 all-gather.20
  492.0 155.1 all-gather.22
  886.5 17.2 reduce-scatter.6
  939.1 16.8 reduce-scatter.8
  1051.9 1063.2 reduce-scatter.10
  2117.4 543.6 reduce-scatter.14
  2663.3 16.6 reduce-scatter.12
  2682.8 10.2 reduce-scatter.16
where the time goes:
time: 2750 us; the launch traced here: 2740 us
  waiting for transfers between devices  1980 us (72%)
  matrix products  445 us (16%)
  other arithmetic  124 us (5%)
  local copies, waits for them, and re-layouts  110 us (4%)
  blocking collectives  63.4 us (2%)
    reduce_scatter x2, waiting for transfers between devices, spread_sum(): lax.psum_scatter(term_of(jnp.int32(0), shard_rows * lax.axis_size('rows')...  1550 us
    all_gather x1, waiting for transfers between devices, body(): lax.all_gather(col_down, 'rows', axis=0, tiled=True)  135 us
    all_gather x1, waiting for transfers between devices, body(): lax.all_gather(col_up, 'rows', axis=0, tiled=True)  122 us
    dot_general x6, matrix products, times_transposed(): jnp.einsum('te,de->td', left_side, right_side, preferred_element_type=jnp...  77.9 us
    dot_general x6, matrix products, outer_product(): jnp.einsum('tc,te->ce', left_side, right_side, preferred_element_type=jnp...  73.5 us
    dot_general x1, matrix products, grad_pieces(): jnp.einsum('rqhd,rkhd->rhqk', grad_heads, value_heads, preferred_element_...  65.9 us
    convert_element_type x1, other arithmetic, attention_grads(): score_grad = (prob_rows * (grad_probs - row_inner)).astype(jnp.bfloat16)  65.5 us
    all_gather x1, waiting for transfers between devices, body(): lax.all_gather(col_value, 'rows', axis=0, tiled=True)  62.5 us
  transfers between devices with their start and end apart: 14, of which 7 were waited for; matrix products, arithmetic and copies ran while one was open for 14% of the time, Pallas kernels for 0%

commit v1 on v0

--- a/solution.py
+++ b/solution.py
@@ -1,6 +1,10 @@
+import functools
+
 import jax
 import jax.numpy as jnp
 from jax import lax
+from jax.experimental import pallas as pl
+from jax.experimental.pallas import tpu as pltpu
 from jax.sharding import PartitionSpec as P
 
 HEADS = 20
@@ -270,9 +274,342 @@
     )
 
 
+LANES = 128
+QUERY_TILE = 256
+NEVER = -1e30
+
+
+def swap_cores(values):
+    return lax.ppermute(values, "seq", [(0, 1), (1, 0)])
+
+
+def both_cores(values, axis):
+    other = swap_cores(values)
+    first = lax.axis_index("seq") == 0
+    return jnp.where(
+        first,
+        jnp.concatenate([values, other], axis),
+        jnp.concatenate([other, values], axis),
+    )
+
+
+def own_half(values, axis, index):
+    half = values.shape[axis] // 2
+    return lax.dynamic_slice_in_dim(values, index * half, half, axis)
+
+
+def attend_kernel(start_ref, count_ref, column_ref, line_ref, q_ref, k_ref, v_ref, out_ref):
+    row = pl.program_id(0)
+    length = k_ref.shape[1]
+    lower = lax.broadcasted_iota(jnp.int32, (QUERY_TILE, LANES), 1) < HEAD_DIM
+
+    def tile_step(tile, carry):
+        begin = pl.multiple_of(start_ref[row, tile] * LANES, LANES)
+        count = count_ref[row, tile]
+        queries = pl.ds(pl.multiple_of(tile * QUERY_TILE, QUERY_TILE), QUERY_TILE)
+
+        def window(tiles):
+            keys = pl.ds(begin, tiles * LANES)
+            query = q_ref[0, queries, :]
+            key = k_ref[0, keys, :]
+            value = v_ref[0, keys, :]
+            allowed = column_ref[0, queries, :1] == line_ref[0, :1, keys]
+            mixed = []
+            for head in range(2):
+                mine = lower if head == 0 else jnp.logical_not(lower)
+                masked = jnp.where(mine, query, jnp.zeros_like(query))
+                scores = lax.dot_general(
+                    masked, key, (((1,), (1,)), ((), ())), preferred_element_type=jnp.float32
+                )
+                scores = jnp.where(allowed, scores * HEAD_DIM ** (-0.5), NEVER)
+                top = jnp.max(scores, -1, keepdims=True)
+                exponent = jnp.exp(scores - top)
+                total = jnp.sum(exponent, -1, keepdims=True)
+                part = jnp.dot(
+                    exponent.astype(jnp.bfloat16), value, preferred_element_type=jnp.float32
+                )
+                mixed.append(part / total)
+            out_ref[0, queries, :] = jnp.where(lower, mixed[0], mixed[1]).astype(jnp.bfloat16)
+
+        for tiles in range(1, length // LANES + 1):
+            pl.when(count == tiles)(functools.partial(window, tiles))
+        return carry
+
+    lax.fori_loop(0, length // QUERY_TILE, tile_step, 0)
+
+
+def attend_back_kernel(
+    start_ref,
+    count_ref,
+    column_ref,
+    line_ref,
+    q_ref,
+    k_ref,
+    v_ref,
+    grad_ref,
+    dq_ref,
+    dk_ref,
+    dv_ref,
+    dk_sum,
+    dv_sum,
+):
+    row = pl.program_id(0)
+    length = k_ref.shape[1]
+    lower = lax.broadcasted_iota(jnp.int32, (QUERY_TILE, LANES), 1) < HEAD_DIM
+    dk_sum[...] = jnp.zeros_like(dk_sum)
+    dv_sum[...] = jnp.zeros_like(dv_sum)
+    scale = HEAD_DIM ** (-0.5)
+
+    def tile_step(tile, carry):
+        begin = pl.multiple_of(start_ref[row, tile] * LANES, LANES)
+        count = count_ref[row, tile]
+        queries = pl.ds(pl.multiple_of(tile * QUERY_TILE, QUERY_TILE), QUERY_TILE)
+
+        def window(tiles):
+            keys = pl.ds(begin, tiles * LANES)
+            query = q_ref[0, queries, :]
+            grad = grad_ref[0, queries, :]
+            key = k_ref[0, keys, :]
+            value = v_ref[0, keys, :]
+            allowed = column_ref[0, keys, :1] == line_ref[0, :1, queries]
+            query_part = []
+            key_part = 0.0
+            value_part = 0.0
+            for head in range(2):
+                mine = lower if head == 0 else jnp.logical_not(lower)
+                head_query = jnp.where(mine, query, jnp.zeros_like(query))
+                head_grad = jnp.where(mine, grad, jnp.zeros_like(grad))
+                scores = lax.dot_general(
+                    key, head_query, (((1,), (1,)), ((), ())), preferred_element_type=jnp.float32
+                )
+                scores = jnp.where(allowed, scores * scale, NEVER)
+                top = jnp.max(scores, 0, keepdims=True)
+                exponent = jnp.exp(scores - top)
+                probs = exponent * (1.0 / jnp.sum(exponent, 0, keepdims=True))
+                grad_probs = lax.dot_general(
+                    value, head_grad, (((1,), (1,)), ((), ())), preferred_element_type=jnp.float32
+                )
+                inner = jnp.sum(grad_probs * probs, 0, keepdims=True)
+                grad_scores = (probs * (grad_probs - inner)).astype(jnp.bfloat16)
+                value_part += jnp.dot(
+                    probs.astype(jnp.bfloat16), head_grad, preferred_element_type=jnp.float32
+                )
+                key_part += jnp.dot(grad_scores, head_query, preferred_element_type=jnp.float32)
+                query_part.append(
+                    lax.dot_general(
+                        grad_scores, key, (((0,), (0,)), ((), ())), preferred_element_type=jnp.float32
+                    )
+                )
+            dq_ref[0, queries, :] = (
+                jnp.where(lower, query_part[0], query_part[1]) * scale
+            ).astype(jnp.bfloat16)
+            dk_sum[keys, :] += key_part
+            dv_sum[keys, :] += value_part
+
+        for tiles in range(1, length // LANES + 1):
+            pl.when(count == tiles)(functools.partial(window, tiles))
+        return carry
+
+    lax.fori_loop(0, length // QUERY_TILE, tile_step, 0)
+    dk_ref[0] = (dk_sum[...] * scale).astype(jnp.bfloat16)
+    dv_ref[0] = dv_sum[...].astype(jnp.bfloat16)
+
+
+def windows_of(segments):
+    heads = segments[:, ::QUERY_TILE]
+    tails = segments[:, QUERY_TILE - 1 :: QUERY_TILE]
+    begin = jnp.sum(segments[:, None, :] < heads[:, :, None], -1, dtype=jnp.int32)
+    end = jnp.sum(segments[:, None, :] <= tails[:, :, None], -1, dtype=jnp.int32)
+    start = begin // LANES
+    return start, (end + LANES - 1) // LANES - start
+
+
+def attention_call(kernel, windows, marks, operands, outputs, scratch):
+    rows, length, width = operands[0].shape
+    block = pl.BlockSpec((1, length, LANES), lambda row, pair, *_: (row, 0, pair))
+    grid = (rows, width // LANES)
+    work = rows * width * length * length
+    return pl.pallas_call(
+        kernel,
+        grid_spec=pltpu.PrefetchScalarGridSpec(
+            num_scalar_prefetch=2,
+            grid=grid,
+            in_specs=[
+                pl.BlockSpec((1, length, LANES), lambda row, pair, *_: (row, 0, 0)),
+                pl.BlockSpec((1, 8, length), lambda row, pair, *_: (row, 0, 0)),
+            ]
+            + [block] * len(operands),
+            out_specs=[block] * outputs,
+            scratch_shapes=scratch,
+        ),
+        out_shape=[jax.ShapeDtypeStruct((rows, length, width), jnp.bfloat16)] * outputs,
+        compiler_params=pltpu.CompilerParams(vmem_limit_bytes=48 * 1024 * 1024),
+        cost_estimate=pl.CostEstimate(
+            flops=4 * len(operands) * work,
+            bytes_accessed=2 * (len(operands) + outputs) * rows * length * width,
+            transcendentals=work // HEAD_DIM,
+        ),
+    )(*windows, *marks, *operands)
+
+
+def norm_stats(values):
+    centred = values - jnp.mean(values, -1, keepdims=True)
+    scale = lax.rsqrt(jnp.mean(centred * centred, -1, keepdims=True) + epsilon)
+    return centred * scale, scale
+
+
+def norm_back_rows(unit, scale, gain_vec, grad):
+    scaled = grad * gain_vec
+    inner = jnp.mean(scaled * unit, -1, keepdims=True)
+    return scale * (scaled - jnp.mean(scaled, -1, keepdims=True) - unit * inner)
+
+
+def gather_rows(piece):
+    return lax.all_gather(piece, "rows", axis=0, tiled=True)
+
+
+def scatter_rows(whole):
+    return lax.psum_scatter(whole, "rows", scatter_dimension=0, tiled=True).astype(jnp.float32)
+
+
+def dot_low(left_side, right_side):
+    return jnp.dot(left_side, right_side, preferred_element_type=jnp.float32)
+
+
+def outer_low(left_side, right_side):
+    return jnp.einsum(
+        "tc,te->ce", left_side, right_side, preferred_element_type=jnp.float32
+    ).astype(jnp.bfloat16)
+
+
+def body_pair(
+    tokens, segments, gain_attn, w_query, w_key, w_value, w_out, gain_ffn, w_up, w_down, cotangent
+):
+    core = lax.axis_index("seq")
+    rows, span, width = tokens.shape
+    flat = rows * span
+
+    w_q = gather_rows(w_query)
+    w_k = gather_rows(w_key)
+    w_v = gather_rows(w_value)
+    w_o = both_cores(gather_rows(w_out), 1)
+    w_u = gather_rows(w_up)
+    down_columns = gather_rows(w_down)
+    down_other = swap_cores(own_half(down_columns, 0, 1 - core))
+    down_mine = own_half(down_columns, 0, core)
+    w_d = jnp.where(
+        core == 0,
+        jnp.concatenate([down_mine, down_other], 1),
+        jnp.concatenate([down_other, down_mine], 1),
+    )
+    w_o_rows = own_half(w_o, 0, core)
+
+    tokens_all = both_cores(tokens, 1).reshape(2 * flat, width).astype(jnp.float32)
+    cot_all = both_cores(cotangent, 1).reshape(2 * flat, width)
+    tokens_own = tokens.reshape(flat, width).astype(jnp.float32)
+    cot_own = cotangent.reshape(flat, width)
+
+    windows = windows_of(segments)
+    marks = (
+        jnp.broadcast_to(segments[:, :, None], segments.shape + (LANES,)),
+        jnp.broadcast_to(segments[:, None, :], (rows, 8, 2 * span)),
+    )
+
+    def split(flat_rows, axis_width):
+        return flat_rows.reshape(rows, 2 * span, axis_width)
+
+    def share(values):
+        wide = split(values, values.shape[-1])
+        received = swap_cores(own_half(wide, 1, 1 - core).astype(jnp.bfloat16))
+        return (own_half(wide, 1, core) + received.astype(jnp.float32)).reshape(flat, -1)
+
+    normed = (norm_stats(tokens_all)[0] * gain_attn).astype(jnp.bfloat16)
+    queries = split(dot_low(normed, w_q).astype(jnp.bfloat16), w_q.shape[1])
+    key_rows = split(dot_low(normed, w_k).astype(jnp.bfloat16), w_k.shape[1])
+    value_rows = split(dot_low(normed, w_v).astype(jnp.bfloat16), w_v.shape[1])
+    (mixed,) = attention_call(
+        attend_kernel, windows, marks, (queries, key_rows, value_rows), 1, []
+    )
+    mixed_other = swap_cores(own_half(mixed, 1, 1 - core))
+    mixed_mine = own_half(mixed, 1, core)
+    mixed_own = jnp.where(
+        core == 0,
+        jnp.concatenate([mixed_mine, mixed_other], 2),
+        jnp.concatenate([mixed_other, mixed_mine], 2),
+    ).reshape(flat, width)
+    residual = tokens_own + dot_low(mixed_own, w_o)
+    unit_two, scale_two = norm_stats(residual)
+    normed_two = (unit_two * gain_ffn).astype(jnp.bfloat16).reshape(rows, span, width)
+    normed_two_all = both_cores(normed_two, 1).reshape(2 * flat, width)
+    hidden_pre = dot_low(normed_two_all, w_u)
+    hidden, gelu_back = jax.vjp(gelu_exact, hidden_pre)
+    hidden_low = hidden.astype(jnp.bfloat16)
+    layer_out = (residual + share(dot_low(hidden_low, w_d))).astype(jnp.bfloat16)
+    grad_pre = gelu_back(times_transposed(cot_all, w_d))[0].astype(jnp.bfloat16)
+    grad_normed_two = share(times_transposed(grad_pre, w_u))
+    grad_residual = cot_own.astype(jnp.float32) + norm_back_rows(
+        unit_two, scale_two, gain_ffn, grad_normed_two
+    )
+    ffn_gain_part = jnp.sum(grad_normed_two * unit_two, 0)
+    grad_attn = grad_residual.astype(jnp.bfloat16).reshape(rows, span, width)
+    grad_attn_all = both_cores(grad_attn, 1).reshape(2 * flat, width)
+    grad_mixed = split(times_transposed(grad_attn_all, w_o_rows).astype(jnp.bfloat16), width // 2)
+    scratch = [pltpu.VMEM((2 * span, LANES), jnp.float32)] * 2
+    grad_queries, grad_keys, grad_values = (
+        grad.reshape(2 * flat, width // 2)
+        for grad in attention_call(
+            attend_back_kernel,
+            windows,
+            marks,
+            (queries, key_rows, value_rows, grad_mixed),
+            3,
+            scratch,
+        )
+    )
+    grad_normed = share(
+        times_transposed(grad_queries, w_q)
+        + times_transposed(grad_keys, w_k)
+        + times_transposed(grad_values, w_v)
+    )
+    unit_own, scale_own = norm_stats(tokens_own)
+    token_grad = grad_residual + norm_back_rows(unit_own, scale_own, gain_attn, grad_normed)
+    attn_gain_part = jnp.sum(grad_normed * unit_own, 0)
+    gain_attn_grad, gain_ffn_grad = lax.psum((attn_gain_part, ffn_gain_part), ("rows", "seq"))
+
+    def to_columns(row_half):
+        received = swap_cores(own_half(row_half, 1, 1 - core))
+        kept = own_half(row_half, 1, core)
+        return jnp.where(
+            core == 0,
+            jnp.concatenate([kept, received], 0),
+            jnp.concatenate([received, kept], 0),
+        )
+
+    down_grad = scatter_rows(to_columns(outer_low(hidden_low, cot_all)))
+    up_grad = scatter_rows(outer_low(normed_two_all, grad_pre))
+    out_grad = scatter_rows(to_columns(outer_low(mixed.reshape(2 * flat, -1), grad_attn_all)))
+    query_grad = scatter_rows(outer_low(normed, grad_queries))
+    key_grad = scatter_rows(outer_low(normed, grad_keys))
+    value_grad = scatter_rows(outer_low(normed, grad_values))
+    return (
+        layer_out.reshape(rows, span, width),
+        token_grad.reshape(rows, span, width),
+        gain_attn_grad,
+        query_grad,
+        key_grad,
+        value_grad,
+        out_grad,
+        gain_ffn_grad,
+        up_grad,
+        down_grad,
+    )
+
+
 def solution(mesh):
+    paired = mesh.shape["seq"] == 2 and mesh.shape["rows"] == 16
+    program = body_pair if paired else body
     return jax.shard_map(
-        body,
+        program,
         mesh=mesh,
         in_specs=(
             P("rows", "seq", None),

time: 2750 us -> 1270 us (0.46)
  waiting for transfers between devices: 1980 us -> 754 us
  matrix products: 445 us -> 225 us
  Pallas kernels: 0 us -> 113 us
  local copies, waits for them, and re-layouts: 110 us -> 22.2 us
  other arithmetic: 124 us -> 91 us
    reduce_scatter x6, waiting for transfers between devices: 1550 us -> 421 us  [scatter_rows(): lax.psum_scatter(whole, 'rows', scatter_dimension=0, tiled=True)]
    dot_general x18 -> x12, matrix products: 367 us -> 149 us  [the longest x6 76.8 us: dot_low(): return jnp.dot(left_side, right_side, preferred_element_type=jnp.float32)]
    all_gather x8 -> x6, waiting for transfers between devices: 432 us -> 313 us  [gather_rows(): return lax.all_gather(piece, 'rows', axis=0, tiled=True)]
    pallas_call x0 -> x2, Pallas kernels: none -> 113 us  [attention_call(): pl.pallas_call(kernel, grid_spec=pltpu.PrefetchScalarGridSpec(num_scalar_...]
    convert_element_type x6 -> x9, other arithmetic: 76.5 us -> 23.5 us  [the longest x6 10.3 us: scatter_rows(): lax.psum_scatter(whole, 'rows', scatter_dimension=0, tiled=True)]
    select_n x0 -> x6, other arithmetic: none -> 35.6 us  [the longest x4 20.9 us: both_cores(): jnp.where(first, jnp.concatenate([values, other], axis), jnp.concatenate(...]
  transfers between devices with their start and end apart: 14 -> 24, of which waited for: 7 -> 16; matrix products, arithmetic and copies ran while one was open for 14% -> 20% of each run, Pallas kernels for 0% -> 3%
where the time goes in v1:
time: 1270 us; the launch traced here: 1260 us
  waiting for transfers between devices  754 us (59%)
  matrix products  225 us (18%)
  Pallas kernels  113 us (9%)
  other arithmetic  91 us (7%)
  blocking collectives  41 us (3%)
  local copies, waits for them, and re-layouts  22.2 us (2%)
  between operations  15.1 us (1%)
    reduce_scatter x6, waiting for transfers between devices, scatter_rows(): lax.psum_scatter(whole, 'rows', scatter_dimension=0, tiled=True)  421 us
    all_gather x6, waiting for transfers between devices, gather_rows(): return lax.all_gather(piece, 'rows', axis=0, tiled=True)  313 us
    pallas_call x2, Pallas kernels, attention_call(): pl.pallas_call(kernel, grid_spec=pltpu.PrefetchScalarGridSpec(num_scalar_...  113 us
    dot_general x6, matrix products, dot_low(): return jnp.dot(left_side, right_side, preferred_element_type=jnp.float32)  76.8 us
    dot_general x6, matrix products, times_transposed(): jnp.einsum('te,de->td', left_side, right_side, preferred_element_type=jnp...  75.5 us
    dot_general x6, matrix products, outer_low(): jnp.einsum('tc,te->ce', left_side, right_side, preferred_element_type=jnp...  72.3 us
    psum x1, blocking collectives, body_pair(): lax.psum((attn_gain_part, ffn_gain_part), ('rows', 'seq'))  41 us
  transfers between devices with their start and end apart: 24, of which 16 were waited for; matrix products, arithmetic and copies ran while one was open for 20% of the time, Pallas kernels for 3%

profile of v1, /device:TPU:0, one launch (start us, length us, event | category | flops | bytes accessed | tf_op | source)
XLA Modules:
  0.0 1264.6 jit_solution(7366407843491532033)
XLA Ops:
  12.8 0.9 convert_reduce_fusion.2
  13.7 2.3 collective-permute-done
  16.0 5.3 convert_reduce_fusion
  21.9 4.7 multiply_reduce_fusion
  27.3 6.6 fusion.2
  33.9 37.6 %all-gather.13.cloned.1.call-done = bf16[1280,640]{1,0:T(8,128)(2,1)} async-done(((bf16[80,640]{1,0:T(8,128)(2,1)}), bf16[1280,640]{1,0:T(8,128)(2,1)}) %all-gather.13.cloned.1.call-update) | async-done | bytes 1638416 | tf_op jit(solution)/shard_map/all_gather | solution.py:468
  71.6 59.7 %all-gather.7.cloned.1.call-done = bf16[1280,640]{1,0:T(8,128)(2,1)} async-done(((bf16[80,640]{1,0:T(8,128)(2,1)}), bf16[1280,640]{1,0:T(8,128)(2,1)}) %all-gather.7.cloned.1.call-update) | async-done | bytes 1638416 | tf_op jit(solution)/shard_map/all_gather | solution.py:468
  131.2 8.7 convolution_convert_fusion.5
  140.0 51.0 %all-gather.9.cloned.1.call-done = bf16[1280,640]{1,0:T(8,128)(2,1)} async-done(((bf16[80,640]{1,0:T(8,128)(2,1)}), bf16[1280,640]{1,0:T(8,128)(2,1)}) %all-gather.9.cloned.1.call-update) | async-done | bytes 1638416 | tf_op jit(solution)/shard_map/all_gather | solution.py:468
  190.9 8.8 convolution_convert_fusion.4
  199.7 50.8 %all-gather.11.cloned.1.call-done = bf16[1280,640]{1,0:T(8,128)(2,1)} async-done(((bf16[80,640]{1,0:T(8,128)(2,1)}), bf16[1280,640]{1,0:T(8,128)(2,1)}) %all-gather.11.cloned.1.call-update) | async-done | bytes 1638416 | tf_op jit(solution)/shard_map/all_gather | solution.py:468
  250.5 8.8 convolution_convert_fusion.3
  259.6 40.4 %shard_map.186 = bf16[2,1024,640]{2,1,0:T(8,128)(2,1)S(1)} custom-call(s32[2,4]{1,0:T(2,128)S(1)} %get-tuple-element.31.start_ref, s32[2,4]{1,0:T(2,128)S(1)} %get-tuple-element.30.count_ref, s32[2,1024,128]{2,1,0:T(8,128)S(1)} %broadcast_in_dim.4.column_ref, s32[2,8,1024]{2,1,0:T(8,128)S(1)} %broadcast_in_dim.5.line_ref, bf16[2,1024,640]{2,1,0:T(8,128)(2,1)} %bitcast.161, ...), custom_call_target="tpu_custom_call" | custom-call | flops 16106127360 | bytes 10485760 | tf_op jit(solution)/shard_map/pallas_call | solution.py:432
  300.9 3.6 collective-permute-done.1
  304.5 5.7 fusion.41
  312.7 7.5 maximum_select_fusion.4
  320.2 28.4 %all-gather.17.cloned.1.call-done = bf16[5120,640]{1,0:T(8,128)(2,1)} async-done(((bf16[320,640]{1,0:T(8,128)(2,1)}), bf16[5120,640]{1,0:T(8,128)(2,1)}) %all-gather.17.cloned.1.call-update) | async-done | bytes 6553616 | tf_op jit(solution)/shard_map/all_gather | solution.py:468
  348.6 6.3 constant_dynamic-slice_fusion.5
  354.9 5.8 maximum_select_fusion.3
  360.7 85.4 %all-gather.15.cloned.1.call-done = bf16[1280,2560]{1,0:T(8,128)(2,1)} async-done(((bf16[80,2560]{1,0:T(8,128)(2,1)}), bf16[1280,2560]{1,0:T(8,128)(2,1)}) %all-gather.15.cloned.1.call-update) | async-done | bytes 6553616 | tf_op jit(solution)/shard_map/all_gather | solution.py:468
  446.1 22.3 %multiply_convert_fusion = (bf16[2048,2560]{1,0:T(8,128)(2,1)}, f32[2048,2560]{1,0:T(8,128)}) fusion(bf16[2048,1280]{1,0:T(8,128)(2,1)} %bitcast.149, bf16[1280,2560]{1,0:T(8,128)(2,1)} %all-gather.15.cloned.1.call-done), kind=kOutput, calls=%fused_computation.1 | convolution fusion | flops 13447987200 | bytes 43253760 | tf_op jit(solution)/shard_map/dot_general | solution.py:476
  468.4 28.6 %add_convert_fusion = bf16[2048,2560]{1,0:T(8,128)(2,1)} fusion(f32[2048,2560]{1,0:T(8,128)} %get-tuple-element.52, bf16[2048,1280]{1,0:T(8,128)(2,1)} %bitcast.147, bf16[2560,640]{1,0:T(8,128)(2,1)} %collective-permute-done.4, bf16[2560,640]{1,0:T(8,128)(2,1)S(1)} %copy-done.14, pred[]{:T(512)S(6)} %eq.2), kind=kOutput, calls=%fused_computation | convolution fusion | flops 13519421440 | bytes 43253760 | tf_op jit(solution)/shard_map/te,de->td/dot_general | solution.py:30
  497.0 16.4 %fusion.42 = f32[2048,1280]{1,0:T(8,128)S(1)} fusion(bf16[2048,2560]{1,0:T(8,128)(2,1)} %add_convert_fusion, bf16[1280,2560]{1,0:T(8,128)(2,1)S(1)} %copy-done.31), kind=kOutput, calls=%fused_computation.120 | convolution fusion | flops 13421772800 | bytes 27525120 | tf_op jit(solution)/shard_map/te,de->td/dot_general | solution.py:30
  513.4 3.8 copy-done.12
  517.6 22.5 %fusion.30 = f32[2048,1280]{1,0:T(8,128)} fusion(bf16[2048,2560]{1,0:T(8,128)(2,1)} %get-tuple-element.51, bf16[2560,640]{1,0:T(8,128)(2,1)} %collective-permute-done.4, bf16[2560,640]{1,0:T(8,128)(2,1)S(1)} %copy-done.14, pred[]{:T(512)S(6)} %eq.2), kind=kOutput, calls=%fused_computation.78 | convolution fusion | flops 13451264000 | bytes 27525120 | tf_op jit(solution)/shard_map/dot_general | solution.py:476
  540.1 2.9 dynamic-slice_convert_fusion.2
  543.5 4.2 multiply_reduce_fusion.2
  547.8 2.8 fusion.7
  551.3 5.9 fusion.40
  557.2 3.7 maximum_select_fusion.6
  560.9 1.3 collective-permute-done.8
  562.2 3.9 maximum_select_fusion.5
  566.1 5.6 convolution_convert_fusion.2
  571.8 72.3 %shard_map.187 = (bf16[2,1024,640]{2,1,0:T(8,128)(2,1)S(1)}, bf16[2,1024,640]{2,1,0:T(8,128)(2,1)}, bf16[2,1024,640]{2,1,0:T(8,128)(2,1)}) custom-call(s32[2,4]{1,0:T(2,128)S(1)} %get-tuple-element.31.start_ref, s32[2,4]{1,0:T(2,128)S(1)} %get-tuple-element.30.count_ref, s32[2,1024,128]{2,1,0:T(8,128)S(1)} %copy-done.3, s32[2,8,1024]{2,1,0:T(8,128)S(1)} %copy-done.5, ...), custom_call_target="tpu_custom_call" | custom-call | flops 21474836480 | bytes 18350080 | tf_op jit(solution)/shard_map/pallas_call | solution.py:432
  644.0 1.5 copy-done.6
  645.5 8.6 fusion.18
  654.2 9.3 fusion.19
  663.6 9.9 fusion.20
  673.6 6.1 fusion.21
  680.1 2.1 collective-permute-done.10
  682.2 1.7 maximum_select_fusion.9
  684.0 20.2 %convolution_convert_fusion.1 = bf16[1280,2560]{1,0:T(8,128)(2,1)} fusion(bf16[2048,1280]{1,0:T(8,128)(2,1)} %bitcast.150, bf16[2048,2560]{1,0:T(8,128)(2,1)} %add_convert_fusion), kind=kOutput, calls=%fused_computation.4 | convolution fusion | flops 13425049600 | bytes 22282240 | tf_op jit(solution)/shard_map/tc,te->ce/dot_general | solution.py:480
  704.4 18.2 %convolution_convert_fusion = bf16[2560,1280]{1,0:T(8,128)(2,1)S(1)} fusion(bf16[2048,2560]{1,0:T(8,128)(2,1)} %get-tuple-element.51, bf16[2048,1280]{1,0:T(8,128)(2,1)} %bitcast.148), kind=kOutput, calls=%fused_computation.3 | convolution fusion | flops 13425049600 | bytes 22282240 | tf_op jit(solution)/shard_map/tc,te->ce/dot_general | solution.py:480
  723.8 5.5 collective-permute-done.11
  729.2 13.1 %maximum_select_fusion.1 = bf16[5120,640]{1,0:T(8,128)(2,1)} fusion(bf16[2560,640]{1,0:T(8,128)(2,1)S(1)} %collective-permute-done.11, bf16[2560,640]{1,0:T(8,128)(2,1)S(1)} %get-tuple-element.32, pred[]{:T(512)S(6)} %eq.2), kind=kLoop, calls=%fused_computation.14 | loop fusion | flops 29491200 | bytes 13107201 | tf_op jit(solution)/shard_map/jit(_where)/select_n | solution.py:582
  742.3 1.7 copy-done.7
  744.0 8.4 fusion.43
  752.5 6.8 fusion.44
  759.2 9.7 add_add_fusion
  769.8 1.0 copy-done.10
  772.0 2.3 collective-permute-done.9
  774.3 4.3 fusion.14
  778.7 41.0 %all-reduce = (f32[1280]{0:T(1024)}, f32[1280]{0:T(1024)}) all-reduce(f32[1280]{0:T(1024)S(1)} %get-tuple-element.18, f32[1280]{0:T(1024)S(1)} %copy-done.29), channel_id=1, replica_groups=mesh['rows'=16,'seq'=2] {'rows','seq'}, use_global_device_ids=true, to_apply=%region_13.14 | all-reduce | flops 2560 | bytes 20480 | tf_op jit(solution)/shard_map/psum | solution.py:577
  819.7 6.4 fusion.6
  826.2 1.6 convert_element_type.154
  827.7 1.6 convert_element_type.156
  829.3 61.9 %reduce-scatter.11.cloned.1.call-done = bf16[80,640]{1,0:T(8,128)(2,1)} async-done(((bf16[1280,640]{1,0:T(8,128)(2,1)}), bf16[80,640]{1,0:T(8,128)(2,1)}) %reduce-scatter.11.cloned.1.call-update) | async-done | bytes 102416 | tf_op jit(solution)/shard_map/reduce_scatter | solution.py:472
  891.3 1.6 convert_element_type.158
  892.9 76.7 %reduce-scatter.13.cloned.1.call-done = bf16[80,640]{1,0:T(8,128)(2,1)} async-done(((bf16[1280,640]{1,0:T(8,128)(2,1)}), bf16[80,640]{1,0:T(8,128)(2,1)}) %reduce-scatter.13.cloned.1.call-update) | async-done | bytes 102416 | tf_op jit(solution)/shard_map/reduce_scatter | solution.py:472
  969.6 1.6 convert_element_type.160
  971.2 138.7 %reduce-scatter.15.cloned.1.call-done = bf16[80,2560]{1,0:T(8,128)(2,1)} async-done(((bf16[1280,2560]{1,0:T(8,128)(2,1)}), bf16[80,2560]{1,0:T(8,128)(2,1)}) %reduce-scatter.15.cloned.1.call-update) | async-done | bytes 409616 | tf_op jit(solution)/shard_map/reduce_scatter | solution.py:472
  1109.9 2.0 convert_element_type.162
  1111.8 143.6 %reduce-scatter.17.cloned.1.call-done = bf16[320,640]{1,0:T(8,128)(2,1)} async-done(((bf16[5120,640]{1,0:T(8,128)(2,1)}), bf16[320,640]{1,0:T(8,128)(2,1)}) %reduce-scatter.17.cloned.1.call-update) | async-done | bytes 409616 | tf_op jit(solution)/shard_map/reduce_scatter | solution.py:472
  1255.5 1.9 convert_element_type.164
  (151 shorter events, 16.0 us)
Async XLA Ops:
  7.2 14.8 %copy-start.8 = (bf16[2,512,1280]{2,1,0:T(8,128)(2,1)S(1)}, bf16[2,512,1280]{2,1,0:T(8,128)(2,1)}, u32[]{:S(2)}) copy-start(bf16[2,512,1280]{2,1,0:T(8,128)(2,1)} %param.11) | copy-start | bytes 7864324
  7.2 64.4 %all-gather.13.cloned.1.call-start = ((), (), s32[]{:S(2)}) async-start(), calls=%async_computation.9 | async-start | bytes 1740800 | tf_op jit(solution)/shard_map/all_gather | solution.py:468
  7.9 123.3 %all-gather.7.cloned.1.call-start = ((), (), s32[]{:S(2)}) async-start(), calls=%async_computation.6 | async-start | bytes 1740800 | tf_op jit(solution)/shard_map/all_gather | solution.py:468
  8.7 182.3 %all-gather.9.cloned.1.call-start = ((), (), s32[]{:S(2)}) async-start(), calls=%async_computation.7 | async-start | bytes 1740800 | tf_op jit(solution)/shard_map/all_gather | solution.py:468
  9.4 241.1 %all-gather.11.cloned.1.call-start = ((), (), s32[]{:S(2)}) async-start(), calls=%async_computation.8 | async-start | bytes 1740800 | tf_op jit(solution)/shard_map/all_gather | solution.py:468
  10.0 338.7 %all-gather.17.cloned.1.call-start = ((), (), s32[]{:S(2)}) async-start(), calls=%async_computation.11 | async-start | bytes 6963200 | tf_op jit(solution)/shard_map/all_gather | solution.py:468
  10.6 435.6 %all-gather.15.cloned.1.call-start = ((), (), s32[]{:S(2)}) async-start(), calls=%async_computation.10 | async-start | bytes 6963200 | tf_op jit(solution)/shard_map/all_gather | solution.py:468
  10.6 5.4 collective-permute-start
  11.2 815.0 %reduce-scatter.7.cloned.1.call-start = ((), (), s32[]{:S(2)}) async-start(), calls=%async_computation.12 | async-start | bytes 1740800 | tf_op jit(solution)/shard_map/reduce_scatter | solution.py:472
  13.7 13.6 %copy-start.23 = (f32[1280]{0:T(1024)S(1)}, f32[1280]{0:T(1024)}, u32[]{:S(2)}) copy-start(f32[1280]{0:T(1024)} %param.13) | copy-start | bytes 15364
  21.3 0.6 copy-start.27
  71.6 232.9 %collective-permute-start.2 = (bf16[1280,640]{1,0:T(8,128)(2,1)}, bf16[1280,640]{1,0:T(8,128)(2,1)}, u32[]{:S(2)}, u32[]{:S(2)}) collective-permute-start(bf16[1280,640]{1,0:T(8,128)(2,1)} %all-gather.13.cloned.1.call-done), channel_id=1, source_target_pairs={{0,1},{1,0},{2,3},{3,2},{4,5},{5,4},{6,7},{7,6},{8,9},{9,8},{10,11... | collective-permute-start | bytes 4915208 | tf_op jit(solution)/shard_map/ppermute | solution.py:283
  199.7 59.5 %copy-start.22 = (s32[2,1024]{1,0:T(2,128)S(1)}, s32[2,1024]{1,0:T(2,128)}, u32[]{:S(2)}) copy-start(s32[2,1024]{1,0:T(2,128)} %param.12) | copy-start | bytes 24580
  259.6 40.4 %copy-start.2 = (s32[2,1024,128]{2,1,0:T(8,128)}, s32[2,1024,128]{2,1,0:T(8,128)S(1)}, u32[]{:S(2)}) copy-start(s32[2,1024,128]{2,1,0:T(8,128)S(1)} %broadcast_in_dim.4.column_ref) | copy-start | bytes 3145732
  259.6 40.4 %copy-start.4 = (s32[2,8,1024]{2,1,0:T(8,128)}, s32[2,8,1024]{2,1,0:T(8,128)S(1)}, u32[]{:S(2)}) copy-start(s32[2,8,1024]{2,1,0:T(8,128)S(1)} %broadcast_in_dim.5.line_ref) | copy-start | bytes 196612
  300.0 10.2 copy-start
  300.0 4.4 copy-start.16
  300.3 4.2 collective-permute-start.1
  300.4 12.3 collective-permute-start.6
  310.2 2.3 copy-start.11
  310.2 0.7 copy-start.18
  310.3 2.3 copy-start.20
  311.0 1.6 copy-start.25
  312.6 42.4 %collective-permute-start.3 = (bf16[2,512,1280]{2,1,0:T(8,128)(2,1)S(1)}, bf16[2,512,1280]{2,1,0:T(8,128)(2,1)}, u32[]{:S(2)}, u32[]{:S(2)}) collective-permute-start(bf16[2,512,1280]{2,1,0:T(8,128)(2,1)S(1)} %bitcast.136), channel_id=1, source_target_pairs={{0,1},{1,0},{2,3},{3,2},{4,5},{5,4},{6,7},{7,6},{8,9},{9,8},{10,11... | collective-permute-start | bytes 7864328 | tf_op jit(solution)/shard_map/ppermute | solution.py:283
  354.9 113.5 %collective-permute-start.4 = (bf16[2560,640]{1,0:T(8,128)(2,1)}, bf16[2560,640]{1,0:T(8,128)(2,1)}, u32[]{:S(2)}, u32[]{:S(2)}) collective-permute-start(bf16[2560,640]{1,0:T(8,128)(2,1)} %get-tuple-element.35), channel_id=1, source_target_pairs={{0,1},{1,0},{2,3},{3,2},{4,5},{5,4},{6,7},{7,6},{8,9},{9,8},{10,11... | collective-permute-start | bytes 9830408 | tf_op jit(solution)/shard_map/ppermute | solution.py:283
  446.1 22.3 %copy-start.14 = (bf16[2560,640]{1,0:T(8,128)(2,1)S(1)}, bf16[2560,640]{1,0:T(8,128)(2,1)}, u32[]{:S(2)}) copy-start(bf16[2560,640]{1,0:T(8,128)(2,1)} %get-tuple-element.34) | copy-start | bytes 9830404
  468.4 28.6 %copy-start.31 = (bf16[1280,2560]{1,0:T(8,128)(2,1)S(1)}, bf16[1280,2560]{1,0:T(8,128)(2,1)}, u32[]{:S(2)}) copy-start(bf16[1280,2560]{1,0:T(8,128)(2,1)} %all-gather.15.cloned.1.call-done) | copy-start | bytes 19660804
  513.4 3.9 copy-start.12
  517.5 26.0 %collective-permute-start.7 = (bf16[2,512,1280]{2,1,0:T(8,128)(2,1)S(1)}, bf16[2,512,1280]{2,1,0:T(8,128)(2,1)}, u32[]{:S(2)}, u32[]{:S(2)}) collective-permute-start(bf16[2,512,1280]{2,1,0:T(8,128)(2,1)S(1)} %dynamic-slice_convert_fusion.1), channel_id=1, source_target_pairs={{0,1},{1,0},{2,3},{3,2},{4,5},{5,4},{6,7},{7,6},{8,9},{9,8},{10,11... | collective-permute-start | bytes 7864328 | tf_op jit(solution)/shard_map/ppermute | solution.py:283
  540.1 3.5 copy-start.19
  540.1 7.7 slice-start
  543.0 4.8 slice-start.1
  543.0 4.8 copy-start.21
  543.0 4.8 copy-start.26
  543.0 7.7 collective-permute-start.5
  543.5 7.2 slice-start.2
  543.5 7.2 slice-start.3
  547.8 2.9 slice-start.4
  557.2 5.0 collective-permute-start.8
  566.1 5.6 copy-start.13
  566.1 5.6 copy-start.3
  566.1 5.6 copy-start.5
  571.7 73.8 %copy-start.9 = (bf16[2,512,1280]{2,1,0:T(8,128)(2,1)S(1)}, bf16[2,512,1280]{2,1,0:T(8,128)(2,1)}, u32[]{:S(2)}) copy-start(bf16[2,512,1280]{2,1,0:T(8,128)(2,1)} %param.11) | copy-start | bytes 7864324
  571.7 73.8 %copy-start.24 = (f32[1280]{0:T(1024)S(1)}, f32[1280]{0:T(1024)}, u32[]{:S(2)}) copy-start(f32[1280]{0:T(1024)} %param.13) | copy-start | bytes 15364
  571.7 73.8 %copy-start.28 = (f32[2,1024]{1,0:T(2,128)S(1)}, f32[2,1024]{1,0:T(2,128)}, u32[]{:S(2)}) copy-start(f32[2,1024]{1,0:T(2,128)} %copy-done.27) | copy-start | bytes 24580
  571.7 73.8 %copy-start.30 = (f32[2,1024]{1,0:T(2,128)S(1)}, f32[2,1024]{1,0:T(2,128)}, u32[]{:S(2)}) copy-start(f32[2,1024]{1,0:T(2,128)} %get-tuple-element.41) | copy-start | bytes 24580
  644.0 1.5 copy-start.6
  654.1 173.6 %reduce-scatter.9.cloned.1.call-start = ((), (), s32[]{:S(2)}) async-start(), calls=%async_computation.13 | async-start | bytes 1740800 | tf_op jit(solution)/shard_map/reduce_scatter | solution.py:472
  663.5 227.8 %reduce-scatter.11.cloned.1.call-start = ((), (), s32[]{:S(2)}) async-start(), calls=%async_computation.14 | async-start | bytes 1740800 | tf_op jit(solution)/shard_map/reduce_scatter | solution.py:472
  663.6 10.0 copy-start.1
  673.5 296.1 %reduce-scatter.13.cloned.1.call-start = ((), (), s32[]{:S(2)}) async-start(), calls=%async_computation.15 | async-start | bytes 1740800 | tf_op jit(solution)/shard_map/reduce_scatter | solution.py:472
  679.8 2.4 collective-permute-start.10
  684.0 425.9 %reduce-scatter.15.cloned.1.call-start = ((), (), s32[]{:S(2)}) async-start(), calls=%async_computation.16 | async-start | bytes 6963200 | tf_op jit(solution)/shard_map/reduce_scatter | solution.py:472
  704.3 551.2 %reduce-scatter.17.cloned.1.call-start = ((), (), s32[]{:S(2)}) async-start(), calls=%async_computation.17 | async-start | bytes 6963200 | tf_op jit(solution)/shard_map/reduce_scatter | solution.py:472
  723.1 6.1 collective-permute-start.11
  742.3 1.7 copy-start.7
  744.0 8.4 copy-start.32
  744.0 8.4 copy-start.33
  752.4 6.8 copy-start.15
  752.4 6.8 copy-start.17
  769.0 1.7 copy-start.10
  769.3 5.0 collective-permute-start.9
  774.3 4.4 copy-start.29
Sparse Core Ops, SparseCore 0:
  10.7 60.7 all-gather.12
  74.2 56.9 all-gather.6
  133.9 56.9 all-gather.8
  193.5 56.9 all-gather.10
  253.0 95.5 all-gather.16
  351.2 94.9 all-gather.14
  654.2 79.9 reduce-scatter.6
  736.6 76.4 reduce-scatter.8
  815.3 75.8 reduce-scatter.10
  893.5 76.0 reduce-scatter.12
  971.9 137.9 reduce-scatter.14
  1112.2 143.2 reduce-scatter.16

commit v2 on v1

--- a/solution.py
+++ b/solution.py
@@ -464,12 +464,233 @@
     return scale * (scaled - jnp.mean(scaled, -1, keepdims=True) - unit * inner)
 
 
-def gather_rows(piece):
-    return lax.all_gather(piece, "rows", axis=0, tiled=True)
-
-
-def scatter_rows(whole):
-    return lax.psum_scatter(whole, "rows", scatter_dimension=0, tiled=True).astype(jnp.float32)
+Z_SIZE = 4
+RING = (0, 1, 3, 2)
+PLACE = (0, 1, 3, 2)
+
+
+def chip_place():
+    index = lax.axis_index("rows")
+    return index // 4, (index // 2) % 2, index % 2
+
+
+def swap_x(values):
+    return lax.ppermute(values, "rows", [(row, row ^ 1) for row in range(16)])
+
+
+def swap_y(values):
+    return lax.ppermute(values, "rows", [(row, row ^ 2) for row in range(16)])
+
+
+def next_z(values):
+    pairs = []
+    for place in range(Z_SIZE):
+        here, there = RING[place], RING[(place + 1) % Z_SIZE]
+        pairs += [(here * 4 + rest, there * 4 + rest) for rest in range(4)]
+    return lax.ppermute(values, "rows", pairs)
+
+
+def ring_place():
+    zed = chip_place()[0]
+    return jnp.where(zed == 2, 3, jnp.where(zed == 3, 2, zed))
+
+
+def tie(value, *after):
+    return lax.optimization_barrier((value, after))[0]
+
+
+def natural_z(steps):
+    place = ring_place()
+    stack = jnp.stack(steps)
+    return jnp.stack(
+        [
+            lax.dynamic_index_in_dim(stack, (place - PLACE[zed]) % Z_SIZE, 0, keepdims=False)
+            for zed in range(Z_SIZE)
+        ]
+    )
+
+
+def load_pieces(place_ref, pieces, target_of, sems):
+    copies = []
+    for part in range(2):
+        for index in range(4):
+            piece = pieces[part * 4 + index]
+            row_y, row_x = place_ref[1] ^ (index // 2), place_ref[2] ^ (index % 2)
+            for zed in range(Z_SIZE):
+                target = target_of(part, zed, row_y, row_x, piece)
+                copies.append(pltpu.make_async_copy(piece.at[zed], target, sems.at[len(copies)]))
+                copies[-1].start()
+    return copies
+
+
+def column_target(whole_ref):
+    def target_of(part, zed, row_y, row_x, piece):
+        _, depth, wide = piece.shape
+        row = pl.multiple_of(((zed * 2 + row_y) * 2 + row_x) * depth, 16)
+        left = 0 if part == 0 else whole_ref.shape[1] - wide
+        return whole_ref.at[pl.ds(row, depth), pl.ds(left, wide)]
+
+    return target_of
+
+
+def assemble_columns_kernel(place_ref, *refs):
+    *pieces, out_ref, sems = refs
+    for copy in load_pieces(place_ref, pieces, column_target(out_ref), sems):
+        copy.wait()
+
+
+def assemble_rows_kernel(place_ref, *refs):
+    *pieces, out_ref, sems = refs
+
+    def target_of(part, zed, row_y, row_x, piece):
+        depth = piece.shape[1]
+        half = (zed // 2) ^ place_ref[3]
+        row = (((zed % 2) * 2 + row_y) * 2 + row_x) * 2 * depth + part * depth
+        return out_ref.at[half, pl.ds(pl.multiple_of(row, 16), depth), :]
+
+    for copy in load_pieces(place_ref, pieces, target_of, sems):
+        copy.wait()
+
+
+def place_vector():
+    return jnp.stack(chip_place() + (lax.axis_index("seq"),)).astype(jnp.int32)
+
+
+def assemble(kernel, shape, parts):
+    return pl.pallas_call(
+        kernel,
+        grid_spec=pltpu.PrefetchScalarGridSpec(
+            num_scalar_prefetch=1,
+            grid=(1,),
+            in_specs=[pl.BlockSpec(memory_space=pl.ANY)] * 8,
+            out_specs=pl.BlockSpec(shape, lambda step, *_: (0,) * len(shape)),
+            scratch_shapes=[pltpu.SemaphoreType.DMA((32,))],
+        ),
+        out_shape=jax.ShapeDtypeStruct(shape, parts[0][0].dtype),
+        compiler_params=pltpu.CompilerParams(vmem_limit_bytes=40 * 1024 * 1024),
+    )(place_vector(), *parts[0], *parts[1])
+
+
+FFN_TILE = 256
+FFN_CHUNK = 640
+
+
+def feed_forward_kernel(
+    place_ref, normed_ref, cot_ref, *refs, begun
+):
+    up_pieces, refs = refs[:8], refs[8:]
+    down_mine, down_other = refs[:2]
+    refs = refs[4:] if begun else refs[2:]
+    hidden_ref, grad_pre_ref, y_ref, grad_ref, up_ref, down_ref, up_sems, down_sems = refs
+    step = pl.program_id(0)
+    wide = down_mine.shape[1]
+
+    def copies():
+        down = []
+        for index, piece in enumerate((down_mine, down_other)):
+            left = pl.multiple_of((place_ref[3] ^ index) * wide, 128)
+            target = down_ref.at[:, pl.ds(left, wide)]
+            down.append(pltpu.make_async_copy(piece, target, down_sems.at[index]))
+        return down
+
+    @pl.when(step == 0)
+    def _():
+        waits = load_pieces(place_ref, up_pieces, column_target(up_ref), up_sems)
+        waits += copies()
+        for copy in waits[-2:]:
+            copy.start()
+        for copy in waits:
+            copy.wait()
+
+    normed = normed_ref[...]
+    cot = cot_ref[...]
+    y_sum = grad_sum = 0.0
+    for chunk in range(hidden_ref.shape[1] // FFN_CHUNK):
+        units = pl.ds(chunk * FFN_CHUNK, FFN_CHUNK)
+        up, down = up_ref[:, units], down_ref[units, :]
+        pre = jnp.dot(normed, up, preferred_element_type=jnp.float32)
+        grad_hidden = lax.dot_general(
+            cot, down, (((1,), (1,)), ((), ())), preferred_element_type=jnp.float32
+        )
+        phi = 0.5 + 0.5 * lax.erf(pre * root_half)
+        hidden = (pre * phi).astype(jnp.bfloat16)
+        slope = phi + pre * (jnp.exp(-0.5 * pre * pre) * root_two_pi)
+        grad_pre = (grad_hidden * slope).astype(jnp.bfloat16)
+        hidden_ref[:, units] = hidden
+        grad_pre_ref[:, units] = grad_pre
+        y_sum += jnp.dot(hidden, down, preferred_element_type=jnp.float32)
+        grad_sum += lax.dot_general(
+            grad_pre, up, (((1,), (1,)), ((), ())), preferred_element_type=jnp.float32
+        )
+    y_ref[...] = y_sum.astype(jnp.bfloat16)
+    grad_ref[...] = grad_sum.astype(jnp.bfloat16)
+
+
+root_two_pi = 0.3989422804014327
+
+
+def feed_forward(normed, cot, up_parts, down_mine, down_other, begun=()):
+    tokens, width = normed.shape
+    units = down_mine.shape[0]
+    tiles = tokens // FFN_TILE
+    offset = tiles if begun else 0
+    tile = pl.BlockSpec((FFN_TILE, width), lambda step, *_: (step, 0))
+    wide_tile = pl.BlockSpec((FFN_TILE, units), lambda step, *_: (step + offset, 0))
+    anywhere = pl.BlockSpec(memory_space=pl.ANY)
+    wide_shape = jax.ShapeDtypeStruct((2 * tokens, units), jnp.bfloat16)
+    shape = jax.ShapeDtypeStruct((tokens, width), jnp.bfloat16)
+    return pl.pallas_call(
+        functools.partial(feed_forward_kernel, begun=bool(begun)),
+        grid_spec=pltpu.PrefetchScalarGridSpec(
+            num_scalar_prefetch=1,
+            grid=(tiles,),
+            in_specs=[tile, tile] + [anywhere] * (10 + len(begun)),
+            out_specs=[wide_tile, wide_tile, tile, tile],
+            scratch_shapes=[
+                pltpu.VMEM((width, units), jnp.bfloat16),
+                pltpu.VMEM((units, width), jnp.bfloat16),
+                pltpu.SemaphoreType.DMA((32,)),
+                pltpu.SemaphoreType.DMA((2,)),
+            ],
+        ),
+        out_shape=[wide_shape, wide_shape, shape, shape],
+        input_output_aliases={13: 0, 14: 1} if begun else {},
+        compiler_params=pltpu.CompilerParams(vmem_limit_bytes=56 * 1024 * 1024),
+        cost_estimate=pl.CostEstimate(
+            flops=8 * tokens * width * units,
+            bytes_accessed=4 * width * units + 4 * tokens * (2 * width + units),
+            transcendentals=2 * tokens * units,
+        ),
+    )(place_vector(), normed, cot, *up_parts[0], *up_parts[1], down_mine, down_other, *begun)
+
+
+def swap_z(values, far):
+    pairs = [(row, row ^ (8 if far else 4)) for row in range(16)]
+    return lax.ppermute(values, "rows", pairs)
+
+
+def halves(block):
+    depth, wide = block.shape
+    if depth > 80:
+        return block[: depth // 2], block[depth // 2 :]
+    cut = (wide // 128 + 1) // 2 * 128
+    return block[:, :cut], block[:, cut:]
+
+
+def halves_z(stack):
+    _, depth, wide = stack.shape
+    if depth > 80:
+        return stack[:, : depth // 2], stack[:, depth // 2 :]
+    cut = (wide // 128 + 1) // 2 * 128
+    return stack[:, :, :cut], stack[:, :, cut:]
+
+
+def start_xy(first, second):
+    return (first, swap_x(first), swap_y(first)), (second, swap_x(second), swap_y(second))
+
+
+def finish_xy(first, second):
+    return first + (swap_x(first[2]),), second + (swap_y(second[1]),)
 
 
 def dot_low(left_side, right_side):
@@ -480,6 +701,65 @@
     return jnp.einsum(
         "tc,te->ce", left_side, right_side, preferred_element_type=jnp.float32
     ).astype(jnp.bfloat16)
+
+
+class Scatter:
+
+    def __init__(self, first, second, by_rows=False):
+        self.parts, self.by_rows = (first, second), by_rows
+
+    def pick(self, which, far_y, far_x):
+        _, here_y, here_x = chip_place()
+        picked = []
+        for whole, row, depth, column, wide in self.parts[which]:
+            blocks = whole.reshape(Z_SIZE, 2, 2, whole.shape[0] // 16, whole.shape[1])
+            picked.append(
+                lax.dynamic_slice(
+                    blocks,
+                    (0, here_y ^ far_y, here_x ^ far_x, row, column),
+                    (Z_SIZE, 1, 1, depth, wide),
+                ).reshape(Z_SIZE, depth, wide)
+            )
+        return picked[0] if len(picked) == 1 else jnp.concatenate(picked, 2)
+
+    def spread(self):
+        self.first_far = swap_x(self.pick(0, 1, 1))
+        self.second_far = swap_y(self.pick(1, 1, 1))
+        self.first_near = swap_x(self.pick(0, 0, 1))
+        self.second_near = swap_y(self.pick(1, 1, 0))
+
+    def turn(self):
+        self.first_turned = swap_y(plus(self.pick(0, 1, 0), self.first_far))
+        self.second_turned = swap_x(plus(self.pick(1, 0, 1), self.second_far))
+
+    def gather(self):
+        first = plus(self.pick(0, 0, 0), self.first_near, self.first_turned)
+        second = plus(self.pick(1, 0, 0), self.second_near, self.second_turned)
+        self.sums = jnp.concatenate([first, second], 1 if self.by_rows else 2)
+        self.moving = next_z(self.block(1))
+
+    def block(self, back):
+        target = (ring_place() - back) % Z_SIZE
+        zed = jnp.where(target == 2, 3, jnp.where(target == 3, 2, target))
+        return lax.dynamic_index_in_dim(self.sums, zed, 0, keepdims=False)
+
+    def step(self, number):
+        self.moving = next_z(plus(self.block(number), self.moving))
+
+    def finish(self):
+        return self.block(0).astype(jnp.float32) + self.moving.astype(jnp.float32)
+
+    def hold(self, names, *after):
+        for name in names:
+            setattr(self, name, tie(getattr(self, name), *after))
+
+
+def plus_wide(*terms):
+    return sum(term.astype(jnp.float32) for term in terms)
+
+
+def plus(*terms):
+    return plus_wide(*terms).astype(jnp.bfloat16)
 
 
 def body_pair(
@@ -489,108 +769,265 @@
     rows, span, width = tokens.shape
     flat = rows * span
 
-    w_q = gather_rows(w_query)
-    w_k = gather_rows(w_key)
-    w_v = gather_rows(w_value)
-    w_o = both_cores(gather_rows(w_out), 1)
-    w_u = gather_rows(w_up)
-    down_columns = gather_rows(w_down)
-    down_other = swap_cores(own_half(down_columns, 0, 1 - core))
-    down_mine = own_half(down_columns, 0, core)
-    w_d = jnp.where(
-        core == 0,
-        jnp.concatenate([down_mine, down_other], 1),
-        jnp.concatenate([down_other, down_mine], 1),
-    )
-    w_o_rows = own_half(w_o, 0, core)
-
-    tokens_all = both_cores(tokens, 1).reshape(2 * flat, width).astype(jnp.float32)
-    cot_all = both_cores(cotangent, 1).reshape(2 * flat, width)
+    def split(flat_rows, axis_width):
+        return flat_rows.reshape(rows, 2 * span, axis_width)
+
+    def sharing(values):
+        wide = split(values, values.shape[-1])
+        return swap_cores(own_half(wide, 1, 1 - core).astype(jnp.bfloat16))
+
+    def shared(values, received):
+        wide = split(values, values.shape[-1])
+        return (own_half(wide, 1, core) + received.astype(jnp.float32)).reshape(flat, -1)
+
+    attn_piece = jnp.concatenate([w_query, w_key, w_value, w_out], 1)
+    qkv_wide = 3 * w_query.shape[1]
+    tokens_other = swap_cores(tokens)
+    attn_steps = [attn_piece]
+    for _ in range(2):
+        attn_steps.append(next_z(attn_steps[-1]))
+
+    first = core == 0
+    tokens_all = jnp.where(
+        first,
+        jnp.concatenate([tokens, tokens_other], 1),
+        jnp.concatenate([tokens_other, tokens], 1),
+    )
+    tokens_all = tokens_all.reshape(2 * flat, width).astype(jnp.float32)
     tokens_own = tokens.reshape(flat, width).astype(jnp.float32)
     cot_own = cotangent.reshape(flat, width)
-
     windows = windows_of(segments)
     marks = (
         jnp.broadcast_to(segments[:, :, None], segments.shape + (LANES,)),
         jnp.broadcast_to(segments[:, None, :], (rows, 8, 2 * span)),
     )
-
-    def split(flat_rows, axis_width):
-        return flat_rows.reshape(rows, 2 * span, axis_width)
-
-    def share(values):
-        wide = split(values, values.shape[-1])
-        received = swap_cores(own_half(wide, 1, 1 - core).astype(jnp.bfloat16))
-        return (own_half(wide, 1, core) + received.astype(jnp.float32)).reshape(flat, -1)
-
     normed = (norm_stats(tokens_all)[0] * gain_attn).astype(jnp.bfloat16)
-    queries = split(dot_low(normed, w_q).astype(jnp.bfloat16), w_q.shape[1])
-    key_rows = split(dot_low(normed, w_k).astype(jnp.bfloat16), w_k.shape[1])
-    value_rows = split(dot_low(normed, w_v).astype(jnp.bfloat16), w_v.shape[1])
-    (mixed,) = attention_call(
-        attend_kernel, windows, marks, (queries, key_rows, value_rows), 1, []
-    )
+
+    attn_steps[2] = tie(attn_steps[2], normed)
+    attn_steps.append(next_z(attn_steps[2]))
+    attn_stack = natural_z(attn_steps)
+    qkv_parts = start_xy(*halves_z(attn_stack[:, :, :qkv_wide]))
+    up_steps, down_steps = [tie(w_up, attn_stack)], [tie(w_down, attn_stack)]
+    up_steps.append(next_z(up_steps[-1]))
+    down_steps.append(next_z(down_steps[-1]))
+    qkv_parts = finish_xy(*qkv_parts)
+    up_steps[1], down_steps[1] = tie((up_steps[1], down_steps[1]), qkv_parts[0][2], qkv_parts[1][1])
+    up_steps.append(next_z(up_steps[-1]))
+    down_steps.append(next_z(down_steps[-1]))
+    cot_other = swap_cores(cotangent)
+    w_qkv = assemble(assemble_columns_kernel, (width, qkv_wide), qkv_parts)
+    out_parts = start_xy(*halves_z(tie(attn_stack[:, :, qkv_wide:], qkv_parts)))
+    w_qkv, up_steps[2], down_steps[2] = tie((w_qkv, up_steps[2], down_steps[2]))
+    up_steps.append(next_z(up_steps[-1]))
+    down_steps.append(next_z(down_steps[-1]))
+    w_q, w_k, w_v = (w_qkv[:, i * (qkv_wide // 3) : (i + 1) * (qkv_wide // 3)] for i in range(3))
+
+    queries = dot_low(normed, w_q).astype(jnp.bfloat16)
+    queries, out_parts = tie((queries, out_parts))
+    out_parts = finish_xy(*out_parts)
+    normed, up_steps[3], down_steps[3] = tie((normed, up_steps[3], down_steps[3]), queries)
+    up_parts = start_xy(*halves_z(natural_z(up_steps)))
+    down_stack = natural_z(down_steps)
+    key_rows = dot_low(normed, w_k).astype(jnp.bfloat16)
+    normed, out_parts = tie((normed, out_parts), key_rows)
+    w_o_half = assemble(assemble_columns_kernel, (width, width // 2), out_parts)
+    w_o_other = swap_cores(w_o_half)
+    value_rows = dot_low(normed, w_v).astype(jnp.bfloat16)
+
+    queries, key_rows, value_rows = (
+        split(array, w_q.shape[1]) for array in (queries, key_rows, value_rows)
+    )
+    queries, w_o_other = tie((queries, w_o_other))
+
+    def attend(row, query_rows):
+        return attention_call(
+            attend_kernel,
+            [array[row : row + 1] for array in windows],
+            [array[row : row + 1] for array in marks],
+            [array[row : row + 1] for array in (query_rows, key_rows, value_rows)],
+            1,
+            [],
+        )[0]
+
+    mixed_rows = [attend(0, queries)]
+    queries, up_parts = tie((queries, up_parts), mixed_rows[0])
+    up_parts = finish_xy(*up_parts)
+    down_parts = start_xy(*halves_z(tie(down_stack, up_parts[0][2])))
+    mixed_rows += [attend(row, queries) for row in range(1, rows)]
+    mixed = jnp.concatenate(mixed_rows, 0)
+    mixed, up_parts, down_parts = tie((mixed, up_parts, down_parts))
+    down_parts = finish_xy(*down_parts)
+    w_o = jnp.where(
+        first,
+        jnp.concatenate([w_o_half, w_o_other], 1),
+        jnp.concatenate([w_o_other, w_o_half], 1),
+    )
+    w_o_rows = own_half(w_o, 0, core)
+
     mixed_other = swap_cores(own_half(mixed, 1, 1 - core))
     mixed_mine = own_half(mixed, 1, core)
     mixed_own = jnp.where(
-        core == 0,
+        first,
         jnp.concatenate([mixed_mine, mixed_other], 2),
         jnp.concatenate([mixed_other, mixed_mine], 2),
     ).reshape(flat, width)
     residual = tokens_own + dot_low(mixed_own, w_o)
     unit_two, scale_two = norm_stats(residual)
-    normed_two = (unit_two * gain_ffn).astype(jnp.bfloat16).reshape(rows, span, width)
-    normed_two_all = both_cores(normed_two, 1).reshape(2 * flat, width)
-    hidden_pre = dot_low(normed_two_all, w_u)
-    hidden, gelu_back = jax.vjp(gelu_exact, hidden_pre)
-    hidden_low = hidden.astype(jnp.bfloat16)
-    layer_out = (residual + share(dot_low(hidden_low, w_d))).astype(jnp.bfloat16)
-    grad_pre = gelu_back(times_transposed(cot_all, w_d))[0].astype(jnp.bfloat16)
-    grad_normed_two = share(times_transposed(grad_pre, w_u))
+    normed_two = (unit_two * gain_ffn).astype(jnp.bfloat16)
+    normed_two, down_parts = tie((normed_two, down_parts))
+    normed_two_other = swap_cores(normed_two)
+    units = w_up.shape[1]
+    down_columns = assemble(assemble_rows_kernel, (2, units, width // 2), down_parts)
+    down_mine = down_columns[0]
+    down_other = swap_cores(down_columns[1])
+    weights = (up_parts, down_mine, down_other)
+    cot_other = cot_other.reshape(flat, width)
+
+    hidden_low, grad_pre, y_own, grad_two_own = feed_forward(normed_two, cot_own, *weights)
+    (normed_two_other, hidden_low, grad_pre) = tie((normed_two_other, hidden_low, grad_pre))
+    hidden_low, grad_pre, y_away, grad_two_away = feed_forward(
+        normed_two_other, cot_other, *weights, begun=(hidden_low, grad_pre)
+    )
+    normed_two_all = jnp.concatenate([normed_two, normed_two_other], 0)
+    cot_all = jnp.concatenate([cot_own, cot_other], 0)
+    grad_two_came = swap_cores(grad_two_away)
+    y_came = swap_cores(y_away)
+
+    hidden_low = tie(hidden_low, grad_two_away, y_away)
+    down_half = outer_low(hidden_low, cot_all)
+    down_away = swap_cores(own_half(down_half, 1, 1 - core))
+    grad_pre, normed_two_all = tie((grad_pre, normed_two_all), down_half)
+    up_whole = outer_low(normed_two_all, grad_pre)
+    down_away = tie(down_away, up_whole)
+    down_kept = own_half(down_half, 1, core)
+    down_whole = jnp.where(
+        first,
+        jnp.concatenate([down_kept, down_away], 0),
+        jnp.concatenate([down_away, down_kept], 0),
+    )
+    depth, wide = w_down.shape
+    down_sum = Scatter(
+        [(down_whole, 0, depth // 2, 0, wide)],
+        [(down_whole, depth // 2, depth // 2, 0, wide)],
+        True,
+    )
+    down_sum.spread()
+    depth, wide = w_up.shape
+    up_sum = Scatter(
+        [(up_whole, 0, depth, 0, wide // 2)], [(up_whole, 0, depth, wide // 2, wide // 2)]
+    )
+    grad_normed_two = plus_wide(grad_two_own, tie(grad_two_came, up_whole))
     grad_residual = cot_own.astype(jnp.float32) + norm_back_rows(
         unit_two, scale_two, gain_ffn, grad_normed_two
     )
     ffn_gain_part = jnp.sum(grad_normed_two * unit_two, 0)
     grad_attn = grad_residual.astype(jnp.bfloat16).reshape(rows, span, width)
+    (grad_attn, down_sum.first_far, down_sum.second_far) = tie(
+        (grad_attn, down_sum.first_far, down_sum.second_far)
+    )
+    down_sum.turn()
+    up_sum.spread()
     grad_attn_all = both_cores(grad_attn, 1).reshape(2 * flat, width)
     grad_mixed = split(times_transposed(grad_attn_all, w_o_rows).astype(jnp.bfloat16), width // 2)
+    down_names = ("first_near", "second_near", "first_turned", "second_turned")
+    down_sum.hold(down_names, grad_mixed)
+    grad_mixed = tie(grad_mixed, *(getattr(down_sum, name) for name in down_names))
+    down_sum.gather()
     scratch = [pltpu.VMEM((2 * span, LANES), jnp.float32)] * 2
-    grad_queries, grad_keys, grad_values = (
-        grad.reshape(2 * flat, width // 2)
-        for grad in attention_call(
+
+    def attend_back(row, grad_rows):
+        return attention_call(
             attend_back_kernel,
-            windows,
-            marks,
-            (queries, key_rows, value_rows, grad_mixed),
+            [array[row : row + 1] for array in windows],
+            [array[row : row + 1] for array in marks],
+            [array[row : row + 1] for array in (queries, key_rows, value_rows, grad_rows)],
             3,
             scratch,
         )
-    )
-    grad_normed = share(
+
+    up_names = ("first_far", "second_far")
+    back_rows = []
+    for row in range(rows):
+        back_rows.append(attend_back(row, grad_mixed))
+        if row == 0:
+            down_sum.hold(("moving",), *back_rows[-1])
+            up_sum.hold(up_names, *back_rows[-1])
+            grad_mixed = tie(
+                grad_mixed, down_sum.moving, up_sum.first_far, up_sum.second_far, *back_rows[-1]
+            )
+            down_sum.step(2)
+            up_sum.turn()
+    grad_queries, grad_keys, grad_values = (
+        jnp.concatenate([parts[member] for parts in back_rows], 0).reshape(2 * flat, width // 2)
+        for member in range(3)
+    )
+    down_sum.hold(("moving",), grad_queries)
+    up_sum.hold(down_names, grad_queries)
+    grad_queries = tie(
+        grad_queries, down_sum.moving, *(getattr(up_sum, name) for name in down_names)
+    )
+    down_sum.step(3)
+    up_sum.gather()
+    out_half = outer_low(mixed.reshape(2 * flat, -1), tie(grad_attn_all, grad_queries))
+    out_away = swap_cores(own_half(out_half, 1, 1 - core))
+    query_whole = outer_low(normed, grad_queries)
+    key_whole = outer_low(normed, grad_keys)
+    value_whole = outer_low(normed, grad_values)
+    out_kept = own_half(out_half, 1, core)
+    out_whole = jnp.where(
+        first,
+        jnp.concatenate([out_kept, out_away], 0),
+        jnp.concatenate([out_away, out_kept], 0),
+    )
+    attn_whole = (query_whole, key_whole, value_whole, out_whole)
+    up_sum.hold(("moving",), attn_whole)
+    attn_whole = tie(attn_whole, up_sum.moving)
+    depth, wide = w_query.shape
+    attn_sum = Scatter(
+        [(whole, 0, depth, 0, wide) for whole in attn_whole[:2]],
+        [(whole, 0, depth, 0, wide) for whole in attn_whole[2:]],
+    )
+    attn_sum.spread()
+    up_sum.step(2)
+    grad_queries = tie(grad_queries, attn_whole)
+    grad_normed_part = (
         times_transposed(grad_queries, w_q)
         + times_transposed(grad_keys, w_k)
         + times_transposed(grad_values, w_v)
     )
+    attn_sum.hold(up_names, grad_normed_part)
+    up_sum.hold(("moving",), grad_normed_part)
+    grad_normed_part = tie(
+        grad_normed_part, attn_sum.first_far, attn_sum.second_far, up_sum.moving
+    )
+    attn_sum.turn()
+    up_sum.step(3)
+    grad_normed = shared(grad_normed_part, sharing(grad_normed_part))
+    y_own, y_came = tie((y_own, y_came), grad_normed_part)
+    layer_out = (residual + plus_wide(y_own, y_came)).astype(jnp.bfloat16)
     unit_own, scale_own = norm_stats(tokens_own)
     token_grad = grad_residual + norm_back_rows(unit_own, scale_own, gain_attn, grad_normed)
     attn_gain_part = jnp.sum(grad_normed * unit_own, 0)
-    gain_attn_grad, gain_ffn_grad = lax.psum((attn_gain_part, ffn_gain_part), ("rows", "seq"))
-
-    def to_columns(row_half):
-        received = swap_cores(own_half(row_half, 1, 1 - core))
-        kept = own_half(row_half, 1, core)
-        return jnp.where(
-            core == 0,
-            jnp.concatenate([kept, received], 0),
-            jnp.concatenate([received, kept], 0),
-        )
-
-    down_grad = scatter_rows(to_columns(outer_low(hidden_low, cot_all)))
-    up_grad = scatter_rows(outer_low(normed_two_all, grad_pre))
-    out_grad = scatter_rows(to_columns(outer_low(mixed.reshape(2 * flat, -1), grad_attn_all)))
-    query_grad = scatter_rows(outer_low(normed, grad_queries))
-    key_grad = scatter_rows(outer_low(normed, grad_keys))
-    value_grad = scatter_rows(outer_low(normed, grad_values))
+    gains = jnp.stack([attn_gain_part, ffn_gain_part])
+    gains = gains + swap_cores(gains)
+    attn_sum.hold(down_names, token_grad)
+    attn_sum.gather()
+    gains = gains + swap_x(gains)
+    gains = gains + swap_y(gains)
+    layer_out, attn_sum.moving = tie((layer_out, attn_sum.moving), gains)
+    attn_sum.step(2)
+    gains = gains + swap_z(gains, False)
+    attn_sum.moving = tie(attn_sum.moving, gains)
+    attn_sum.step(3)
+    gains = gains + swap_z(gains, True)
+    gain_attn_grad, gain_ffn_grad = gains
+    down_grad = down_sum.finish()
+    up_grad = up_sum.finish()
+    attn_grad = attn_sum.finish()
+    column_width = w_query.shape[1]
+    query_grad, key_grad, value_grad, out_grad = (
+        attn_grad[:, index * column_width : (index + 1) * column_width] for index in range(4)
+    )
     return (
         layer_out.reshape(rows, span, width),
         token_grad.reshape(rows, span, width),

time: 1270 us -> 749 us (0.59)
  waiting for transfers between devices: 754 us -> 203 us
  matrix products: 225 us -> 102 us
  Pallas kernels: 113 us -> 210 us
  starting transfers between devices: 3.78 us -> 88.2 us
  blocking collectives: 41 us -> 0 us
  local copies, waits for them, and re-layouts: 22.2 us -> 46.3 us
    reduce_scatter x6 -> x0, waiting for transfers between devices: 421 us -> none  [scatter_rows(): lax.psum_scatter(whole, 'rows', scatter_dimension=0, tiled=True)]
    all_gather x6 -> x0, waiting for transfers between devices: 313 us -> none  [gather_rows(): return lax.all_gather(piece, 'rows', axis=0, tiled=True)]
    ppermute x0 -> x64, waiting for transfers between devices: none -> 197 us  [the longest x22 97.4 us: swap_x(): return lax.ppermute(values, 'rows', [(row, row ^ 1) for row in range(16)])]
    pallas_call x0 -> x5, Pallas kernels: none -> 97.2 us  [the longest x2 84 us: feed_forward(): pl.pallas_call(functools.partial(feed_forward_kernel, begun=bool(begun)),...]
    ppermute x0 -> x64, starting transfers between devices: none -> 85.4 us  [the longest x18 36.3 us: next_z(): return lax.ppermute(values, 'rows', pairs)]
    dot_general x6 -> x4, matrix products: 76.8 us -> 17.1 us  [dot_low(): return jnp.dot(left_side, right_side, preferred_element_type=jnp.float32)]
    dot_general x6 -> x4, matrix products: 75.5 us -> 29.9 us  [times_transposed(): jnp.einsum('te,de->td', left_side, right_side, preferred_element_type=jnp...]
    psum x1 -> x0, blocking collectives: 41 us -> none  [body_pair(): lax.psum((attn_gain_part, ffn_gain_part), ('rows', 'seq'))]
  transfers between devices with their start and end apart: 24 -> 77, of which waited for: 16 -> 29; matrix products, arithmetic and copies ran while one was open for 20% -> 28% of each run, Pallas kernels for 3% -> 21%
where the time goes in v2:
time: 749 us; the launch traced here: 743 us
  Pallas kernels  210 us (28%)
  waiting for transfers between devices  203 us (27%)
  matrix products  102 us (14%)
  other arithmetic  91.1 us (12%)
  starting transfers between devices  88.2 us (12%)
  local copies, waits for them, and re-layouts  46.3 us (6%)
    pallas_call x4, Pallas kernels, attention_call(): pl.pallas_call(kernel, grid_spec=pltpu.PrefetchScalarGridSpec(num_scalar_...  113 us
    ppermute x22, waiting for transfers between devices, swap_x(): return lax.ppermute(values, 'rows', [(row, row ^ 1) for row in range(16)])  97.4 us
    pallas_call x2, Pallas kernels, feed_forward(): pl.pallas_call(functools.partial(feed_forward_kernel, begun=bool(begun)),...  84 us
    ppermute x18, waiting for transfers between devices, next_z(): return lax.ppermute(values, 'rows', pairs)  59.4 us
    dot_general x6, matrix products, outer_low(): jnp.einsum('tc,te->ce', left_side, right_side, preferred_element_type=jnp...  54.8 us
    ppermute x18, starting transfers between devices, next_z(): return lax.ppermute(values, 'rows', pairs)  36.3 us
    dot_general x4, matrix products, times_transposed(): jnp.einsum('te,de->td', left_side, right_side, preferred_element_type=jnp...  29.9 us
    ppermute x22, waiting for transfers between devices, swap_y(): return lax.ppermute(values, 'rows', [(row, row ^ 2) for row in range(16)])  28.5 us
  transfers between devices with their start and end apart: 77, of which 29 were waited for; matrix products, arithmetic and copies ran while one was open for 28% of the time, Pallas kernels for 21%

profile of v2, /device:TPU:0, one launch (start us, length us, event | category | flops | bytes accessed | tf_op | source)
XLA Modules:
  0.0 742.9 jit_solution(15237392077358898911)
XLA Ops:
  7.5 11.1 %collective-permute-done.1 = bf16[80,2560]{1,0:T(8,128)(2,1)S(1)} collective-permute-done((bf16[80,2560]{1,0:T(8,128)(2,1)S(1)}, bf16[80,2560]{1,0:T(8,128)(2,1)S(1)}, u32[]{:S(2)}, u32[]{:S(2)}) %collective-permute-start.1) | collective-permute-done | bytes 409632 | tf_op jit(solution)/shard_map/ppermute | solution.py:490
  19.4 4.1 fusion.87
  23.6 5.5 multiply_reduce_fusion
  30.5 3.6 fusion.2
  34.1 3.4 collective-permute-start.3
  37.5 8.6 %collective-permute-done.3 = bf16[80,2560]{1,0:T(8,128)(2,1)S(1)} collective-permute-done((bf16[80,2560]{1,0:T(8,128)(2,1)}, bf16[80,2560]{1,0:T(8,128)(2,1)S(1)}, u32[]{:S(2)}, u32[]{:S(2)}) %collective-permute-start.3) | collective-permute-done | bytes 409632 | tf_op jit(solution)/shard_map/ppermute | solution.py:490
  54.4 11.1 %collective-permute-done.5.refs_2_ = bf16[4,80,1024]{2,1,0:T(8,128)(2,1)S(1)} collective-permute-done((bf16[4,80,1024]{2,1,0:T(8,128)(2,1)S(1)}, bf16[4,80,1024]{2,1,0:T(8,128)(2,1)S(1)}, u32[]{:S(2)}, u32[]{:S(2)}) %collective-permute-start.5) | collective-permute-done | bytes 655392 | tf_op jit(solution)/shard_map/ppermute | solution.py:482
  71.5 7.1 collective-permute-done.11
  82.6 5.1 collective-permute-done.9.refs_7_
  87.7 3.0 collective-permute-done.6.refs_3_
  94.6 2.9 shard_map.186
  103.3 4.4 convolution_convert_fusion.9
  112.3 4.4 collective-permute-done.19
  121.3 4.4 convolution_convert_fusion.8
  133.6 4.4 convolution_convert_fusion.7
  140.6 19.7 %shard_map.188 = bf16[1,1024,640]{2,1,0:T(8,128)(2,1)S(1)} custom-call(s32[1,4]{1,0:T(1,128)S(1)} %get-tuple-element.352.start_ref, s32[1,4]{1,0:T(1,128)S(1)} %get-tuple-element.343.count_ref, s32[1,1024,128]{2,1,0:T(8,128)S(1)} %broadcast_in_dim.8.column_ref, s32[1,8,1024]{2,1,0:T(8,128)S(1)} %broadcast_in_dim.9.line_ref, ...), custom_call_target="tpu_custom_call" | custom-call | flops 8053063680 | bytes 5242880 | tf_op jit(solution)/shard_map/pallas_call | solution.py:432
  167.0 3.0 fusion.89
  170.0 12.5 %collective-permute-done.29.refs_1_ = bf16[4,160,640]{2,1,0:T(8,128)(2,1)} collective-permute-done((bf16[4,160,640]{2,1,0:T(8,128)(2,1)S(1)}, bf16[4,160,640]{2,1,0:T(8,128)(2,1)}, u32[]{:S(2)}, u32[]{:S(2)}) %collective-permute-start.29) | collective-permute-done | bytes 819232 | tf_op jit(solution)/shard_map/ppermute | solution.py:478
  184.5 20.2 %shard_map.189 = bf16[1,1024,640]{2,1,0:T(8,128)(2,1)S(1)} custom-call(s32[1,4]{1,0:T(1,128)S(1)} %get-tuple-element.351.start_ref, s32[1,4]{1,0:T(1,128)S(1)} %get-tuple-element.344.count_ref, s32[1,1024,128]{2,1,0:T(8,128)S(1)} %broadcast_in_dim.10.column_ref, s32[1,8,1024]{2,1,0:T(8,128)S(1)} %broadcast_in_dim.11.line_ref, ...), custom_call_target="tpu_custom_call" | custom-call | flops 8053063680 | bytes 5242880 | tf_op jit(solution)/shard_map/pallas_call | solution.py:432
  205.1 12.0 %collective-permute-done.27.refs_3_ = bf16[4,80,1280]{2,1,0:T(8,128)(2,1)S(1)} collective-permute-done((bf16[4,80,1280]{2,1,0:T(8,128)(2,1)}, bf16[4,80,1280]{2,1,0:T(8,128)(2,1)S(1)}, u32[]{:S(2)}, u32[]{:S(2)}) %collective-permute-start.27) | collective-permute-done | bytes 819232 | tf_op jit(solution)/shard_map/ppermute | solution.py:478
  222.2 3.9 fusion.96
  230.6 9.3 %collective-permute-done.34.refs_3_ = bf16[4,160,640]{2,1,0:T(8,128)(2,1)S(1)} collective-permute-done((bf16[4,160,640]{2,1,0:T(8,128)(2,1)S(1)}, bf16[4,160,640]{2,1,0:T(8,128)(2,1)S(1)}, u32[]{:S(2)}, u32[]{:S(2)}) %collective-permute-start.34) | collective-permute-done | bytes 819232 | tf_op jit(solution)/shard_map/ppermute | solution.py:478
  240.3 9.1 %shard_map.190 = bf16[2,2560,640]{2,1,0:T(8,128)(2,1)S(1)} custom-call(s32[4]{0:T(128)S(1)} %pad_add_fusion.place_ref, bf16[4,160,640]{2,1,0:T(8,128)(2,1)S(1)} %get-tuple-element.186.refs_0_, bf16[4,160,640]{2,1,0:T(8,128)(2,1)} %collective-permute-done.29.refs_1_, bf16[4,160,640]{2,1,0:T(8,128)(2,1)S(1)} %collective-permute-done.30.refs_2_, ...), custom_call_target="tpu_custom_call" | custom-call | tf_op jit(solution)/shard_map/pallas_call | solution.py:560
  249.4 3.4 slice_bitcast_fusion
  253.3 5.7 collective-permute-done.36.refs_9_
  259.0 41.8 %shard_map.191 = (bf16[2048,2560]{1,0:T(8,128)(2,1)}, bf16[2048,2560]{1,0:T(8,128)(2,1)}, bf16[1024,1280]{1,0:T(8,128)(2,1)}, bf16[1024,1280]{1,0:T(8,128)(2,1)}) custom-call(s32[4]{0:T(128)} %copy-done.18, bf16[1024,1280]{1,0:T(8,128)(2,1)} %multiply_convert_fusion.normed_ref, bf16[1024,1280]{1,0:T(8,128)(2,1)} %bitcast.27.cot_ref, ...), custom_call_target="tpu_custom_call" | custom-call | flops 26843545600 | bytes 34078720 | tf_op jit(solution)/shard_map/pallas_call | solution.py:642
  300.7 5.2 pad_maximum_fusion
  305.9 42.3 %shard_map.192 = (bf16[2048,2560]{1,0:T(8,128)(2,1)}, bf16[2048,2560]{1,0:T(8,128)(2,1)}, bf16[1024,1280]{1,0:T(8,128)(2,1)}, bf16[1024,1280]{1,0:T(8,128)(2,1)}) custom-call(s32[4]{0:T(128)} %copy-done.18, bf16[1024,1280]{1,0:T(8,128)(2,1)} %collective-permute-done.37.normed_ref, ...), custom_call_target="tpu_custom_call", output_to_operand_aliasing={{0}: (13, {}), {1}: (14, {})} | custom-call | flops 26843545600 | bytes 34078720 | tf_op jit(solution)/shard_map/pallas_call | solution.py:642
  348.4 17.9 %convolution_convert_fusion.1 = bf16[2560,1280]{1,0:T(8,128)(2,1)S(1)} fusion(bf16[2048,2560]{1,0:T(8,128)(2,1)} %get-tuple-element.205, bf16[1024,1280]{1,0:T(8,128)(2,1)} %bitcast.30.cot_ref, bf16[1024,1280]{1,0:T(8,128)(2,1)} %bitcast.27.cot_ref), kind=kOutput, calls=%fused_computation.1 | convolution fusion | flops 13435535360 | bytes 22282240 | tf_op jit(solution)/shard_map/tc,te->ce/dot_general | solution.py:701
  369.4 20.3 %convolution_convert_fusion = bf16[1280,2560]{1,0:T(8,128)(2,1)} fusion(bf16[2048,1280]{1,0:T(8,128)(2,1)} %pad_maximum_fusion, bf16[2048,2560]{1,0:T(8,128)(2,1)} %get-tuple-element.207), kind=kOutput, calls=%fused_computation | convolution fusion | flops 13425049600 | bytes 22282240 | tf_op jit(solution)/shard_map/tc,te->ce/dot_general | solution.py:701
  392.5 11.9 %maximum_select_fusion = bf16[5120,640]{1,0:T(8,128)(2,1)S(1)} fusion(bf16[2560,640]{1,0:T(8,128)(2,1)S(1)} %collective-permute-done.41, bf16[2560,640]{1,0:T(8,128)(2,1)S(1)} %get-tuple-element.285, pred[]{:T(512)S(6)} %eq.161), kind=kLoop, calls=%fused_computation.8 | loop fusion | flops 29491200 | bytes 13107201 | tf_op jit(solution)/shard_map/jit(_where)/select_n | solution.py:903
  410.8 5.8 fusion.88
  416.5 11.4 %collective-permute-done.42 = bf16[4,160,640]{2,1,0:T(8,128)(2,1)S(1)} collective-permute-done((bf16[4,160,640]{2,1,0:T(8,128)(2,1)S(1)}, bf16[4,160,640]{2,1,0:T(8,128)(2,1)S(1)}, u32[]{:S(2)}, u32[]{:S(2)}) %collective-permute-start.42) | collective-permute-done | bytes 819232 | tf_op jit(solution)/shard_map/ppermute | solution.py:478
  433.6 3.2 dynamic-slice_bitcast_fusion
  441.3 5.0 maximum_select_fusion.2
  446.4 4.5 convolution_convert_fusion.6
  450.9 25.0 %collective-permute-done.48 = bf16[4,160,640]{2,1,0:T(8,128)(2,1)S(1)} collective-permute-done((bf16[4,160,640]{2,1,0:T(8,128)(2,1)S(1)}, bf16[4,160,640]{2,1,0:T(8,128)(2,1)S(1)}, u32[]{:S(2)}, u32[]{:S(2)}) %collective-permute-start.48) | collective-permute-done | bytes 819232 | tf_op jit(solution)/shard_map/ppermute | solution.py:478
  483.2 35.7 %shard_map.193 = (bf16[1,1024,640]{2,1,0:T(8,128)(2,1)S(1)}, bf16[1,1024,640]{2,1,0:T(8,128)(2,1)S(1)}, bf16[1,1024,640]{2,1,0:T(8,128)(2,1)S(1)}) custom-call(s32[1,4]{1,0:T(1,128)S(1)} %get-tuple-element.352.start_ref, s32[1,4]{1,0:T(1,128)S(1)} %get-tuple-element.343.count_ref, s32[1,1024,128]{2,1,0:T(8,128)S(1)} %copy-done.11, ...), custom_call_target="tpu_custom_call" | custom-call | flops 10737418240 | bytes 9175040 | tf_op jit(solution)/shard_map/pallas_call | solution.py:432
  518.9 3.7 collective-permute-start.49
  522.5 3.4 fusion.32
  527.2 4.0 collective-permute-done.49
  532.5 37.1 %shard_map.194 = (bf16[1,1024,640]{2,1,0:T(8,128)(2,1)S(1)}, bf16[1,1024,640]{2,1,0:T(8,128)(2,1)S(1)}, bf16[1,1024,640]{2,1,0:T(8,128)(2,1)S(1)}) custom-call(s32[1,4]{1,0:T(1,128)S(1)} %get-tuple-element.351.start_ref, s32[1,4]{1,0:T(1,128)S(1)} %get-tuple-element.344.count_ref, s32[1,1024,128]{2,1,0:T(8,128)S(1)} %copy-done.13, ...), custom_call_target="tpu_custom_call" | custom-call | flops 10737418240 | bytes 9175040 | tf_op jit(solution)/shard_map/pallas_call | solution.py:432
  570.0 3.6 collective-permute-start.52
  573.9 6.9 fusion.43
  580.8 4.3 convolution_convert_fusion.4
  585.4 4.3 convolution_convert_fusion.3
  589.8 3.1 fusion.29
  595.3 3.7 convolution_convert_fusion.2
  599.2 4.3 convolution_convert_fusion.5
  606.2 6.9 fusion.46
  619.6 11.7 %add_add_fusion = f32[2048,1280]{1,0:T(8,128)} fusion(f32[2048,1280]{1,0:T(8,128)} %fusion.46, f32[2048,1280]{1,0:T(8,128)} %fusion.43, bf16[2048,640]{1,0:T(8,128)(2,1)S(1)} %bitcast.273, bf16[1280,1920]{1,0:T(8,128)(2,1)S(1)} %bitcast.258), kind=kOutput, calls=%fused_computation.6 | convolution fusion | flops 3360686080 | bytes 35717120 | tf_op jit(solution)/shard_map/te,de->td/dot_general | solution.py:30
  631.4 4.5 collective-permute-done.60
  635.9 3.8 collective-permute-done.59
  639.7 4.6 dynamic-slice_convert_fusion
  648.5 10.9 %collective-permute-done.76 = bf16[320,640]{1,0:T(8,128)(2,1)} collective-permute-done((bf16[320,640]{1,0:T(8,128)(2,1)}, bf16[320,640]{1,0:T(8,128)(2,1)}, u32[]{:S(2)}, u32[]{:S(2)}) %collective-permute-start.76) | collective-permute-done | bytes 409632 | tf_op jit(solution)/shard_map/ppermute | solution.py:490
  672.2 4.2 fusion.16
  676.6 3.7 fusion.10
  680.3 4.5 collective-permute-done.65
  684.8 17.5 %collective-permute-done.66 = bf16[4,80,1280]{2,1,0:T(8,128)(2,1)S(1)} collective-permute-done((bf16[4,80,1280]{2,1,0:T(8,128)(2,1)S(1)}, bf16[4,80,1280]{2,1,0:T(8,128)(2,1)S(1)}, u32[]{:S(2)}, u32[]{:S(2)}) %collective-permute-start.66) | collective-permute-done | bytes 819232 | tf_op jit(solution)/shard_map/ppermute | solution.py:478
  704.0 2.8 collective-permute-done.69
  708.6 4.0 add_convert_fusion
  717.1 11.6 %collective-permute-done.71 = f32[2,1280]{1,0:T(2,128)S(1)} collective-permute-done((f32[2,1280]{1,0:T(2,128)S(1)}, f32[2,1280]{1,0:T(2,128)S(1)}, u32[]{:S(2)}, u32[]{:S(2)}) %collective-permute-start.71) | collective-permute-done | bytes 10272 | tf_op jit(solution)/shard_map/ppermute | solution.py:669
  730.5 6.0 collective-permute-done.75
  738.1 3.6 collective-permute-done.74
  (409 shorter events, 149.8 us)
Async XLA Ops:
  0.6 18.8 %collective-permute-start = (bf16[2,512,1280]{2,1,0:T(8,128)(2,1)}, bf16[2,512,1280]{2,1,0:T(8,128)(2,1)S(1)}, u32[]{:S(2)}, u32[]{:S(2)}) collective-permute-start(bf16[2,512,1280]{2,1,0:T(8,128)(2,1)} %param.11), channel_id=1, source_target_pairs={{0,1},{1,0},{2,3},{3,2},{4,5},{5,4},{6,7},{7,6},{8,9},{9,8},{10,11... | collective-permute-start | bytes 7864328 | tf_op jit(solution)/shard_map/ppermute | solution.py:283
  4.8 13.8 %collective-permute-start.1 = (bf16[80,2560]{1,0:T(8,128)(2,1)S(1)}, bf16[80,2560]{1,0:T(8,128)(2,1)S(1)}, u32[]{:S(2)}, u32[]{:S(2)}) collective-permute-start(bf16[80,2560]{1,0:T(8,128)(2,1)S(1)} %constant_dynamic-update-slice_fusion), channel_id=1, source_target_pairs={{0,8},{2,10},{4,12},{6,14},{8,24},{10,26},{12,28},{14,30},{24,16},... | collective-permute-start | bytes 1228808 | tf_op jit(solution)/shard_map/ppermute | solution.py:490
  18.6 15.5 %collective-permute-start.2 = (bf16[80,2560]{1,0:T(8,128)(2,1)S(1)}, bf16[80,2560]{1,0:T(8,128)(2,1)}, u32[]{:S(2)}, u32[]{:S(2)}) collective-permute-start(bf16[80,2560]{1,0:T(8,128)(2,1)S(1)} %collective-permute-done.1), channel_id=1, source_target_pairs={{0,8},{2,10},{4,12},{6,14},{8,24},{10,26},{12,28},{14,30},{24,16},... | collective-permute-start | bytes 1228808 | tf_op jit(solution)/shard_map/ppermute | solution.py:490
  34.1 12.0 %collective-permute-start.3 = (bf16[80,2560]{1,0:T(8,128)(2,1)}, bf16[80,2560]{1,0:T(8,128)(2,1)S(1)}, u32[]{:S(2)}, u32[]{:S(2)}) collective-permute-start(bf16[80,2560]{1,0:T(8,128)(2,1)} %collective-permute-done.2), channel_id=1, source_target_pairs={{0,8},{2,10},{4,12},{6,14},{8,24},{10,26},{12,28},{14,30},{24,16},... | collective-permute-start | bytes 1228808 | tf_op jit(solution)/shard_map/ppermute | solution.py:490
  47.8 17.7 %collective-permute-start.5 = (bf16[4,80,1024]{2,1,0:T(8,128)(2,1)S(1)}, bf16[4,80,1024]{2,1,0:T(8,128)(2,1)S(1)}, u32[]{:S(2)}, u32[]{:S(2)}) collective-permute-start(bf16[4,80,1024]{2,1,0:T(8,128)(2,1)S(1)} %slice.192.refs_0_), channel_id=1, source_target_pairs={{0,4},{2,6},{4,0},{6,2},{8,12},{10,14},{12,8},{14,10},{16,20},{18,... | collective-permute-start | bytes 1966088 | tf_op jit(solution)/shard_map/ppermute | solution.py:482
  49.5 20.0 %collective-permute-start.7 = (bf16[4,80,896]{2,1,0:T(8,128)(2,1)S(1)}, bf16[4,80,896]{2,1,0:T(8,128)(2,1)}, u32[]{:S(2)}, u32[]{:S(2)}) collective-permute-start(bf16[4,80,896]{2,1,0:T(8,128)(2,1)S(1)} %slice.193.refs_4_), channel_id=1, source_target_pairs={{0,2},{2,0},{4,6},{6,4},{8,10},{10,8},{12,14},{14,12},{16,18},{18,... | collective-permute-start | bytes 1720328 | tf_op jit(solution)/shard_map/ppermute | solution.py:478
  51.0 16.0 %collective-permute-start.10 = (bf16[80,2560]{1,0:T(8,128)(2,1)S(1)}, bf16[80,2560]{1,0:T(8,128)(2,1)S(1)}, u32[]{:S(2)}, u32[]{:S(2)}) collective-permute-start(bf16[80,2560]{1,0:T(8,128)(2,1)S(1)} %copy-done.54), channel_id=1, source_target_pairs={{0,8},{2,10},{4,12},{6,14},{8,24},{10,26},{12,28},{14,30},{24,16},... | collective-permute-start | bytes 1228808 | tf_op jit(solution)/shard_map/ppermute | solution.py:490
  53.4 27.3 %collective-permute-start.8 = (bf16[4,80,896]{2,1,0:T(8,128)(2,1)S(1)}, bf16[4,80,896]{2,1,0:T(8,128)(2,1)}, u32[]{:S(2)}, u32[]{:S(2)}) collective-permute-start(bf16[4,80,896]{2,1,0:T(8,128)(2,1)S(1)} %slice.193.refs_4_), channel_id=1, source_target_pairs={{0,4},{2,6},{4,0},{6,2},{8,12},{10,14},{12,8},{14,10},{16,20},{18,... | collective-permute-start | bytes 1720328 | tf_op jit(solution)/shard_map/ppermute | solution.py:482
  53.9 28.7 %collective-permute-start.4 = (bf16[4,80,1024]{2,1,0:T(8,128)(2,1)S(1)}, bf16[4,80,1024]{2,1,0:T(8,128)(2,1)S(1)}, u32[]{:S(2)}, u32[]{:S(2)}) collective-permute-start(bf16[4,80,1024]{2,1,0:T(8,128)(2,1)S(1)} %slice.192.refs_0_), channel_id=1, source_target_pairs={{0,2},{2,0},{4,6},{6,4},{8,10},{10,8},{12,14},{14,12},{16,18},{18,... | collective-permute-start | bytes 1966088 | tf_op jit(solution)/shard_map/ppermute | solution.py:478
  65.6 25.2 %collective-permute-start.6 = (bf16[4,80,1024]{2,1,0:T(8,128)(2,1)S(1)}, bf16[4,80,1024]{2,1,0:T(8,128)(2,1)S(1)}, u32[]{:S(2)}, u32[]{:S(2)}) collective-permute-start(bf16[4,80,1024]{2,1,0:T(8,128)(2,1)S(1)} %collective-permute-done.5.refs_2_), channel_id=1, source_target_pairs={{0,2},{2,0},{4,6},{6,4},{8,10},{10,8},{12,14},{14,12},{16,18},{18,... | collective-permute-start | bytes 1966088 | tf_op jit(solution)/shard_map/ppermute | solution.py:478
  69.4 18.3 %collective-permute-start.9 = (bf16[4,80,896]{2,1,0:T(8,128)(2,1)}, bf16[4,80,896]{2,1,0:T(8,128)(2,1)}, u32[]{:S(2)}, u32[]{:S(2)}) collective-permute-start(bf16[4,80,896]{2,1,0:T(8,128)(2,1)} %collective-permute-done.7.refs_5_), channel_id=1, source_target_pairs={{0,4},{2,6},{4,0},{6,2},{8,12},{10,14},{12,8},{14,10},{16,20},{18,... | collective-permute-start | bytes 1720328 | tf_op jit(solution)/shard_map/ppermute | solution.py:482
  78.6 19.0 %collective-permute-start.12 = (bf16[80,2560]{1,0:T(8,128)(2,1)}, bf16[80,2560]{1,0:T(8,128)(2,1)}, u32[]{:S(2)}, u32[]{:S(2)}) collective-permute-start(bf16[80,2560]{1,0:T(8,128)(2,1)} %copy-done.56), channel_id=1, source_target_pairs={{0,8},{2,10},{4,12},{6,14},{8,24},{10,26},{12,28},{14,30},{24,16},... | collective-permute-start | bytes 1228808 | tf_op jit(solution)/shard_map/ppermute | solution.py:490
  80.7 18.5 %collective-permute-start.13 = (bf16[320,640]{1,0:T(8,128)(2,1)}, bf16[320,640]{1,0:T(8,128)(2,1)}, u32[]{:S(2)}, u32[]{:S(2)}) collective-permute-start(bf16[320,640]{1,0:T(8,128)(2,1)} %collective-permute-done.11), channel_id=1, source_target_pairs={{0,8},{2,10},{4,12},{6,14},{8,24},{10,26},{12,28},{14,30},{24,16},... | collective-permute-start | bytes 1228808 | tf_op jit(solution)/shard_map/ppermute | solution.py:490
  93.5 14.3 %collective-permute-start.14 = (bf16[4,80,384]{2,1,0:T(8,128)(2,1)S(1)}, bf16[4,80,384]{2,1,0:T(8,128)(2,1)S(1)}, u32[]{:S(2)}, u32[]{:S(2)}) collective-permute-start(bf16[4,80,384]{2,1,0:T(8,128)(2,1)S(1)} %slice.161.refs_0_), channel_id=1, source_target_pairs={{0,2},{2,0},{4,6},{6,4},{8,10},{10,8},{12,14},{14,12},{16,18},{18,... | collective-permute-start | bytes 737288 | tf_op jit(solution)/shard_map/ppermute | solution.py:478
  94.1 13.7 %collective-permute-start.15 = (bf16[4,80,384]{2,1,0:T(8,128)(2,1)S(1)}, bf16[4,80,384]{2,1,0:T(8,128)(2,1)S(1)}, u32[]{:S(2)}, u32[]{:S(2)}) collective-permute-start(bf16[4,80,384]{2,1,0:T(8,128)(2,1)S(1)} %slice.161.refs_0_), channel_id=1, source_target_pairs={{0,4},{2,6},{4,0},{6,2},{8,12},{10,14},{12,8},{14,10},{16,20},{18,... | collective-permute-start | bytes 737288 | tf_op jit(solution)/shard_map/ppermute | solution.py:482
  99.2 13.2 %collective-permute-start.18 = (bf16[80,2560]{1,0:T(8,128)(2,1)}, bf16[80,2560]{1,0:T(8,128)(2,1)S(1)}, u32[]{:S(2)}, u32[]{:S(2)}) collective-permute-start(bf16[80,2560]{1,0:T(8,128)(2,1)} %collective-permute-done.12), channel_id=1, source_target_pairs={{0,8},{2,10},{4,12},{6,14},{8,24},{10,26},{12,28},{14,30},{24,16},... | collective-permute-start | bytes 1228808 | tf_op jit(solution)/shard_map/ppermute | solution.py:490
  101.5 15.2 %collective-permute-start.19 = (bf16[320,640]{1,0:T(8,128)(2,1)}, bf16[320,640]{1,0:T(8,128)(2,1)S(1)}, u32[]{:S(2)}, u32[]{:S(2)}) collective-permute-start(bf16[320,640]{1,0:T(8,128)(2,1)} %collective-permute-done.13), channel_id=1, source_target_pairs={{0,8},{2,10},{4,12},{6,14},{8,24},{10,26},{12,28},{14,30},{24,16},... | collective-permute-start | bytes 1228808 | tf_op jit(solution)/shard_map/ppermute | solution.py:490
  107.8 21.8 %collective-permute-start.20 = (bf16[4,80,384]{2,1,0:T(8,128)(2,1)S(1)}, bf16[4,80,384]{2,1,0:T(8,128)(2,1)S(1)}, u32[]{:S(2)}, u32[]{:S(2)}) collective-permute-start(bf16[4,80,384]{2,1,0:T(8,128)(2,1)S(1)} %collective-permute-done.15.refs_2_), channel_id=1, source_target_pairs={{0,2},{2,0},{4,6},{6,4},{8,10},{10,8},{12,14},{14,12},{16,18},{18,... | collective-permute-start | bytes 737288 | tf_op jit(solution)/shard_map/ppermute | solution.py:478
  109.4 18.6 %collective-permute-start.21 = (bf16[4,80,256]{2,1,0:T(8,128)(2,1)S(1)}, bf16[4,80,256]{2,1,0:T(8,128)(2,1)S(1)}, u32[]{:S(2)}, u32[]{:S(2)}) collective-permute-start(bf16[4,80,256]{2,1,0:T(8,128)(2,1)S(1)} %collective-permute-done.16.refs_5_), channel_id=1, source_target_pairs={{0,4},{2,6},{4,0},{6,2},{8,12},{10,14},{12,8},{14,10},{16,20},{18,... | collective-permute-start | bytes 491528 | tf_op jit(solution)/shard_map/ppermute | solution.py:482
  119.3 41.0 %collective-permute-start.23 = (bf16[4,80,1280]{2,1,0:T(8,128)(2,1)}, bf16[4,80,1280]{2,1,0:T(8,128)(2,1)}, u32[]{:S(2)}, u32[]{:S(2)}) collective-permute-start(bf16[4,80,1280]{2,1,0:T(8,128)(2,1)} %get-tuple-element.178.refs_0_), channel_id=1, source_target_pairs={{0,2},{2,0},{4,6},{6,4},{8,10},{10,8},{12,14},{14,12},{16,18},{18,... | collective-permute-start | bytes 2457608 | tf_op jit(solution)/shard_map/ppermute | solution.py:478
  120.8 39.5 %collective-permute-start.24 = (bf16[4,80,1280]{2,1,0:T(8,128)(2,1)}, bf16[4,80,1280]{2,1,0:T(8,128)(2,1)}, u32[]{:S(2)}, u32[]{:S(2)}) collective-permute-start(bf16[4,80,1280]{2,1,0:T(8,128)(2,1)} %get-tuple-element.178.refs_0_), channel_id=1, source_target_pairs={{0,4},{2,6},{4,0},{6,2},{8,12},{10,14},{12,8},{14,10},{16,20},{18,... | collective-permute-start | bytes 2457608 | tf_op jit(solution)/shard_map/ppermute | solution.py:482
  125.7 34.6 %collective-permute-start.25 = (bf16[4,80,1280]{2,1,0:T(8,128)(2,1)S(1)}, bf16[4,80,1280]{2,1,0:T(8,128)(2,1)}, u32[]{:S(2)}, u32[]{:S(2)}) collective-permute-start(bf16[4,80,1280]{2,1,0:T(8,128)(2,1)S(1)} %get-tuple-element.182.refs_4_), channel_id=1, source_target_pairs={{0,2},{2,0},{4,6},{6,4},{8,10},{10,8},{12,14},{14,12},{16,18},{18,... | collective-permute-start | bytes 2457608 | tf_op jit(solution)/shard_map/ppermute | solution.py:478
  128.0 32.3 %collective-permute-start.26 = (bf16[4,80,1280]{2,1,0:T(8,128)(2,1)S(1)}, bf16[4,80,1280]{2,1,0:T(8,128)(2,1)}, u32[]{:S(2)}, u32[]{:S(2)}) collective-permute-start(bf16[4,80,1280]{2,1,0:T(8,128)(2,1)S(1)} %get-tuple-element.182.refs_4_), channel_id=1, source_target_pairs={{0,4},{2,6},{4,0},{6,2},{8,12},{10,14},{12,8},{14,10},{16,20},{18,... | collective-permute-start | bytes 2457608 | tf_op jit(solution)/shard_map/ppermute | solution.py:482
  161.4 21.1 %collective-permute-start.29 = (bf16[4,160,640]{2,1,0:T(8,128)(2,1)S(1)}, bf16[4,160,640]{2,1,0:T(8,128)(2,1)}, u32[]{:S(2)}, u32[]{:S(2)}) collective-permute-start(bf16[4,160,640]{2,1,0:T(8,128)(2,1)S(1)} %get-tuple-element.186.refs_0_), channel_id=1, source_target_pairs={{0,2},{2,0},{4,6},{6,4},{8,10},{10,8},{12,14},{14,12},{16,18},{18,... | collective-permute-start | bytes 2457608 | tf_op jit(solution)/shard_map/ppermute | solution.py:478
  162.9 42.2 %collective-permute-start.30 = (bf16[4,160,640]{2,1,0:T(8,128)(2,1)S(1)}, bf16[4,160,640]{2,1,0:T(8,128)(2,1)S(1)}, u32[]{:S(2)}, u32[]{:S(2)}) collective-permute-start(bf16[4,160,640]{2,1,0:T(8,128)(2,1)S(1)} %get-tuple-element.186.refs_0_), channel_id=1, source_target_pairs={{0,4},{2,6},{4,0},{6,2},{8,12},{10,14},{12,8},{14,10},{16,20},{18,... | collective-permute-start | bytes 2457608 | tf_op jit(solution)/shard_map/ppermute | solution.py:482
  165.0 40.1 %collective-permute-start.31 = (bf16[4,160,640]{2,1,0:T(8,128)(2,1)S(1)}, bf16[4,160,640]{2,1,0:T(8,128)(2,1)S(1)}, u32[]{:S(2)}, u32[]{:S(2)}) collective-permute-start(bf16[4,160,640]{2,1,0:T(8,128)(2,1)S(1)} %get-tuple-element.190.refs_4_), channel_id=1, source_target_pairs={{0,2},{2,0},{4,6},{6,4},{8,10},{10,8},{12,14},{14,12},{16,18},{18,... | collective-permute-start | bytes 2457608 | tf_op jit(solution)/shard_map/ppermute | solution.py:478
  165.0 40.1 %collective-permute-start.32 = (bf16[4,160,640]{2,1,0:T(8,128)(2,1)S(1)}, bf16[4,160,640]{2,1,0:T(8,128)(2,1)S(1)}, u32[]{:S(2)}, u32[]{:S(2)}) collective-permute-start(bf16[4,160,640]{2,1,0:T(8,128)(2,1)S(1)} %get-tuple-element.190.refs_4_), channel_id=1, source_target_pairs={{0,4},{2,6},{4,0},{6,2},{8,12},{10,14},{12,8},{14,10},{16,20},{18,... | collective-permute-start | bytes 2457608 | tf_op jit(solution)/shard_map/ppermute | solution.py:482
  165.4 51.7 %collective-permute-start.27 = (bf16[4,80,1280]{2,1,0:T(8,128)(2,1)}, bf16[4,80,1280]{2,1,0:T(8,128)(2,1)S(1)}, u32[]{:S(2)}, u32[]{:S(2)}) collective-permute-start(bf16[4,80,1280]{2,1,0:T(8,128)(2,1)} %collective-permute-done.24.refs_2_), channel_id=1, source_target_pairs={{0,2},{2,0},{4,6},{6,4},{8,10},{10,8},{12,14},{14,12},{16,18},{18,... | collective-permute-start | bytes 2457608 | tf_op jit(solution)/shard_map/ppermute | solution.py:478
  182.5 36.3 %collective-permute-start.28 = (bf16[4,80,1280]{2,1,0:T(8,128)(2,1)}, bf16[4,80,1280]{2,1,0:T(8,128)(2,1)}, u32[]{:S(2)}, u32[]{:S(2)}) collective-permute-start(bf16[4,80,1280]{2,1,0:T(8,128)(2,1)} %collective-permute-done.25.refs_5_), channel_id=1, source_target_pairs={{0,4},{2,6},{4,0},{6,2},{8,12},{10,14},{12,8},{14,10},{16,20},{18,... | collective-permute-start | bytes 2457608 | tf_op jit(solution)/shard_map/ppermute | solution.py:482
  219.2 20.7 %collective-permute-start.34 = (bf16[4,160,640]{2,1,0:T(8,128)(2,1)S(1)}, bf16[4,160,640]{2,1,0:T(8,128)(2,1)S(1)}, u32[]{:S(2)}, u32[]{:S(2)}) collective-permute-start(bf16[4,160,640]{2,1,0:T(8,128)(2,1)S(1)} %collective-permute-done.30.refs_2_), channel_id=1, source_target_pairs={{0,2},{2,0},{4,6},{6,4},{8,10},{10,8},{12,14},{14,12},{16,18},{18,... | collective-permute-start | bytes 2457608 | tf_op jit(solution)/shard_map/ppermute | solution.py:478
  219.5 20.8 %collective-permute-start.35 = (bf16[4,160,640]{2,1,0:T(8,128)(2,1)S(1)}, bf16[4,160,640]{2,1,0:T(8,128)(2,1)S(1)}, u32[]{:S(2)}, u32[]{:S(2)}) collective-permute-start(bf16[4,160,640]{2,1,0:T(8,128)(2,1)S(1)} %collective-permute-done.31.refs_5_), channel_id=1, source_target_pairs={{0,4},{2,6},{4,0},{6,2},{8,12},{10,14},{12,8},{14,10},{16,20},{18,... | collective-permute-start | bytes 2457608 | tf_op jit(solution)/shard_map/ppermute | solution.py:482
  252.8 48.0 %collective-permute-start.37 = (bf16[1024,1280]{1,0:T(8,128)(2,1)}, bf16[1024,1280]{1,0:T(8,128)(2,1)}, u32[]{:S(2)}, u32[]{:S(2)}) collective-permute-start(bf16[1024,1280]{1,0:T(8,128)(2,1)} %multiply_convert_fusion.normed_ref), channel_id=1, source_target_pairs={{0,1},{1,0},{2,3},{3,2},{4,5},{5,4},{6,7},{7,6},{8,9},{9,8},{10,11... | collective-permute-start | bytes 7864328 | tf_op jit(solution)/shard_map/ppermute | solution.py:283
  253.3 52.7 %collective-permute-start.38 = (bf16[2,512,1280]{2,1,0:T(8,128)(2,1)}, bf16[2,512,1280]{2,1,0:T(8,128)(2,1)}, u32[]{:S(2)}, u32[]{:S(2)}) collective-permute-start(bf16[2,512,1280]{2,1,0:T(8,128)(2,1)} %param.21), channel_id=1, source_target_pairs={{0,1},{1,0},{2,3},{3,2},{4,5},{5,4},{6,7},{7,6},{8,9},{9,8},{10,11... | collective-permute-start | bytes 7864328 | tf_op jit(solution)/shard_map/ppermute | solution.py:283
  348.2 41.5 %collective-permute-start.40 = (bf16[1024,1280]{1,0:T(8,128)(2,1)}, bf16[1024,1280]{1,0:T(8,128)(2,1)S(1)}, u32[]{:S(2)}, u32[]{:S(2)}) collective-permute-start(bf16[1024,1280]{1,0:T(8,128)(2,1)} %get-tuple-element.202), channel_id=1, source_target_pairs={{0,1},{1,0},{2,3},{3,2},{4,5},{5,4},{6,7},{7,6},{8,9},{9,8},{10,11... | collective-permute-start | bytes 7864328 | tf_op jit(solution)/shard_map/ppermute | solution.py:283
  368.7 23.8 %collective-permute-start.41 = (bf16[2560,640]{1,0:T(8,128)(2,1)}, bf16[2560,640]{1,0:T(8,128)(2,1)S(1)}, u32[]{:S(2)}, u32[]{:S(2)}) collective-permute-start(bf16[2560,640]{1,0:T(8,128)(2,1)} %get-tuple-element.286), channel_id=1, source_target_pairs={{0,1},{1,0},{2,3},{3,2},{4,5},{5,4},{6,7},{7,6},{8,9},{9,8},{10,11... | collective-permute-start | bytes 9830408 | tf_op jit(solution)/shard_map/ppermute | solution.py:283
  407.7 20.2 %collective-permute-start.42 = (bf16[4,160,640]{2,1,0:T(8,128)(2,1)S(1)}, bf16[4,160,640]{2,1,0:T(8,128)(2,1)S(1)}, u32[]{:S(2)}, u32[]{:S(2)}) collective-permute-start(bf16[4,160,640]{2,1,0:T(8,128)(2,1)S(1)} %get-tuple-element.284), channel_id=1, source_target_pairs={{0,2},{2,0},{4,6},{6,4},{8,10},{10,8},{12,14},{14,12},{16,18},{18,... | collective-permute-start | bytes 2457608 | tf_op jit(solution)/shard_map/ppermute | solution.py:478
  409.0 19.9 %collective-permute-start.43 = (bf16[4,160,640]{2,1,0:T(8,128)(2,1)S(1)}, bf16[4,160,640]{2,1,0:T(8,128)(2,1)S(1)}, u32[]{:S(2)}, u32[]{:S(2)}) collective-permute-start(bf16[4,160,640]{2,1,0:T(8,128)(2,1)S(1)} %get-tuple-element.283), channel_id=1, source_target_pairs={{0,4},{2,6},{4,0},{6,2},{8,12},{10,14},{12,8},{14,10},{16,20},{18,... | collective-permute-start | bytes 2457608 | tf_op jit(solution)/shard_map/ppermute | solution.py:482
  433.0 237.4 %collective-permute-start.39 = (bf16[1024,1280]{1,0:T(8,128)(2,1)}, bf16[1024,1280]{1,0:T(8,128)(2,1)}, u32[]{:S(2)}, u32[]{:S(2)}) collective-permute-start(bf16[1024,1280]{1,0:T(8,128)(2,1)} %get-tuple-element.200), channel_id=1, source_target_pairs={{0,1},{1,0},{2,3},{3,2},{4,5},{5,4},{6,7},{7,6},{8,9},{9,8},{10,11... | collective-permute-start | bytes 7864328 | tf_op jit(solution)/shard_map/ppermute | solution.py:283
  436.7 40.8 %collective-permute-start.46 = (bf16[4,160,640]{2,1,0:T(8,128)(2,1)S(1)}, bf16[4,160,640]{2,1,0:T(8,128)(2,1)S(1)}, u32[]{:S(2)}, u32[]{:S(2)}) collective-permute-start(bf16[4,160,640]{2,1,0:T(8,128)(2,1)S(1)} %copy-done.46), channel_id=1, source_target_pairs={{0,4},{2,6},{4,0},{6,2},{8,12},{10,14},{12,8},{14,10},{16,20},{18,... | collective-permute-start | bytes 2457608 | tf_op jit(solution)/shard_map/ppermute | solution.py:482
  438.5 40.7 %collective-permute-start.45 = (bf16[4,160,640]{2,1,0:T(8,128)(2,1)S(1)}, bf16[4,160,640]{2,1,0:T(8,128)(2,1)S(1)}, u32[]{:S(2)}, u32[]{:S(2)}) collective-permute-start(bf16[4,160,640]{2,1,0:T(8,128)(2,1)S(1)} %copy-done.45), channel_id=1, source_target_pairs={{0,2},{2,0},{4,6},{6,4},{8,10},{10,8},{12,14},{14,12},{16,18},{18,... | collective-permute-start | bytes 2457608 | tf_op jit(solution)/shard_map/ppermute | solution.py:478
  440.2 35.8 %collective-permute-start.48 = (bf16[4,160,640]{2,1,0:T(8,128)(2,1)S(1)}, bf16[4,160,640]{2,1,0:T(8,128)(2,1)S(1)}, u32[]{:S(2)}, u32[]{:S(2)}) collective-permute-start(bf16[4,160,640]{2,1,0:T(8,128)(2,1)S(1)} %get-tuple-element.279), channel_id=1, source_target_pairs={{0,2},{2,0},{4,6},{6,4},{8,10},{10,8},{12,14},{14,12},{16,18},{18,... | collective-permute-start | bytes 2457608 | tf_op jit(solution)/shard_map/ppermute | solution.py:478
  441.1 35.3 %collective-permute-start.47 = (bf16[4,160,640]{2,1,0:T(8,128)(2,1)S(1)}, bf16[4,160,640]{2,1,0:T(8,128)(2,1)S(1)}, u32[]{:S(2)}, u32[]{:S(2)}) collective-permute-start(bf16[4,160,640]{2,1,0:T(8,128)(2,1)S(1)} %get-tuple-element.280), channel_id=1, source_target_pairs={{0,4},{2,6},{4,0},{6,2},{8,12},{10,14},{12,8},{14,10},{16,20},{18,... | collective-permute-start | bytes 2457608 | tf_op jit(solution)/shard_map/ppermute | solution.py:482
  476.0 42.9 %collective-permute-start.51 = (bf16[4,80,1280]{2,1,0:T(8,128)(2,1)S(1)}, bf16[4,80,1280]{2,1,0:T(8,128)(2,1)S(1)}, u32[]{:S(2)}, u32[]{:S(2)}) collective-permute-start(bf16[4,80,1280]{2,1,0:T(8,128)(2,1)S(1)} %get-tuple-element.275), channel_id=1, source_target_pairs={{0,4},{2,6},{4,0},{6,2},{8,12},{10,14},{12,8},{14,10},{16,20},{18,... | collective-permute-start | bytes 2457608 | tf_op jit(solution)/shard_map/ppermute | solution.py:482
  476.3 46.2 %collective-permute-start.50 = (bf16[4,80,1280]{2,1,0:T(8,128)(2,1)S(1)}, bf16[4,80,1280]{2,1,0:T(8,128)(2,1)}, u32[]{:S(2)}, u32[]{:S(2)}) collective-permute-start(bf16[4,80,1280]{2,1,0:T(8,128)(2,1)S(1)} %get-tuple-element.276), channel_id=1, source_target_pairs={{0,2},{2,0},{4,6},{6,4},{8,10},{10,8},{12,14},{14,12},{16,18},{18,... | collective-permute-start | bytes 2457608 | tf_op jit(solution)/shard_map/ppermute | solution.py:478
  477.5 92.5 %collective-permute-start.54 = (bf16[4,80,1280]{2,1,0:T(8,128)(2,1)}, bf16[4,80,1280]{2,1,0:T(8,128)(2,1)}, u32[]{:S(2)}, u32[]{:S(2)}) collective-permute-start(bf16[4,80,1280]{2,1,0:T(8,128)(2,1)} %get-tuple-element.273), channel_id=1, source_target_pairs={{0,4},{2,6},{4,0},{6,2},{8,12},{10,14},{12,8},{14,10},{16,20},{18,... | collective-permute-start | bytes 2457608 | tf_op jit(solution)/shard_map/ppermute | solution.py:482
  479.2 105.9 %collective-permute-start.53 = (bf16[4,80,1280]{2,1,0:T(8,128)(2,1)S(1)}, bf16[4,80,1280]{2,1,0:T(8,128)(2,1)}, u32[]{:S(2)}, u32[]{:S(2)}) collective-permute-start(bf16[4,80,1280]{2,1,0:T(8,128)(2,1)S(1)} %get-tuple-element.274), channel_id=1, source_target_pairs={{0,2},{2,0},{4,6},{6,4},{8,10},{10,8},{12,14},{14,12},{16,18},{18,... | collective-permute-start | bytes 2457608 | tf_op jit(solution)/shard_map/ppermute | solution.py:478
  518.9 12.4 %collective-permute-start.49 = (bf16[320,640]{1,0:T(8,128)(2,1)S(1)}, bf16[320,640]{1,0:T(8,128)(2,1)S(1)}, u32[]{:S(2)}, u32[]{:S(2)}) collective-permute-start(bf16[320,640]{1,0:T(8,128)(2,1)S(1)} %fusion.74), channel_id=1, source_target_pairs={{0,8},{2,10},{4,12},{6,14},{8,24},{10,26},{12,28},{14,30},{24,16},... | collective-permute-start | bytes 1228808 | tf_op jit(solution)/shard_map/ppermute | solution.py:490
  525.9 63.9 %collective-permute-start.56 = (bf16[4,80,1280]{2,1,0:T(8,128)(2,1)}, bf16[4,80,1280]{2,1,0:T(8,128)(2,1)}, u32[]{:S(2)}, u32[]{:S(2)}) collective-permute-start(bf16[4,80,1280]{2,1,0:T(8,128)(2,1)} %get-tuple-element.271), channel_id=1, source_target_pairs={{0,2},{2,0},{4,6},{6,4},{8,10},{10,8},{12,14},{14,12},{16,18},{18,... | collective-permute-start | bytes 2457608 | tf_op jit(solution)/shard_map/ppermute | solution.py:478
  531.3 58.5 %collective-permute-start.55 = (bf16[4,80,1280]{2,1,0:T(8,128)(2,1)}, bf16[4,80,1280]{2,1,0:T(8,128)(2,1)}, u32[]{:S(2)}, u32[]{:S(2)}) collective-permute-start(bf16[4,80,1280]{2,1,0:T(8,128)(2,1)} %get-tuple-element.272), channel_id=1, source_target_pairs={{0,4},{2,6},{4,0},{6,2},{8,12},{10,14},{12,8},{14,10},{16,20},{18,... | collective-permute-start | bytes 2457608 | tf_op jit(solution)/shard_map/ppermute | solution.py:482
  570.0 25.3 %collective-permute-start.52 = (bf16[320,640]{1,0:T(8,128)(2,1)S(1)}, bf16[320,640]{1,0:T(8,128)(2,1)S(1)}, u32[]{:S(2)}, u32[]{:S(2)}) collective-permute-start(bf16[320,640]{1,0:T(8,128)(2,1)S(1)} %fusion.54), channel_id=1, source_target_pairs={{0,8},{2,10},{4,12},{6,14},{8,24},{10,26},{12,28},{14,30},{24,16},... | collective-permute-start | bytes 1228808 | tf_op jit(solution)/shard_map/ppermute | solution.py:490
  604.3 27.0 %collective-permute-start.61 = (bf16[80,2560]{1,0:T(8,128)(2,1)S(1)}, bf16[80,2560]{1,0:T(8,128)(2,1)S(1)}, u32[]{:S(2)}, u32[]{:S(2)}) collective-permute-start(bf16[80,2560]{1,0:T(8,128)(2,1)S(1)} %fusion.53), channel_id=1, source_target_pairs={{0,8},{2,10},{4,12},{6,14},{8,24},{10,26},{12,28},{14,30},{24,16},... | collective-permute-start | bytes 1228808 | tf_op jit(solution)/shard_map/ppermute | solution.py:490
  615.3 20.6 %collective-permute-start.60 = (bf16[4,80,1280]{2,1,0:T(8,128)(2,1)S(1)}, bf16[4,80,1280]{2,1,0:T(8,128)(2,1)S(1)}, u32[]{:S(2)}, u32[]{:S(2)}) collective-permute-start(bf16[4,80,1280]{2,1,0:T(8,128)(2,1)S(1)} %pad_maximum_fusion.12), channel_id=1, source_target_pairs={{0,4},{2,6},{4,0},{6,2},{8,12},{10,14},{12,8},{14,10},{16,20},{18,... | collective-permute-start | bytes 2457608 | tf_op jit(solution)/shard_map/ppermute | solution.py:482
  619.6 20.1 %collective-permute-start.59 = (bf16[4,80,1280]{2,1,0:T(8,128)(2,1)S(1)}, bf16[4,80,1280]{2,1,0:T(8,128)(2,1)S(1)}, u32[]{:S(2)}, u32[]{:S(2)}) collective-permute-start(bf16[4,80,1280]{2,1,0:T(8,128)(2,1)S(1)} %pad_maximum_fusion.11), channel_id=1, source_target_pairs={{0,2},{2,0},{4,6},{6,4},{8,10},{10,8},{12,14},{14,12},{16,18},{18,... | collective-permute-start | bytes 2457608 | tf_op jit(solution)/shard_map/ppermute | solution.py:478
  644.3 27.9 %collective-permute-start.63 = (bf16[2,512,1280]{2,1,0:T(8,128)(2,1)}, bf16[2,512,1280]{2,1,0:T(8,128)(2,1)}, u32[]{:S(2)}, u32[]{:S(2)}) collective-permute-start(bf16[2,512,1280]{2,1,0:T(8,128)(2,1)} %dynamic-slice_convert_fusion), channel_id=1, source_target_pairs={{0,1},{1,0},{2,3},{3,2},{4,5},{5,4},{6,7},{7,6},{8,9},{9,8},{10,11... | collective-permute-start | bytes 7864328 | tf_op jit(solution)/shard_map/ppermute | solution.py:283
  646.3 13.0 %collective-permute-start.76 = (bf16[320,640]{1,0:T(8,128)(2,1)}, bf16[320,640]{1,0:T(8,128)(2,1)}, u32[]{:S(2)}, u32[]{:S(2)}) collective-permute-start(bf16[320,640]{1,0:T(8,128)(2,1)} %fusion.49), channel_id=1, source_target_pairs={{0,8},{2,10},{4,12},{6,14},{8,24},{10,26},{12,28},{14,30},{24,16},... | collective-permute-start | bytes 1228808 | tf_op jit(solution)/shard_map/ppermute | solution.py:490
  663.6 21.2 %collective-permute-start.65 = (bf16[4,80,1280]{2,1,0:T(8,128)(2,1)S(1)}, bf16[4,80,1280]{2,1,0:T(8,128)(2,1)S(1)}, u32[]{:S(2)}, u32[]{:S(2)}) collective-permute-start(bf16[4,80,1280]{2,1,0:T(8,128)(2,1)S(1)} %pad_maximum_fusion.14), channel_id=1, source_target_pairs={{0,4},{2,6},{4,0},{6,2},{8,12},{10,14},{12,8},{14,10},{16,20},{18,... | collective-permute-start | bytes 2457608 | tf_op jit(solution)/shard_map/ppermute | solution.py:482
  665.2 37.2 %collective-permute-start.62 = (bf16[4,80,1280]{2,1,0:T(8,128)(2,1)S(1)}, bf16[4,80,1280]{2,1,0:T(8,128)(2,1)S(1)}, u32[]{:S(2)}, u32[]{:S(2)}) collective-permute-start(bf16[4,80,1280]{2,1,0:T(8,128)(2,1)S(1)} %pad_maximum_fusion.13), channel_id=1, source_target_pairs={{0,2},{2,0},{4,6},{6,4},{8,10},{10,8},{12,14},{14,12},{16,18},{18,... | collective-permute-start | bytes 2457608 | tf_op jit(solution)/shard_map/ppermute | solution.py:478
  667.0 35.4 %collective-permute-start.66 = (bf16[4,80,1280]{2,1,0:T(8,128)(2,1)S(1)}, bf16[4,80,1280]{2,1,0:T(8,128)(2,1)S(1)}, u32[]{:S(2)}, u32[]{:S(2)}) collective-permute-start(bf16[4,80,1280]{2,1,0:T(8,128)(2,1)S(1)} %add_convert_fusion.2), channel_id=1, source_target_pairs={{0,2},{2,0},{4,6},{6,4},{8,10},{10,8},{12,14},{14,12},{16,18},{18,... | collective-permute-start | bytes 2457608 | tf_op jit(solution)/shard_map/ppermute | solution.py:478
  670.4 32.0 %collective-permute-start.64 = (bf16[4,80,1280]{2,1,0:T(8,128)(2,1)S(1)}, bf16[4,80,1280]{2,1,0:T(8,128)(2,1)S(1)}, u32[]{:S(2)}, u32[]{:S(2)}) collective-permute-start(bf16[4,80,1280]{2,1,0:T(8,128)(2,1)S(1)} %add_convert_fusion.4), channel_id=1, source_target_pairs={{0,4},{2,6},{4,0},{6,2},{8,12},{10,14},{12,8},{14,10},{16,20},{18,... | collective-permute-start | bytes 2457608 | tf_op jit(solution)/shard_map/ppermute | solution.py:482
  676.4 26.6 %collective-permute-start.68 = (f32[2,1280]{1,0:T(2,128)S(1)}, f32[2,1280]{1,0:T(2,128)S(1)}, u32[]{:S(2)}, u32[]{:S(2)}) collective-permute-start(f32[2,1280]{1,0:T(2,128)S(1)} %pad_maximum_fusion.15), channel_id=1, source_target_pairs={{0,1},{1,0},{2,3},{3,2},{4,5},{5,4},{6,7},{7,6},{8,9},{9,8},{10,11... | collective-permute-start | bytes 30728 | tf_op jit(solution)/shard_map/ppermute | solution.py:283
  712.6 16.1 %collective-permute-start.71 = (f32[2,1280]{1,0:T(2,128)S(1)}, f32[2,1280]{1,0:T(2,128)S(1)}, u32[]{:S(2)}, u32[]{:S(2)}) collective-permute-start(f32[2,1280]{1,0:T(2,128)S(1)} %add.445), channel_id=1, source_target_pairs={{0,8},{2,10},{4,12},{6,14},{8,0},{10,2},{12,4},{14,6},{16,24},{18,... | collective-permute-start | bytes 30728 | tf_op jit(solution)/shard_map/ppermute | solution.py:669
  714.2 14.6 %collective-permute-start.73 = (bf16[80,2560]{1,0:T(8,128)(2,1)S(1)}, bf16[80,2560]{1,0:T(8,128)(2,1)S(1)}, u32[]{:S(2)}, u32[]{:S(2)}) collective-permute-start(bf16[80,2560]{1,0:T(8,128)(2,1)S(1)} %fusion.51), channel_id=1, source_target_pairs={{0,8},{2,10},{4,12},{6,14},{8,24},{10,26},{12,28},{14,30},{24,16},... | collective-permute-start | bytes 1228808 | tf_op jit(solution)/shard_map/ppermute | solution.py:490
  715.0 21.5 %collective-permute-start.75 = (bf16[80,2560]{1,0:T(8,128)(2,1)S(1)}, bf16[80,2560]{1,0:T(8,128)(2,1)S(1)}, u32[]{:S(2)}, u32[]{:S(2)}) collective-permute-start(bf16[80,2560]{1,0:T(8,128)(2,1)S(1)} %fusion.50), channel_id=1, source_target_pairs={{0,8},{2,10},{4,12},{6,14},{8,24},{10,26},{12,28},{14,30},{24,16},... | collective-permute-start | bytes 1228808 | tf_op jit(solution)/shard_map/ppermute | solution.py:490
  728.9 12.8 %collective-permute-start.74 = (bf16[80,2560]{1,0:T(8,128)(2,1)S(1)}, bf16[80,2560]{1,0:T(8,128)(2,1)S(1)}, u32[]{:S(2)}, u32[]{:S(2)}) collective-permute-start(bf16[80,2560]{1,0:T(8,128)(2,1)S(1)} %fusion.52), channel_id=1, source_target_pairs={{0,8},{2,10},{4,12},{6,14},{8,24},{10,26},{12,28},{14,30},{24,16},... | collective-permute-start | bytes 1228808 | tf_op jit(solution)/shard_map/ppermute | solution.py:490
  (97 other events, 1383.6 us)

commit v3 on v2

--- a/solution.py
+++ b/solution.py
@@ -298,8 +298,10 @@
     return lax.dynamic_slice_in_dim(values, index * half, half, axis)
 
 
-def attend_kernel(start_ref, count_ref, column_ref, line_ref, q_ref, k_ref, v_ref, out_ref):
-    row = pl.program_id(0)
+def attend_kernel(
+    row, begun, start_ref, count_ref, column_ref, line_ref, q_ref, k_ref, v_ref, *rest
+):
+    (out_ref,) = rest[begun:]
     length = k_ref.shape[1]
     lower = lax.broadcasted_iota(jnp.int32, (QUERY_TILE, LANES), 1) < HEAD_DIM
 
@@ -339,21 +341,9 @@
 
 
 def attend_back_kernel(
-    start_ref,
-    count_ref,
-    column_ref,
-    line_ref,
-    q_ref,
-    k_ref,
-    v_ref,
-    grad_ref,
-    dq_ref,
-    dk_ref,
-    dv_ref,
-    dk_sum,
-    dv_sum,
+    row, begun, start_ref, count_ref, column_ref, line_ref, q_ref, k_ref, v_ref, grad_ref, *rest
 ):
-    row = pl.program_id(0)
+    dq_ref, dk_ref, dv_ref, dk_sum, dv_sum = rest[begun:]
     length = k_ref.shape[1]
     lower = lax.broadcasted_iota(jnp.int32, (QUERY_TILE, LANES), 1) < HEAD_DIM
     dk_sum[...] = jnp.zeros_like(dk_sum)
@@ -424,32 +414,39 @@
     return start, (end + LANES - 1) // LANES - start
 
 
-def attention_call(kernel, windows, marks, operands, outputs, scratch):
-    rows, length, width = operands[0].shape
-    block = pl.BlockSpec((1, length, LANES), lambda row, pair, *_: (row, 0, pair))
-    grid = (rows, width // LANES)
-    work = rows * width * length * length
+def attention_call(kernel, row, windows, marks, operands, outputs, scratch, begun=()):
+    rows, length, width = operands[0][0].shape
+    wide = outputs[0]
+    pairs = wide // LANES
+
+    def block(first):
+        return pl.BlockSpec((1, length, LANES), lambda pair, *_: (row, 0, first + pair))
+
+    work = wide * length * length
+    shape = jax.ShapeDtypeStruct((rows, length, wide), jnp.bfloat16)
     return pl.pallas_call(
-        kernel,
+        functools.partial(kernel, row, len(begun)),
         grid_spec=pltpu.PrefetchScalarGridSpec(
             num_scalar_prefetch=2,
-            grid=grid,
+            grid=(pairs,),
             in_specs=[
-                pl.BlockSpec((1, length, LANES), lambda row, pair, *_: (row, 0, 0)),
-                pl.BlockSpec((1, 8, length), lambda row, pair, *_: (row, 0, 0)),
+                pl.BlockSpec((1, length, LANES), lambda pair, *_: (row, 0, 0)),
+                pl.BlockSpec((1, 8, length), lambda pair, *_: (row, 0, 0)),
             ]
-            + [block] * len(operands),
-            out_specs=[block] * outputs,
+            + [block(first) for _, first in operands]
+            + [pl.BlockSpec(memory_space=pl.ANY)] * len(begun),
+            out_specs=[block(0)] * len(outputs),
             scratch_shapes=scratch,
         ),
-        out_shape=[jax.ShapeDtypeStruct((rows, length, width), jnp.bfloat16)] * outputs,
+        out_shape=[shape] * len(outputs),
+        input_output_aliases={4 + len(operands) + index: index for index in range(len(begun))},
         compiler_params=pltpu.CompilerParams(vmem_limit_bytes=48 * 1024 * 1024),
         cost_estimate=pl.CostEstimate(
             flops=4 * len(operands) * work,
-            bytes_accessed=2 * (len(operands) + outputs) * rows * length * width,
+            bytes_accessed=2 * (len(operands) + len(outputs)) * length * wide,
             transcendentals=work // HEAD_DIM,
         ),
-    )(*windows, *marks, *operands)
+    )(*windows, *marks, *(array for array, _ in operands), *begun)
 
 
 def norm_stats(values):
@@ -664,9 +661,513 @@
     )(place_vector(), normed, cot, *up_parts[0], *up_parts[1], down_mine, down_other, *begun)
 
 
-def swap_z(values, far):
-    pairs = [(row, row ^ (8 if far else 4)) for row in range(16)]
-    return lax.ppermute(values, "rows", pairs)
+def following(zed):
+    return (2 * zed + 1) % 5
+
+
+def preceding(zed):
+    return (3 * zed + 2) % 5
+
+
+NORM_TILE = 64
+
+
+def head_kernel(
+    tokens_ref,
+    gain_ref,
+    cot_ref,
+    piece_ref,
+    up_ref,
+    normed_out,
+    cot_out,
+    weights_out,
+    up_out,
+    token_buf,
+    normed_buf,
+    local_sems,
+    send_sems,
+    recv_sems,
+):
+    row, core = lax.axis_index("rows"), lax.axis_index("seq")
+    zed, here_y, here_x = row // 4, (row // 2) % 2, row % 2
+    rest = row - 4 * zed
+    over_x, over_y = row + 1 - 2 * here_x, row + 2 - 4 * here_y
+    onward, backward = following(zed) * 4 + rest, preceding(zed) * 4 + rest
+    places = [zed]
+    for _ in range(3):
+        places.append(preceding(places[-1]))
+    depth, wide = piece_ref.shape
+    half = wide // 2
+
+    barrier = pltpu.get_barrier_semaphore()
+    for target in ((onward, core), (backward, core), (over_x, core), (over_y, core), (row, 1 - core)):
+        pl.semaphore_signal(
+            barrier, inc=1, device_id=target, device_id_type=pl.DeviceIdType.MESH
+        )
+    load = pltpu.make_async_copy(tokens_ref, token_buf, local_sems.at[0])
+    load.start()
+    own_rows = pl.ds(pl.multiple_of(row * depth, 16), depth)
+    keeps = [
+        pltpu.make_async_copy(piece_ref, weights_out.at[own_rows, :], local_sems.at[1]),
+        pltpu.make_async_copy(up_ref, up_out.at[zed], local_sems.at[2]),
+    ]
+    for keep in keeps:
+        keep.start()
+    pl.semaphore_wait(barrier, 5)
+
+    sent = []
+
+    def send(src, dst, target):
+        number = len(sent)
+        copy = pltpu.make_async_remote_copy(
+            src_ref=src,
+            dst_ref=dst,
+            send_sem=send_sems.at[number],
+            recv_sem=recv_sems.at[number],
+            device_id=target,
+            device_id_type=pl.DeviceIdType.MESH,
+        )
+        copy.start()
+        sent.append(copy)
+        return copy
+
+    def block(place, far_y, far_x, columns):
+        at_y = 1 - here_y if far_y else here_y
+        at_x = 1 - here_x if far_x else here_x
+        index = (place * 2 + at_y) * 2 + at_x
+        rows = pl.ds(pl.multiple_of(index * depth, 16), depth)
+        return weights_out.at[rows, columns]
+
+    everything, left, right = pl.ds(0, wide), pl.ds(0, half), pl.ds(half, half)
+
+    def source(step, columns):
+        if step == 0:
+            return piece_ref.at[:, columns]
+        return block(places[step], False, False, columns)
+
+    def around(step):
+        return send(
+            source(step, everything), block(places[step], False, False, everything), (onward, core)
+        )
+
+    def around_up(step):
+        src = up_ref if step == 0 else up_out.at[places[step]]
+        return send(src, up_out.at[places[step]], (onward, core))
+
+    def across(step):
+        place = places[step]
+        return (
+            send(source(step, left), block(place, False, False, left), (over_y, core)),
+            send(source(step, right), block(place, False, False, right), (over_x, core)),
+            send(source(step, left), block(place, False, False, left), (over_x, core)),
+            send(source(step, right), block(place, False, False, right), (over_y, core)),
+        )
+
+    def corner(step, crossing):
+        place = places[step]
+        crossing[0].wait_recv()
+        far_left = block(place, True, False, left)
+        first = send(far_left, far_left, (over_x, core))
+        crossing[1].wait_recv()
+        far_right = block(place, False, True, right)
+        return first, send(far_right, far_right, (over_y, core))
+
+    ring = around(0)
+    crossing = across(0)
+    arrivals = [crossing[2], crossing[3]]
+    arrivals.append(send(cot_ref, cot_out, (row, 1 - core)))
+
+    load.wait()
+    span = token_buf.shape[1]
+    for member in range(token_buf.shape[0]):
+
+        def norm_tile(tile, carry, member=member):
+            rows = pl.ds(pl.multiple_of(tile * NORM_TILE, NORM_TILE), NORM_TILE)
+            unit, _ = norm_stats(token_buf[member, rows, :].astype(jnp.float32))
+            normed_buf[member, rows, :] = (unit * gain_ref[...]).astype(jnp.bfloat16)
+            return carry
+
+        lax.fori_loop(0, span // NORM_TILE, norm_tile, 0)
+    mine = normed_out.at[:, pl.ds(pl.multiple_of(core * span, 16), span), :]
+    keeps.append(pltpu.make_async_copy(normed_buf, mine, local_sems.at[3]))
+    keeps[-1].start()
+    arrivals.append(send(normed_buf, mine, (row, 1 - core)))
+
+    up_ring = None
+    for step in range(1, 4):
+        ring.wait_recv()
+        if step < 3:
+            ring = around(step)
+        else:
+            up_ring = around_up(0)
+        arrivals += corner(step - 1, crossing)
+        crossing = across(step)
+        arrivals += crossing[2:]
+    up_ring.wait_recv()
+    up_ring = around_up(1)
+    arrivals += corner(3, crossing)
+    up_ring.wait_recv()
+    arrivals.append(around_up(2))
+    for copy in arrivals:
+        copy.wait_recv()
+    for copy in sent:
+        copy.wait_send()
+    for keep in keeps:
+        keep.wait()
+
+
+def head_call(tokens, gain, cotangent, piece, w_up):
+    rows, span, width = tokens.shape
+    depth, wide = piece.shape
+    anywhere = pl.BlockSpec(memory_space=pl.ANY)
+    return pl.pallas_call(
+        head_kernel,
+        in_specs=[anywhere, pl.BlockSpec(memory_space=pltpu.VMEM)] + [anywhere] * 3,
+        out_specs=[anywhere] * 4,
+        out_shape=[
+            jax.ShapeDtypeStruct((rows, 2 * span, width), jnp.bfloat16),
+            jax.ShapeDtypeStruct(cotangent.shape, jnp.bfloat16),
+            jax.ShapeDtypeStruct((16 * depth, wide), jnp.bfloat16),
+            jax.ShapeDtypeStruct((Z_SIZE,) + w_up.shape, jnp.bfloat16),
+        ],
+        scratch_shapes=[
+            pltpu.VMEM(tokens.shape, jnp.bfloat16),
+            pltpu.VMEM(tokens.shape, jnp.bfloat16),
+            pltpu.SemaphoreType.DMA((4,)),
+            pltpu.SemaphoreType.DMA((32,)),
+            pltpu.SemaphoreType.DMA((32,)),
+        ],
+        compiler_params=pltpu.CompilerParams(
+            collective_id=0, has_side_effects=True, vmem_limit_bytes=32 * 1024 * 1024
+        ),
+    )(tokens, gain.reshape(1, width), cotangent, piece, w_up)
+
+
+def plus_wide(*terms):
+    return sum(term.astype(jnp.float32) for term in terms)
+
+
+def plus(*terms):
+    return plus_wide(*terms).astype(jnp.bfloat16)
+
+
+TAIL_TILE = 256
+
+
+def tail_kernel(
+    dq_ref,
+    dk_ref,
+    dv_ref,
+    weights_ref,
+    query_ref,
+    key_ref,
+    value_ref,
+    tokens_ref,
+    residual_ref,
+    gain_ref,
+    ffn_gain_ref,
+    hidden_ref,
+    token_out,
+    query_out,
+    key_out,
+    value_out,
+    gain_out,
+    hidden_out,
+    weight_buf,
+    dq_buf,
+    dk_buf,
+    dv_buf,
+    own_buf,
+    away_buf,
+    came_buf,
+    token_buf,
+    residual_buf,
+    far_buf,
+    near_buf,
+    turned_buf,
+    turned_came,
+    sum_buf,
+    ring_buf,
+    ring_came,
+    gain_buf,
+    gain_came,
+    hidden_buf,
+    hidden_came,
+    local_sems,
+    send_sems,
+    recv_sems,
+):
+    row, core = lax.axis_index("rows"), lax.axis_index("seq")
+    zed, here_y, here_x = row // 4, (row // 2) % 2, row % 2
+    rest = row - 4 * zed
+    over_x, over_y = row + 1 - 2 * here_x, row + 2 - 4 * here_y
+    onward, backward = following(zed) * 4 + rest, preceding(zed) * 4 + rest
+    beside = (zed + 1 - 2 * (zed % 2)) * 4 + rest
+    beyond = (zed + 2 - 4 * (zed // 2)) * 4 + rest
+    places = [zed]
+    for _ in range(3):
+        places.append(preceding(places[-1]))
+    depth = query_out.shape[0]
+    half_wide = query_ref.shape[1]
+    span = own_buf.shape[0] // 2
+
+    barrier = pltpu.get_barrier_semaphore()
+    for target in ((onward, core), (backward, core), (over_x, core), (over_y, core), (row, 1 - core)):
+        pl.semaphore_signal(
+            barrier, inc=1, device_id=target, device_id_type=pl.DeviceIdType.MESH
+        )
+    loads = [
+        pltpu.make_async_copy(
+            weights_ref.at[:, pl.ds(0, 3 * half_wide)], weight_buf, local_sems.at[0]
+        )
+    ]
+    for index, (source, target) in enumerate(
+        (
+            (dq_ref, dq_buf),
+            (dk_ref, dk_buf),
+            (dv_ref, dv_buf),
+            (tokens_ref, token_buf),
+            (residual_ref, residual_buf),
+        )
+    ):
+        loads.append(pltpu.make_async_copy(source, target, local_sems.at[1 + index]))
+    for load in loads:
+        load.start()
+    pl.semaphore_wait(barrier, 5)
+
+    sent = []
+
+    def send(src, dst, target):
+        number = len(sent)
+        copy = pltpu.make_async_remote_copy(
+            src_ref=src,
+            dst_ref=dst,
+            send_sem=send_sems.at[number],
+            recv_sem=recv_sems.at[number],
+            device_id=target,
+            device_id_type=pl.DeviceIdType.MESH,
+        )
+        copy.start()
+        sent.append(copy)
+        return copy
+
+    cut = (half_wide // 128 + 1) // 2 * 128
+    streams = (
+        (query_ref, 0, half_wide, 0, False),
+        (key_ref, 0, cut, half_wide, False),
+        (key_ref, cut, half_wide - cut, half_wide, True),
+        (value_ref, 0, half_wide, 2 * half_wide, True),
+    )
+
+    def block_of(step, far_y, far_x):
+        at_y = 1 - here_y if far_y else here_y
+        at_x = 1 - here_x if far_x else here_x
+        index = (places[step] * 2 + at_y) * 2 + at_x
+        return pl.ds(pl.multiple_of(index * depth, 16), depth)
+
+    far, near, turned = {}, {}, {}
+
+    def issue(step):
+        for which, (grad, column, wide, base, flip) in enumerate(streams):
+            columns, place = pl.ds(column, wide), pl.ds(base + column, wide)
+            target = (over_y if flip else over_x, core)
+            far[step, which] = send(
+                grad.at[block_of(step, True, True), columns], far_buf.at[step, :, place], target
+            )
+        for which, (grad, column, wide, base, flip) in enumerate(streams):
+            columns, place = pl.ds(column, wide), pl.ds(base + column, wide)
+            target = (over_y if flip else over_x, core)
+            near[step, which] = send(
+                grad.at[block_of(step, flip, not flip), columns],
+                near_buf.at[step, :, place],
+                target,
+            )
+
+    def turn(step):
+        for which, (grad, column, wide, base, flip) in enumerate(streams):
+            columns, place = pl.ds(column, wide), pl.ds(base + column, wide)
+            far[step, which].wait_recv()
+            turned_buf[step, :, place] = plus(
+                grad[block_of(step, not flip, flip), columns], far_buf[step, :, place]
+            )
+            target = (over_x if flip else over_y, core)
+            turned[step, which] = send(
+                turned_buf.at[step, :, place], turned_came.at[step, :, place], target
+            )
+
+    def total(step):
+        for which, (grad, column, wide, base, _) in enumerate(streams):
+            columns, place = pl.ds(column, wide), pl.ds(base + column, wide)
+            near[step, which].wait_recv()
+            turned[step, which].wait_recv()
+            sum_buf[step, :, place] = plus_wide(
+                grad[block_of(step, False, False), columns],
+                near_buf[step, :, place],
+                turned_came[step, :, place],
+            )
+
+    ring = []
+
+    def around(step):
+        value = sum_buf[step]
+        if step > 1:
+            ring[-1].wait_recv()
+            value = value + ring_came[step - 2].astype(jnp.float32)
+        ring_buf[step - 1] = value.astype(jnp.bfloat16)
+        ring.append(send(ring_buf.at[step - 1], ring_came.at[step - 1], (onward, core)))
+
+    hidden_ring = []
+
+    def around_hidden(step):
+        value = hidden_ref[places[step]].astype(jnp.float32)
+        if step > 1:
+            hidden_ring[-1].wait_recv()
+            value = value + hidden_came[step - 2].astype(jnp.float32)
+        hidden_buf[step - 1] = value.astype(jnp.bfloat16)
+        hidden_ring.append(
+            send(hidden_buf.at[step - 1], hidden_came.at[step - 1], (onward, core))
+        )
+
+    def normed_tile(tile, half):
+        first = (tile // 2) * 2 * span + half * span + (tile % 2) * TAIL_TILE
+        rows = pl.ds(pl.multiple_of(first, TAIL_TILE), TAIL_TILE)
+        part = 0.0
+        for index, grad in enumerate((dq_buf, dk_buf, dv_buf)):
+            part += lax.dot_general(
+                grad[rows, :],
+                weight_buf[:, pl.ds(index * half_wide, half_wide)],
+                (((1,), (1,)), ((), ())),
+                preferred_element_type=jnp.float32,
+            )
+        return pl.ds(pl.multiple_of(tile * TAIL_TILE, TAIL_TILE), TAIL_TILE), part
+
+    def away_tile(tile, carry):
+        rows, part = normed_tile(tile, 1 - core)
+        away_buf[rows, :] = part.astype(jnp.bfloat16)
+        return carry
+
+    def own_tile(tile, carry):
+        rows, part = normed_tile(tile, core)
+        own_buf[rows, :] = part
+        return carry
+
+    def norm_tile(tile, carry):
+        rows = pl.ds(pl.multiple_of(tile * NORM_TILE, NORM_TILE), NORM_TILE)
+        grad = own_buf[rows, :] + came_buf[rows, :].astype(jnp.float32)
+        unit, scale = norm_stats(token_buf[rows, :].astype(jnp.float32))
+        residual_buf[rows, :] += norm_back_rows(unit, scale, gain_ref[...], grad)
+        return carry + jnp.sum(grad * unit, 0, keepdims=True)
+
+    tiles = own_buf.shape[0] // TAIL_TILE
+    norm_tiles = own_buf.shape[0] // NORM_TILE
+    issue(1)
+    around_hidden(1)
+    issue(2)
+    for load in loads[:4]:
+        load.wait()
+    lax.fori_loop(0, tiles, away_tile, 0)
+    away = send(away_buf, came_buf, (row, 1 - core))
+    turn(1)
+    around_hidden(2)
+    issue(3)
+    lax.fori_loop(0, tiles, own_tile, 0)
+    total(1)
+    around(1)
+    turn(2)
+    issue(0)
+    for load in loads[4:]:
+        load.wait()
+    away.wait_recv()
+    gain_part = jnp.zeros((1, own_buf.shape[1]), jnp.float32)
+    gain_part = lax.fori_loop(0, norm_tiles // 2, norm_tile, gain_part)
+    total(2)
+    around_hidden(3)
+    around(2)
+    turn(3)
+    gain_part = lax.fori_loop(norm_tiles // 2, norm_tiles, norm_tile, gain_part)
+    store = pltpu.make_async_copy(residual_buf, token_out, local_sems.at[6])
+    store.start()
+    gain_buf[0] = jnp.zeros_like(gain_buf[0])
+    gain_buf[0, 0:1] = gain_part
+    gain_buf[0, 1:2] = ffn_gain_ref[...]
+
+    def exchange(number, target):
+        copy = send(gain_buf.at[number], gain_came.at[number], target)
+        copy.wait_recv()
+        gain_buf[number + 1] = gain_buf[number] + gain_came[number]
+
+    exchange(0, (row, 1 - core))
+    total(3)
+    around(3)
+    turn(0)
+    exchange(1, (over_x, core))
+    exchange(2, (over_y, core))
+    exchange(3, (beside, core))
+    exchange(4, (beyond, core))
+    gain_out[...] = gain_buf[5]
+    hidden_ring[-1].wait_recv()
+    hidden_out[...] = hidden_ref[zed].astype(jnp.float32) + hidden_came[2].astype(jnp.float32)
+    total(0)
+    ring[-1].wait_recv()
+    for index, out in enumerate((query_out, key_out, value_out)):
+        columns = pl.ds(index * half_wide, half_wide)
+        out[...] = sum_buf[0, :, columns] + ring_came[2, :, columns].astype(jnp.float32)
+    for copy in sent:
+        copy.wait_send()
+    store.wait()
+
+
+def tail_call(grads, weights, sums, tokens, grad_residual, gain, ffn_gain, hidden_sums):
+    flat, width = grad_residual.shape
+    half_wide = sums[0].shape[1]
+    depth = sums[0].shape[0] // 16
+    anywhere, here = pl.BlockSpec(memory_space=pl.ANY), pl.BlockSpec(memory_space=pltpu.VMEM)
+    block = pltpu.VMEM((4, depth, 3 * half_wide), jnp.bfloat16)
+    moving = pltpu.VMEM((3, depth, 3 * half_wide), jnp.bfloat16)
+    gains = pltpu.VMEM((6, 8, width), jnp.float32)
+    sum_shape = jax.ShapeDtypeStruct((depth, half_wide), jnp.float32)
+    return pl.pallas_call(
+        tail_kernel,
+        in_specs=[anywhere] * 4 + [here] * 3 + [anywhere] * 2 + [here] * 3,
+        out_specs=[anywhere] + [here] * 5,
+        out_shape=[
+            jax.ShapeDtypeStruct((flat, width), jnp.float32),
+            sum_shape,
+            sum_shape,
+            sum_shape,
+            jax.ShapeDtypeStruct((8, width), jnp.float32),
+            jax.ShapeDtypeStruct(hidden_sums.shape[1:], jnp.float32),
+        ],
+        scratch_shapes=[pltpu.VMEM((width, 3 * half_wide), jnp.bfloat16)]
+        + [pltpu.VMEM((2 * flat, half_wide), jnp.bfloat16)] * 3
+        + [
+            pltpu.VMEM((flat, width), jnp.float32),
+            pltpu.VMEM((flat, width), jnp.bfloat16),
+            pltpu.VMEM((flat, width), jnp.bfloat16),
+            pltpu.VMEM((flat, width), jnp.bfloat16),
+            pltpu.VMEM((flat, width), jnp.float32),
+        ]
+        + [block] * 4
+        + [pltpu.VMEM((4, depth, 3 * half_wide), jnp.float32), moving, moving, gains, gains]
+        + [pltpu.VMEM((3,) + hidden_sums.shape[1:], jnp.bfloat16)] * 2
+        + [
+            pltpu.SemaphoreType.DMA((7,)),
+            pltpu.SemaphoreType.DMA((64,)),
+            pltpu.SemaphoreType.DMA((64,)),
+        ],
+        compiler_params=pltpu.CompilerParams(
+            collective_id=1, has_side_effects=True, vmem_limit_bytes=60 * 1024 * 1024
+        ),
+    )(
+        *grads,
+        weights,
+        *sums,
+        tokens,
+        grad_residual,
+        gain.reshape(1, width),
+        ffn_gain.reshape(1, width),
+        hidden_sums,
+    )
 
 
 def halves(block):
@@ -732,10 +1233,13 @@
         self.first_turned = swap_y(plus(self.pick(0, 1, 0), self.first_far))
         self.second_turned = swap_x(plus(self.pick(1, 0, 1), self.second_far))
 
-    def gather(self):
+    def near_sums(self):
         first = plus(self.pick(0, 0, 0), self.first_near, self.first_turned)
         second = plus(self.pick(1, 0, 0), self.second_near, self.second_turned)
-        self.sums = jnp.concatenate([first, second], 1 if self.by_rows else 2)
+        return jnp.concatenate([first, second], 1 if self.by_rows else 2)
+
+    def gather(self):
+        self.sums = self.near_sums()
         self.moving = next_z(self.block(1))
 
     def block(self, back):
@@ -752,14 +1256,6 @@
     def hold(self, names, *after):
         for name in names:
             setattr(self, name, tie(getattr(self, name), *after))
-
-
-def plus_wide(*terms):
-    return sum(term.astype(jnp.float32) for term in terms)
-
-
-def plus(*terms):
-    return plus_wide(*terms).astype(jnp.bfloat16)
 
 
 def body_pair(
@@ -781,19 +1277,11 @@
         return (own_half(wide, 1, core) + received.astype(jnp.float32)).reshape(flat, -1)
 
     attn_piece = jnp.concatenate([w_query, w_key, w_value, w_out], 1)
-    qkv_wide = 3 * w_query.shape[1]
-    tokens_other = swap_cores(tokens)
-    attn_steps = [attn_piece]
-    for _ in range(2):
-        attn_steps.append(next_z(attn_steps[-1]))
-
+    half_wide = w_query.shape[1]
+    normed, cot_other, attn_weights, up_stack = head_call(
+        tokens, gain_attn, cotangent, attn_piece, w_up
+    )
     first = core == 0
-    tokens_all = jnp.where(
-        first,
-        jnp.concatenate([tokens, tokens_other], 1),
-        jnp.concatenate([tokens_other, tokens], 1),
-    )
-    tokens_all = tokens_all.reshape(2 * flat, width).astype(jnp.float32)
     tokens_own = tokens.reshape(flat, width).astype(jnp.float32)
     cot_own = cotangent.reshape(flat, width)
     windows = windows_of(segments)
@@ -801,62 +1289,37 @@
         jnp.broadcast_to(segments[:, :, None], segments.shape + (LANES,)),
         jnp.broadcast_to(segments[:, None, :], (rows, 8, 2 * span)),
     )
-    normed = (norm_stats(tokens_all)[0] * gain_attn).astype(jnp.bfloat16)
-
-    attn_steps[2] = tie(attn_steps[2], normed)
-    attn_steps.append(next_z(attn_steps[2]))
-    attn_stack = natural_z(attn_steps)
-    qkv_parts = start_xy(*halves_z(attn_stack[:, :, :qkv_wide]))
-    up_steps, down_steps = [tie(w_up, attn_stack)], [tie(w_down, attn_stack)]
-    up_steps.append(next_z(up_steps[-1]))
+    normed = normed.reshape(2 * flat, width)
+    w_qkv = attn_weights[:, : 3 * half_wide]
+    w_q, w_k, w_v = (w_qkv[:, i * half_wide : (i + 1) * half_wide] for i in range(3))
+
+    up_parts = start_xy(*halves_z(up_stack))
+    down_steps = [tie(w_down, up_stack)]
     down_steps.append(next_z(down_steps[-1]))
-    qkv_parts = finish_xy(*qkv_parts)
-    up_steps[1], down_steps[1] = tie((up_steps[1], down_steps[1]), qkv_parts[0][2], qkv_parts[1][1])
-    up_steps.append(next_z(up_steps[-1]))
+    w_o_half = attn_weights[:, 3 * half_wide :]
+    w_o_other = swap_cores(w_o_half)
+    qkv = dot_low(normed, w_qkv).astype(jnp.bfloat16)
+    qkv, w_o_other, down_steps[1] = tie((qkv, w_o_other, down_steps[1]))
     down_steps.append(next_z(down_steps[-1]))
-    cot_other = swap_cores(cotangent)
-    w_qkv = assemble(assemble_columns_kernel, (width, qkv_wide), qkv_parts)
-    out_parts = start_xy(*halves_z(tie(attn_stack[:, :, qkv_wide:], qkv_parts)))
-    w_qkv, up_steps[2], down_steps[2] = tie((w_qkv, up_steps[2], down_steps[2]))
-    up_steps.append(next_z(up_steps[-1]))
+    qkv = split(qkv, 3 * half_wide)
+    pairs = half_wide // LANES
+    operands = [(qkv, 0), (qkv, pairs), (qkv, 2 * pairs)]
+
+    def attend(row, operands, begun=()):
+        return attention_call(
+            attend_kernel, row, windows, marks, operands, [half_wide], [], begun
+        )
+
+    mixed = attend(0, operands)
+    mixed, up_parts, down_steps[2] = tie((mixed, up_parts, down_steps[2]))
+    up_parts = finish_xy(*up_parts)
     down_steps.append(next_z(down_steps[-1]))
-    w_q, w_k, w_v = (w_qkv[:, i * (qkv_wide // 3) : (i + 1) * (qkv_wide // 3)] for i in range(3))
-
-    queries = dot_low(normed, w_q).astype(jnp.bfloat16)
-    queries, out_parts = tie((queries, out_parts))
-    out_parts = finish_xy(*out_parts)
-    normed, up_steps[3], down_steps[3] = tie((normed, up_steps[3], down_steps[3]), queries)
-    up_parts = start_xy(*halves_z(natural_z(up_steps)))
-    down_stack = natural_z(down_steps)
-    key_rows = dot_low(normed, w_k).astype(jnp.bfloat16)
-    normed, out_parts = tie((normed, out_parts), key_rows)
-    w_o_half = assemble(assemble_columns_kernel, (width, width // 2), out_parts)
-    w_o_other = swap_cores(w_o_half)
-    value_rows = dot_low(normed, w_v).astype(jnp.bfloat16)
-
-    queries, key_rows, value_rows = (
-        split(array, w_q.shape[1]) for array in (queries, key_rows, value_rows)
-    )
-    queries, w_o_other = tie((queries, w_o_other))
-
-    def attend(row, query_rows):
-        return attention_call(
-            attend_kernel,
-            [array[row : row + 1] for array in windows],
-            [array[row : row + 1] for array in marks],
-            [array[row : row + 1] for array in (query_rows, key_rows, value_rows)],
-            1,
-            [],
-        )[0]
-
-    mixed_rows = [attend(0, queries)]
-    queries, up_parts = tie((queries, up_parts), mixed_rows[0])
-    up_parts = finish_xy(*up_parts)
-    down_parts = start_xy(*halves_z(tie(down_stack, up_parts[0][2])))
-    mixed_rows += [attend(row, queries) for row in range(1, rows)]
-    mixed = jnp.concatenate(mixed_rows, 0)
-    mixed, up_parts, down_parts = tie((mixed, up_parts, down_parts))
-    down_parts = finish_xy(*down_parts)
+    for row in range(1, rows):
+        mixed = attend(row, operands, mixed)
+    (mixed,) = mixed
+    mixed, down_steps[3] = tie((mixed, down_steps[3]))
+    down_parts = start_xy(*halves_z(natural_z(down_steps)))
+    mixed, up_parts = tie((mixed, up_parts))
     w_o = jnp.where(
         first,
         jnp.concatenate([w_o_half, w_o_other], 1),
@@ -874,8 +1337,9 @@
     residual = tokens_own + dot_low(mixed_own, w_o)
     unit_two, scale_two = norm_stats(residual)
     normed_two = (unit_two * gain_ffn).astype(jnp.bfloat16)
+    normed_two_other = swap_cores(normed_two)
     normed_two, down_parts = tie((normed_two, down_parts))
-    normed_two_other = swap_cores(normed_two)
+    down_parts = finish_xy(*down_parts)
     units = w_up.shape[1]
     down_columns = assemble(assemble_rows_kernel, (2, units, width // 2), down_parts)
     down_mine = down_columns[0]
@@ -912,122 +1376,91 @@
         True,
     )
     down_sum.spread()
-    depth, wide = w_up.shape
-    up_sum = Scatter(
-        [(up_whole, 0, depth, 0, wide // 2)], [(up_whole, 0, depth, wide // 2, wide // 2)]
-    )
     grad_normed_two = plus_wide(grad_two_own, tie(grad_two_came, up_whole))
     grad_residual = cot_own.astype(jnp.float32) + norm_back_rows(
         unit_two, scale_two, gain_ffn, grad_normed_two
     )
     ffn_gain_part = jnp.sum(grad_normed_two * unit_two, 0)
     grad_attn = grad_residual.astype(jnp.bfloat16).reshape(rows, span, width)
-    (grad_attn, down_sum.first_far, down_sum.second_far) = tie(
-        (grad_attn, down_sum.first_far, down_sum.second_far)
+    grad_attn_other = swap_cores(grad_attn)
+    grad_attn_all = jnp.where(
+        first,
+        jnp.concatenate([grad_attn, grad_attn_other], 1),
+        jnp.concatenate([grad_attn_other, grad_attn], 1),
+    ).reshape(2 * flat, width)
+    out_half = outer_low(mixed.reshape(2 * flat, -1), grad_attn_all)
+    out_away = swap_cores(own_half(out_half, 1, 1 - core))
+    grad_attn_all = tie(grad_attn_all, out_half)
+    (grad_attn_all, down_sum.first_far, down_sum.second_far) = tie(
+        (grad_attn_all, down_sum.first_far, down_sum.second_far)
     )
     down_sum.turn()
-    up_sum.spread()
-    grad_attn_all = both_cores(grad_attn, 1).reshape(2 * flat, width)
     grad_mixed = split(times_transposed(grad_attn_all, w_o_rows).astype(jnp.bfloat16), width // 2)
-    down_names = ("first_near", "second_near", "first_turned", "second_turned")
-    down_sum.hold(down_names, grad_mixed)
-    grad_mixed = tie(grad_mixed, *(getattr(down_sum, name) for name in down_names))
-    down_sum.gather()
-    scratch = [pltpu.VMEM((2 * span, LANES), jnp.float32)] * 2
-
-    def attend_back(row, grad_rows):
-        return attention_call(
-            attend_back_kernel,
-            [array[row : row + 1] for array in windows],
-            [array[row : row + 1] for array in marks],
-            [array[row : row + 1] for array in (queries, key_rows, value_rows, grad_rows)],
-            3,
-            scratch,
-        )
-
-    up_names = ("first_far", "second_far")
-    back_rows = []
-    for row in range(rows):
-        back_rows.append(attend_back(row, grad_mixed))
-        if row == 0:
-            down_sum.hold(("moving",), *back_rows[-1])
-            up_sum.hold(up_names, *back_rows[-1])
-            grad_mixed = tie(
-                grad_mixed, down_sum.moving, up_sum.first_far, up_sum.second_far, *back_rows[-1]
-            )
-            down_sum.step(2)
-            up_sum.turn()
-    grad_queries, grad_keys, grad_values = (
-        jnp.concatenate([parts[member] for parts in back_rows], 0).reshape(2 * flat, width // 2)
-        for member in range(3)
-    )
-    down_sum.hold(("moving",), grad_queries)
-    up_sum.hold(down_names, grad_queries)
-    grad_queries = tie(
-        grad_queries, down_sum.moving, *(getattr(up_sum, name) for name in down_names)
-    )
-    down_sum.step(3)
-    up_sum.gather()
-    out_half = outer_low(mixed.reshape(2 * flat, -1), tie(grad_attn_all, grad_queries))
-    out_away = swap_cores(own_half(out_half, 1, 1 - core))
-    query_whole = outer_low(normed, grad_queries)
-    key_whole = outer_low(normed, grad_keys)
-    value_whole = outer_low(normed, grad_values)
     out_kept = own_half(out_half, 1, core)
     out_whole = jnp.where(
         first,
         jnp.concatenate([out_kept, out_away], 0),
         jnp.concatenate([out_away, out_kept], 0),
     )
-    attn_whole = (query_whole, key_whole, value_whole, out_whole)
-    up_sum.hold(("moving",), attn_whole)
-    attn_whole = tie(attn_whole, up_sum.moving)
-    depth, wide = w_query.shape
-    attn_sum = Scatter(
-        [(whole, 0, depth, 0, wide) for whole in attn_whole[:2]],
-        [(whole, 0, depth, 0, wide) for whole in attn_whole[2:]],
-    )
-    attn_sum.spread()
-    up_sum.step(2)
-    grad_queries = tie(grad_queries, attn_whole)
-    grad_normed_part = (
-        times_transposed(grad_queries, w_q)
-        + times_transposed(grad_keys, w_k)
-        + times_transposed(grad_values, w_v)
-    )
-    attn_sum.hold(up_names, grad_normed_part)
-    up_sum.hold(("moving",), grad_normed_part)
-    grad_normed_part = tie(
-        grad_normed_part, attn_sum.first_far, attn_sum.second_far, up_sum.moving
-    )
-    attn_sum.turn()
-    up_sum.step(3)
-    grad_normed = shared(grad_normed_part, sharing(grad_normed_part))
-    y_own, y_came = tie((y_own, y_came), grad_normed_part)
+    depth, wide = w_up.shape
+    cut = (wide + half_wide) // 256 * 128
+    up_sum = Scatter(
+        [(up_whole, 0, depth, 0, cut)],
+        [(up_whole, 0, depth, cut, wide - cut), (out_whole, 0, depth, 0, half_wide)],
+    )
+    up_sum.spread()
+    y_own, y_came = tie((y_own, y_came), grad_mixed)
     layer_out = (residual + plus_wide(y_own, y_came)).astype(jnp.bfloat16)
-    unit_own, scale_own = norm_stats(tokens_own)
-    token_grad = grad_residual + norm_back_rows(unit_own, scale_own, gain_attn, grad_normed)
-    attn_gain_part = jnp.sum(grad_normed * unit_own, 0)
-    gains = jnp.stack([attn_gain_part, ffn_gain_part])
-    gains = gains + swap_cores(gains)
-    attn_sum.hold(down_names, token_grad)
-    attn_sum.gather()
-    gains = gains + swap_x(gains)
-    gains = gains + swap_y(gains)
-    layer_out, attn_sum.moving = tie((layer_out, attn_sum.moving), gains)
-    attn_sum.step(2)
-    gains = gains + swap_z(gains, False)
-    attn_sum.moving = tie(attn_sum.moving, gains)
-    attn_sum.step(3)
-    gains = gains + swap_z(gains, True)
-    gain_attn_grad, gain_ffn_grad = gains
+    down_names = ("first_near", "second_near", "first_turned", "second_turned")
+    down_sum.hold(down_names, layer_out)
+    grad_mixed = tie(grad_mixed, *(getattr(down_sum, name) for name in down_names))
+    down_sum.gather()
+    scratch = [pltpu.VMEM((2 * span, LANES), jnp.float32)] * 2
+
+    def attend_back(row, grad_rows, begun=()):
+        return attention_call(
+            attend_back_kernel,
+            row,
+            windows,
+            marks,
+            operands + [(grad_rows, 0)],
+            [half_wide] * 3,
+            scratch,
+            begun,
+        )
+
+    up_names = ("first_far", "second_far")
+    grads = ()
+    for row in range(rows):
+        grads = attend_back(row, grad_mixed, grads)
+        if row == 0:
+            down_sum.hold(("moving",), *grads)
+            up_sum.hold(up_names, *grads)
+            grads = tie(grads, down_sum.moving, up_sum.first_far, up_sum.second_far)
+            down_sum.step(2)
+            up_sum.turn()
+    grad_queries, grad_keys, grad_values = (grad.reshape(2 * flat, half_wide) for grad in grads)
+    query_whole = outer_low(normed, grad_queries)
+    key_whole = outer_low(normed, grad_keys)
+    value_whole = outer_low(normed, grad_values)
+    down_sum.hold(("moving",), query_whole)
+    key_whole = tie(key_whole, down_sum.moving)
+    down_sum.step(3)
+    up_sum.hold(down_names, key_whole)
+    sums = tie((query_whole, key_whole, value_whole), down_sum.moving)
+    token_grad, query_grad, key_grad, value_grad, gains, up_out_grad = tail_call(
+        (grad_queries, grad_keys, grad_values),
+        attn_weights,
+        sums,
+        tokens.reshape(flat, width),
+        grad_residual,
+        gain_attn,
+        ffn_gain_part,
+        up_sum.near_sums(),
+    )
+    gain_attn_grad, gain_ffn_grad = gains[0], gains[1]
     down_grad = down_sum.finish()
-    up_grad = up_sum.finish()
-    attn_grad = attn_sum.finish()
-    column_width = w_query.shape[1]
-    query_grad, key_grad, value_grad, out_grad = (
-        attn_grad[:, index * column_width : (index + 1) * column_width] for index in range(4)
-    )
+    up_grad, out_grad = up_out_grad[:, : w_up.shape[1]], up_out_grad[:, w_up.shape[1] :]
     return (
         layer_out.reshape(rows, span, width),
         token_grad.reshape(rows, span, width),

time: 749 us -> 658 us (0.88)
  Pallas kernels: 210 us -> 338 us
  waiting for transfers between devices: 203 us -> 86.6 us
  starting transfers between devices: 88.2 us -> 40.7 us
  other arithmetic: 91.1 us -> 55.5 us
  matrix products: 102 us -> 81.9 us
    pallas_call x4 -> x6, Pallas kernels: 113 us -> 247 us  [the longest x4 114 us: attention_call(): pl.pallas_call(functools.partial(kernel, row, len(begun)), grid_spec=pltp...]
    ppermute x18 -> x6, waiting for transfers between devices: 59.4 us -> 0.02 us  [next_z(): return lax.ppermute(values, 'rows', pairs)]
    ppermute x18 -> x6, starting transfers between devices: 36.3 us -> 8.89 us  [next_z(): return lax.ppermute(values, 'rows', pairs)]
    dot_general x4 -> x1, matrix products: 29.9 us -> 5.55 us  [times_transposed(): jnp.einsum('te,de->td', left_side, right_side, preferred_element_type=jnp...]
    ppermute x22 -> x12, waiting for transfers between devices: 28.5 us -> 4.44 us  [swap_y(): return lax.ppermute(values, 'rows', [(row, row ^ 2) for row in range(16)])]
    ppermute x22 -> x12, waiting for transfers between devices: 97.4 us -> 76.5 us  [swap_x(): return lax.ppermute(values, 'rows', [(row, row ^ 1) for row in range(16)])]
    ppermute x22 -> x12, starting transfers between devices: 26.5 us -> 13.8 us  [swap_y(): return lax.ppermute(values, 'rows', [(row, row ^ 2) for row in range(16)])]
    ppermute x2 -> x0, waiting for transfers between devices: 11.6 us -> none  [swap_z(): return lax.ppermute(values, 'rows', pairs)]
  transfers between devices with their start and end apart: 77 -> 39, of which waited for: 29 -> 10; matrix products, arithmetic and copies ran while one was open for 28% -> 21% of each run, Pallas kernels for 21% -> 24%
where the time goes in v3:
time: 658 us; the launch traced here: 649 us
  Pallas kernels  338 us (51%)
  waiting for transfers between devices  86.6 us (13%)
  matrix products  81.9 us (12%)
  other arithmetic  55.5 us (8%)
  local copies, waits for them, and re-layouts  44 us (7%)
  starting transfers between devices  40.7 us (6%)
    pallas_call x4, Pallas kernels, attention_call(): pl.pallas_call(functools.partial(kernel, row, len(begun)), grid_spec=pltp...  114 us
    pallas_call x2, Pallas kernels, feed_forward(): pl.pallas_call(functools.partial(feed_forward_kernel, begun=bool(begun)),...  84.8 us
    ppermute x12, waiting for transfers between devices, swap_x(): return lax.ppermute(values, 'rows', [(row, row ^ 1) for row in range(16)])  76.5 us
    pallas_call x1, Pallas kernels, tail_call(): pl.pallas_call(tail_kernel, in_specs=[anywhere] * 4 + [here] * 3 + [anywh...  72 us
    pallas_call x1, Pallas kernels, head_call(): pl.pallas_call(head_kernel, in_specs=[anywhere, pl.BlockSpec(memory_space...  61.3 us
    dot_general x6, matrix products, outer_low(): jnp.einsum('tc,te->ce', left_side, right_side, preferred_element_type=jnp...  56.7 us
    unnamed x108, local copies, waits for them, and re-layouts  22.7 us
    dot_general x2, matrix products, dot_low(): return jnp.dot(left_side, right_side, preferred_element_type=jnp.float32)  19.7 us
  transfers between devices with their start and end apart: 39, of which 10 were waited for; matrix products, arithmetic and copies ran while one was open for 21% of the time, Pallas kernels for 24%

profile of v3, /device:TPU:0, one launch (start us, length us, event | category | flops | bytes accessed | tf_op | source)
XLA Modules:
  0.0 648.5 jit_solution(11150952110674916967)
XLA Ops:
  2.4 1.7 copy-done
  4.2 1.7 copy-done.2
  6.9 61.3 %shard_map.186 = (bf16[2,1024,1280]{2,1,0:T(8,128)(2,1)S(1)}, bf16[2,512,1280]{2,1,0:T(8,128)(2,1)S(1)}, bf16[1280,2560]{1,0:T(8,128)(2,1)S(1)}, bf16[4,80,2560]{2,1,0:T(8,128)(2,1)S(1)}) custom-call(bf16[2,512,1280]{2,1,0:T(8,128)(2,1)S(1)} %copy-done.2, f32[1,1280]{1,0:T(1,128)S(1)} %reshape.197.gain_ref, bf16[2,512,1280]{2,1,0:T(8,128)(2,1)S(1)} %copy-done, ...), custom_call_target="tpu_custom_call" | custom-call | tf_op jit(solution)/shard_map/pallas_call | solution.py:823
  68.3 1.4 copy-done.25
  70.7 1.8 collective-permute-start.2
  75.1 12.9 %convolution_convert_fusion.2 = bf16[2048,1920]{1,0:T(8,128)(2,1)} fusion(bf16[2048,1280]{1,0:T(8,128)(2,1)S(1)} %bitcast.149, bf16[1280,2560]{1,0:T(8,128)(2,1)S(1)} %get-tuple-element.99.weights_ref), kind=kOutput, calls=%fused_computation.2 | convolution fusion | flops 10070261760 | bytes 18022400 | tf_op jit(solution)/shard_map/dot_general | solution.py:1198
  88.4 1.7 collective-permute-start.5
  91.2 19.6 %shard_map.187.rest_0_ = bf16[2,1024,640]{2,1,0:T(8,128)(2,1)S(1)} custom-call(s32[2,4]{1,0:T(2,128)S(1)} %get-tuple-element.196.start_ref, s32[2,4]{1,0:T(2,128)S(1)} %get-tuple-element.195.count_ref, s32[2,1024,128]{2,1,0:T(8,128)S(1)} %broadcast_in_dim.4.column_ref, s32[2,8,1024]{2,1,0:T(8,128)S(1)} %broadcast_in_dim.5.line_ref, ...), custom_call_target="tpu_custom_call" | custom-call | flops 8053063680 | bytes 5242880 | tf_op jit(solution)/shard_map/pallas_call | solution.py:427
  111.8 3.6 collective-permute-start.8
  116.0 1.9 collective-permute-start.7
  119.1 20.8 %shard_map.188 = bf16[2,1024,640]{2,1,0:T(8,128)(2,1)S(1)} custom-call(s32[2,4]{1,0:T(2,128)S(1)} %get-tuple-element.196.start_ref, s32[2,4]{1,0:T(2,128)S(1)} %get-tuple-element.195.count_ref, s32[2,1024,128]{2,1,0:T(8,128)S(1)} %copy-done.6, s32[2,8,1024]{2,1,0:T(8,128)S(1)} %broadcast_in_dim.5.line_ref, ...), custom_call_target="tpu_custom_call", output_to_operand_aliasing={{}: (7, {})} | custom-call | flops 8053063680 | bytes 5242880 | tf_op jit(solution)/shard_map/pallas_call | solution.py:427
  140.0 1.7 constant_dynamic-slice_fusion.9
  141.7 1.4 pad_maximum_fusion.2
  143.8 1.5 collective-permute-start.12
  145.3 1.5 collective-permute-start.13
  147.8 6.8 %fusion.43 = (f32[1024]{0:T(1024)S(1)}, f32[1024,1280]{1,0:T(8,128)S(1)}) fusion(bf16[1280,640]{1,0:T(8,128)(2,1)} %collective-permute-done, bf16[1280,640]{1,0:T(8,128)(2,1)S(1)} %copy-done.32, pred[]{:T(512)S(6)} %eq.88, bf16[1024,640]{1,0:T(8,128)(2,1)} %bitcast.4, bf16[1024,640]{1,0:T(8,128)(2,1)S(1)} %bitcast.183, bf16[1024,1280]{1,0:T(8,128)(2,1)S(1)} %bitcast.147), kind=kOutput, calls=%fused_computation.134 | convolution fusion | flops 3385916416 | bytes 13766657 | tf_op jit(solution)/shard_map/dot_general | solution.py:1198
  155.3 2.5 multiply_convert_fusion.normed_ref
  157.8 7.0 %collective-permute-done.11.refs_1_ = bf16[4,160,640]{2,1,0:T(8,128)(2,1)S(1)} collective-permute-done((bf16[4,160,640]{2,1,0:T(8,128)(2,1)S(1)}, bf16[4,160,640]{2,1,0:T(8,128)(2,1)S(1)}, u32[]{:S(2)}, u32[]{:S(2)}) %collective-permute-start.11) | collective-permute-done | bytes 819232 | tf_op jit(solution)/shard_map/ppermute | solution.py:475
  165.7 16.4 %collective-permute-done.13.refs_5_ = bf16[4,160,640]{2,1,0:T(8,128)(2,1)} collective-permute-done((bf16[4,160,640]{2,1,0:T(8,128)(2,1)S(1)}, bf16[4,160,640]{2,1,0:T(8,128)(2,1)}, u32[]{:S(2)}, u32[]{:S(2)}) %collective-permute-start.13) | collective-permute-done | bytes 819232 | tf_op jit(solution)/shard_map/ppermute | solution.py:475
  183.0 1.6 collective-permute-start.15
  185.8 17.5 %collective-permute-done.15.refs_3_ = bf16[4,160,640]{2,1,0:T(8,128)(2,1)} collective-permute-done((bf16[4,160,640]{2,1,0:T(8,128)(2,1)}, bf16[4,160,640]{2,1,0:T(8,128)(2,1)}, u32[]{:S(2)}, u32[]{:S(2)}) %collective-permute-start.15) | collective-permute-done | bytes 819232 | tf_op jit(solution)/shard_map/ppermute | solution.py:475
  207.6 6.4 shard_map.189
  214.0 3.2 slice_bitcast_fusion
  217.8 5.7 collective-permute-done.17.refs_9_
  223.4 42.2 %shard_map.190 = (bf16[2048,2560]{1,0:T(8,128)(2,1)}, bf16[2048,2560]{1,0:T(8,128)(2,1)}, bf16[1024,1280]{1,0:T(8,128)(2,1)}, bf16[1024,1280]{1,0:T(8,128)(2,1)}) custom-call(s32[4]{0:T(128)} %copy-done.23, bf16[1024,1280]{1,0:T(8,128)(2,1)} %multiply_convert_fusion.normed_ref, bf16[1024,1280]{1,0:T(8,128)(2,1)} %bitcast.144, ...), custom_call_target="tpu_custom_call" | custom-call | flops 26843545600 | bytes 34078720 | tf_op jit(solution)/shard_map/pallas_call | solution.py:639
  265.7 5.3 pad_maximum_fusion
  270.9 42.6 %shard_map.191 = (bf16[2048,2560]{1,0:T(8,128)(2,1)}, bf16[2048,2560]{1,0:T(8,128)(2,1)}, bf16[1024,1280]{1,0:T(8,128)(2,1)}, bf16[1024,1280]{1,0:T(8,128)(2,1)}) custom-call(s32[4]{0:T(128)} %copy-done.23, bf16[1024,1280]{1,0:T(8,128)(2,1)} %collective-permute-done.18.normed_ref, ...), custom_call_target="tpu_custom_call", output_to_operand_aliasing={{0}: (13, {}), {1}: (14, {})} | custom-call | flops 26843545600 | bytes 34078720 | tf_op jit(solution)/shard_map/pallas_call | solution.py:639
  313.7 16.3 %convolution_convert_fusion.1 = bf16[2560,1280]{1,0:T(8,128)(2,1)S(1)} fusion(bf16[2048,2560]{1,0:T(8,128)(2,1)} %get-tuple-element.143, bf16[1024,1280]{1,0:T(8,128)(2,1)S(1)} %bitcast.153, bf16[1024,1280]{1,0:T(8,128)(2,1)S(1)} %bitcast.145), kind=kOutput, calls=%fused_computation.1 | convolution fusion | flops 13435535360 | bytes 22282240 | tf_op jit(solution)/shard_map/tc,te->ce/dot_general | solution.py:1202
  330.0 3.2 constant_dynamic-slice_fusion.3
  334.0 20.3 %convolution_convert_fusion = bf16[1280,2560]{1,0:T(8,128)(2,1)} fusion(bf16[2048,1280]{1,0:T(8,128)(2,1)} %pad_maximum_fusion, bf16[2048,2560]{1,0:T(8,128)(2,1)} %get-tuple-element.145), kind=kOutput, calls=%fused_computation | convolution fusion | flops 13425049600 | bytes 22282240 | tf_op jit(solution)/shard_map/tc,te->ce/dot_general | solution.py:1202
  354.3 2.9 multiply_reduce_fusion
  357.2 4.7 fusion.40
  361.9 3.7 maximum_select_fusion.2
  367.1 1.5 dynamic-slice_bitcast_fusion
  369.7 5.5 maximum_select_fusion
  375.3 1.5 dynamic-slice_bitcast_fusion.2
  380.8 5.2 maximum_select_fusion.1
  386.0 3.7 fusion.6
  389.7 8.1 %collective-permute-done.23 = bf16[4,160,640]{2,1,0:T(8,128)(2,1)S(1)} collective-permute-done((bf16[4,160,640]{2,1,0:T(8,128)(2,1)S(1)}, bf16[4,160,640]{2,1,0:T(8,128)(2,1)S(1)}, u32[]{:S(2)}, u32[]{:S(2)}) %collective-permute-start.23) | collective-permute-done | bytes 819232 | tf_op jit(solution)/shard_map/ppermute | solution.py:475
  402.2 5.5 convolution_convert_fusion.3
  408.9 4.8 add_convert_fusion
  413.7 2.6 collective-permute-done.26
  418.3 14.6 %collective-permute-done.28 = bf16[4,160,640]{2,1,0:T(8,128)(2,1)S(1)} collective-permute-done((bf16[4,160,640]{2,1,0:T(8,128)(2,1)}, bf16[4,160,640]{2,1,0:T(8,128)(2,1)S(1)}, u32[]{:S(2)}, u32[]{:S(2)}) %collective-permute-start.28) | collective-permute-done | bytes 819232 | tf_op jit(solution)/shard_map/ppermute | solution.py:475
  433.8 2.2 fusion.20
  436.8 2.3 collective-permute-start.29
  442.1 35.6 %shard_map.192 = (bf16[2,1024,640]{2,1,0:T(8,128)(2,1)S(1)}, bf16[2,1024,640]{2,1,0:T(8,128)(2,1)}, bf16[2,1024,640]{2,1,0:T(8,128)(2,1)}) custom-call(s32[2,4]{1,0:T(2,128)S(1)} %copy-done.22, s32[2,4]{1,0:T(2,128)S(1)} %copy-done.20, s32[2,1024,128]{2,1,0:T(8,128)S(1)} %copy-done.7, s32[2,8,1024]{2,1,0:T(8,128)S(1)} %copy-done.17, ...), custom_call_target="tpu_custom_call" | custom-call | flops 10737418240 | bytes 9175040 | tf_op jit(solution)/shard_map/pallas_call | solution.py:427
  477.7 2.4 fusion.16
  480.1 2.7 collective-permute-start.36
  485.1 1.3 collective-permute-start.33
  486.4 37.8 %shard_map.193 = (bf16[2,1024,640]{2,1,0:T(8,128)(2,1)S(1)}, bf16[2,1024,640]{2,1,0:T(8,128)(2,1)}, bf16[2,1024,640]{2,1,0:T(8,128)(2,1)}) custom-call(s32[2,4]{1,0:T(2,128)S(1)} %copy-done.22, s32[2,4]{1,0:T(2,128)S(1)} %copy-done.20, s32[2,1024,128]{2,1,0:T(8,128)S(1)} %copy-done.7, ...), custom_call_target="tpu_custom_call", output_to_operand_aliasing={{0}: (8, {}), {1}: (9, {}), {2}: (10, {})} | custom-call | flops 10737418240 | bytes 9175040 | tf_op jit(solution)/shard_map/pallas_call | solution.py:427
  524.3 5.5 fusion.7.query_ref
  529.9 1.7 collective-permute-start.34
  531.6 5.5 fusion.8.key_ref
  537.4 1.8 collective-permute-start.38
  539.1 5.5 fusion.9.value_ref
  544.7 2.2 fusion.18
  547.8 12.9 %collective-permute-done.38 = bf16[4,80,1664]{2,1,0:T(8,128)(2,1)S(1)} collective-permute-done((bf16[4,80,1664]{2,1,0:T(8,128)(2,1)S(1)}, bf16[4,80,1664]{2,1,0:T(8,128)(2,1)S(1)}, u32[]{:S(2)}, u32[]{:S(2)}) %collective-permute-start.38) | collective-permute-done | bytes 1064992 | tf_op jit(solution)/shard_map/ppermute | solution.py:475
  560.8 1.6 add_convert_fusion.1
  562.4 1.5 pad_maximum_fusion.1.hidden_ref
  563.8 72.0 %shard_map.194 = (f32[1024,1280]{1,0:T(8,128)}, f32[80,640]{1,0:T(8,128)}, f32[80,640]{1,0:T(8,128)}, f32[80,640]{1,0:T(8,128)}, f32[8,1280]{1,0:T(8,128)}, /*index=5*/f32[80,3200]{1,0:T(8,128)}) custom-call(bf16[2048,640]{1,0:T(8,128)(2,1)} %bitcast.148, bf16[2048,640]{1,0:T(8,128)(2,1)} %bitcast.181, bf16[2048,640]{1,0:T(8,128)(2,1)} %bitcast.182, ...), custom_call_target="tpu_custom_call" | custom-call | tf_op jit(solution)/shard_map/pallas_call | solution.py:1129
  635.8 2.1 slice.55
  637.9 1.6 slice.53
  639.5 1.5 slice_reduce_fusion
  641.0 5.2 copy.91
  (196 shorter events, 46.3 us)
Async XLA Ops:
  1.3 66.9 %copy-start.18 = (f32[1,1280]{1,0:T(1,128)}, f32[1,1280]{1,0:T(1,128)S(1)}, u32[]{:S(2)}) copy-start(f32[1,1280]{1,0:T(1,128)S(1)} %reshape.197.gain_ref) | copy-start | bytes 15364
  69.7 5.4 copy-start.24
  70.7 17.7 %copy-start.36 = (bf16[4,80,1280]{2,1,0:T(8,128)(2,1)}, bf16[4,80,1280]{2,1,0:T(8,128)(2,1)S(1)}, u32[]{:S(2)}) copy-start(bf16[4,80,1280]{2,1,0:T(8,128)(2,1)S(1)} %get-tuple-element.121.refs_4_) | copy-start | bytes 2457604
  70.7 40.1 %collective-permute-start.2 = (bf16[4,80,1280]{2,1,0:T(8,128)(2,1)}, bf16[4,80,1280]{2,1,0:T(8,128)(2,1)}, u32[]{:S(2)}, u32[]{:S(2)}) collective-permute-start(bf16[4,80,1280]{2,1,0:T(8,128)(2,1)} %get-tuple-element.117.refs_0_), channel_id=1, source_target_pairs={{0,2},{2,0},{4,6},{6,4},{8,10},{10,8},{12,14},{14,12},{16,18},{18,... | collective-permute-start | bytes 2457608 | tf_op jit(solution)/shard_map/ppermute | solution.py:475
  72.5 38.3 %collective-permute-start.3 = (bf16[4,80,1280]{2,1,0:T(8,128)(2,1)}, bf16[4,80,1280]{2,1,0:T(8,128)(2,1)}, u32[]{:S(2)}, u32[]{:S(2)}) collective-permute-start(bf16[4,80,1280]{2,1,0:T(8,128)(2,1)} %get-tuple-element.117.refs_0_), channel_id=1, source_target_pairs={{0,4},{2,6},{4,0},{6,2},{8,12},{10,14},{12,8},{14,10},{16,20},{18,... | collective-permute-start | bytes 2457608 | tf_op jit(solution)/shard_map/ppermute | solution.py:479
  73.8 14.2 %copy-start.31 = (bf16[1280,640]{1,0:T(8,128)(2,1)}, bf16[1280,640]{1,0:T(8,128)(2,1)S(1)}, u32[]{:S(2)}) copy-start(bf16[1280,640]{1,0:T(8,128)(2,1)S(1)} %slice.45) | copy-start | bytes 4915204
  73.8 16.3 %collective-permute-start = (bf16[1280,640]{1,0:T(8,128)(2,1)S(1)}, bf16[1280,640]{1,0:T(8,128)(2,1)}, u32[]{:S(2)}, u32[]{:S(2)}) collective-permute-start(bf16[1280,640]{1,0:T(8,128)(2,1)S(1)} %slice.45), channel_id=1, source_target_pairs={{0,1},{1,0},{2,3},{3,2},{4,5},{5,4},{6,7},{7,6},{8,9},{9,8},{10,11... | collective-permute-start | bytes 4915208 | tf_op jit(solution)/shard_map/ppermute | solution.py:283
  73.9 14.5 %collective-permute-start.1 = (bf16[320,640]{1,0:T(8,128)(2,1)S(1)}, bf16[320,640]{1,0:T(8,128)(2,1)}, u32[]{:S(2)}, u32[]{:S(2)}) collective-permute-start(bf16[320,640]{1,0:T(8,128)(2,1)S(1)} %copy-done.38), channel_id=1, source_target_pairs={{0,8},{2,10},{4,12},{6,14},{8,24},{10,26},{12,28},{14,30},{24,16},... | collective-permute-start | bytes 1228808 | tf_op jit(solution)/shard_map/ppermute | solution.py:487
  74.8 36.0 %collective-permute-start.4 = (bf16[4,80,1280]{2,1,0:T(8,128)(2,1)S(1)}, bf16[4,80,1280]{2,1,0:T(8,128)(2,1)}, u32[]{:S(2)}, u32[]{:S(2)}) collective-permute-start(bf16[4,80,1280]{2,1,0:T(8,128)(2,1)S(1)} %get-tuple-element.121.refs_4_), channel_id=1, source_target_pairs={{0,2},{2,0},{4,6},{6,4},{8,10},{10,8},{12,14},{14,12},{16,18},{18,... | collective-permute-start | bytes 2457608 | tf_op jit(solution)/shard_map/ppermute | solution.py:475
  75.1 12.9 %copy-start.43 = (s32[2,1024]{1,0:T(2,128)S(1)}, s32[2,1024]{1,0:T(2,128)}, u32[]{:S(2)}) copy-start(s32[2,1024]{1,0:T(2,128)} %param.12) | copy-start | bytes 24580
  88.4 22.4 %collective-permute-start.5 = (bf16[4,80,1280]{2,1,0:T(8,128)(2,1)S(1)}, bf16[4,80,1280]{2,1,0:T(8,128)(2,1)S(1)}, u32[]{:S(2)}, u32[]{:S(2)}) collective-permute-start(bf16[4,80,1280]{2,1,0:T(8,128)(2,1)S(1)} %get-tuple-element.121.refs_4_), channel_id=1, source_target_pairs={{0,4},{2,6},{4,0},{6,2},{8,12},{10,14},{12,8},{14,10},{16,20},{18,... | collective-permute-start | bytes 2457608 | tf_op jit(solution)/shard_map/ppermute | solution.py:479
  90.1 27.7 %copy-start.19 = (s32[2,4]{1,0:T(2,128)}, s32[2,4]{1,0:T(2,128)S(1)}, u32[]{:S(2)}) copy-start(s32[2,4]{1,0:T(2,128)S(1)} %get-tuple-element.195.count_ref) | copy-start | bytes 100
  90.1 27.7 %copy-start.21 = (s32[2,4]{1,0:T(2,128)}, s32[2,4]{1,0:T(2,128)S(1)}, u32[]{:S(2)}) copy-start(s32[2,4]{1,0:T(2,128)S(1)} %get-tuple-element.196.start_ref) | copy-start | bytes 100
  90.2 21.6 %collective-permute-start.6 = (bf16[320,640]{1,0:T(8,128)(2,1)}, bf16[320,640]{1,0:T(8,128)(2,1)}, u32[]{:S(2)}, u32[]{:S(2)}) collective-permute-start(bf16[320,640]{1,0:T(8,128)(2,1)} %collective-permute-done.1), channel_id=1, source_target_pairs={{0,8},{2,10},{4,12},{6,14},{8,24},{10,26},{12,28},{14,30},{24,16},... | collective-permute-start | bytes 1228808 | tf_op jit(solution)/shard_map/ppermute | solution.py:487
  91.2 19.6 %copy-start.5 = (s32[2,1024,128]{2,1,0:T(8,128)}, s32[2,1024,128]{2,1,0:T(8,128)S(1)}, u32[]{:S(2)}) copy-start(s32[2,1024,128]{2,1,0:T(8,128)S(1)} %broadcast_in_dim.4.column_ref) | copy-start | bytes 3145732
  91.2 26.6 %copy-start.16 = (s32[2,8,1024]{2,1,0:T(8,128)}, s32[2,8,1024]{2,1,0:T(8,128)S(1)}, u32[]{:S(2)}) copy-start(s32[2,8,1024]{2,1,0:T(8,128)S(1)} %broadcast_in_dim.5.line_ref) | copy-start | bytes 196612
  111.8 28.2 %collective-permute-start.8 = (bf16[4,80,1280]{2,1,0:T(8,128)(2,1)}, bf16[4,80,1280]{2,1,0:T(8,128)(2,1)}, u32[]{:S(2)}, u32[]{:S(2)}) collective-permute-start(bf16[4,80,1280]{2,1,0:T(8,128)(2,1)} %collective-permute-done.3.refs_2_), channel_id=1, source_target_pairs={{0,2},{2,0},{4,6},{6,4},{8,10},{10,8},{12,14},{14,12},{16,18},{18,... | collective-permute-start | bytes 2457608 | tf_op jit(solution)/shard_map/ppermute | solution.py:475
  115.4 24.6 %collective-permute-start.9 = (bf16[4,80,1280]{2,1,0:T(8,128)(2,1)}, bf16[4,80,1280]{2,1,0:T(8,128)(2,1)}, u32[]{:S(2)}, u32[]{:S(2)}) collective-permute-start(bf16[4,80,1280]{2,1,0:T(8,128)(2,1)} %collective-permute-done.4.refs_5_), channel_id=1, source_target_pairs={{0,4},{2,6},{4,0},{6,2},{8,12},{10,14},{12,8},{14,10},{16,20},{18,... | collective-permute-start | bytes 2457608 | tf_op jit(solution)/shard_map/ppermute | solution.py:479
  116.0 24.0 %collective-permute-start.7 = (bf16[320,640]{1,0:T(8,128)(2,1)}, bf16[320,640]{1,0:T(8,128)(2,1)S(1)}, u32[]{:S(2)}, u32[]{:S(2)}) collective-permute-start(bf16[320,640]{1,0:T(8,128)(2,1)} %collective-permute-done.6), channel_id=1, source_target_pairs={{0,8},{2,10},{4,12},{6,14},{8,24},{10,26},{12,28},{14,30},{24,16},... | collective-permute-start | bytes 1228808 | tf_op jit(solution)/shard_map/ppermute | solution.py:487
  141.7 6.1 collective-permute-start.10
  143.7 10.9 %copy-start.8 = (bf16[4,160,640]{2,1,0:T(8,128)(2,1)}, bf16[4,160,640]{2,1,0:T(8,128)(2,1)S(1)}, u32[]{:S(2)}) copy-start(bf16[4,160,640]{2,1,0:T(8,128)(2,1)S(1)} %get-tuple-element.125.refs_0_) | copy-start | bytes 2457604
  143.7 21.1 %collective-permute-start.11 = (bf16[4,160,640]{2,1,0:T(8,128)(2,1)S(1)}, bf16[4,160,640]{2,1,0:T(8,128)(2,1)S(1)}, u32[]{:S(2)}, u32[]{:S(2)}) collective-permute-start(bf16[4,160,640]{2,1,0:T(8,128)(2,1)S(1)} %get-tuple-element.125.refs_0_), channel_id=1, source_target_pairs={{0,2},{2,0},{4,6},{6,4},{8,10},{10,8},{12,14},{14,12},{16,18},{18,... | collective-permute-start | bytes 2457608 | tf_op jit(solution)/shard_map/ppermute | solution.py:475
  143.8 21.9 %collective-permute-start.12 = (bf16[4,160,640]{2,1,0:T(8,128)(2,1)S(1)}, bf16[4,160,640]{2,1,0:T(8,128)(2,1)}, u32[]{:S(2)}, u32[]{:S(2)}) collective-permute-start(bf16[4,160,640]{2,1,0:T(8,128)(2,1)S(1)} %get-tuple-element.125.refs_0_), channel_id=1, source_target_pairs={{0,4},{2,6},{4,0},{6,2},{8,12},{10,14},{12,8},{14,10},{16,20},{18,... | collective-permute-start | bytes 2457608 | tf_op jit(solution)/shard_map/ppermute | solution.py:479
  145.3 36.8 %collective-permute-start.13 = (bf16[4,160,640]{2,1,0:T(8,128)(2,1)S(1)}, bf16[4,160,640]{2,1,0:T(8,128)(2,1)}, u32[]{:S(2)}, u32[]{:S(2)}) collective-permute-start(bf16[4,160,640]{2,1,0:T(8,128)(2,1)S(1)} %get-tuple-element.128.refs_4_), channel_id=1, source_target_pairs={{0,2},{2,0},{4,6},{6,4},{8,10},{10,8},{12,14},{14,12},{16,18},{18,... | collective-permute-start | bytes 2457608 | tf_op jit(solution)/shard_map/ppermute | solution.py:475
  146.9 35.2 %collective-permute-start.14 = (bf16[4,160,640]{2,1,0:T(8,128)(2,1)S(1)}, bf16[4,160,640]{2,1,0:T(8,128)(2,1)S(1)}, u32[]{:S(2)}, u32[]{:S(2)}) collective-permute-start(bf16[4,160,640]{2,1,0:T(8,128)(2,1)S(1)} %get-tuple-element.128.refs_4_), channel_id=1, source_target_pairs={{0,4},{2,6},{4,0},{6,2},{8,12},{10,14},{12,8},{14,10},{16,20},{18,... | collective-permute-start | bytes 2457608 | tf_op jit(solution)/shard_map/ppermute | solution.py:479
  183.0 20.3 %collective-permute-start.15 = (bf16[4,160,640]{2,1,0:T(8,128)(2,1)}, bf16[4,160,640]{2,1,0:T(8,128)(2,1)}, u32[]{:S(2)}, u32[]{:S(2)}) collective-permute-start(bf16[4,160,640]{2,1,0:T(8,128)(2,1)} %collective-permute-done.12.refs_2_), channel_id=1, source_target_pairs={{0,2},{2,0},{4,6},{6,4},{8,10},{10,8},{12,14},{14,12},{16,18},{18,... | collective-permute-start | bytes 2457608 | tf_op jit(solution)/shard_map/ppermute | solution.py:475
  184.6 19.6 %collective-permute-start.16 = (bf16[4,160,640]{2,1,0:T(8,128)(2,1)}, bf16[4,160,640]{2,1,0:T(8,128)(2,1)}, u32[]{:S(2)}, u32[]{:S(2)}) collective-permute-start(bf16[4,160,640]{2,1,0:T(8,128)(2,1)} %collective-permute-done.13.refs_5_), channel_id=1, source_target_pairs={{0,4},{2,6},{4,0},{6,2},{8,12},{10,14},{12,8},{14,10},{16,20},{18,... | collective-permute-start | bytes 2457608 | tf_op jit(solution)/shard_map/ppermute | solution.py:479
  185.8 28.2 %copy-start.23 = (s32[4]{0:T(128)}, s32[4]{0:T(128)S(1)}, u32[]{:S(2)}) copy-start(s32[4]{0:T(128)S(1)} %pad_add_fusion.place_ref) | copy-start | bytes 52
  217.2 6.2 collective-permute-start.17
  217.2 48.4 %collective-permute-start.18 = (bf16[1024,1280]{1,0:T(8,128)(2,1)}, bf16[1024,1280]{1,0:T(8,128)(2,1)}, u32[]{:S(2)}, u32[]{:S(2)}) collective-permute-start(bf16[1024,1280]{1,0:T(8,128)(2,1)} %multiply_convert_fusion.normed_ref), channel_id=1, source_target_pairs={{0,1},{1,0},{2,3},{3,2},{4,5},{5,4},{6,7},{7,6},{8,9},{9,8},{10,11... | collective-permute-start | bytes 7864328 | tf_op jit(solution)/shard_map/ppermute | solution.py:283
  270.9 42.8 %copy-start.1 = (bf16[2,512,1280]{2,1,0:T(8,128)(2,1)S(1)}, bf16[2,512,1280]{2,1,0:T(8,128)(2,1)}, u32[]{:S(2)}) copy-start(bf16[2,512,1280]{2,1,0:T(8,128)(2,1)} %cot_ref.1) | copy-start | bytes 7864324
  270.9 42.8 %copy-start.26 = (bf16[2,512,1280]{2,1,0:T(8,128)(2,1)S(1)}, bf16[2,512,1280]{2,1,0:T(8,128)(2,1)}, u32[]{:S(2)}) copy-start(bf16[2,512,1280]{2,1,0:T(8,128)(2,1)} %copy-done.25) | copy-start | bytes 7864324
  313.5 40.7 %collective-permute-start.20 = (bf16[1024,1280]{1,0:T(8,128)(2,1)}, bf16[1024,1280]{1,0:T(8,128)(2,1)S(1)}, u32[]{:S(2)}, u32[]{:S(2)}) collective-permute-start(bf16[1024,1280]{1,0:T(8,128)(2,1)} %get-tuple-element.140), channel_id=1, source_target_pairs={{0,1},{1,0},{2,3},{3,2},{4,5},{5,4},{6,7},{7,6},{8,9},{9,8},{10,11... | collective-permute-start | bytes 7864328 | tf_op jit(solution)/shard_map/ppermute | solution.py:283
  333.3 36.0 %collective-permute-start.22 = (bf16[2560,640]{1,0:T(8,128)(2,1)}, bf16[2560,640]{1,0:T(8,128)(2,1)}, u32[]{:S(2)}, u32[]{:S(2)}) collective-permute-start(bf16[2560,640]{1,0:T(8,128)(2,1)} %get-tuple-element.212), channel_id=1, source_target_pairs={{0,1},{1,0},{2,3},{3,2},{4,5},{5,4},{6,7},{7,6},{8,9},{9,8},{10,11... | collective-permute-start | bytes 9830408 | tf_op jit(solution)/shard_map/ppermute | solution.py:283
  334.0 20.3 %slice-start.2 = ((s8[5242880]{0:T(1024)(128)(4,1)}), s8[4194304]{0:T(1024)(128)(4,1)S(1)}, s32[]{:S(2)}) async-start(s8[5242880]{0:T(1024)(128)(4,1)} %bitcast.154), calls=%async_computation.2 | async-start | bytes 8388608
  334.0 20.3 %slice-start.3 = ((s8[5242880]{0:T(1024)(128)(4,1)}), s8[1048576]{0:T(1024)(128)(4,1)S(1)}, s32[]{:S(2)}) async-start(s8[5242880]{0:T(1024)(128)(4,1)} %bitcast.154), calls=%async_computation.3 | async-start | bytes 2097152
  334.0 20.3 %copy-start.29 = (bf16[1024,1280]{1,0:T(8,128)(2,1)S(1)}, bf16[1024,1280]{1,0:T(8,128)(2,1)}, u32[]{:S(2)}) copy-start(bf16[1024,1280]{1,0:T(8,128)(2,1)} %get-tuple-element.139) | copy-start | bytes 7864324
  361.9 17.7 %collective-permute-start.21 = (bf16[2,512,1280]{2,1,0:T(8,128)(2,1)}, bf16[2,512,1280]{2,1,0:T(8,128)(2,1)}, u32[]{:S(2)}, u32[]{:S(2)}) collective-permute-start(bf16[2,512,1280]{2,1,0:T(8,128)(2,1)} %bitcast.17), channel_id=1, source_target_pairs={{0,1},{1,0},{2,3},{3,2},{4,5},{5,4},{6,7},{7,6},{8,9},{9,8},{10,11... | collective-permute-start | bytes 7864328 | tf_op jit(solution)/shard_map/ppermute | solution.py:283
  365.6 42.2 %collective-permute-start.19 = (bf16[1024,1280]{1,0:T(8,128)(2,1)}, bf16[1024,1280]{1,0:T(8,128)(2,1)}, u32[]{:S(2)}, u32[]{:S(2)}) collective-permute-start(bf16[1024,1280]{1,0:T(8,128)(2,1)} %get-tuple-element.138), channel_id=1, source_target_pairs={{0,1},{1,0},{2,3},{3,2},{4,5},{5,4},{6,7},{7,6},{8,9},{9,8},{10,11... | collective-permute-start | bytes 7864328 | tf_op jit(solution)/shard_map/ppermute | solution.py:283
  376.8 21.0 %collective-permute-start.23 = (bf16[4,160,640]{2,1,0:T(8,128)(2,1)S(1)}, bf16[4,160,640]{2,1,0:T(8,128)(2,1)S(1)}, u32[]{:S(2)}, u32[]{:S(2)}) collective-permute-start(bf16[4,160,640]{2,1,0:T(8,128)(2,1)S(1)} %get-tuple-element.210), channel_id=1, source_target_pairs={{0,2},{2,0},{4,6},{6,4},{8,10},{10,8},{12,14},{14,12},{16,18},{18,... | collective-permute-start | bytes 2457608 | tf_op jit(solution)/shard_map/ppermute | solution.py:475
  377.6 21.1 %collective-permute-start.24 = (bf16[4,160,640]{2,1,0:T(8,128)(2,1)S(1)}, bf16[4,160,640]{2,1,0:T(8,128)(2,1)S(1)}, u32[]{:S(2)}, u32[]{:S(2)}) collective-permute-start(bf16[4,160,640]{2,1,0:T(8,128)(2,1)S(1)} %get-tuple-element.209), channel_id=1, source_target_pairs={{0,4},{2,6},{4,0},{6,2},{8,12},{10,14},{12,8},{14,10},{16,20},{18,... | collective-permute-start | bytes 2457608 | tf_op jit(solution)/shard_map/ppermute | solution.py:479
  378.6 37.7 %collective-permute-start.26 = (bf16[4,160,640]{2,1,0:T(8,128)(2,1)}, bf16[4,160,640]{2,1,0:T(8,128)(2,1)}, u32[]{:S(2)}, u32[]{:S(2)}) collective-permute-start(bf16[4,160,640]{2,1,0:T(8,128)(2,1)} %get-tuple-element.207), channel_id=1, source_target_pairs={{0,4},{2,6},{4,0},{6,2},{8,12},{10,14},{12,8},{14,10},{16,20},{18,... | collective-permute-start | bytes 2457608 | tf_op jit(solution)/shard_map/ppermute | solution.py:479
  379.6 37.9 %collective-permute-start.25 = (bf16[4,160,640]{2,1,0:T(8,128)(2,1)}, bf16[4,160,640]{2,1,0:T(8,128)(2,1)}, u32[]{:S(2)}, u32[]{:S(2)}) collective-permute-start(bf16[4,160,640]{2,1,0:T(8,128)(2,1)} %get-tuple-element.208), channel_id=1, source_target_pairs={{0,2},{2,0},{4,6},{6,4},{8,10},{10,8},{12,14},{14,12},{16,18},{18,... | collective-permute-start | bytes 2457608 | tf_op jit(solution)/shard_map/ppermute | solution.py:475
  400.0 32.9 %collective-permute-start.28 = (bf16[4,160,640]{2,1,0:T(8,128)(2,1)}, bf16[4,160,640]{2,1,0:T(8,128)(2,1)S(1)}, u32[]{:S(2)}, u32[]{:S(2)}) collective-permute-start(bf16[4,160,640]{2,1,0:T(8,128)(2,1)} %get-tuple-element.205), channel_id=1, source_target_pairs={{0,2},{2,0},{4,6},{6,4},{8,10},{10,8},{12,14},{14,12},{16,18},{18,... | collective-permute-start | bytes 2457608 | tf_op jit(solution)/shard_map/ppermute | solution.py:475
  401.2 7.7 %slice-start.4 = ((s8[5242880]{0:T(1024)(128)(4,1)}), s8[4194304]{0:T(1024)(128)(4,1)S(1)}, s32[]{:S(2)}) async-start(s8[5242880]{0:T(1024)(128)(4,1)} %bitcast.156), calls=%async_computation.4 | async-start | bytes 8388608
  402.2 6.6 %slice-start.5 = ((s8[5242880]{0:T(1024)(128)(4,1)}), s8[1048576]{0:T(1024)(128)(4,1)S(1)}, s32[]{:S(2)}) async-start(s8[5242880]{0:T(1024)(128)(4,1)} %bitcast.156), calls=%async_computation.5 | async-start | bytes 2097152
  407.8 26.0 %collective-permute-start.27 = (bf16[4,160,640]{2,1,0:T(8,128)(2,1)S(1)}, bf16[4,160,640]{2,1,0:T(8,128)(2,1)S(1)}, u32[]{:S(2)}, u32[]{:S(2)}) collective-permute-start(bf16[4,160,640]{2,1,0:T(8,128)(2,1)S(1)} %get-tuple-element.206), channel_id=1, source_target_pairs={{0,4},{2,6},{4,0},{6,2},{8,12},{10,14},{12,8},{14,10},{16,20},{18,... | collective-permute-start | bytes 2457608 | tf_op jit(solution)/shard_map/ppermute | solution.py:479
  408.9 30.3 %collective-permute-start.31 = (bf16[640,640]{1,0:T(8,128)(2,1)}, bf16[640,640]{1,0:T(8,128)(2,1)S(1)}, u32[]{:S(2)}, u32[]{:S(2)}) collective-permute-start(bf16[640,640]{1,0:T(8,128)(2,1)} %get-tuple-element.222), channel_id=1, source_target_pairs={{0,1},{1,0},{2,3},{3,2},{4,5},{5,4},{6,7},{7,6},{8,9},{9,8},{10,11... | collective-permute-start | bytes 2457608 | tf_op jit(solution)/shard_map/ppermute | solution.py:283
  416.3 61.4 %collective-permute-start.30 = (bf16[4,80,1536]{2,1,0:T(8,128)(2,1)}, bf16[4,80,1536]{2,1,0:T(8,128)(2,1)}, u32[]{:S(2)}, u32[]{:S(2)}) collective-permute-start(bf16[4,80,1536]{2,1,0:T(8,128)(2,1)} %get-tuple-element.198), channel_id=1, source_target_pairs={{0,2},{2,0},{4,6},{6,4},{8,10},{10,8},{12,14},{14,12},{16,18},{18,... | collective-permute-start | bytes 2949128 | tf_op jit(solution)/shard_map/ppermute | solution.py:475
  417.5 127.1 %collective-permute-start.35 = (bf16[4,80,1536]{2,1,0:T(8,128)(2,1)}, bf16[4,80,1536]{2,1,0:T(8,128)(2,1)}, u32[]{:S(2)}, u32[]{:S(2)}) collective-permute-start(bf16[4,80,1536]{2,1,0:T(8,128)(2,1)} %get-tuple-element.197), channel_id=1, source_target_pairs={{0,2},{2,0},{4,6},{6,4},{8,10},{10,8},{12,14},{14,12},{16,18},{18,... | collective-permute-start | bytes 2949128 | tf_op jit(solution)/shard_map/ppermute | solution.py:475
  436.8 47.0 %collective-permute-start.29 = (bf16[320,640]{1,0:T(8,128)(2,1)}, bf16[320,640]{1,0:T(8,128)(2,1)}, u32[]{:S(2)}, u32[]{:S(2)}) collective-permute-start(bf16[320,640]{1,0:T(8,128)(2,1)} %fusion.31), channel_id=1, source_target_pairs={{0,8},{2,10},{4,12},{6,14},{8,24},{10,26},{12,28},{14,30},{24,16},... | collective-permute-start | bytes 1228808 | tf_op jit(solution)/shard_map/ppermute | solution.py:487
  441.0 45.5 %collective-permute-start.32 = (bf16[4,80,1664]{2,1,0:T(8,128)(2,1)}, bf16[4,80,1664]{2,1,0:T(8,128)(2,1)S(1)}, u32[]{:S(2)}, u32[]{:S(2)}) collective-permute-start(bf16[4,80,1664]{2,1,0:T(8,128)(2,1)} %pad_maximum_fusion.4), channel_id=1, source_target_pairs={{0,4},{2,6},{4,0},{6,2},{8,12},{10,14},{12,8},{14,10},{16,20},{18,... | collective-permute-start | bytes 3194888 | tf_op jit(solution)/shard_map/ppermute | solution.py:479
  480.1 64.6 %collective-permute-start.36 = (bf16[4,80,1536]{2,1,0:T(8,128)(2,1)}, bf16[4,80,1536]{2,1,0:T(8,128)(2,1)}, u32[]{:S(2)}, u32[]{:S(2)}) collective-permute-start(bf16[4,80,1536]{2,1,0:T(8,128)(2,1)} %fusion.16), channel_id=1, source_target_pairs={{0,4},{2,6},{4,0},{6,2},{8,12},{10,14},{12,8},{14,10},{16,20},{18,... | collective-permute-start | bytes 2949128 | tf_op jit(solution)/shard_map/ppermute | solution.py:479
  483.8 60.9 %collective-permute-start.37 = (bf16[4,80,1664]{2,1,0:T(8,128)(2,1)}, bf16[4,80,1664]{2,1,0:T(8,128)(2,1)}, u32[]{:S(2)}, u32[]{:S(2)}) collective-permute-start(bf16[4,80,1664]{2,1,0:T(8,128)(2,1)} %pad_maximum_fusion.5), channel_id=1, source_target_pairs={{0,4},{2,6},{4,0},{6,2},{8,12},{10,14},{12,8},{14,10},{16,20},{18,... | collective-permute-start | bytes 3194888 | tf_op jit(solution)/shard_map/ppermute | solution.py:479
  483.8 40.4 %slice-start = ((s8[5242880]{0:T(1024)(128)(4,1)}), s8[4194304]{0:T(1024)(128)(4,1)S(1)}, s32[]{:S(2)}) async-start(s8[5242880]{0:T(1024)(128)(4,1)} %bitcast.150), calls=%async_computation | async-start | bytes 8388608
  485.1 39.1 %slice-start.1 = ((s8[5242880]{0:T(1024)(128)(4,1)}), s8[1048576]{0:T(1024)(128)(4,1)S(1)}, s32[]{:S(2)}) async-start(s8[5242880]{0:T(1024)(128)(4,1)} %bitcast.150), calls=%async_computation.1 | async-start | bytes 2097152
  485.1 44.6 %collective-permute-start.33 = (bf16[320,640]{1,0:T(8,128)(2,1)S(1)}, bf16[320,640]{1,0:T(8,128)(2,1)S(1)}, u32[]{:S(2)}, u32[]{:S(2)}) collective-permute-start(bf16[320,640]{1,0:T(8,128)(2,1)S(1)} %fusion.27), channel_id=1, source_target_pairs={{0,8},{2,10},{4,12},{6,14},{8,24},{10,26},{12,28},{14,30},{24,16},... | collective-permute-start | bytes 1228808 | tf_op jit(solution)/shard_map/ppermute | solution.py:487
  524.2 5.5 copy-start.10
  524.3 7.4 %copy-start.33 = (bf16[2,1024,640]{2,1,0:T(8,128)(2,1)S(1)}, bf16[2,1024,640]{2,1,0:T(8,128)(2,1)}, u32[]{:S(2)}) copy-start(bf16[2,1024,640]{2,1,0:T(8,128)(2,1)} %get-tuple-element.169) | copy-start | bytes 7864324
  529.9 17.0 %collective-permute-start.34 = (bf16[320,640]{1,0:T(8,128)(2,1)S(1)}, bf16[320,640]{1,0:T(8,128)(2,1)S(1)}, u32[]{:S(2)}, u32[]{:S(2)}) collective-permute-start(bf16[320,640]{1,0:T(8,128)(2,1)S(1)} %fusion.26), channel_id=1, source_target_pairs={{0,8},{2,10},{4,12},{6,14},{8,24},{10,26},{12,28},{14,30},{24,16},... | collective-permute-start | bytes 1228808 | tf_op jit(solution)/shard_map/ppermute | solution.py:487
  531.6 7.5 %copy-start.34 = (bf16[2,1024,640]{2,1,0:T(8,128)(2,1)S(1)}, bf16[2,1024,640]{2,1,0:T(8,128)(2,1)}, u32[]{:S(2)}) copy-start(bf16[2,1024,640]{2,1,0:T(8,128)(2,1)} %get-tuple-element.170) | copy-start | bytes 7864324
  537.4 23.4 %collective-permute-start.38 = (bf16[4,80,1664]{2,1,0:T(8,128)(2,1)S(1)}, bf16[4,80,1664]{2,1,0:T(8,128)(2,1)S(1)}, u32[]{:S(2)}, u32[]{:S(2)}) collective-permute-start(bf16[4,80,1664]{2,1,0:T(8,128)(2,1)S(1)} %add_convert_fusion.2), channel_id=1, source_target_pairs={{0,2},{2,0},{4,6},{6,4},{8,10},{10,8},{12,14},{14,12},{16,18},{18,... | collective-permute-start | bytes 3194888 | tf_op jit(solution)/shard_map/ppermute | solution.py:475
  641.0 5.9 copy-start.41
  641.0 6.6 %copy-start.40 = (f32[80,640]{1,0:T(8,128)S(1)}, f32[80,640]{1,0:T(8,128)}, u32[]{:S(2)}) copy-start(f32[80,640]{1,0:T(8,128)} %get-tuple-element.250) | copy-start | bytes 614404
  (27 other events, 65.3 us)

commit v4 on v3

--- a/solution.py
+++ b/solution.py
@@ -275,7 +275,8 @@
 
 
 LANES = 128
-QUERY_TILE = 256
+QUERY_TILE = 128
+BACK_TILE = 256
 NEVER = -1e30
 
 
@@ -298,140 +299,145 @@
     return lax.dynamic_slice_in_dim(values, index * half, half, axis)
 
 
+def two_heads(ref, rows, columns):
+    values = ref[0, rows, columns]
+    lower = lax.broadcasted_iota(jnp.int32, values.shape, 1) < HEAD_DIM
+    zero = jnp.zeros_like(values)
+    return jnp.concatenate([jnp.where(lower, values, zero), jnp.where(lower, zero, values)], 0)
+
+
+def merge_heads(values):
+    half = values.shape[0] // 2
+    lower = lax.broadcasted_iota(jnp.int32, (half, LANES), 1) < HEAD_DIM
+    return jnp.where(lower, values[:half], values[half:])
+
+
+def over_windows(first_row, query_tile, start_ref, count_ref, length, window):
+    row = first_row + pl.program_id(0)
+
+    def tile_step(tile, carry):
+        begin = pl.multiple_of(start_ref[row, tile] * LANES, LANES)
+        count = count_ref[row, tile]
+        queries = pl.ds(pl.multiple_of(tile * query_tile, query_tile), query_tile)
+        for tiles in range(1, length // LANES + 1):
+            keys = pl.ds(begin, tiles * LANES)
+            pl.when(count == tiles)(functools.partial(window, queries, keys))
+        return carry
+
+    lax.fori_loop(0, length // query_tile, tile_step, 0)
+
+
+last_dims = (((1,), (1,)), ((), ()))
+first_dims = (((0,), (0,)), ((), ()))
+exponent_scale = HEAD_DIM ** (-0.5) * 1.4426950408889634
+
+
 def attend_kernel(
     row, begun, start_ref, count_ref, column_ref, line_ref, q_ref, k_ref, v_ref, *rest
 ):
     (out_ref,) = rest[begun:]
-    length = k_ref.shape[1]
-    lower = lax.broadcasted_iota(jnp.int32, (QUERY_TILE, LANES), 1) < HEAD_DIM
-
-    def tile_step(tile, carry):
-        begin = pl.multiple_of(start_ref[row, tile] * LANES, LANES)
-        count = count_ref[row, tile]
-        queries = pl.ds(pl.multiple_of(tile * QUERY_TILE, QUERY_TILE), QUERY_TILE)
-
-        def window(tiles):
-            keys = pl.ds(begin, tiles * LANES)
-            query = q_ref[0, queries, :]
-            key = k_ref[0, keys, :]
-            value = v_ref[0, keys, :]
-            allowed = column_ref[0, queries, :1] == line_ref[0, :1, keys]
-            mixed = []
-            for head in range(2):
-                mine = lower if head == 0 else jnp.logical_not(lower)
-                masked = jnp.where(mine, query, jnp.zeros_like(query))
-                scores = lax.dot_general(
-                    masked, key, (((1,), (1,)), ((), ())), preferred_element_type=jnp.float32
-                )
-                scores = jnp.where(allowed, scores * HEAD_DIM ** (-0.5), NEVER)
-                top = jnp.max(scores, -1, keepdims=True)
-                exponent = jnp.exp(scores - top)
-                total = jnp.sum(exponent, -1, keepdims=True)
-                part = jnp.dot(
-                    exponent.astype(jnp.bfloat16), value, preferred_element_type=jnp.float32
-                )
-                mixed.append(part / total)
-            out_ref[0, queries, :] = jnp.where(lower, mixed[0], mixed[1]).astype(jnp.bfloat16)
-
-        for tiles in range(1, length // LANES + 1):
-            pl.when(count == tiles)(functools.partial(window, tiles))
-        return carry
-
-    lax.fori_loop(0, length // QUERY_TILE, tile_step, 0)
+    _, length, wide = q_ref.shape
+
+    def window(queries, keys):
+        allowed = column_ref[0, queries, :1] == line_ref[0, :1, keys]
+        bias = jnp.where(allowed, 0.0, NEVER)[None]
+
+        def scores_of(pair):
+            columns = pl.ds(pair * LANES, LANES)
+            return lax.dot_general(
+                two_heads(q_ref, queries, columns),
+                k_ref[0, keys, columns],
+                last_dims,
+                preferred_element_type=jnp.float32,
+            )
+
+        ahead = scores_of(0)
+        for pair in range(wide // LANES):
+            scores = ahead
+            if (pair + 1) * LANES < wide:
+                ahead = scores_of(pair + 1)
+            shape = scores.shape
+            scores = (scores.reshape((2, QUERY_TILE) + shape[1:]) + bias).reshape(shape)
+            top = jnp.max(scores, -1, keepdims=True)
+            exponent = jnp.exp2((scores - top) * exponent_scale)
+            columns = pl.ds(pair * LANES, LANES)
+            part = jnp.dot(
+                exponent.astype(jnp.bfloat16),
+                v_ref[0, keys, columns],
+                preferred_element_type=jnp.float32,
+            )
+            part = part / jnp.sum(exponent, -1, keepdims=True)
+            out_ref[0, queries, columns] = merge_heads(part).astype(jnp.bfloat16)
+
+    over_windows(row, QUERY_TILE, start_ref, count_ref, length, window)
 
 
 def attend_back_kernel(
     row, begun, start_ref, count_ref, column_ref, line_ref, q_ref, k_ref, v_ref, grad_ref, *rest
 ):
     dq_ref, dk_ref, dv_ref, dk_sum, dv_sum = rest[begun:]
-    length = k_ref.shape[1]
-    lower = lax.broadcasted_iota(jnp.int32, (QUERY_TILE, LANES), 1) < HEAD_DIM
     dk_sum[...] = jnp.zeros_like(dk_sum)
     dv_sum[...] = jnp.zeros_like(dv_sum)
     scale = HEAD_DIM ** (-0.5)
-
-    def tile_step(tile, carry):
-        begin = pl.multiple_of(start_ref[row, tile] * LANES, LANES)
-        count = count_ref[row, tile]
-        queries = pl.ds(pl.multiple_of(tile * QUERY_TILE, QUERY_TILE), QUERY_TILE)
-
-        def window(tiles):
-            keys = pl.ds(begin, tiles * LANES)
-            query = q_ref[0, queries, :]
-            grad = grad_ref[0, queries, :]
-            key = k_ref[0, keys, :]
-            value = v_ref[0, keys, :]
-            allowed = column_ref[0, keys, :1] == line_ref[0, :1, queries]
-            query_part = []
-            key_part = 0.0
-            value_part = 0.0
-            for head in range(2):
-                mine = lower if head == 0 else jnp.logical_not(lower)
-                head_query = jnp.where(mine, query, jnp.zeros_like(query))
-                head_grad = jnp.where(mine, grad, jnp.zeros_like(grad))
-                scores = lax.dot_general(
-                    key, head_query, (((1,), (1,)), ((), ())), preferred_element_type=jnp.float32
-                )
-                scores = jnp.where(allowed, scores * scale, NEVER)
-                top = jnp.max(scores, 0, keepdims=True)
-                exponent = jnp.exp(scores - top)
-                probs = exponent * (1.0 / jnp.sum(exponent, 0, keepdims=True))
-                grad_probs = lax.dot_general(
-                    value, head_grad, (((1,), (1,)), ((), ())), preferred_element_type=jnp.float32
-                )
-                inner = jnp.sum(grad_probs * probs, 0, keepdims=True)
-                grad_scores = (probs * (grad_probs - inner)).astype(jnp.bfloat16)
-                value_part += jnp.dot(
-                    probs.astype(jnp.bfloat16), head_grad, preferred_element_type=jnp.float32
-                )
-                key_part += jnp.dot(grad_scores, head_query, preferred_element_type=jnp.float32)
-                query_part.append(
-                    lax.dot_general(
-                        grad_scores, key, (((0,), (0,)), ((), ())), preferred_element_type=jnp.float32
-                    )
-                )
-            dq_ref[0, queries, :] = (
-                jnp.where(lower, query_part[0], query_part[1]) * scale
-            ).astype(jnp.bfloat16)
-            dk_sum[keys, :] += key_part
-            dv_sum[keys, :] += value_part
-
-        for tiles in range(1, length // LANES + 1):
-            pl.when(count == tiles)(functools.partial(window, tiles))
-        return carry
-
-    lax.fori_loop(0, length // QUERY_TILE, tile_step, 0)
+    columns = pl.ds(0, LANES)
+
+    def window(queries, keys):
+        query, grad = two_heads(q_ref, queries, columns), two_heads(grad_ref, queries, columns)
+        key, value = k_ref[0, keys, :], v_ref[0, keys, :]
+        bias = jnp.where(column_ref[0, keys, :1] == line_ref[0, :1, queries], 0.0, NEVER)
+        scores = lax.dot_general(key, query, last_dims, preferred_element_type=jnp.float32)
+        scores = scores + jnp.concatenate([bias, bias], 1)
+        top = jnp.max(scores, 0, keepdims=True)
+        exponent = jnp.exp2((scores - top) * exponent_scale)
+        probs = exponent * (1.0 / jnp.sum(exponent, 0, keepdims=True))
+        grad_probs = lax.dot_general(value, grad, last_dims, preferred_element_type=jnp.float32)
+        inner = jnp.sum(grad_probs * probs, 0, keepdims=True)
+        grad_scores = (probs * (grad_probs - inner)).astype(jnp.bfloat16)
+        dv_sum[keys, :] += jnp.dot(
+            probs.astype(jnp.bfloat16), grad, preferred_element_type=jnp.float32
+        )
+        dk_sum[keys, :] += jnp.dot(grad_scores, query, preferred_element_type=jnp.float32)
+        query_part = lax.dot_general(
+            grad_scores, key, first_dims, preferred_element_type=jnp.float32
+        )
+        dq_ref[0, queries, :] = (merge_heads(query_part) * scale).astype(jnp.bfloat16)
+
+    over_windows(row, BACK_TILE, start_ref, count_ref, k_ref.shape[1], window)
     dk_ref[0] = (dk_sum[...] * scale).astype(jnp.bfloat16)
     dv_ref[0] = dv_sum[...].astype(jnp.bfloat16)
 
 
-def windows_of(segments):
-    heads = segments[:, ::QUERY_TILE]
-    tails = segments[:, QUERY_TILE - 1 :: QUERY_TILE]
+def windows_of(segments, query_tile):
+    heads = segments[:, ::query_tile]
+    tails = segments[:, query_tile - 1 :: query_tile]
     begin = jnp.sum(segments[:, None, :] < heads[:, :, None], -1, dtype=jnp.int32)
     end = jnp.sum(segments[:, None, :] <= tails[:, :, None], -1, dtype=jnp.int32)
     start = begin // LANES
     return start, (end + LANES - 1) // LANES - start
 
 
-def attention_call(kernel, row, windows, marks, operands, outputs, scratch, begun=()):
-    rows, length, width = operands[0][0].shape
+def attention_call(
+    kernel, row, rows, windows, marks, operands, outputs, scratch, block_wide, begun=()
+):
+    all_rows, length, _ = operands[0][0].shape
     wide = outputs[0]
-    pairs = wide // LANES
-
-    def block(first):
-        return pl.BlockSpec((1, length, LANES), lambda pair, *_: (row, 0, first + pair))
-
-    work = wide * length * length
-    shape = jax.ShapeDtypeStruct((rows, length, wide), jnp.bfloat16)
+    steps = wide // block_wide
+
+    def block(part):
+        return pl.BlockSpec(
+            (1, length, block_wide), lambda at, step, *_: (row + at, 0, part * steps + step)
+        )
+
+    work = rows * wide * length * length
+    shape = jax.ShapeDtypeStruct((all_rows, length, wide), jnp.bfloat16)
     return pl.pallas_call(
         functools.partial(kernel, row, len(begun)),
         grid_spec=pltpu.PrefetchScalarGridSpec(
             num_scalar_prefetch=2,
-            grid=(pairs,),
+            grid=(rows, steps),
             in_specs=[
-                pl.BlockSpec((1, length, LANES), lambda pair, *_: (row, 0, 0)),
-                pl.BlockSpec((1, 8, length), lambda pair, *_: (row, 0, 0)),
+                pl.BlockSpec((1, length, LANES), lambda at, *_: (row + at, 0, 0)),
+                pl.BlockSpec((1, 8, length), lambda at, *_: (row + at, 0, 0)),
             ]
             + [block(first) for _, first in operands]
             + [pl.BlockSpec(memory_space=pl.ANY)] * len(begun),
@@ -443,7 +449,7 @@
         compiler_params=pltpu.CompilerParams(vmem_limit_bytes=48 * 1024 * 1024),
         cost_estimate=pl.CostEstimate(
             flops=4 * len(operands) * work,
-            bytes_accessed=2 * (len(operands) + len(outputs)) * length * wide,
+            bytes_accessed=2 * (len(operands) + len(outputs)) * rows * length * wide,
             transcendentals=work // HEAD_DIM,
         ),
     )(*windows, *marks, *(array for array, _ in operands), *begun)
@@ -510,13 +516,17 @@
 def load_pieces(place_ref, pieces, target_of, sems):
     copies = []
     for part in range(2):
-        for index in range(4):
-            piece = pieces[part * 4 + index]
-            row_y, row_x = place_ref[1] ^ (index // 2), place_ref[2] ^ (index % 2)
-            for zed in range(Z_SIZE):
-                target = target_of(part, zed, row_y, row_x, piece)
-                copies.append(pltpu.make_async_copy(piece.at[zed], target, sems.at[len(copies)]))
-                copies[-1].start()
+        for across in range(2):
+            for along in range(2):
+                far_y, far_x = (along, across) if part == 0 else (across, along)
+                row_y, row_x = place_ref[1] ^ far_y, place_ref[2] ^ far_x
+                piece = pieces[part * 2 + across].at[along]
+                for zed in range(Z_SIZE):
+                    target = target_of(part, zed, row_y, row_x, piece)
+                    copies.append(
+                        pltpu.make_async_copy(piece.at[zed], target, sems.at[len(copies)])
+                    )
+                    copies[-1].start()
     return copies
 
 
@@ -536,19 +546,6 @@
         copy.wait()
 
 
-def assemble_rows_kernel(place_ref, *refs):
-    *pieces, out_ref, sems = refs
-
-    def target_of(part, zed, row_y, row_x, piece):
-        depth = piece.shape[1]
-        half = (zed // 2) ^ place_ref[3]
-        row = (((zed % 2) * 2 + row_y) * 2 + row_x) * 2 * depth + part * depth
-        return out_ref.at[half, pl.ds(pl.multiple_of(row, 16), depth), :]
-
-    for copy in load_pieces(place_ref, pieces, target_of, sems):
-        copy.wait()
-
-
 def place_vector():
     return jnp.stack(chip_place() + (lax.axis_index("seq"),)).astype(jnp.int32)
 
@@ -559,7 +556,7 @@
         grid_spec=pltpu.PrefetchScalarGridSpec(
             num_scalar_prefetch=1,
             grid=(1,),
-            in_specs=[pl.BlockSpec(memory_space=pl.ANY)] * 8,
+            in_specs=[pl.BlockSpec(memory_space=pl.ANY)] * 4,
             out_specs=pl.BlockSpec(shape, lambda step, *_: (0,) * len(shape)),
             scratch_shapes=[pltpu.SemaphoreType.DMA((32,))],
         ),
@@ -569,46 +566,124 @@
 
 
 FFN_TILE = 256
-FFN_CHUNK = 640
-
-
-def feed_forward_kernel(
-    place_ref, normed_ref, cot_ref, *refs, begun
-):
-    up_pieces, refs = refs[:8], refs[8:]
-    down_mine, down_other = refs[:2]
-    refs = refs[4:] if begun else refs[2:]
-    hidden_ref, grad_pre_ref, y_ref, grad_ref, up_ref, down_ref, up_sems, down_sems = refs
+FFN_CHUNK = 512
+root_two_pi = 0.3989422804014327
+
+
+def feed_forward_kernel(*refs):
+    normed_ref, cot_ref, *refs = refs
+    up_pieces, down_pieces, refs = refs[:4], refs[4:8], refs[8:]
+    hidden_ref, grad_pre_ref, y_ref, grad_ref, normed_out, y_came, grad_came, *refs = refs
+    up_ref, down_ref, normed_buf, y_away, grad_away, *refs = refs
+    up_sems, down_sems, sent_sems, came_sems, normed_sems, away_sends, away_recvs = refs
     step = pl.program_id(0)
-    wide = down_mine.shape[1]
-
-    def copies():
-        down = []
-        for index, piece in enumerate((down_mine, down_other)):
-            left = pl.multiple_of((place_ref[3] ^ index) * wide, 128)
-            target = down_ref.at[:, pl.ds(left, wide)]
-            down.append(pltpu.make_async_copy(piece, target, down_sems.at[index]))
-        return down
+    row, core = lax.axis_index("rows"), lax.axis_index("seq")
+    here_y, here_x = (row // 2) % 2, row % 2
+    twin = (row, 1 - core)
+    span = normed_ref.shape[0]
+    tiles = span // FFN_TILE
+
+    def remote(src, dst, send_sem, recv_sem):
+        return pltpu.make_async_remote_copy(
+            src_ref=src,
+            dst_ref=dst,
+            send_sem=send_sem,
+            recv_sem=recv_sem,
+            device_id=twin,
+            device_id_type=pl.DeviceIdType.MESH,
+        )
+
+    def normed_copies():
+        own, others = normed_buf.at[pl.ds(0, span), :], normed_buf.at[pl.ds(span, span), :]
+        return (
+            pltpu.make_async_copy(normed_ref, own, normed_sems.at[0]),
+            remote(normed_ref, others, normed_sems.at[1], normed_sems.at[2]),
+        )
+
+    def up_copies():
+        copies = []
+        for part in range(2):
+            for across in range(2):
+                for along in range(2):
+                    far_y, far_x = (along, across) if part == 0 else (across, along)
+                    row_y = 1 - here_y if far_y else here_y
+                    row_x = 1 - here_x if far_x else here_x
+                    for zed in range(Z_SIZE):
+                        piece = up_pieces[part * 2 + across].at[along, zed]
+                        depth, wide = piece.shape
+                        first = pl.multiple_of(((zed * 2 + row_y) * 2 + row_x) * depth, 16)
+                        left = 0 if part == 0 else up_ref.shape[1] - wide
+                        target = up_ref.at[pl.ds(first, depth), pl.ds(left, wide)]
+                        copies.append(pltpu.make_async_copy(piece, target, up_sems.at[len(copies)]))
+        return copies
+
+    def down_copies():
+        kept, given = [], []
+        for part in range(2):
+            for across in range(2):
+                for along in range(2):
+                    far_y, far_x = (along, across) if part == 0 else (across, along)
+                    row_y = 1 - here_y if far_y else here_y
+                    row_x = 1 - here_x if far_x else here_x
+                    for lower in range(2):
+                        pieces = down_pieces[part * 2 + across]
+                        depth, wide = pieces.shape[2:]
+                        first = (((lower * 2 + row_y) * 2 + row_x) * 2 + part) * depth
+                        rows = pl.ds(pl.multiple_of(first, 16), depth)
+                        target = down_ref.at[rows, pl.ds(pl.multiple_of(core * wide, 128), wide)]
+                        number = len(kept)
+                        kept.append(
+                            pltpu.make_async_copy(
+                                pieces.at[along, 2 * core + lower], target, down_sems.at[number]
+                            )
+                        )
+                        given.append(
+                            remote(
+                                pieces.at[along, 2 * (1 - core) + lower],
+                                target,
+                                sent_sems.at[number],
+                                came_sems.at[number],
+                            )
+                        )
+        return kept, given
+
+    def away_copies(tile):
+        rows = pl.ds(pl.multiple_of(tile * FFN_TILE, FFN_TILE), FFN_TILE)
+        return [
+            remote(buf.at[tile], out.at[rows, :], away_sends.at[which, tile], away_recvs.at[which, tile])
+            for which, (buf, out) in enumerate(((y_away, y_came), (grad_away, grad_came)))
+        ]
 
     @pl.when(step == 0)
     def _():
-        waits = load_pieces(place_ref, up_pieces, column_target(up_ref), up_sems)
-        waits += copies()
-        for copy in waits[-2:]:
+        barrier = pltpu.get_barrier_semaphore()
+        pl.semaphore_signal(barrier, inc=1, device_id=twin, device_id_type=pl.DeviceIdType.MESH)
+        kept, given = down_copies()
+        own, others = normed_copies()
+        ups = up_copies()
+        for copy in [own] + ups + kept:
             copy.start()
-        for copy in waits:
+        pl.semaphore_wait(barrier, 1)
+        for copy in given:
+            copy.start()
+        others.start()
+        for copy in [own] + ups + kept:
             copy.wait()
-
-    normed = normed_ref[...]
+        for copy in given:
+            copy.wait_recv()
+
+    @pl.when(step == tiles)
+    def _():
+        normed_copies()[1].wait_recv()
+
+    normed = normed_buf[pl.ds(pl.multiple_of(step * FFN_TILE, FFN_TILE), FFN_TILE), :]
     cot = cot_ref[...]
     y_sum = grad_sum = 0.0
     for chunk in range(hidden_ref.shape[1] // FFN_CHUNK):
         units = pl.ds(chunk * FFN_CHUNK, FFN_CHUNK)
         up, down = up_ref[:, units], down_ref[units, :]
         pre = jnp.dot(normed, up, preferred_element_type=jnp.float32)
-        grad_hidden = lax.dot_general(
-            cot, down, (((1,), (1,)), ((), ())), preferred_element_type=jnp.float32
-        )
+        grad_hidden = lax.dot_general(cot, down, last_dims, preferred_element_type=jnp.float32)
         phi = 0.5 + 0.5 * lax.erf(pre * root_half)
         hidden = (pre * phi).astype(jnp.bfloat16)
         slope = phi + pre * (jnp.exp(-0.5 * pre * pre) * root_two_pi)
@@ -616,49 +691,83 @@
         hidden_ref[:, units] = hidden
         grad_pre_ref[:, units] = grad_pre
         y_sum += jnp.dot(hidden, down, preferred_element_type=jnp.float32)
-        grad_sum += lax.dot_general(
-            grad_pre, up, (((1,), (1,)), ((), ())), preferred_element_type=jnp.float32
-        )
-    y_ref[...] = y_sum.astype(jnp.bfloat16)
-    grad_ref[...] = grad_sum.astype(jnp.bfloat16)
-
-
-root_two_pi = 0.3989422804014327
-
-
-def feed_forward(normed, cot, up_parts, down_mine, down_other, begun=()):
+        grad_sum += lax.dot_general(grad_pre, up, last_dims, preferred_element_type=jnp.float32)
+
+    @pl.when(step < tiles)
+    def _():
+        y_ref[...] = y_sum.astype(jnp.bfloat16)
+        grad_ref[...] = grad_sum.astype(jnp.bfloat16)
+
+    for tile in range(tiles):
+
+        @pl.when(step == tiles + tile)
+        def _(tile=tile):
+            y_away[tile] = y_sum.astype(jnp.bfloat16)
+            grad_away[tile] = grad_sum.astype(jnp.bfloat16)
+            for copy in away_copies(tile):
+                copy.start()
+
+    @pl.when(step == 2 * tiles - 1)
+    def _():
+        store = pltpu.make_async_copy(normed_buf, normed_out, normed_sems.at[0])
+        store.start()
+        for copy in (*down_copies()[1], normed_copies()[1]):
+            copy.wait_send()
+        for tile in range(tiles):
+            for copy in away_copies(tile):
+                copy.wait()
+        store.wait()
+
+
+def feed_forward(normed, cot_all, up_parts, down_parts):
     tokens, width = normed.shape
-    units = down_mine.shape[0]
+    units = up_parts[0][0].shape[3] + up_parts[1][0].shape[3]
     tiles = tokens // FFN_TILE
-    offset = tiles if begun else 0
-    tile = pl.BlockSpec((FFN_TILE, width), lambda step, *_: (step, 0))
-    wide_tile = pl.BlockSpec((FFN_TILE, units), lambda step, *_: (step + offset, 0))
+    tile = pl.BlockSpec((FFN_TILE, width), lambda step: (step, 0))
+    own_tile = pl.BlockSpec((FFN_TILE, width), lambda step: (jnp.minimum(step, tiles - 1), 0))
+    wide_tile = pl.BlockSpec((FFN_TILE, units), lambda step: (step, 0))
     anywhere = pl.BlockSpec(memory_space=pl.ANY)
     wide_shape = jax.ShapeDtypeStruct((2 * tokens, units), jnp.bfloat16)
     shape = jax.ShapeDtypeStruct((tokens, width), jnp.bfloat16)
+    away = pltpu.VMEM((tiles, FFN_TILE, width), jnp.bfloat16)
+    sems = pltpu.SemaphoreType.DMA
     return pl.pallas_call(
-        functools.partial(feed_forward_kernel, begun=bool(begun)),
-        grid_spec=pltpu.PrefetchScalarGridSpec(
-            num_scalar_prefetch=1,
-            grid=(tiles,),
-            in_specs=[tile, tile] + [anywhere] * (10 + len(begun)),
-            out_specs=[wide_tile, wide_tile, tile, tile],
-            scratch_shapes=[
-                pltpu.VMEM((width, units), jnp.bfloat16),
-                pltpu.VMEM((units, width), jnp.bfloat16),
-                pltpu.SemaphoreType.DMA((32,)),
-                pltpu.SemaphoreType.DMA((2,)),
-            ],
+        feed_forward_kernel,
+        grid=(2 * tiles,),
+        in_specs=[anywhere, tile] + [anywhere] * 8,
+        out_specs=[wide_tile, wide_tile, own_tile, own_tile] + [anywhere] * 3,
+        out_shape=[
+            wide_shape,
+            wide_shape,
+            shape,
+            shape,
+            jax.ShapeDtypeStruct((2 * tokens, width), jnp.bfloat16),
+            shape,
+            shape,
+        ],
+        scratch_shapes=[
+            pltpu.VMEM((width, units), jnp.bfloat16),
+            pltpu.VMEM((units, width), jnp.bfloat16),
+            pltpu.VMEM((2 * tokens, width), jnp.bfloat16),
+            away,
+            away,
+            sems((32,)),
+            sems((16,)),
+            sems((16,)),
+            sems((16,)),
+            sems((3,)),
+            sems((2, tiles)),
+            sems((2, tiles)),
+        ],
+        compiler_params=pltpu.CompilerParams(
+            collective_id=2, has_side_effects=True, vmem_limit_bytes=60 * 1024 * 1024
         ),
-        out_shape=[wide_shape, wide_shape, shape, shape],
-        input_output_aliases={13: 0, 14: 1} if begun else {},
-        compiler_params=pltpu.CompilerParams(vmem_limit_bytes=56 * 1024 * 1024),
         cost_estimate=pl.CostEstimate(
-            flops=8 * tokens * width * units,
-            bytes_accessed=4 * width * units + 4 * tokens * (2 * width + units),
-            transcendentals=2 * tokens * units,
+            flops=16 * tokens * width * units,
+            bytes_accessed=4 * width * units + 8 * tokens * (2 * width + units),
+            transcendentals=4 * tokens * units,
         ),
-    )(place_vector(), normed, cot, *up_parts[0], *up_parts[1], down_mine, down_other, *begun)
+    )(normed, cot_all, *up_parts[0], *up_parts[1], *down_parts[0], *down_parts[1])
 
 
 def following(zed):
@@ -872,7 +981,8 @@
     key_out,
     value_out,
     gain_out,
-    hidden_out,
+    up_out,
+    out_out,
     weight_buf,
     dq_buf,
     dk_buf,
@@ -1060,31 +1170,37 @@
 
     tiles = own_buf.shape[0] // TAIL_TILE
     norm_tiles = own_buf.shape[0] // NORM_TILE
+    middle, quarter = tiles // 2, norm_tiles // 4
     issue(1)
     around_hidden(1)
     issue(2)
     for load in loads[:4]:
         load.wait()
-    lax.fori_loop(0, tiles, away_tile, 0)
+    lax.fori_loop(0, middle, away_tile, 0)
+    turn(1)
+    issue(3)
+    lax.fori_loop(middle, tiles, away_tile, 0)
     away = send(away_buf, came_buf, (row, 1 - core))
-    turn(1)
     around_hidden(2)
-    issue(3)
-    lax.fori_loop(0, tiles, own_tile, 0)
+    lax.fori_loop(0, middle, own_tile, 0)
+    turn(2)
     total(1)
     around(1)
-    turn(2)
     issue(0)
+    lax.fori_loop(middle, tiles, own_tile, 0)
     for load in loads[4:]:
         load.wait()
     away.wait_recv()
     gain_part = jnp.zeros((1, own_buf.shape[1]), jnp.float32)
-    gain_part = lax.fori_loop(0, norm_tiles // 2, norm_tile, gain_part)
+    gain_part = lax.fori_loop(0, quarter, norm_tile, gain_part)
+    turn(3)
+    around_hidden(3)
+    gain_part = lax.fori_loop(quarter, 2 * quarter, norm_tile, gain_part)
     total(2)
-    around_hidden(3)
     around(2)
-    turn(3)
-    gain_part = lax.fori_loop(norm_tiles // 2, norm_tiles, norm_tile, gain_part)
+    gain_part = lax.fori_loop(2 * quarter, 3 * quarter, norm_tile, gain_part)
+    turn(0)
+    gain_part = lax.fori_loop(3 * quarter, norm_tiles, norm_tile, gain_part)
     store = pltpu.make_async_copy(residual_buf, token_out, local_sems.at[6])
     store.start()
     gain_buf[0] = jnp.zeros_like(gain_buf[0])
@@ -1097,16 +1213,17 @@
         gain_buf[number + 1] = gain_buf[number] + gain_came[number]
 
     exchange(0, (row, 1 - core))
+    exchange(1, (over_x, core))
     total(3)
     around(3)
-    turn(0)
-    exchange(1, (over_x, core))
     exchange(2, (over_y, core))
     exchange(3, (beside, core))
     exchange(4, (beyond, core))
     gain_out[...] = gain_buf[5]
     hidden_ring[-1].wait_recv()
-    hidden_out[...] = hidden_ref[zed].astype(jnp.float32) + hidden_came[2].astype(jnp.float32)
+    up_wide = up_out.shape[1]
+    for out, columns in ((up_out, pl.ds(0, up_wide)), (out_out, pl.ds(up_wide, half_wide))):
+        out[...] = plus_wide(hidden_ref[zed, :, columns], hidden_came[2, :, columns])
     total(0)
     ring[-1].wait_recv()
     for index, out in enumerate((query_out, key_out, value_out)):
@@ -1129,14 +1246,15 @@
     return pl.pallas_call(
         tail_kernel,
         in_specs=[anywhere] * 4 + [here] * 3 + [anywhere] * 2 + [here] * 3,
-        out_specs=[anywhere] + [here] * 5,
+        out_specs=[anywhere] + [here] * 6,
         out_shape=[
             jax.ShapeDtypeStruct((flat, width), jnp.float32),
             sum_shape,
             sum_shape,
             sum_shape,
             jax.ShapeDtypeStruct((8, width), jnp.float32),
-            jax.ShapeDtypeStruct(hidden_sums.shape[1:], jnp.float32),
+            jax.ShapeDtypeStruct((depth, hidden_sums.shape[2] - half_wide), jnp.float32),
+            sum_shape,
         ],
         scratch_shapes=[pltpu.VMEM((width, 3 * half_wide), jnp.bfloat16)]
         + [pltpu.VMEM((2 * flat, half_wide), jnp.bfloat16)] * 3
@@ -1170,14 +1288,6 @@
     )
 
 
-def halves(block):
-    depth, wide = block.shape
-    if depth > 80:
-        return block[: depth // 2], block[depth // 2 :]
-    cut = (wide // 128 + 1) // 2 * 128
-    return block[:, :cut], block[:, cut:]
-
-
 def halves_z(stack):
     _, depth, wide = stack.shape
     if depth > 80:
@@ -1186,12 +1296,12 @@
     return stack[:, :, :cut], stack[:, :, cut:]
 
 
-def start_xy(first, second):
-    return (first, swap_x(first), swap_y(first)), (second, swap_x(second), swap_y(second))
-
-
-def finish_xy(first, second):
-    return first + (swap_x(first[2]),), second + (swap_y(second[1]),)
+def gather_first(first, second):
+    return jnp.stack([first, swap_y(first)]), jnp.stack([second, swap_x(second)])
+
+
+def gather_second(first, second):
+    return (first, swap_x(first)), (second, swap_y(second))
 
 
 def dot_low(left_side, right_side):
@@ -1209,33 +1319,47 @@
     def __init__(self, first, second, by_rows=False):
         self.parts, self.by_rows = (first, second), by_rows
 
-    def pick(self, which, far_y, far_x):
-        _, here_y, here_x = chip_place()
+    def pick(self, which, start_y, start_x, count_y=1, count_x=1):
         picked = []
         for whole, row, depth, column, wide in self.parts[which]:
             blocks = whole.reshape(Z_SIZE, 2, 2, whole.shape[0] // 16, whole.shape[1])
             picked.append(
                 lax.dynamic_slice(
                     blocks,
-                    (0, here_y ^ far_y, here_x ^ far_x, row, column),
-                    (Z_SIZE, 1, 1, depth, wide),
-                ).reshape(Z_SIZE, depth, wide)
+                    (0, start_y, start_x, row, column),
+                    (Z_SIZE, count_y, count_x, depth, wide),
+                ).reshape(Z_SIZE, count_y * count_x, depth, wide)
             )
-        return picked[0] if len(picked) == 1 else jnp.concatenate(picked, 2)
+        return picked[0] if len(picked) == 1 else jnp.concatenate(picked, 3)
+
+    def prepare(self, *after):
+        _, here_y, here_x = chip_place()
+        here_x, here_y = tie((here_x, here_y), *after)
+        self.away = (self.pick(0, 0, 1 - here_x, 2, 1), self.pick(1, 1 - here_y, 0, 1, 2))
 
     def spread(self):
-        self.first_far = swap_x(self.pick(0, 1, 1))
-        self.second_far = swap_y(self.pick(1, 1, 1))
-        self.first_near = swap_x(self.pick(0, 0, 1))
-        self.second_near = swap_y(self.pick(1, 1, 0))
+        self.came = (swap_x(self.away[0]), swap_y(self.away[1]))
+
+    def of_came(self, which, far):
+        _, here_y, here_x = chip_place()
+        here = here_x if which else here_y
+        return lax.dynamic_slice_in_dim(self.came[which], here ^ far, 1, 1)
 
     def turn(self):
-        self.first_turned = swap_y(plus(self.pick(0, 1, 0), self.first_far))
-        self.second_turned = swap_x(plus(self.pick(1, 0, 1), self.second_far))
+        _, here_y, here_x = chip_place()
+        first = plus(self.pick(0, 1 - here_y, here_x), self.of_came(0, 1))
+        second = plus(self.pick(1, here_y, 1 - here_x), self.of_came(1, 1))
+        self.turning = (first, second)
+        self.turned = (swap_y(first), swap_x(second))
 
     def near_sums(self):
-        first = plus(self.pick(0, 0, 0), self.first_near, self.first_turned)
-        second = plus(self.pick(1, 0, 0), self.second_near, self.second_turned)
+        _, here_y, here_x = chip_place()
+        first, second = (
+            plus(
+                self.pick(which, here_y, here_x), self.of_came(which, 0), self.turned[which]
+            ).reshape((Z_SIZE,) + self.turned[which].shape[2:])
+            for which in range(2)
+        )
         return jnp.concatenate([first, second], 1 if self.by_rows else 2)
 
     def gather(self):
@@ -1284,7 +1408,8 @@
     first = core == 0
     tokens_own = tokens.reshape(flat, width).astype(jnp.float32)
     cot_own = cotangent.reshape(flat, width)
-    windows = windows_of(segments)
+    windows = windows_of(segments, QUERY_TILE)
+    back_windows = windows_of(segments, BACK_TILE)
     marks = (
         jnp.broadcast_to(segments[:, :, None], segments.shape + (LANES,)),
         jnp.broadcast_to(segments[:, None, :], (rows, 8, 2 * span)),
@@ -1293,33 +1418,30 @@
     w_qkv = attn_weights[:, : 3 * half_wide]
     w_q, w_k, w_v = (w_qkv[:, i * half_wide : (i + 1) * half_wide] for i in range(3))
 
-    up_parts = start_xy(*halves_z(up_stack))
+    up_parts = gather_first(*halves_z(up_stack))
     down_steps = [tie(w_down, up_stack)]
     down_steps.append(next_z(down_steps[-1]))
     w_o_half = attn_weights[:, 3 * half_wide :]
     w_o_other = swap_cores(w_o_half)
-    qkv = dot_low(normed, w_qkv).astype(jnp.bfloat16)
-    qkv, w_o_other, down_steps[1] = tie((qkv, w_o_other, down_steps[1]))
+    qk_rows = dot_low(normed, w_qkv[:, : 2 * half_wide]).astype(jnp.bfloat16)
+    normed, w_o_other, down_steps[1], up_parts = tie(
+        (normed, w_o_other, down_steps[1], up_parts), qk_rows
+    )
     down_steps.append(next_z(down_steps[-1]))
-    qkv = split(qkv, 3 * half_wide)
-    pairs = half_wide // LANES
-    operands = [(qkv, 0), (qkv, pairs), (qkv, 2 * pairs)]
-
-    def attend(row, operands, begun=()):
-        return attention_call(
-            attend_kernel, row, windows, marks, operands, [half_wide], [], begun
-        )
-
-    mixed = attend(0, operands)
-    mixed, up_parts, down_steps[2] = tie((mixed, up_parts, down_steps[2]))
-    up_parts = finish_xy(*up_parts)
+    up_near = up_parts
+    up_parts = gather_second(*up_parts)
+    normed = tie(normed, up_near)
+    value_rows = dot_low(normed, w_qkv[:, 2 * half_wide :]).astype(jnp.bfloat16)
+    value_rows, down_steps[2] = tie((value_rows, down_steps[2]))
     down_steps.append(next_z(down_steps[-1]))
-    for row in range(1, rows):
-        mixed = attend(row, operands, mixed)
-    (mixed,) = mixed
-    mixed, down_steps[3] = tie((mixed, down_steps[3]))
-    down_parts = start_xy(*halves_z(natural_z(down_steps)))
-    mixed, up_parts = tie((mixed, up_parts))
+    qk_rows, value_rows = split(qk_rows, 2 * half_wide), split(value_rows, half_wide)
+    qk_rows = tie(qk_rows, up_near)
+    operands = [(qk_rows, 0), (qk_rows, 1), (value_rows, 0)]
+    (mixed,) = attention_call(
+        attend_kernel, 0, rows, windows, marks, operands, [half_wide], [], half_wide
+    )
+    mixed, down_steps[3], up_parts = tie((mixed, down_steps[3], up_parts))
+    down_parts = gather_first(*halves_z(natural_z(down_steps)))
     w_o = jnp.where(
         first,
         jnp.concatenate([w_o_half, w_o_other], 1),
@@ -1334,35 +1456,27 @@
         jnp.concatenate([mixed_mine, mixed_other], 2),
         jnp.concatenate([mixed_other, mixed_mine], 2),
     ).reshape(flat, width)
+    mixed_own, down_parts = tie((mixed_own, down_parts))
+    mixed_own = tie(mixed_own, down_parts)
+    down_parts = gather_second(*down_parts)
     residual = tokens_own + dot_low(mixed_own, w_o)
     unit_two, scale_two = norm_stats(residual)
     normed_two = (unit_two * gain_ffn).astype(jnp.bfloat16)
-    normed_two_other = swap_cores(normed_two)
-    normed_two, down_parts = tie((normed_two, down_parts))
-    down_parts = finish_xy(*down_parts)
-    units = w_up.shape[1]
-    down_columns = assemble(assemble_rows_kernel, (2, units, width // 2), down_parts)
-    down_mine = down_columns[0]
-    down_other = swap_cores(down_columns[1])
-    weights = (up_parts, down_mine, down_other)
-    cot_other = cot_other.reshape(flat, width)
-
-    hidden_low, grad_pre, y_own, grad_two_own = feed_forward(normed_two, cot_own, *weights)
-    (normed_two_other, hidden_low, grad_pre) = tie((normed_two_other, hidden_low, grad_pre))
-    hidden_low, grad_pre, y_away, grad_two_away = feed_forward(
-        normed_two_other, cot_other, *weights, begun=(hidden_low, grad_pre)
-    )
-    normed_two_all = jnp.concatenate([normed_two, normed_two_other], 0)
-    cot_all = jnp.concatenate([cot_own, cot_other], 0)
-    grad_two_came = swap_cores(grad_two_away)
-    y_came = swap_cores(y_away)
-
-    hidden_low = tie(hidden_low, grad_two_away, y_away)
+    cot_all = jnp.concatenate([cot_own, cot_other.reshape(flat, width)], 0)
+    hidden_low, grad_pre, y_own, grad_two_own, normed_two_all, y_came, grad_two_came = feed_forward(
+        normed_two, cot_all, up_parts, down_parts
+    )
+
     down_half = outer_low(hidden_low, cot_all)
     down_away = swap_cores(own_half(down_half, 1, 1 - core))
-    grad_pre, normed_two_all = tie((grad_pre, normed_two_all), down_half)
-    up_whole = outer_low(normed_two_all, grad_pre)
-    down_away = tie(down_away, up_whole)
+    grad_normed_two = plus_wide(grad_two_own, tie(grad_two_came, down_half))
+    grad_residual = cot_own.astype(jnp.float32) + norm_back_rows(
+        unit_two, scale_two, gain_ffn, grad_normed_two
+    )
+    ffn_gain_part = jnp.sum(grad_normed_two * unit_two, 0)
+    grad_attn = grad_residual.astype(jnp.bfloat16).reshape(rows, span, width)
+    grad_attn_other = swap_cores(grad_attn)
+    down_away = tie(down_away, grad_attn, ffn_gain_part)
     down_kept = own_half(down_half, 1, core)
     down_whole = jnp.where(
         first,
@@ -1375,14 +1489,10 @@
         [(down_whole, depth // 2, depth // 2, 0, wide)],
         True,
     )
+    down_sum.prepare()
     down_sum.spread()
-    grad_normed_two = plus_wide(grad_two_own, tie(grad_two_came, up_whole))
-    grad_residual = cot_own.astype(jnp.float32) + norm_back_rows(
-        unit_two, scale_two, gain_ffn, grad_normed_two
-    )
-    ffn_gain_part = jnp.sum(grad_normed_two * unit_two, 0)
-    grad_attn = grad_residual.astype(jnp.bfloat16).reshape(rows, span, width)
-    grad_attn_other = swap_cores(grad_attn)
+    up_whole = outer_low(normed_two_all, tie(grad_pre, *down_sum.away))
+    grad_attn_other = tie(grad_attn_other, up_whole)
     grad_attn_all = jnp.where(
         first,
         jnp.concatenate([grad_attn, grad_attn_other], 1),
@@ -1390,12 +1500,8 @@
     ).reshape(2 * flat, width)
     out_half = outer_low(mixed.reshape(2 * flat, -1), grad_attn_all)
     out_away = swap_cores(own_half(out_half, 1, 1 - core))
-    grad_attn_all = tie(grad_attn_all, out_half)
-    (grad_attn_all, down_sum.first_far, down_sum.second_far) = tie(
-        (grad_attn_all, down_sum.first_far, down_sum.second_far)
-    )
-    down_sum.turn()
     grad_mixed = split(times_transposed(grad_attn_all, w_o_rows).astype(jnp.bfloat16), width // 2)
+    out_away = tie(out_away, grad_mixed)
     out_kept = own_half(out_half, 1, core)
     out_whole = jnp.where(
         first,
@@ -1408,47 +1514,51 @@
         [(up_whole, 0, depth, 0, cut)],
         [(up_whole, 0, depth, cut, wide - cut), (out_whole, 0, depth, 0, half_wide)],
     )
+    down_sum.hold(("came",), grad_mixed)
+    down_sum.turn()
+    y_own, y_came = tie((y_own, y_came), *down_sum.turning)
+    layer_out = (residual + plus_wide(y_own, y_came)).astype(jnp.bfloat16)
+    up_sum.prepare(*down_sum.turning)
     up_sum.spread()
-    y_own, y_came = tie((y_own, y_came), grad_mixed)
-    layer_out = (residual + plus_wide(y_own, y_came)).astype(jnp.bfloat16)
-    down_names = ("first_near", "second_near", "first_turned", "second_turned")
-    down_sum.hold(down_names, layer_out)
-    grad_mixed = tie(grad_mixed, *(getattr(down_sum, name) for name in down_names))
-    down_sum.gather()
+    grad_mixed = tie(grad_mixed, layer_out, *up_sum.away, *down_sum.turning)
     scratch = [pltpu.VMEM((2 * span, LANES), jnp.float32)] * 2
 
     def attend_back(row, grad_rows, begun=()):
         return attention_call(
             attend_back_kernel,
             row,
-            windows,
+            1,
+            back_windows,
             marks,
             operands + [(grad_rows, 0)],
             [half_wide] * 3,
             scratch,
+            LANES,
             begun,
         )
 
-    up_names = ("first_far", "second_far")
-    grads = ()
-    for row in range(rows):
+    grads = attend_back(0, grad_mixed)
+    down_sum.hold(("turned",), *grads)
+    down_sum.gather()
+    grads = tie(grads, down_sum.sums)
+    for row in range(1, rows):
         grads = attend_back(row, grad_mixed, grads)
-        if row == 0:
-            down_sum.hold(("moving",), *grads)
-            up_sum.hold(up_names, *grads)
-            grads = tie(grads, down_sum.moving, up_sum.first_far, up_sum.second_far)
-            down_sum.step(2)
-            up_sum.turn()
+    down_sum.hold(("moving",), *grads)
+    up_sum.hold(("came",), *grads)
+    grads = tie(grads, down_sum.moving, up_sum.came)
+    up_sum.turn()
+    down_sum.step(2)
+    grads = tie(grads, *up_sum.turning)
     grad_queries, grad_keys, grad_values = (grad.reshape(2 * flat, half_wide) for grad in grads)
     query_whole = outer_low(normed, grad_queries)
     key_whole = outer_low(normed, grad_keys)
+    down_sum.hold(("moving",), query_whole, key_whole)
+    grad_values = tie(grad_values, down_sum.moving)
+    down_sum.step(3)
     value_whole = outer_low(normed, grad_values)
-    down_sum.hold(("moving",), query_whole)
-    key_whole = tie(key_whole, down_sum.moving)
-    down_sum.step(3)
-    up_sum.hold(down_names, key_whole)
+    up_sum.hold(("turned",), value_whole)
     sums = tie((query_whole, key_whole, value_whole), down_sum.moving)
-    token_grad, query_grad, key_grad, value_grad, gains, up_out_grad = tail_call(
+    token_grad, query_grad, key_grad, value_grad, gains, up_grad, out_grad = tail_call(
         (grad_queries, grad_keys, grad_values),
         attn_weights,
         sums,
@@ -1460,7 +1570,6 @@
     )
     gain_attn_grad, gain_ffn_grad = gains[0], gains[1]
     down_grad = down_sum.finish()
-    up_grad, out_grad = up_out_grad[:, : w_up.shape[1]], up_out_grad[:, w_up.shape[1] :]
     return (
         layer_out.reshape(rows, span, width),
         token_grad.reshape(rows, span, width),

time: 658 us -> 553 us (0.84)
  Pallas kernels: 338 us -> 280 us
  waiting for transfers between devices: 86.6 us -> 53.1 us
  starting transfers between devices: 40.7 us -> 27.3 us
  other arithmetic: 55.5 us -> 64.3 us
    pallas_call x4 -> x3, Pallas kernels: 114 us -> 79.8 us  [attention_call(): pl.pallas_call(functools.partial(kernel, row, len(begun)), grid_spec=pltp...]
    ppermute x12 -> x8, waiting for transfers between devices: 76.5 us -> 44.2 us  [swap_x(): return lax.ppermute(values, 'rows', [(row, row ^ 1) for row in range(16)])]
    pallas_call x3 -> x1, Pallas kernels: 91.2 us -> 72 us  [feed_forward(): pl.pallas_call(feed_forward_kernel, grid=(2 * tiles,), in_specs=[anywhere...]
    ppermute x12 -> x8, starting transfers between devices: 15.9 us -> 8.08 us  [swap_x(): return lax.ppermute(values, 'rows', [(row, row ^ 1) for row in range(16)])]
    ppermute x6, waiting for transfers between devices: 0.02 us -> 7.28 us  [next_z(): return lax.ppermute(values, 'rows', pairs)]
    ppermute x12 -> x8, starting transfers between devices: 13.8 us -> 7.78 us  [swap_y(): return lax.ppermute(values, 'rows', [(row, row ^ 2) for row in range(16)])]
    unnamed x108 -> x112, local copies, waits for them, and re-layouts: 22.7 us -> 21.1 us
    dot_general x2 -> x3, matrix products: 19.7 us -> 19.2 us  [dot_low(): return jnp.dot(left_side, right_side, preferred_element_type=jnp.float32)]
  transfers between devices with their start and end apart: 39 -> 27, of which waited for: 10 -> 8; matrix products, arithmetic and copies ran while one was open for 21% -> 23% of each run, Pallas kernels for 24% -> 15%
where the time goes in v4:
time: 553 us; the launch traced here: 549 us
  Pallas kernels  280 us (51%)
  matrix products  78.9 us (14%)
  other arithmetic  64.3 us (12%)
  waiting for transfers between devices  53.1 us (10%)
  local copies, waits for them, and re-layouts  42.7 us (8%)
  starting transfers between devices  27.3 us (5%)
    pallas_call x3, Pallas kernels, attention_call(): pl.pallas_call(functools.partial(kernel, row, len(begun)), grid_spec=pltp...  79.8 us
    pallas_call x1, Pallas kernels, feed_forward(): pl.pallas_call(feed_forward_kernel, grid=(2 * tiles,), in_specs=[anywhere...  72 us
    pallas_call x1, Pallas kernels, tail_call(): pl.pallas_call(tail_kernel, in_specs=[anywhere] * 4 + [here] * 3 + [anywh...  67.4 us
    pallas_call x1, Pallas kernels, head_call(): pl.pallas_call(head_kernel, in_specs=[anywhere, pl.BlockSpec(memory_space...  61.3 us
    dot_general x6, matrix products, outer_low(): jnp.einsum('tc,te->ce', left_side, right_side, preferred_element_type=jnp...  54.2 us
    ppermute x8, waiting for transfers between devices, swap_x(): return lax.ppermute(values, 'rows', [(row, row ^ 1) for row in range(16)])  44.2 us
    unnamed x112, local copies, waits for them, and re-layouts  21.1 us
    dot_general x3, matrix products, dot_low(): return jnp.dot(left_side, right_side, preferred_element_type=jnp.float32)  19.2 us
  transfers between devices with their start and end apart: 27, of which 8 were waited for; matrix products, arithmetic and copies ran while one was open for 23% of the time, Pallas kernels for 15%

profile of v4, /device:TPU:0, one launch (start us, length us, event | category | flops | bytes accessed | tf_op | source)
XLA Modules:
  0.0 548.6 jit_solution(15612455799638302294)
XLA Ops:
  1.3 1.1 pad_maximum_fusion.10.piece_ref
  2.4 1.7 copy-done
  4.2 1.7 copy-done.2
  6.9 61.3 %shard_map.186 = (bf16[2,1024,1280]{2,1,0:T(8,128)(2,1)S(1)}, bf16[2,512,1280]{2,1,0:T(8,128)(2,1)S(1)}, bf16[1280,2560]{1,0:T(8,128)(2,1)S(1)}, bf16[4,80,2560]{2,1,0:T(8,128)(2,1)S(1)}) custom-call(bf16[2,512,1280]{2,1,0:T(8,128)(2,1)S(1)} %copy-done.2, f32[1,1280]{1,0:T(1,128)S(1)} %reshape.330.gain_ref, bf16[2,512,1280]{2,1,0:T(8,128)(2,1)S(1)} %copy-done, ...), custom_call_target="tpu_custom_call" | custom-call | tf_op jit(solution)/shard_map/pallas_call | solution.py:932
  68.3 1.5 copy-done.5
  69.8 1.7 slice_bitcast_fusion.2
  71.5 1.8 collective-permute-start.3
  73.3 1.1 collective-permute-start.2
  74.4 1.3 slice.45
  76.6 8.6 %convolution_convert_fusion.2 = bf16[2048,1280]{1,0:T(8,128)(2,1)} fusion(bf16[2048,1280]{1,0:T(8,128)(2,1)S(1)} %bitcast.142, bf16[1280,2560]{1,0:T(8,128)(2,1)S(1)} %get-tuple-element.90.weights_ref), kind=kOutput, calls=%fused_computation.2 | convolution fusion | flops 6713507840 | bytes 13762560 | tf_op jit(solution)/shard_map/dot_general | solution.py:1308
  85.7 4.5 pad_maximum_fusion.refs_1_
  90.2 1.4 pad_maximum_fusion.5.refs_4_
  91.7 2.2 pad_maximum_fusion.4.refs_2_
  95.6 1.6 collective-permute-start.4
  97.3 6.9 %convolution_convert_fusion.7 = bf16[2048,640]{1,0:T(8,128)(2,1)} fusion(bf16[2048,1280]{1,0:T(8,128)(2,1)S(1)} %bitcast.143, bf16[1280,2560]{1,0:T(8,128)(2,1)} %copy-done.4), kind=kOutput, calls=%fused_computation.25 | convolution fusion | flops 3356753920 | bytes 9502720 | tf_op jit(solution)/shard_map/dot_general | solution.py:1308
  104.2 3.5 collective-permute-done.4
  109.0 21.2 %shard_map.187 = bf16[2,1024,640]{2,1,0:T(8,128)(2,1)S(1)} custom-call(s32[2,8]{1,0:T(2,128)S(1)} %get-tuple-element.181.start_ref, s32[2,8]{1,0:T(2,128)S(1)} %get-tuple-element.180.count_ref, s32[2,1024,128]{2,1,0:T(8,128)S(1)} %broadcast_in_dim.2.column_ref, s32[2,8,1024]{2,1,0:T(8,128)S(1)} %lt.189.line_ref, bf16[2,1024,1280]{2,1,0:T(8,128)(2,1)} %bitcast.177, ...), custom_call_target="tpu_custom_call" | custom-call | flops 16106127360 | bytes 10485760 | tf_op jit(solution)/shard_map/pallas_call | solution.py:433
  130.3 1.6 collective-permute-done.6.refs_3_
  131.9 1.2 copy-done.45
  133.4 1.4 pad_maximum_fusion.6
  135.5 1.2 collective-permute-start.10
  137.2 4.1 maximum_select_fusion.2
  141.4 14.9 %collective-permute-done.10 = bf16[4,160,640]{2,1,0:T(8,128)(2,1)S(1)} collective-permute-done((bf16[4,160,640]{2,1,0:T(8,128)(2,1)S(1)}, bf16[4,160,640]{2,1,0:T(8,128)(2,1)S(1)}, u32[]{:S(2)}, u32[]{:S(2)}) %collective-permute-start.10) | collective-permute-done | bytes 819232 | tf_op jit(solution)/shard_map/ppermute | solution.py:481
  160.3 3.7 fusion.33
  164.7 1.6 copy-done.17
  166.3 2.2 multiply_convert_fusion.refs_0_
  168.5 27.2 %collective-permute-done.11.refs_7_ = bf16[2,4,160,640]{3,2,1,0:T(8,128)(2,1)S(1)} collective-permute-done((bf16[2,4,160,640]{3,2,1,0:T(8,128)(2,1)S(1)}, bf16[2,4,160,640]{3,2,1,0:T(8,128)(2,1)S(1)}, u32[]{:S(2)}, u32[]{:S(2)}) %collective-permute-start.11) | collective-permute-done | bytes 1638432 | tf_op jit(solution)/shard_map/ppermute | solution.py:481
  195.7 1.2 copy-done.46
  196.9 72.0 %shard_map.188 = (bf16[2048,2560]{1,0:T(8,128)(2,1)}, bf16[2048,2560]{1,0:T(8,128)(2,1)}, bf16[1024,1280]{1,0:T(8,128)(2,1)}, bf16[1024,1280]{1,0:T(8,128)(2,1)}...) custom-call(bf16[1024,1280]{1,0:T(8,128)(2,1)} %multiply_convert_fusion.refs_0_, ...), custom_call_target="tpu_custom_call" | custom-call | flops 53687091200 | bytes 55050240 | tf_op jit(solution)/shard_map/pallas_call | solution.py:734
  268.9 17.1 %convolution_convert_fusion.1 = bf16[2560,1280]{1,0:T(8,128)(2,1)S(1)} fusion(bf16[2048,2560]{1,0:T(8,128)(2,1)} %get-tuple-element.114, bf16[1024,1280]{1,0:T(8,128)(2,1)} %bitcast.139, bf16[1024,1280]{1,0:T(8,128)(2,1)S(1)} %bitcast.135), kind=kOutput, calls=%fused_computation.1 | convolution fusion | flops 13435535360 | bytes 22282240 | tf_op jit(solution)/shard_map/tc,te->ce/dot_general | solution.py:1312
  286.0 3.3 constant_dynamic-slice_fusion.8
  290.6 6.5 %multiply_reduce_fusion = (f32[1280]{0:T(1024)S(1)}, f32[1024]{0:T(1024)S(1)}, f32[1024]{0:T(1024)S(1)}) fusion(bf16[1024,1280]{1,0:T(8,128)(2,1)} %get-tuple-element.117, bf16[1024,1280]{1,0:T(8,128)(2,1)} %get-tuple-element.115, f32[1024,1280]{1,0:T(8,128)} %copy-done.17, f32[1024]{0:T(1024)S(1)} %add_rsqrt_fusion, f32[1024]{0:T(1024)S(1)} %broadcast_multiply_fusion.2, ...), kind=kLoop, calls=%fused_computation.7 | loop fusion | flops 14414592 | bytes 10512384 | tf_op jit(solution)/shard_map/reduce_sum | solution.py:1476
  297.7 4.2 fusion.32
  302.5 5.3 maximum_select_fusion
  307.8 1.4 copy_bitcast_fusion.1
  309.2 1.9 copy_bitcast_fusion.2
  312.8 16.7 %convolution_convert_fusion = bf16[1280,2560]{1,0:T(8,128)(2,1)S(1)} fusion(bf16[2048,1280]{1,0:T(8,128)(2,1)S(1)} %bitcast.189, bf16[2048,2560]{1,0:T(8,128)(2,1)} %get-tuple-element.123), kind=kOutput, calls=%fused_computation | convolution fusion | flops 13425049600 | bytes 22282240 | tf_op jit(solution)/shard_map/tc,te->ce/dot_general | solution.py:1312
  329.5 6.2 %maximum_select_fusion.1 = bf16[2,1024,1280]{2,1,0:T(8,128)(2,1)S(1)} fusion(bf16[2,512,1280]{2,1,0:T(8,128)(2,1)S(1)} %collective-permute-done.16, bf16[2,512,1280]{2,1,0:T(8,128)(2,1)S(1)} %bitcast.156, pred[]{:T(512)S(6)} %eq.70), kind=kLoop, calls=%fused_computation.5 | loop fusion | flops 23592960 | bytes 10485761 | tf_op jit(solution)/shard_map/jit(_where)/select_n | solution.py:1496
  335.7 3.7 fusion.3
  341.6 5.5 %convolution_convert_fusion.6 = bf16[2048,640]{1,0:T(8,128)(2,1)} fusion(bf16[2048,1280]{1,0:T(8,128)(2,1)S(1)} %bitcast.165, bf16[1280,1280]{1,0:T(8,128)(2,1)S(1)} %copy-done.26, s32[]{:T(128)S(6)} %select_n.312), kind=kOutput, calls=%fused_computation.24 | convolution fusion | flops 3356753920 | bytes 9502724 | tf_op jit(solution)/shard_map/te,de->td/dot_general | solution.py:30
  350.1 2.9 fusion.11
  353.0 2.5 copy_bitcast_fusion.3
  355.6 1.4 collective-permute-start.18
  356.9 1.1 collective-permute-start.19
  358.0 3.1 copy_bitcast_fusion
  361.2 1.5 pad_maximum_fusion.2
  364.4 4.8 add_convert_fusion
  369.1 28.5 %shard_map.189 = (bf16[2,1024,640]{2,1,0:T(8,128)(2,1)S(1)}, bf16[2,1024,640]{2,1,0:T(8,128)(2,1)}, bf16[2,1024,640]{2,1,0:T(8,128)(2,1)}) custom-call(s32[2,4]{1,0:T(2,128)S(1)} %get-tuple-element.177.start_ref, s32[2,4]{1,0:T(2,128)S(1)} %get-tuple-element.176.count_ref, s32[2,1024,128]{2,1,0:T(8,128)S(1)} %copy-done.10, s32[2,8,1024]{2,1,0:T(8,128)S(1)} %copy-done.13, ...), custom_call_target="tpu_custom_call" | custom-call | flops 10737418240 | bytes 9175040 | tf_op jit(solution)/shard_map/pallas_call | solution.py:433
  397.6 3.1 fusion.18
  400.8 6.3 %collective-permute-start.20 = (bf16[320,640]{1,0:T(8,128)(2,1)S(1)}, bf16[320,640]{1,0:T(8,128)(2,1)S(1)}, u32[]{:S(2)}, u32[]{:S(2)}) collective-permute-start(bf16[320,640]{1,0:T(8,128)(2,1)S(1)} %fusion.22), channel_id=1, source_target_pairs={{0,8},{2,10},{4,12},{6,14},{8,24},{10,26},{12,28},{14,30},{24,16},... | collective-permute-start | bytes 1228808 | tf_op jit(solution)/shard_map/ppermute | solution.py:493
  407.1 30.1 %shard_map.190 = (bf16[2,1024,640]{2,1,0:T(8,128)(2,1)S(1)}, bf16[2,1024,640]{2,1,0:T(8,128)(2,1)}, bf16[2,1024,640]{2,1,0:T(8,128)(2,1)}) custom-call(s32[2,4]{1,0:T(2,128)S(1)} %get-tuple-element.177.start_ref, s32[2,4]{1,0:T(2,128)S(1)} %get-tuple-element.176.count_ref, ...), custom_call_target="tpu_custom_call", output_to_operand_aliasing={{0}: (8, {}), {1}: (9, {}), {2}: (10, {})} | custom-call | flops 10737418240 | bytes 9175040 | tf_op jit(solution)/shard_map/pallas_call | solution.py:433
  437.5 2.5 fusion.6
  440.0 1.5 add_convert_fusion.2
  441.5 2.0 collective-permute-start.25
  443.5 5.7 %convolution_convert_fusion.4.key_ref = bf16[1280,640]{1,0:T(8,128)(2,1)} fusion(bf16[2048,1280]{1,0:T(8,128)(2,1)S(1)} %bitcast.146, bf16[2048,640]{1,0:T(8,128)(2,1)S(1)} %bitcast.169), kind=kOutput, calls=%fused_computation.22 | convolution fusion | flops 3356262400 | bytes 9502720 | tf_op jit(solution)/shard_map/tc,te->ce/dot_general | solution.py:1312
  449.2 5.5 %convolution_convert_fusion.5.query_ref = bf16[1280,640]{1,0:T(8,128)(2,1)} fusion(bf16[2048,1280]{1,0:T(8,128)(2,1)S(1)} %bitcast.147, bf16[2048,640]{1,0:T(8,128)(2,1)S(1)} %bitcast.140), kind=kOutput, calls=%fused_computation.23 | convolution fusion | flops 3356262400 | bytes 9502720 | tf_op jit(solution)/shard_map/tc,te->ce/dot_general | solution.py:1312
  455.6 5.5 convolution_convert_fusion.3.value_ref
  461.0 3.8 collective-permute-done.24
  465.8 1.6 fusion.16
  467.5 1.7 fusion.15
  469.1 1.4 pad_maximum_fusion.3.hidden_ref
  470.6 67.4 %shard_map.191 = (f32[1024,1280]{1,0:T(8,128)}, f32[80,640]{1,0:T(8,128)}, f32[80,640]{1,0:T(8,128)}, f32[80,640]{1,0:T(8,128)}, f32[8,1280]{1,0:T(8,128)}, /*index=5*/f32[80,2560]{1,0:T(8,128)}, f32[80,640]{1,0:T(8,128)}) custom-call(bf16[2048,640]{1,0:T(8,128)(2,1)} %bitcast.141, bf16[2048,640]{1,0:T(8,128)(2,1)} %bitcast.168, ...), custom_call_target="tpu_custom_call" | custom-call | tf_op jit(solution)/shard_map/pallas_call | solution.py:1246
  537.9 1.5 slice_reduce_fusion
  539.4 5.3 copy.86
  (181 shorter events, 28.8 us)
Async XLA Ops:
  1.3 66.9 %copy-start.14 = (f32[1,1280]{1,0:T(1,128)}, f32[1,1280]{1,0:T(1,128)S(1)}, u32[]{:S(2)}) copy-start(f32[1,1280]{1,0:T(1,128)S(1)} %reshape.330.gain_ref) | copy-start | bytes 15364
  69.8 6.8 %copy-start.4 = (bf16[1280,2560]{1,0:T(8,128)(2,1)}, bf16[1280,2560]{1,0:T(8,128)(2,1)S(1)}, u32[]{:S(2)}) copy-start(bf16[1280,2560]{1,0:T(8,128)(2,1)S(1)} %get-tuple-element.90.weights_ref) | copy-start | bytes 19660804
  69.8 6.8 %copy-start.15 = (bf16[2,1024,1280]{2,1,0:T(8,128)(2,1)}, bf16[2,1024,1280]{2,1,0:T(8,128)(2,1)S(1)}, u32[]{:S(2)}) copy-start(bf16[2,1024,1280]{2,1,0:T(8,128)(2,1)S(1)} %get-tuple-element.89) | copy-start | bytes 15728644
  71.5 18.7 %collective-permute-start.3 = (bf16[4,80,1280]{2,1,0:T(8,128)(2,1)}, bf16[4,80,1280]{2,1,0:T(8,128)(2,1)}, u32[]{:S(2)}, u32[]{:S(2)}) collective-permute-start(bf16[4,80,1280]{2,1,0:T(8,128)(2,1)} %get-tuple-element.206), channel_id=1, source_target_pairs={{0,2},{2,0},{4,6},{6,4},{8,10},{10,8},{12,14},{14,12},{16,18},{18,... | collective-permute-start | bytes 2457608 | tf_op jit(solution)/shard_map/ppermute | solution.py:481
  73.3 18.4 %collective-permute-start.2 = (bf16[4,80,1280]{2,1,0:T(8,128)(2,1)}, bf16[4,80,1280]{2,1,0:T(8,128)(2,1)}, u32[]{:S(2)}, u32[]{:S(2)}) collective-permute-start(bf16[4,80,1280]{2,1,0:T(8,128)(2,1)} %get-tuple-element.207), channel_id=1, source_target_pairs={{0,4},{2,6},{4,0},{6,2},{8,12},{10,14},{12,8},{14,10},{16,20},{18,... | collective-permute-start | bytes 2457608 | tf_op jit(solution)/shard_map/ppermute | solution.py:485
  75.7 18.2 %collective-permute-start = (bf16[1280,640]{1,0:T(8,128)(2,1)}, bf16[1280,640]{1,0:T(8,128)(2,1)}, u32[]{:S(2)}, u32[]{:S(2)}) collective-permute-start(bf16[1280,640]{1,0:T(8,128)(2,1)} %slice.45), channel_id=1, source_target_pairs={{0,1},{1,0},{2,3},{3,2},{4,5},{5,4},{6,7},{7,6},{8,9},{9,8},{10,11... | collective-permute-start | bytes 4915208 | tf_op jit(solution)/shard_map/ppermute | solution.py:284
  75.7 18.2 %collective-permute-start.1 = (bf16[320,640]{1,0:T(8,128)(2,1)}, bf16[320,640]{1,0:T(8,128)(2,1)}, u32[]{:S(2)}, u32[]{:S(2)}) collective-permute-start(bf16[320,640]{1,0:T(8,128)(2,1)} %param.20), channel_id=1, source_target_pairs={{0,8},{2,10},{4,12},{6,14},{8,24},{10,26},{12,28},{14,30},{24,16},... | collective-permute-start | bytes 1228808 | tf_op jit(solution)/shard_map/ppermute | solution.py:493
  76.6 8.6 %copy-start.43 = (s32[2,1024]{1,0:T(2,128)S(1)}, s32[2,1024]{1,0:T(2,128)}, u32[]{:S(2)}) copy-start(s32[2,1024]{1,0:T(2,128)} %param.12) | copy-start | bytes 24580
  76.6 9.1 %copy-start.1 = (bf16[2,512,1280]{2,1,0:T(8,128)(2,1)S(1)}, bf16[2,512,1280]{2,1,0:T(8,128)(2,1)}, u32[]{:S(2)}) copy-start(bf16[2,512,1280]{2,1,0:T(8,128)(2,1)} %cot_ref.1) | copy-start | bytes 7864324
  85.7 4.5 copy-start.24
  90.2 7.0 %copy-start.16 = (bf16[2,1024,1280]{2,1,0:T(8,128)(2,1)S(1)}, bf16[2,1024,1280]{2,1,0:T(8,128)(2,1)}, u32[]{:S(2)}) copy-start(bf16[2,1024,1280]{2,1,0:T(8,128)(2,1)} %copy-done.15) | copy-start | bytes 15728644
  91.7 12.5 %copy-start.33 = (bf16[2,4,80,1280]{3,2,1,0:T(8,128)(2,1)}, bf16[2,4,80,1280]{3,2,1,0:T(8,128)(2,1)S(1)}, u32[]{:S(2)}) copy-start(bf16[2,4,80,1280]{3,2,1,0:T(8,128)(2,1)S(1)} %pad_maximum_fusion.5.refs_4_) | copy-start | bytes 4915204
  93.9 10.3 %copy-start.34 = (bf16[2,4,80,1280]{3,2,1,0:T(8,128)(2,1)}, bf16[2,4,80,1280]{3,2,1,0:T(8,128)(2,1)S(1)}, u32[]{:S(2)}) copy-start(bf16[2,4,80,1280]{3,2,1,0:T(8,128)(2,1)S(1)} %pad_maximum_fusion.4.refs_2_) | copy-start | bytes 4915204
  93.9 38.0 %collective-permute-start.6 = (bf16[2,4,80,1280]{3,2,1,0:T(8,128)(2,1)S(1)}, bf16[2,4,80,1280]{3,2,1,0:T(8,128)(2,1)S(1)}, u32[]{:S(2)}, u32[]{:S(2)}) collective-permute-start(bf16[2,4,80,1280]{3,2,1,0:T(8,128)(2,1)S(1)} %pad_maximum_fusion.4.refs_2_), channel_id=1, source_target_pairs={{0,2},{2,0},{4,6},{6,4},{8,10},{10,8},{12,14},{14,12},{16,18},{18,... | collective-permute-start | bytes 4915208 | tf_op jit(solution)/shard_map/ppermute | solution.py:481
  94.9 38.2 %collective-permute-start.7 = (bf16[2,4,80,1280]{3,2,1,0:T(8,128)(2,1)S(1)}, bf16[2,4,80,1280]{3,2,1,0:T(8,128)(2,1)}, u32[]{:S(2)}, u32[]{:S(2)}) collective-permute-start(bf16[2,4,80,1280]{3,2,1,0:T(8,128)(2,1)S(1)} %pad_maximum_fusion.5.refs_4_), channel_id=1, source_target_pairs={{0,4},{2,6},{4,0},{6,2},{8,12},{10,14},{12,8},{14,10},{16,20},{18,... | collective-permute-start | bytes 4915208 | tf_op jit(solution)/shard_map/ppermute | solution.py:485
  95.6 12.1 %collective-permute-start.4 = (bf16[320,640]{1,0:T(8,128)(2,1)}, bf16[320,640]{1,0:T(8,128)(2,1)S(1)}, u32[]{:S(2)}, u32[]{:S(2)}) collective-permute-start(bf16[320,640]{1,0:T(8,128)(2,1)} %collective-permute-done.1), channel_id=1, source_target_pairs={{0,8},{2,10},{4,12},{6,14},{8,24},{10,26},{12,28},{14,30},{24,16},... | collective-permute-start | bytes 1228808 | tf_op jit(solution)/shard_map/ppermute | solution.py:493
  107.7 22.6 %collective-permute-start.5 = (bf16[320,640]{1,0:T(8,128)(2,1)S(1)}, bf16[320,640]{1,0:T(8,128)(2,1)S(1)}, u32[]{:S(2)}, u32[]{:S(2)}) collective-permute-start(bf16[320,640]{1,0:T(8,128)(2,1)S(1)} %collective-permute-done.4), channel_id=1, source_target_pairs={{0,8},{2,10},{4,12},{6,14},{8,24},{10,26},{12,28},{14,30},{24,16},... | collective-permute-start | bytes 1228808 | tf_op jit(solution)/shard_map/ppermute | solution.py:493
  109.0 21.3 %copy-start.9 = (s32[2,1024,128]{2,1,0:T(8,128)}, s32[2,1024,128]{2,1,0:T(8,128)S(1)}, u32[]{:S(2)}) copy-start(s32[2,1024,128]{2,1,0:T(8,128)S(1)} %broadcast_in_dim.2.column_ref) | copy-start | bytes 3145732
  109.0 21.2 %copy-start.12 = (s32[2,8,1024]{2,1,0:T(8,128)}, s32[2,8,1024]{2,1,0:T(8,128)S(1)}, u32[]{:S(2)}) copy-start(s32[2,8,1024]{2,1,0:T(8,128)S(1)} %lt.189.line_ref) | copy-start | bytes 196612
  133.3 24.0 %collective-permute-start.8 = (bf16[2,512,640]{2,1,0:T(8,128)(2,1)S(1)}, bf16[2,512,640]{2,1,0:T(8,128)(2,1)S(1)}, u32[]{:S(2)}, u32[]{:S(2)}) collective-permute-start(bf16[2,512,640]{2,1,0:T(8,128)(2,1)S(1)} %get-tuple-element.191), channel_id=1, source_target_pairs={{0,1},{1,0},{2,3},{3,2},{4,5},{5,4},{6,7},{7,6},{8,9},{9,8},{10,11... | collective-permute-start | bytes 3932168 | tf_op jit(solution)/shard_map/ppermute | solution.py:284
  135.5 20.7 %collective-permute-start.10 = (bf16[4,160,640]{2,1,0:T(8,128)(2,1)S(1)}, bf16[4,160,640]{2,1,0:T(8,128)(2,1)S(1)}, u32[]{:S(2)}, u32[]{:S(2)}) collective-permute-start(bf16[4,160,640]{2,1,0:T(8,128)(2,1)S(1)} %get-tuple-element.198), channel_id=1, source_target_pairs={{0,2},{2,0},{4,6},{6,4},{8,10},{10,8},{12,14},{14,12},{16,18},{18,... | collective-permute-start | bytes 2457608 | tf_op jit(solution)/shard_map/ppermute | solution.py:481
  136.7 20.4 %collective-permute-start.9 = (bf16[4,160,640]{2,1,0:T(8,128)(2,1)S(1)}, bf16[4,160,640]{2,1,0:T(8,128)(2,1)S(1)}, u32[]{:S(2)}, u32[]{:S(2)}) collective-permute-start(bf16[4,160,640]{2,1,0:T(8,128)(2,1)S(1)} %get-tuple-element.199), channel_id=1, source_target_pairs={{0,4},{2,6},{4,0},{6,2},{8,12},{10,14},{12,8},{14,10},{16,20},{18,... | collective-permute-start | bytes 2457608 | tf_op jit(solution)/shard_map/ppermute | solution.py:485
  141.3 18.9 %copy-start.25 = (bf16[1280,1280]{1,0:T(8,128)(2,1)}, bf16[1280,1280]{1,0:T(8,128)(2,1)S(1)}, u32[]{:S(2)}) copy-start(bf16[1280,1280]{1,0:T(8,128)(2,1)S(1)} %maximum_select_fusion.2) | copy-start | bytes 9830404
  158.5 37.2 %collective-permute-start.11 = (bf16[2,4,160,640]{3,2,1,0:T(8,128)(2,1)S(1)}, bf16[2,4,160,640]{3,2,1,0:T(8,128)(2,1)S(1)}, u32[]{:S(2)}, u32[]{:S(2)}) collective-permute-start(bf16[2,4,160,640]{3,2,1,0:T(8,128)(2,1)S(1)} %pad_maximum_fusion.8.refs_6_), channel_id=1, source_target_pairs={{0,2},{2,0},{4,6},{6,4},{8,10},{10,8},{12,14},{14,12},{16,18},{18,... | collective-permute-start | bytes 4915208 | tf_op jit(solution)/shard_map/ppermute | solution.py:481
  159.4 37.5 %collective-permute-start.12 = (bf16[2,4,160,640]{3,2,1,0:T(8,128)(2,1)S(1)}, bf16[2,4,160,640]{3,2,1,0:T(8,128)(2,1)}, u32[]{:S(2)}, u32[]{:S(2)}) collective-permute-start(bf16[2,4,160,640]{3,2,1,0:T(8,128)(2,1)S(1)} %pad_maximum_fusion.9.refs_8_), channel_id=1, source_target_pairs={{0,4},{2,6},{4,0},{6,2},{8,12},{10,14},{12,8},{14,10},{16,20},{18,... | collective-permute-start | bytes 4915208 | tf_op jit(solution)/shard_map/ppermute | solution.py:485
  289.4 13.1 %collective-permute-start.13 = (bf16[2560,640]{1,0:T(8,128)(2,1)}, bf16[2560,640]{1,0:T(8,128)(2,1)}, u32[]{:S(2)}, u32[]{:S(2)}) collective-permute-start(bf16[2560,640]{1,0:T(8,128)(2,1)} %get-tuple-element.189), channel_id=1, source_target_pairs={{0,1},{1,0},{2,3},{3,2},{4,5},{5,4},{6,7},{7,6},{8,9},{9,8},{10,11... | collective-permute-start | bytes 9830408 | tf_op jit(solution)/shard_map/ppermute | solution.py:284
  290.6 6.5 %slice-start.2 = ((s8[5242880]{0:T(1024)(128)(4,1)}), s8[4194304]{0:T(1024)(128)(4,1)S(1)}, s32[]{:S(2)}) async-start(s8[5242880]{0:T(1024)(128)(4,1)} %bitcast.149), calls=%async_computation.2 | async-start | bytes 8388608
  290.6 6.5 %slice-start.3 = ((s8[5242880]{0:T(1024)(128)(4,1)}), s8[1048576]{0:T(1024)(128)(4,1)S(1)}, s32[]{:S(2)}) async-start(s8[5242880]{0:T(1024)(128)(4,1)} %bitcast.149), calls=%async_computation.3 | async-start | bytes 2097152
  290.6 6.5 %copy-start.20 = (bf16[1024,1280]{1,0:T(8,128)(2,1)S(1)}, bf16[1024,1280]{1,0:T(8,128)(2,1)}, u32[]{:S(2)}) copy-start(bf16[1024,1280]{1,0:T(8,128)(2,1)} %get-tuple-element.115) | copy-start | bytes 7864324
  290.6 7.1 %copy-start.21 = (bf16[1024,1280]{1,0:T(8,128)(2,1)S(1)}, bf16[1024,1280]{1,0:T(8,128)(2,1)}, u32[]{:S(2)}) copy-start(bf16[1024,1280]{1,0:T(8,128)(2,1)} %get-tuple-element.117) | copy-start | bytes 7864324
  290.6 22.2 %slice-start.4 = ((s8[5242880]{0:T(1024)(128)(4,1)}), s8[4194304]{0:T(1024)(128)(4,1)S(1)}, s32[]{:S(2)}) async-start(s8[5242880]{0:T(1024)(128)(4,1)} %bitcast.188), calls=%async_computation.4 | async-start | bytes 8388608
  297.7 4.8 copy-start.19
  297.7 15.1 %slice-start.5 = ((s8[5242880]{0:T(1024)(128)(4,1)}), s8[1048576]{0:T(1024)(128)(4,1)S(1)}, s32[]{:S(2)}) async-start(s8[5242880]{0:T(1024)(128)(4,1)} %bitcast.188), calls=%async_computation.5 | async-start | bytes 2097152
  301.9 27.6 %collective-permute-start.16 = (bf16[2,512,1280]{2,1,0:T(8,128)(2,1)S(1)}, bf16[2,512,1280]{2,1,0:T(8,128)(2,1)S(1)}, u32[]{:S(2)}, u32[]{:S(2)}) collective-permute-start(bf16[2,512,1280]{2,1,0:T(8,128)(2,1)S(1)} %bitcast.155), channel_id=1, source_target_pairs={{0,1},{1,0},{2,3},{3,2},{4,5},{5,4},{6,7},{7,6},{8,9},{9,8},{10,11... | collective-permute-start | bytes 7864328 | tf_op jit(solution)/shard_map/ppermute | solution.py:284
  307.8 42.3 %copy-start.18 = (bf16[5120,640]{1,0:T(8,128)(2,1)}, bf16[5120,640]{1,0:T(8,128)(2,1)S(1)}, u32[]{:S(2)}) copy-start(bf16[5120,640]{1,0:T(8,128)(2,1)S(1)} %maximum_select_fusion) | copy-start | bytes 19660804
  311.1 38.5 %collective-permute-start.15 = (bf16[4,2,160,640]{3,2,0,1:T(8,128)(2,1)}, bf16[4,2,160,640]{3,2,0,1:T(8,128)(2,1)}, u32[]{:S(2)}, u32[]{:S(2)}) collective-permute-start(bf16[4,2,160,640]{3,2,0,1:T(8,128)(2,1)} %copy_bitcast_fusion.1), channel_id=1, source_target_pairs={{0,4},{2,6},{4,0},{6,2},{8,12},{10,14},{12,8},{14,10},{16,20},{18,... | collective-permute-start | bytes 4915208 | tf_op jit(solution)/shard_map/ppermute | solution.py:485
  311.8 38.2 %collective-permute-start.14 = (bf16[4,2,160,640]{3,2,0,1:T(8,128)(2,1)}, bf16[4,2,160,640]{3,2,0,1:T(8,128)(2,1)}, u32[]{:S(2)}, u32[]{:S(2)}) collective-permute-start(bf16[4,2,160,640]{3,2,0,1:T(8,128)(2,1)} %copy_bitcast_fusion.2), channel_id=1, source_target_pairs={{0,2},{2,0},{4,6},{6,4},{8,10},{10,8},{12,14},{14,12},{16,18},{18,... | collective-permute-start | bytes 4915208 | tf_op jit(solution)/shard_map/ppermute | solution.py:481
  329.5 10.2 %copy-start.22 = (bf16[1280,2560]{1,0:T(8,128)(2,1)}, bf16[1280,2560]{1,0:T(8,128)(2,1)S(1)}, u32[]{:S(2)}) copy-start(bf16[1280,2560]{1,0:T(8,128)(2,1)S(1)} %convolution_convert_fusion) | copy-start | bytes 19660804
  329.5 6.2 %copy-start.7 = (bf16[2,1024,640]{2,1,0:T(8,128)(2,1)S(1)}, bf16[2,1024,640]{2,1,0:T(8,128)(2,1)}, u32[]{:S(2)}) copy-start(bf16[2,1024,640]{2,1,0:T(8,128)(2,1)} %copy-done.6) | copy-start | bytes 7864324
  339.6 7.5 %collective-permute-start.17 = (bf16[640,640]{1,0:T(8,128)(2,1)S(1)}, bf16[640,640]{1,0:T(8,128)(2,1)S(1)}, u32[]{:S(2)}, u32[]{:S(2)}) collective-permute-start(bf16[640,640]{1,0:T(8,128)(2,1)S(1)} %get-tuple-element.195), channel_id=1, source_target_pairs={{0,1},{1,0},{2,3},{3,2},{4,5},{5,4},{6,7},{7,6},{8,9},{9,8},{10,11... | collective-permute-start | bytes 2457608 | tf_op jit(solution)/shard_map/ppermute | solution.py:284
  355.5 5.6 %copy-start.23 = (bf16[4,2,80,1024]{3,2,0,1:T(8,128)(2,1)S(1)}, bf16[4,2,80,1024]{3,2,0,1:T(8,128)(2,1)}, u32[]{:S(2)}) copy-start(bf16[4,2,80,1024]{3,2,0,1:T(8,128)(2,1)} %copy_bitcast_fusion.3) | copy-start | bytes 3932164
  355.6 42.0 %collective-permute-start.18 = (bf16[4,1,160,640]{3,2,0,1:T(8,128)(2,1)}, bf16[4,1,160,640]{3,2,0,1:T(8,128)(2,1)}, u32[]{:S(2)}, u32[]{:S(2)}) collective-permute-start(bf16[4,1,160,640]{3,2,0,1:T(8,128)(2,1)} %get-tuple-element.187), channel_id=1, source_target_pairs={{0,4},{2,6},{4,0},{6,2},{8,12},{10,14},{12,8},{14,10},{16,20},{18,... | collective-permute-start | bytes 2457608 | tf_op jit(solution)/shard_map/ppermute | solution.py:485
  356.9 40.7 %collective-permute-start.19 = (bf16[4,1,160,640]{3,2,0,1:T(8,128)(2,1)}, bf16[4,1,160,640]{3,2,0,1:T(8,128)(2,1)}, u32[]{:S(2)}, u32[]{:S(2)}) collective-permute-start(bf16[4,1,160,640]{3,2,0,1:T(8,128)(2,1)} %get-tuple-element.186), channel_id=1, source_target_pairs={{0,2},{2,0},{4,6},{6,4},{8,10},{10,8},{12,14},{14,12},{16,18},{18,... | collective-permute-start | bytes 2457608 | tf_op jit(solution)/shard_map/ppermute | solution.py:481
  358.0 6.3 %copy-start.28 = (bf16[1024,1280]{1,0:T(8,128)(2,1)S(1)}, bf16[1024,1280]{1,0:T(8,128)(2,1)}, u32[]{:S(2)}) copy-start(bf16[1024,1280]{1,0:T(8,128)(2,1)} %get-tuple-element.128) | copy-start | bytes 7864324
  361.2 3.2 copy-start.27
  362.7 6.4 %copy-start.10 = (s32[2,1024,128]{2,1,0:T(8,128)S(1)}, s32[2,1024,128]{2,1,0:T(8,128)}, u32[]{:S(2)}) copy-start(s32[2,1024,128]{2,1,0:T(8,128)} %copy-done.9) | copy-start | bytes 3145732
  362.7 6.4 %copy-start.13 = (s32[2,8,1024]{2,1,0:T(8,128)S(1)}, s32[2,8,1024]{2,1,0:T(8,128)}, u32[]{:S(2)}) copy-start(s32[2,8,1024]{2,1,0:T(8,128)} %copy-done.12) | copy-start | bytes 196612
  362.7 74.8 %collective-permute-start.22 = (bf16[4,2,80,1664]{3,2,0,1:T(8,128)(2,1)}, bf16[4,2,80,1664]{3,2,0,1:T(8,128)(2,1)}, u32[]{:S(2)}, u32[]{:S(2)}) collective-permute-start(bf16[4,2,80,1664]{3,2,0,1:T(8,128)(2,1)} %pad_maximum_fusion.2), channel_id=1, source_target_pairs={{0,4},{2,6},{4,0},{6,2},{8,12},{10,14},{12,8},{14,10},{16,20},{18,... | collective-permute-start | bytes 6389768 | tf_op jit(solution)/shard_map/ppermute | solution.py:485
  363.3 74.2 %collective-permute-start.21 = (bf16[4,2,80,1536]{3,2,0,1:T(8,128)(2,1)}, bf16[4,2,80,1536]{3,2,0,1:T(8,128)(2,1)S(1)}, u32[]{:S(2)}, u32[]{:S(2)}) collective-permute-start(bf16[4,2,80,1536]{3,2,0,1:T(8,128)(2,1)} %copy_bitcast_fusion), channel_id=1, source_target_pairs={{0,2},{2,0},{4,6},{6,4},{8,10},{10,8},{12,14},{14,12},{16,18},{18,... | collective-permute-start | bytes 5898248 | tf_op jit(solution)/shard_map/ppermute | solution.py:481
  397.6 45.9 %slice-start = ((s8[5242880]{0:T(1024)(128)(4,1)}), s8[4194304]{0:T(1024)(128)(4,1)S(1)}, s32[]{:S(2)}) async-start(s8[5242880]{0:T(1024)(128)(4,1)} %bitcast.144), calls=%async_computation | async-start | bytes 8388608
  400.8 36.4 %collective-permute-start.20 = (bf16[320,640]{1,0:T(8,128)(2,1)S(1)}, bf16[320,640]{1,0:T(8,128)(2,1)S(1)}, u32[]{:S(2)}, u32[]{:S(2)}) collective-permute-start(bf16[320,640]{1,0:T(8,128)(2,1)S(1)} %fusion.22), channel_id=1, source_target_pairs={{0,8},{2,10},{4,12},{6,14},{8,24},{10,26},{12,28},{14,30},{24,16},... | collective-permute-start | bytes 1228808 | tf_op jit(solution)/shard_map/ppermute | solution.py:493
  407.1 36.4 %slice-start.1 = ((s8[5242880]{0:T(1024)(128)(4,1)}), s8[1048576]{0:T(1024)(128)(4,1)S(1)}, s32[]{:S(2)}) async-start(s8[5242880]{0:T(1024)(128)(4,1)} %bitcast.144), calls=%async_computation.1 | async-start | bytes 2097152
  437.2 12.0 %copy-start.8 = (bf16[2,1024,640]{2,1,0:T(8,128)(2,1)}, bf16[2,1024,640]{2,1,0:T(8,128)(2,1)S(1)}, u32[]{:S(2)}) copy-start(bf16[2,1024,640]{2,1,0:T(8,128)(2,1)S(1)} %get-tuple-element.150) | copy-start | bytes 7864324
  437.4 6.2 %copy-start.30 = (bf16[2,1024,640]{2,1,0:T(8,128)(2,1)S(1)}, bf16[2,1024,640]{2,1,0:T(8,128)(2,1)}, u32[]{:S(2)}) copy-start(bf16[2,1024,640]{2,1,0:T(8,128)(2,1)} %get-tuple-element.151) | copy-start | bytes 7864324
  437.4 17.4 %collective-permute-start.23 = (bf16[320,640]{1,0:T(8,128)(2,1)S(1)}, bf16[320,640]{1,0:T(8,128)(2,1)S(1)}, u32[]{:S(2)}, u32[]{:S(2)}) collective-permute-start(bf16[320,640]{1,0:T(8,128)(2,1)S(1)} %fusion.20), channel_id=1, source_target_pairs={{0,8},{2,10},{4,12},{6,14},{8,24},{10,26},{12,28},{14,30},{24,16},... | collective-permute-start | bytes 1228808 | tf_op jit(solution)/shard_map/ppermute | solution.py:493
  441.5 24.4 %collective-permute-start.26 = (bf16[4,1,80,1664]{3,2,0,1:T(8,128)(2,1)S(1)}, bf16[4,1,80,1664]{3,2,0,1:T(8,128)(2,1)S(1)}, u32[]{:S(2)}, u32[]{:S(2)}) collective-permute-start(bf16[4,1,80,1664]{3,2,0,1:T(8,128)(2,1)S(1)} %add_convert_fusion.2), channel_id=1, source_target_pairs={{0,2},{2,0},{4,6},{6,4},{8,10},{10,8},{12,14},{14,12},{16,18},{18,... | collective-permute-start | bytes 3194888 | tf_op jit(solution)/shard_map/ppermute | solution.py:481
  441.5 24.3 %collective-permute-start.25 = (bf16[4,1,80,1536]{3,2,0,1:T(8,128)(2,1)S(1)}, bf16[4,1,80,1536]{3,2,0,1:T(8,128)(2,1)S(1)}, u32[]{:S(2)}, u32[]{:S(2)}) collective-permute-start(bf16[4,1,80,1536]{3,2,0,1:T(8,128)(2,1)S(1)} %fusion.6), channel_id=1, source_target_pairs={{0,4},{2,6},{4,0},{6,2},{8,12},{10,14},{12,8},{14,10},{16,20},{18,... | collective-permute-start | bytes 2949128 | tf_op jit(solution)/shard_map/ppermute | solution.py:485
  449.2 6.3 %copy-start.31 = (bf16[2,1024,640]{2,1,0:T(8,128)(2,1)S(1)}, bf16[2,1024,640]{2,1,0:T(8,128)(2,1)}, u32[]{:S(2)}) copy-start(bf16[2,1024,640]{2,1,0:T(8,128)(2,1)} %get-tuple-element.152) | copy-start | bytes 7864324
  454.9 10.0 %collective-permute-start.24 = (bf16[320,640]{1,0:T(8,128)(2,1)S(1)}, bf16[320,640]{1,0:T(8,128)(2,1)S(1)}, u32[]{:S(2)}, u32[]{:S(2)}) collective-permute-start(bf16[320,640]{1,0:T(8,128)(2,1)S(1)} %fusion.19), channel_id=1, source_target_pairs={{0,8},{2,10},{4,12},{6,14},{8,24},{10,26},{12,28},{14,30},{24,16},... | collective-permute-start | bytes 1228808 | tf_op jit(solution)/shard_map/ppermute | solution.py:493
  539.4 5.3 copy-start.42
  539.4 6.0 %copy-start.41 = (f32[80,640]{1,0:T(8,128)S(1)}, f32[80,640]{1,0:T(8,128)}, u32[]{:S(2)}) copy-start(f32[80,640]{1,0:T(8,128)} %get-tuple-element.226) | copy-start | bytes 614404
  539.4 6.7 %copy-start.40 = (f32[80,640]{1,0:T(8,128)S(1)}, f32[80,640]{1,0:T(8,128)}, u32[]{:S(2)}) copy-start(f32[80,640]{1,0:T(8,128)} %get-tuple-element.227) | copy-start | bytes 614404
  539.4 7.4 %copy-start.39 = (f32[80,640]{1,0:T(8,128)S(1)}, f32[80,640]{1,0:T(8,128)}, u32[]{:S(2)}) copy-start(f32[80,640]{1,0:T(8,128)} %get-tuple-element.228) | copy-start | bytes 614404
  539.4 8.0 %copy-start.38 = (f32[80,2560]{1,0:T(8,128)S(1)}, f32[80,2560]{1,0:T(8,128)}, u32[]{:S(2)}) copy-start(f32[80,2560]{1,0:T(8,128)} %get-tuple-element.230) | copy-start | bytes 2457604
  (16 other events, 32.4 us)

commit v5 on v4

--- a/solution.py
+++ b/solution.py
@@ -572,14 +572,16 @@
 
 def feed_forward_kernel(*refs):
     normed_ref, cot_ref, *refs = refs
-    up_pieces, down_pieces, refs = refs[:4], refs[4:8], refs[8:]
+    up_pieces, down_pieces, refs = refs[:4], refs[4:10], refs[10:]
     hidden_ref, grad_pre_ref, y_ref, grad_ref, normed_out, y_came, grad_came, *refs = refs
     up_ref, down_ref, normed_buf, y_away, grad_away, *refs = refs
-    up_sems, down_sems, sent_sems, came_sems, normed_sems, away_sends, away_recvs = refs
+    up_sems, down_sems, sent_sems, came_sems, normed_sems, away_sends, away_recvs, *refs = refs
+    corner_sends, corner_recvs = refs
     step = pl.program_id(0)
     row, core = lax.axis_index("rows"), lax.axis_index("seq")
     here_y, here_x = (row // 2) % 2, row % 2
     twin = (row, 1 - core)
+    over_x, over_y = row + 1 - 2 * here_x, row + 2 - 4 * here_y
     span = normed_ref.shape[0]
     tiles = span // FFN_TILE
 
@@ -617,35 +619,73 @@
                         copies.append(pltpu.make_async_copy(piece, target, up_sems.at[len(copies)]))
         return copies
 
+    def down_rows(part, lower, row_y, row_x, depth):
+        first = (((lower * 2 + row_y) * 2 + row_x) * 2 + part) * depth
+        return pl.ds(pl.multiple_of(first, 16), depth)
+
     def down_copies():
         kept, given = [], []
         for part in range(2):
-            for across in range(2):
-                for along in range(2):
-                    far_y, far_x = (along, across) if part == 0 else (across, along)
-                    row_y = 1 - here_y if far_y else here_y
-                    row_x = 1 - here_x if far_x else here_x
-                    for lower in range(2):
-                        pieces = down_pieces[part * 2 + across]
-                        depth, wide = pieces.shape[2:]
-                        first = (((lower * 2 + row_y) * 2 + row_x) * 2 + part) * depth
-                        rows = pl.ds(pl.multiple_of(first, 16), depth)
-                        target = down_ref.at[rows, pl.ds(pl.multiple_of(core * wide, 128), wide)]
-                        number = len(kept)
-                        kept.append(
-                            pltpu.make_async_copy(
-                                pieces.at[along, 2 * core + lower], target, down_sems.at[number]
-                            )
+            for which, (far_y, far_x) in enumerate(
+                ((0, 0), (1, 0), (0, 1)) if part == 0 else ((0, 0), (0, 1), (1, 0))
+            ):
+                row_y = 1 - here_y if far_y else here_y
+                row_x = 1 - here_x if far_x else here_x
+                for lower in range(2):
+                    pieces = down_pieces[part * 3 + which]
+                    depth, wide = pieces.shape[1:]
+                    rows = down_rows(part, lower, row_y, row_x, depth)
+                    target = down_ref.at[rows, pl.ds(pl.multiple_of(core * wide, 128), wide)]
+                    number = len(kept)
+                    kept.append(
+                        pltpu.make_async_copy(
+                            pieces.at[2 * core + lower], target, down_sems.at[number]
                         )
-                        given.append(
-                            remote(
-                                pieces.at[along, 2 * (1 - core) + lower],
-                                target,
-                                sent_sems.at[number],
-                                came_sems.at[number],
-                            )
+                    )
+                    given.append(
+                        remote(
+                            pieces.at[2 * (1 - core) + lower],
+                            target,
+                            sent_sems.at[number],
+                            came_sems.at[number],
                         )
+                    )
         return kept, given
+
+    def corner_copies():
+        sends, arrivals = [], []
+        for part in range(2):
+            pieces = down_pieces[part * 3 + 1]
+            depth, wide = pieces.shape[1:]
+            row_y, row_x = (1 - here_y, here_x) if part == 0 else (here_y, 1 - here_x)
+            for other in range(2):
+                for lower in range(2):
+                    number = len(sends)
+                    rows = down_rows(part, lower, row_y, row_x, depth)
+                    target = down_ref.at[rows, pl.ds(pl.multiple_of(core * wide, 128), wide)]
+                    sends.append(
+                        pltpu.make_async_remote_copy(
+                            src_ref=pieces.at[2 * other + lower],
+                            dst_ref=target,
+                            send_sem=corner_sends.at[number],
+                            recv_sem=corner_recvs.at[part, core, lower],
+                            device_id=(over_x if part == 0 else over_y, other),
+                            device_id_type=pl.DeviceIdType.MESH,
+                        )
+                    )
+                    rows = down_rows(part, lower, 1 - here_y, 1 - here_x, depth)
+                    target = down_ref.at[rows, pl.ds(other * wide, wide)]
+                    arrivals.append(
+                        pltpu.make_async_remote_copy(
+                            src_ref=target,
+                            dst_ref=target,
+                            send_sem=corner_sends.at[number],
+                            recv_sem=corner_recvs.at[part, other, lower],
+                            device_id=(over_x if part == 0 else over_y, other),
+                            device_id_type=pl.DeviceIdType.MESH,
+                        )
+                    )
+        return sends, arrivals
 
     def away_copies(tile):
         rows = pl.ds(pl.multiple_of(tile * FFN_TILE, FFN_TILE), FFN_TILE)
@@ -657,19 +697,20 @@
     @pl.when(step == 0)
     def _():
         barrier = pltpu.get_barrier_semaphore()
-        pl.semaphore_signal(barrier, inc=1, device_id=twin, device_id_type=pl.DeviceIdType.MESH)
+        for target in (twin, (over_x, 0), (over_x, 1), (over_y, 0), (over_y, 1)):
+            pl.semaphore_signal(
+                barrier, inc=1, device_id=target, device_id_type=pl.DeviceIdType.MESH
+            )
         kept, given = down_copies()
+        corners, arrivals = corner_copies()
         own, others = normed_copies()
         ups = up_copies()
-        for copy in [own] + ups + kept:
+        pl.semaphore_wait(barrier, 5)
+        for copy in corners + [own] + ups + kept + given + [others]:
             copy.start()
-        pl.semaphore_wait(barrier, 1)
-        for copy in given:
-            copy.start()
-        others.start()
         for copy in [own] + ups + kept:
             copy.wait()
-        for copy in given:
+        for copy in given + arrivals:
             copy.wait_recv()
 
     @pl.when(step == tiles)
@@ -711,7 +752,7 @@
     def _():
         store = pltpu.make_async_copy(normed_buf, normed_out, normed_sems.at[0])
         store.start()
-        for copy in (*down_copies()[1], normed_copies()[1]):
+        for copy in (*down_copies()[1], *corner_copies()[0], normed_copies()[1]):
             copy.wait_send()
         for tile in range(tiles):
             for copy in away_copies(tile):
@@ -734,7 +775,7 @@
     return pl.pallas_call(
         feed_forward_kernel,
         grid=(2 * tiles,),
-        in_specs=[anywhere, tile] + [anywhere] * 8,
+        in_specs=[anywhere, tile] + [anywhere] * 10,
         out_specs=[wide_tile, wide_tile, own_tile, own_tile] + [anywhere] * 3,
         out_shape=[
             wide_shape,
@@ -758,6 +799,8 @@
             sems((3,)),
             sems((2, tiles)),
             sems((2, tiles)),
+            sems((8,)),
+            sems((2, 2, 2)),
         ],
         compiler_params=pltpu.CompilerParams(
             collective_id=2, has_side_effects=True, vmem_limit_bytes=60 * 1024 * 1024
@@ -767,7 +810,100 @@
             bytes_accessed=4 * width * units + 8 * tokens * (2 * width + units),
             transcendentals=4 * tokens * units,
         ),
-    )(normed, cot_all, *up_parts[0], *up_parts[1], *down_parts[0], *down_parts[1])
+    )(normed, cot_all, *up_parts[0], *up_parts[1], *down_parts)
+
+
+RESIDUAL_TILE = 128
+
+
+def residual_kernel(*refs):
+    residual_ref, cot_ref, y_ref, y_came, grad_ref, grad_came, gain_ref, *refs = refs
+    layer_ref, out_ref, gain_out, both_out, buf, local_sems, send_sems, recv_sems = refs
+    step = pl.program_id(0)
+    steps = buf.shape[0]
+    row, core = lax.axis_index("rows"), lax.axis_index("seq")
+    twin = (row, 1 - core)
+    span = both_out.shape[1] // 2
+
+    def copies(tile):
+        each = span // RESIDUAL_TILE
+        first = core * span + (tile % each) * RESIDUAL_TILE
+        rows = pl.ds(pl.multiple_of(first, RESIDUAL_TILE), RESIDUAL_TILE)
+        target = both_out.at[tile // each, rows, :]
+        return (
+            pltpu.make_async_copy(buf.at[tile], target, local_sems.at[tile]),
+            pltpu.make_async_remote_copy(
+                src_ref=buf.at[tile],
+                dst_ref=target,
+                send_sem=send_sems.at[tile],
+                recv_sem=recv_sems.at[tile],
+                device_id=twin,
+                device_id_type=pl.DeviceIdType.MESH,
+            ),
+        )
+
+    @pl.when(step == 0)
+    def _():
+        barrier = pltpu.get_barrier_semaphore()
+        pl.semaphore_signal(barrier, inc=1, device_id=twin, device_id_type=pl.DeviceIdType.MESH)
+        pl.semaphore_wait(barrier, 1)
+        gain_out[...] = jnp.zeros_like(gain_out)
+
+    residual = residual_ref[...]
+    layer_ref[...] = plus(residual, y_ref[...], y_came[...])
+    unit, scale = norm_stats(residual)
+    grad = plus_wide(grad_ref[...], grad_came[...])
+    grad_residual = cot_ref[...].astype(jnp.float32) + norm_back_rows(
+        unit, scale, gain_ref[...], grad
+    )
+    out_ref[...] = grad_residual
+    gain_out[0:1, :] += jnp.sum(grad * unit, 0, keepdims=True)
+    for tile in range(steps):
+
+        @pl.when(step == tile)
+        def _(tile=tile):
+            buf[tile] = grad_residual.astype(jnp.bfloat16)
+            for copy in copies(tile):
+                copy.start()
+
+    @pl.when(step == steps - 1)
+    def _():
+        for tile in range(steps):
+            for copy in copies(tile):
+                copy.wait()
+
+
+def residual_call(rows, residual, cot, y_own, y_came, grad_own, grad_came, gain):
+    flat, width = residual.shape
+    steps = flat // RESIDUAL_TILE
+    tile = pl.BlockSpec((RESIDUAL_TILE, width), lambda step: (step, 0))
+    sems = pltpu.SemaphoreType.DMA((steps,))
+    return pl.pallas_call(
+        residual_kernel,
+        grid=(steps,),
+        in_specs=[tile] * 6 + [pl.BlockSpec((1, width), lambda step: (0, 0))],
+        out_specs=[
+            tile,
+            tile,
+            pl.BlockSpec((8, width), lambda step: (0, 0)),
+            pl.BlockSpec(memory_space=pl.ANY),
+        ],
+        out_shape=[
+            jax.ShapeDtypeStruct((flat, width), jnp.bfloat16),
+            jax.ShapeDtypeStruct((flat, width), jnp.float32),
+            jax.ShapeDtypeStruct((8, width), jnp.float32),
+            jax.ShapeDtypeStruct((rows, 2 * flat // rows, width), jnp.bfloat16),
+        ],
+        scratch_shapes=[
+            pltpu.VMEM((steps, RESIDUAL_TILE, width), jnp.bfloat16),
+            sems,
+            sems,
+            sems,
+        ],
+        compiler_params=pltpu.CompilerParams(
+            collective_id=3, has_side_effects=True, vmem_limit_bytes=32 * 1024 * 1024
+        ),
+    )(residual, cot, y_own, y_came, grad_own, grad_came, gain.reshape(1, width))
 
 
 def following(zed):
@@ -907,13 +1043,14 @@
         ring.wait_recv()
         if step < 3:
             ring = around(step)
-        else:
+        if step == 2:
             up_ring = around_up(0)
         arrivals += corner(step - 1, crossing)
         crossing = across(step)
         arrivals += crossing[2:]
-    up_ring.wait_recv()
-    up_ring = around_up(1)
+        if step == 3:
+            up_ring.wait_recv()
+            up_ring = around_up(1)
     arrivals += corner(3, crossing)
     up_ring.wait_recv()
     arrivals.append(around_up(2))
@@ -1322,15 +1459,17 @@
     def pick(self, which, start_y, start_x, count_y=1, count_x=1):
         picked = []
         for whole, row, depth, column, wide in self.parts[which]:
-            blocks = whole.reshape(Z_SIZE, 2, 2, whole.shape[0] // 16, whole.shape[1])
+            planes = Z_SIZE // len(self.parts[which]) if self.by_rows else Z_SIZE
+            blocks = whole.reshape(planes, 2, 2, whole.shape[0] // planes // 4, whole.shape[1])
             picked.append(
                 lax.dynamic_slice(
                     blocks,
                     (0, start_y, start_x, row, column),
-                    (Z_SIZE, count_y, count_x, depth, wide),
-                ).reshape(Z_SIZE, count_y * count_x, depth, wide)
+                    (planes, count_y, count_x, depth, wide),
+                ).reshape(planes, count_y * count_x, depth, wide)
             )
-        return picked[0] if len(picked) == 1 else jnp.concatenate(picked, 3)
+        axis = 0 if self.by_rows else 3
+        return picked[0] if len(picked) == 1 else jnp.concatenate(picked, axis)
 
     def prepare(self, *after):
         _, here_y, here_x = chip_place()
@@ -1369,6 +1508,8 @@
     def block(self, back):
         target = (ring_place() - back) % Z_SIZE
         zed = jnp.where(target == 2, 3, jnp.where(target == 3, 2, target))
+        if self.by_rows:
+            zed = zed ^ (2 * lax.axis_index("seq"))
         return lax.dynamic_index_in_dim(self.sums, zed, 0, keepdims=False)
 
     def step(self, number):
@@ -1441,7 +1582,8 @@
         attend_kernel, 0, rows, windows, marks, operands, [half_wide], [], half_wide
     )
     mixed, down_steps[3], up_parts = tie((mixed, down_steps[3], up_parts))
-    down_parts = gather_first(*halves_z(natural_z(down_steps)))
+    down_first, down_second = halves_z(natural_z(down_steps))
+    down_came = swap_y(down_first), swap_x(down_second), swap_x(down_first), swap_y(down_second)
     w_o = jnp.where(
         first,
         jnp.concatenate([w_o_half, w_o_other], 1),
@@ -1456,12 +1598,14 @@
         jnp.concatenate([mixed_mine, mixed_other], 2),
         jnp.concatenate([mixed_other, mixed_mine], 2),
     ).reshape(flat, width)
-    mixed_own, down_parts = tie((mixed_own, down_parts))
-    mixed_own = tie(mixed_own, down_parts)
-    down_parts = gather_second(*down_parts)
+    mixed_own, w_o, w_o_rows = tie((mixed_own, w_o, w_o_rows))
     residual = tokens_own + dot_low(mixed_own, w_o)
-    unit_two, scale_two = norm_stats(residual)
+    unit_two, _ = norm_stats(residual)
     normed_two = (unit_two * gain_ffn).astype(jnp.bfloat16)
+    normed_two, down_came = tie((normed_two, down_came))
+    first_y, second_x, first_x, second_y = down_came
+    down_parts = (down_first, first_y, first_x, down_second, second_x, second_y)
+    cot_other = tie(cot_other, mixed_own)
     cot_all = jnp.concatenate([cot_own, cot_other.reshape(flat, width)], 0)
     hidden_low, grad_pre, y_own, grad_two_own, normed_two_all, y_came, grad_two_came = feed_forward(
         normed_two, cot_all, up_parts, down_parts
@@ -1469,35 +1613,25 @@
 
     down_half = outer_low(hidden_low, cot_all)
     down_away = swap_cores(own_half(down_half, 1, 1 - core))
-    grad_normed_two = plus_wide(grad_two_own, tie(grad_two_came, down_half))
-    grad_residual = cot_own.astype(jnp.float32) + norm_back_rows(
-        unit_two, scale_two, gain_ffn, grad_normed_two
-    )
-    ffn_gain_part = jnp.sum(grad_normed_two * unit_two, 0)
-    grad_attn = grad_residual.astype(jnp.bfloat16).reshape(rows, span, width)
-    grad_attn_other = swap_cores(grad_attn)
-    down_away = tie(down_away, grad_attn, ffn_gain_part)
-    down_kept = own_half(down_half, 1, core)
-    down_whole = jnp.where(
-        first,
-        jnp.concatenate([down_kept, down_away], 0),
-        jnp.concatenate([down_away, down_kept], 0),
-    )
+    layer_out, grad_residual, ffn_gain_rows, grad_attn_all = residual_call(
+        rows, residual, cot_own, y_own, y_came, grad_two_own, tie(grad_two_came, down_half), gain_ffn
+    )
+    ffn_gain_part = ffn_gain_rows[0]
+    grad_attn_all = grad_attn_all.reshape(2 * flat, width)
+    down_away = tie(down_away, grad_residual)
     depth, wide = w_down.shape
+    down_halves = ((down_half, core * wide), (down_away, 0))
     down_sum = Scatter(
-        [(down_whole, 0, depth // 2, 0, wide)],
-        [(down_whole, depth // 2, depth // 2, 0, wide)],
+        *(
+            [(whole, row, depth // 2, column, wide) for whole, column in down_halves]
+            for row in (0, depth // 2)
+        ),
         True,
     )
     down_sum.prepare()
     down_sum.spread()
     up_whole = outer_low(normed_two_all, tie(grad_pre, *down_sum.away))
-    grad_attn_other = tie(grad_attn_other, up_whole)
-    grad_attn_all = jnp.where(
-        first,
-        jnp.concatenate([grad_attn, grad_attn_other], 1),
-        jnp.concatenate([grad_attn_other, grad_attn], 1),
-    ).reshape(2 * flat, width)
+    grad_attn_all = tie(grad_attn_all, up_whole)
     out_half = outer_low(mixed.reshape(2 * flat, -1), grad_attn_all)
     out_away = swap_cores(own_half(out_half, 1, 1 - core))
     grad_mixed = split(times_transposed(grad_attn_all, w_o_rows).astype(jnp.bfloat16), width // 2)
@@ -1516,11 +1650,9 @@
     )
     down_sum.hold(("came",), grad_mixed)
     down_sum.turn()
-    y_own, y_came = tie((y_own, y_came), *down_sum.turning)
-    layer_out = (residual + plus_wide(y_own, y_came)).astype(jnp.bfloat16)
     up_sum.prepare(*down_sum.turning)
     up_sum.spread()
-    grad_mixed = tie(grad_mixed, layer_out, *up_sum.away, *down_sum.turning)
+    grad_mixed = tie(grad_mixed, *up_sum.away, *down_sum.turning)
     scratch = [pltpu.VMEM((2 * span, LANES), jnp.float32)] * 2
 
     def attend_back(row, grad_rows, begun=()):

time: 553 us -> 548 us (level)
  other arithmetic: 64.3 us -> 31.2 us
  Pallas kernels: 280 us -> 311 us
  waiting for transfers between devices: 53.1 us -> 35.4 us
  local copies, waits for them, and re-layouts: 42.7 us -> 54.8 us
    pallas_call x1, Pallas kernels: 72 us -> 86.8 us  [feed_forward(): pl.pallas_call(feed_forward_kernel, grid=(2 * tiles,), in_specs=[anywhere...]
    ppermute x8, waiting for transfers between devices: 44.2 us -> 30 us  [swap_x(): return lax.ppermute(values, 'rows', [(row, row ^ 1) for row in range(16)])]
    select_n x2 -> x0, other arithmetic: 11.4 us -> none  [the longest x1 6.19 us: body_pair(): jnp.where(first, jnp.concatenate([grad_attn, grad_attn_other], 1), jnp.co...]
    pallas_call x0 -> x1, Pallas kernels: none -> 10.5 us  [residual_call(): pl.pallas_call(residual_kernel, grid=(steps,), in_specs=[tile] * 6 + [pl....]
    unnamed x112 -> x135, local copies, waits for them, and re-layouts: 21.1 us -> 31.2 us
    convert_element_type x2 -> x0, other arithmetic: 8.94 us -> none  [the longest x1 4.76 us: body_pair(): layer_out = (residual + plus_wide(y_own, y_came)).astype(jnp.bfloat16)]
    reduce_sum x1 -> x0, other arithmetic: 6.47 us -> none  [body_pair(): ffn_gain_part = jnp.sum(grad_normed_two * unit_two, 0)]
  transfers between devices with their start and end apart: 27 -> 26, of which waited for: 8 -> 7; matrix products, arithmetic and copies ran while one was open for 23% -> 18% of each run, Pallas kernels for 15% -> 17%
where the time goes in v5:
time: 548 us; the launch traced here: 543 us
  Pallas kernels  311 us (57%)
  matrix products  83.2 us (15%)
  local copies, waits for them, and re-layouts  54.8 us (10%)
  waiting for transfers between devices  35.4 us (6%)
  other arithmetic  31.2 us (6%)
  starting transfers between devices  25.1 us (5%)
    pallas_call x1, Pallas kernels, feed_forward(): pl.pallas_call(feed_forward_kernel, grid=(2 * tiles,), in_specs=[anywhere...  86.8 us
    pallas_call x3, Pallas kernels, attention_call(): pl.pallas_call(functools.partial(kernel, row, len(begun)), grid_spec=pltp...  83.8 us
    pallas_call x1, Pallas kernels, tail_call(): pl.pallas_call(tail_kernel, in_specs=[anywhere] * 4 + [here] * 3 + [anywh...  68.7 us
    pallas_call x1, Pallas kernels, head_call(): pl.pallas_call(head_kernel, in_specs=[anywhere, pl.BlockSpec(memory_space...  61.3 us
    dot_general x6, matrix products, outer_low(): jnp.einsum('tc,te->ce', left_side, right_side, preferred_element_type=jnp...  55.9 us
    unnamed x135, local copies, waits for them, and re-layouts  31.2 us
    ppermute x8, waiting for transfers between devices, swap_x(): return lax.ppermute(values, 'rows', [(row, row ^ 1) for row in range(16)])  30 us
    dot_general x3, matrix products, dot_low(): return jnp.dot(left_side, right_side, preferred_element_type=jnp.float32)  19.1 us
  transfers between devices with their start and end apart: 26, of which 7 were waited for; matrix products, arithmetic and copies ran while one was open for 18% of the time, Pallas kernels for 17%

profile of v5, /device:TPU:0, one launch (start us, length us, event | category | flops | bytes accessed | tf_op | source)
XLA Modules:
  0.0 542.8 jit_solution(10018497069062284197)
XLA Ops:
  2.4 1.7 copy-done
  4.2 1.7 copy-done.2
  6.9 61.3 %shard_map.186 = (bf16[2,1024,1280]{2,1,0:T(8,128)(2,1)S(1)}, bf16[2,512,1280]{2,1,0:T(8,128)(2,1)S(1)}, bf16[1280,2560]{1,0:T(8,128)(2,1)S(1)}, bf16[4,80,2560]{2,1,0:T(8,128)(2,1)S(1)}) custom-call(bf16[2,512,1280]{2,1,0:T(8,128)(2,1)S(1)} %copy-done.2, f32[1,1280]{1,0:T(1,128)S(1)} %reshape.421.gain_ref, bf16[2,512,1280]{2,1,0:T(8,128)(2,1)S(1)} %copy-done, ...), custom_call_target="tpu_custom_call" | custom-call | tf_op jit(solution)/shard_map/pallas_call | solution.py:1069
  68.3 1.4 copy-done.6
  69.7 1.5 slice_bitcast_fusion
  71.3 1.8 collective-permute-start.3
  75.4 8.6 %convolution_convert_fusion.2 = bf16[2048,1280]{1,0:T(8,128)(2,1)} fusion(bf16[2048,1280]{1,0:T(8,128)(2,1)S(1)} %bitcast.135, bf16[1280,2560]{1,0:T(8,128)(2,1)S(1)} %get-tuple-element.97.weights_ref), kind=kOutput, calls=%fused_computation.2 | convolution fusion | flops 6713507840 | bytes 13762560 | tf_op jit(solution)/shard_map/dot_general | solution.py:1445
  84.4 5.0 collective-permute-done.3
  89.4 1.4 pad_maximum_fusion.5.refs_4_
  90.9 2.2 pad_maximum_fusion.4.refs_2_
  93.1 1.6 collective-permute-start.6
  95.9 6.9 %convolution_convert_fusion.8 = bf16[2048,640]{1,0:T(8,128)(2,1)} fusion(bf16[2048,1280]{1,0:T(8,128)(2,1)S(1)} %bitcast.136, bf16[1280,2560]{1,0:T(8,128)(2,1)} %copy-done.4), kind=kOutput, calls=%fused_computation.14 | convolution fusion | flops 3356753920 | bytes 9502720 | tf_op jit(solution)/shard_map/dot_general | solution.py:1445
  102.8 3.2 collective-permute-done.4
  106.6 22.2 %shard_map.187 = bf16[2,1024,640]{2,1,0:T(8,128)(2,1)S(1)} custom-call(s32[2,8]{1,0:T(2,128)S(1)} %get-tuple-element.191.start_ref, s32[2,8]{1,0:T(2,128)S(1)} %get-tuple-element.190.count_ref, s32[2,1024,128]{2,1,0:T(8,128)S(1)} %broadcast_in_dim.4.column_ref, s32[2,8,1024]{2,1,0:T(8,128)S(1)} %lt.204.line_ref, bf16[2,1024,1280]{2,1,0:T(8,128)(2,1)} %bitcast.165, ...), custom_call_target="tpu_custom_call" | custom-call | flops 16106127360 | bytes 10485760 | tf_op jit(solution)/shard_map/pallas_call | solution.py:433
  130.7 3.0 maximum_select_fusion
  133.7 1.3 constant_dynamic-slice_fusion.14
  135.0 1.4 pad_maximum_fusion.6
  138.3 1.9 collective-permute-start.11
  142.9 3.7 fusion.22
  147.2 1.6 copy-done.23
  148.8 2.2 multiply_convert_fusion.refs_0_
  151.0 7.1 %collective-permute-done.10.refs_10_ = bf16[4,160,640]{2,1,0:T(8,128)(2,1)S(1)} collective-permute-done((bf16[4,160,640]{2,1,0:T(8,128)(2,1)S(1)}, bf16[4,160,640]{2,1,0:T(8,128)(2,1)S(1)}, u32[]{:S(2)}, u32[]{:S(2)}) %collective-permute-start.10) | collective-permute-done | bytes 819232 | tf_op jit(solution)/shard_map/ppermute | solution.py:481
  158.1 17.2 %collective-permute-done.11.refs_8_ = bf16[4,160,640]{2,1,0:T(8,128)(2,1)S(1)} collective-permute-done((bf16[4,160,640]{2,1,0:T(8,128)(2,1)S(1)}, bf16[4,160,640]{2,1,0:T(8,128)(2,1)S(1)}, u32[]{:S(2)}, u32[]{:S(2)}) %collective-permute-start.11) | collective-permute-done | bytes 819232 | tf_op jit(solution)/shard_map/ppermute | solution.py:481
  176.9 2.6 pad_maximum_fusion.refs_1_
  179.6 86.8 %shard_map.188 = (bf16[2048,2560]{1,0:T(8,128)(2,1)}, bf16[2048,2560]{1,0:T(8,128)(2,1)}, bf16[1024,1280]{1,0:T(8,128)(2,1)}, bf16[1024,1280]{1,0:T(8,128)(2,1)}...) custom-call(bf16[1024,1280]{1,0:T(8,128)(2,1)} %multiply_convert_fusion.refs_0_, ...), custom_call_target="tpu_custom_call" | custom-call | flops 53687091200 | bytes 55050240 | tf_op jit(solution)/shard_map/pallas_call | solution.py:775
  266.3 17.1 %convolution_convert_fusion.1 = bf16[2560,1280]{1,0:T(8,128)(2,1)S(1)} fusion(bf16[2048,2560]{1,0:T(8,128)(2,1)} %get-tuple-element.128, bf16[1024,1280]{1,0:T(8,128)(2,1)} %bitcast.129, bf16[1024,1280]{1,0:T(8,128)(2,1)S(1)} %bitcast.125), kind=kOutput, calls=%fused_computation.1 | convolution fusion | flops 13435535360 | bytes 22282240 | tf_op jit(solution)/shard_map/tc,te->ce/dot_general | solution.py:1449
  283.5 2.1 constant_dynamic-slice_fusion.8
  285.6 1.6 copy-done.24
  287.8 1.7 copy-done.12
  289.6 1.7 copy-done.13
  291.3 1.7 copy-done.14
  293.0 1.7 copy-done.15
  294.8 10.5 %shard_map.189 = (bf16[1024,1280]{1,0:T(8,128)(2,1)S(1)}, f32[1024,1280]{1,0:T(8,128)S(1)}, f32[8,1280]{1,0:T(8,128)S(1)}, bf16[2,1024,1280]{2,1,0:T(8,128)(2,1)}) custom-call(f32[1024,1280]{1,0:T(8,128)} %copy-done.23, bf16[1024,1280]{1,0:T(8,128)(2,1)S(1)} %bitcast.126, bf16[1024,1280]{1,0:T(8,128)(2,1)S(1)} %copy-done.12, ...), custom_call_target="tpu_custom_call" | custom-call | tf_op jit(solution)/shard_map/pallas_call | solution.py:881
  305.3 1.4 copy-done.8
  307.4 1.5 dynamic-slice_bitcast_fusion.5
  308.9 1.3 copy_bitcast_fusion.3
  310.2 1.3 copy_bitcast_fusion.5
  312.8 1.3 collective-permute-start.14
  314.1 18.5 %convolution_convert_fusion = bf16[1280,2560]{1,0:T(8,128)(2,1)S(1)} fusion(bf16[2048,1280]{1,0:T(8,128)(2,1)} %get-tuple-element.132, bf16[2048,2560]{1,0:T(8,128)(2,1)} %get-tuple-element.138), kind=kOutput, calls=%fused_computation | convolution fusion | flops 13425049600 | bytes 22282240 | tf_op jit(solution)/shard_map/tc,te->ce/dot_general | solution.py:1449
  332.7 3.6 convolution_convert_fusion.6
  337.6 2.5 dynamic-slice_bitcast_fusion.4
  340.1 8.2 %convolution_convert_fusion.7 = bf16[2048,640]{1,0:T(8,128)(2,1)} fusion(bf16[2048,1280]{1,0:T(8,128)(2,1)} %bitcast.161, bf16[640,1280]{1,0:T(8,128)(2,1)S(1)} %copy-done.37), kind=kOutput, calls=%fused_computation.13 | convolution fusion | flops 3356753920 | bytes 9502720 | tf_op jit(solution)/shard_map/te,de->td/dot_general | solution.py:30
  350.7 1.3 add_convert_fusion.4
  353.2 2.6 copy_bitcast_fusion.1
  358.0 3.0 copy_bitcast_fusion
  361.0 1.5 pad_maximum_fusion.2
  364.6 31.6 %shard_map.190 = (bf16[2,1024,640]{2,1,0:T(8,128)(2,1)S(1)}, bf16[2,1024,640]{2,1,0:T(8,128)(2,1)}, bf16[2,1024,640]{2,1,0:T(8,128)(2,1)}) custom-call(s32[2,4]{1,0:T(2,128)S(1)} %get-tuple-element.189.start_ref, s32[2,4]{1,0:T(2,128)S(1)} %get-tuple-element.188.count_ref, s32[2,1024,128]{2,1,0:T(8,128)S(1)} %copy-done.18, s32[2,8,1024]{2,1,0:T(8,128)S(1)} %lt.204.line_ref, ...), custom_call_target="tpu_custom_call" | custom-call | flops 10737418240 | bytes 9175040 | tf_op jit(solution)/shard_map/pallas_call | solution.py:433
  396.2 1.6 fusion.8
  398.0 1.6 fusion.7
  400.3 30.1 %shard_map.191 = (bf16[2,1024,640]{2,1,0:T(8,128)(2,1)S(1)}, bf16[2,1024,640]{2,1,0:T(8,128)(2,1)}, bf16[2,1024,640]{2,1,0:T(8,128)(2,1)}) custom-call(s32[2,4]{1,0:T(2,128)S(1)} %get-tuple-element.189.start_ref, s32[2,4]{1,0:T(2,128)S(1)} %get-tuple-element.188.count_ref, ...), custom_call_target="tpu_custom_call", output_to_operand_aliasing={{0}: (8, {}), {1}: (9, {}), {2}: (10, {})} | custom-call | flops 10737418240 | bytes 9175040 | tf_op jit(solution)/shard_map/pallas_call | solution.py:433
  431.6 2.0 fusion.3
  433.9 1.4 collective-permute-start.25
  435.4 5.7 %convolution_convert_fusion.4.key_ref = bf16[1280,640]{1,0:T(8,128)(2,1)} fusion(bf16[2048,1280]{1,0:T(8,128)(2,1)S(1)} %bitcast.139, bf16[2048,640]{1,0:T(8,128)(2,1)S(1)} %bitcast.155), kind=kOutput, calls=%fused_computation.10 | convolution fusion | flops 3356262400 | bytes 9502720 | tf_op jit(solution)/shard_map/tc,te->ce/dot_general | solution.py:1449
  441.1 5.4 %convolution_convert_fusion.5.query_ref = bf16[1280,640]{1,0:T(8,128)(2,1)} fusion(bf16[2048,1280]{1,0:T(8,128)(2,1)S(1)} %bitcast.140, bf16[2048,640]{1,0:T(8,128)(2,1)S(1)} %bitcast.133), kind=kOutput, calls=%fused_computation.11 | convolution fusion | flops 3356262400 | bytes 9502720 | tf_op jit(solution)/shard_map/tc,te->ce/dot_general | solution.py:1449
  446.7 4.5 collective-permute-start.23
  451.2 5.4 %convolution_convert_fusion.3.value_ref = bf16[1280,640]{1,0:T(8,128)(2,1)} fusion(bf16[2048,1280]{1,0:T(8,128)(2,1)S(1)} %bitcast.141, bf16[2048,640]{1,0:T(8,128)(2,1)S(1)} %bitcast.157), kind=kOutput, calls=%fused_computation.9 | convolution fusion | flops 3356262400 | bytes 9502720 | tf_op jit(solution)/shard_map/tc,te->ce/dot_general | solution.py:1449
  456.6 1.4 collective-permute-done.23
  459.0 1.9 fusion.6
  461.4 1.4 pad_maximum_fusion.3.hidden_ref
  462.8 68.7 %shard_map.192 = (f32[1024,1280]{1,0:T(8,128)}, f32[80,640]{1,0:T(8,128)}, f32[80,640]{1,0:T(8,128)}, f32[80,640]{1,0:T(8,128)}, f32[8,1280]{1,0:T(8,128)}, /*index=5*/f32[80,2560]{1,0:T(8,128)}, f32[80,640]{1,0:T(8,128)}) custom-call(bf16[2048,640]{1,0:T(8,128)(2,1)} %bitcast.134, bf16[2048,640]{1,0:T(8,128)(2,1)} %bitcast.154, ...), custom_call_target="tpu_custom_call" | custom-call | tf_op jit(solution)/shard_map/pallas_call | solution.py:1383
  531.5 1.5 slice_reduce_fusion
  533.0 1.5 copy.75
  534.5 1.9 copy-done.27
  536.5 2.4 copy.76
  (202 shorter events, 35.2 us)
Async XLA Ops:
  1.3 66.9 %copy-start.20 = (f32[1,1280]{1,0:T(1,128)}, f32[1,1280]{1,0:T(1,128)S(1)}, u32[]{:S(2)}) copy-start(f32[1,1280]{1,0:T(1,128)S(1)} %reshape.421.gain_ref) | copy-start | bytes 15364
  69.7 5.6 %copy-start.4 = (bf16[1280,2560]{1,0:T(8,128)(2,1)}, bf16[1280,2560]{1,0:T(8,128)(2,1)S(1)}, u32[]{:S(2)}) copy-start(bf16[1280,2560]{1,0:T(8,128)(2,1)S(1)} %get-tuple-element.97.weights_ref) | copy-start | bytes 19660804
  69.7 5.6 %copy-start.21 = (bf16[2,1024,1280]{2,1,0:T(8,128)(2,1)}, bf16[2,1024,1280]{2,1,0:T(8,128)(2,1)S(1)}, u32[]{:S(2)}) copy-start(bf16[2,1024,1280]{2,1,0:T(8,128)(2,1)S(1)} %get-tuple-element.96) | copy-start | bytes 15728644
  71.3 18.1 %collective-permute-start.3 = (bf16[4,80,1280]{2,1,0:T(8,128)(2,1)}, bf16[4,80,1280]{2,1,0:T(8,128)(2,1)}, u32[]{:S(2)}, u32[]{:S(2)}) collective-permute-start(bf16[4,80,1280]{2,1,0:T(8,128)(2,1)} %get-tuple-element.216), channel_id=1, source_target_pairs={{0,2},{2,0},{4,6},{6,4},{8,10},{10,8},{12,14},{14,12},{16,18},{18,... | collective-permute-start | bytes 2457608 | tf_op jit(solution)/shard_map/ppermute | solution.py:481
  73.1 17.8 %collective-permute-start.2 = (bf16[4,80,1280]{2,1,0:T(8,128)(2,1)}, bf16[4,80,1280]{2,1,0:T(8,128)(2,1)}, u32[]{:S(2)}, u32[]{:S(2)}) collective-permute-start(bf16[4,80,1280]{2,1,0:T(8,128)(2,1)} %get-tuple-element.217), channel_id=1, source_target_pairs={{0,4},{2,6},{4,0},{6,2},{8,12},{10,14},{12,8},{14,10},{16,20},{18,... | collective-permute-start | bytes 2457608 | tf_op jit(solution)/shard_map/ppermute | solution.py:485
  74.3 18.8 %collective-permute-start = (bf16[1280,640]{1,0:T(8,128)(2,1)S(1)}, bf16[1280,640]{1,0:T(8,128)(2,1)}, u32[]{:S(2)}, u32[]{:S(2)}) collective-permute-start(bf16[1280,640]{1,0:T(8,128)(2,1)S(1)} %slice.48), channel_id=1, source_target_pairs={{0,1},{1,0},{2,3},{3,2},{4,5},{5,4},{6,7},{7,6},{8,9},{9,8},{10,11... | collective-permute-start | bytes 4915208 | tf_op jit(solution)/shard_map/ppermute | solution.py:284
  74.4 18.7 %collective-permute-start.1 = (bf16[320,640]{1,0:T(8,128)(2,1)}, bf16[320,640]{1,0:T(8,128)(2,1)}, u32[]{:S(2)}, u32[]{:S(2)}) collective-permute-start(bf16[320,640]{1,0:T(8,128)(2,1)} %param.20), channel_id=1, source_target_pairs={{0,8},{2,10},{4,12},{6,14},{8,24},{10,26},{12,28},{14,30},{24,16},... | collective-permute-start | bytes 1228808 | tf_op jit(solution)/shard_map/ppermute | solution.py:493
  75.4 8.6 %copy-start.52 = (s32[2,1024]{1,0:T(2,128)S(1)}, s32[2,1024]{1,0:T(2,128)}, u32[]{:S(2)}) copy-start(s32[2,1024]{1,0:T(2,128)} %param.12) | copy-start | bytes 24580
  89.4 6.5 %copy-start.22 = (bf16[2,1024,1280]{2,1,0:T(8,128)(2,1)S(1)}, bf16[2,1024,1280]{2,1,0:T(8,128)(2,1)}, u32[]{:S(2)}) copy-start(bf16[2,1024,1280]{2,1,0:T(8,128)(2,1)} %copy-done.21) | copy-start | bytes 15728644
  90.9 11.9 %copy-start.33 = (bf16[2,4,80,1280]{3,2,1,0:T(8,128)(2,1)}, bf16[2,4,80,1280]{3,2,1,0:T(8,128)(2,1)S(1)}, u32[]{:S(2)}) copy-start(bf16[2,4,80,1280]{3,2,1,0:T(8,128)(2,1)S(1)} %pad_maximum_fusion.5.refs_4_) | copy-start | bytes 4915204
  93.1 9.7 %copy-start.34 = (bf16[2,4,80,1280]{3,2,1,0:T(8,128)(2,1)}, bf16[2,4,80,1280]{3,2,1,0:T(8,128)(2,1)S(1)}, u32[]{:S(2)}) copy-start(bf16[2,4,80,1280]{3,2,1,0:T(8,128)(2,1)S(1)} %pad_maximum_fusion.4.refs_2_) | copy-start | bytes 4915204
  93.1 35.6 %collective-permute-start.6 = (bf16[2,4,80,1280]{3,2,1,0:T(8,128)(2,1)S(1)}, bf16[2,4,80,1280]{3,2,1,0:T(8,128)(2,1)S(1)}, u32[]{:S(2)}, u32[]{:S(2)}) collective-permute-start(bf16[2,4,80,1280]{3,2,1,0:T(8,128)(2,1)S(1)} %pad_maximum_fusion.4.refs_2_), channel_id=1, source_target_pairs={{0,2},{2,0},{4,6},{6,4},{8,10},{10,8},{12,14},{14,12},{16,18},{18,... | collective-permute-start | bytes 4915208 | tf_op jit(solution)/shard_map/ppermute | solution.py:481
  94.7 34.1 %collective-permute-start.7 = (bf16[2,4,80,1280]{3,2,1,0:T(8,128)(2,1)S(1)}, bf16[2,4,80,1280]{3,2,1,0:T(8,128)(2,1)S(1)}, u32[]{:S(2)}, u32[]{:S(2)}) collective-permute-start(bf16[2,4,80,1280]{3,2,1,0:T(8,128)(2,1)S(1)} %pad_maximum_fusion.5.refs_4_), channel_id=1, source_target_pairs={{0,4},{2,6},{4,0},{6,2},{8,12},{10,14},{12,8},{14,10},{16,20},{18,... | collective-permute-start | bytes 4915208 | tf_op jit(solution)/shard_map/ppermute | solution.py:485
  95.2 10.8 %collective-permute-start.4 = (bf16[320,640]{1,0:T(8,128)(2,1)}, bf16[320,640]{1,0:T(8,128)(2,1)S(1)}, u32[]{:S(2)}, u32[]{:S(2)}) collective-permute-start(bf16[320,640]{1,0:T(8,128)(2,1)} %collective-permute-done.1), channel_id=1, source_target_pairs={{0,8},{2,10},{4,12},{6,14},{8,24},{10,26},{12,28},{14,30},{24,16},... | collective-permute-start | bytes 1228808 | tf_op jit(solution)/shard_map/ppermute | solution.py:493
  106.0 22.7 %collective-permute-start.5 = (bf16[320,640]{1,0:T(8,128)(2,1)S(1)}, bf16[320,640]{1,0:T(8,128)(2,1)S(1)}, u32[]{:S(2)}, u32[]{:S(2)}) collective-permute-start(bf16[320,640]{1,0:T(8,128)(2,1)S(1)} %collective-permute-done.4), channel_id=1, source_target_pairs={{0,8},{2,10},{4,12},{6,14},{8,24},{10,26},{12,28},{14,30},{24,16},... | collective-permute-start | bytes 1228808 | tf_op jit(solution)/shard_map/ppermute | solution.py:493
  106.5 22.2 %copy-start.17 = (s32[2,1024,128]{2,1,0:T(8,128)}, s32[2,1024,128]{2,1,0:T(8,128)S(1)}, u32[]{:S(2)}) copy-start(s32[2,1024,128]{2,1,0:T(8,128)S(1)} %broadcast_in_dim.4.column_ref) | copy-start | bytes 3145732
  128.8 7.6 %copy-start.55 = (bf16[2,4,80,1280]{3,2,1,0:T(8,128)(2,1)}, bf16[2,4,80,1280]{3,2,1,0:T(8,128)(2,1)S(1)}, u32[]{:S(2)}) copy-start(bf16[2,4,80,1280]{3,2,1,0:T(8,128)(2,1)S(1)} %collective-permute-done.7.refs_5_) | copy-start | bytes 4915204
  130.7 10.4 %collective-permute-start.8 = (bf16[2,512,640]{2,1,0:T(8,128)(2,1)S(1)}, bf16[2,512,640]{2,1,0:T(8,128)(2,1)S(1)}, u32[]{:S(2)}, u32[]{:S(2)}) collective-permute-start(bf16[2,512,640]{2,1,0:T(8,128)(2,1)S(1)} %get-tuple-element.203), channel_id=1, source_target_pairs={{0,1},{1,0},{2,3},{3,2},{4,5},{5,4},{6,7},{7,6},{8,9},{9,8},{10,11... | collective-permute-start | bytes 3932168 | tf_op jit(solution)/shard_map/ppermute | solution.py:284
  137.0 4.8 copy-start.45
  137.0 4.8 copy-start.46
  137.0 21.1 %collective-permute-start.10 = (bf16[4,160,640]{2,1,0:T(8,128)(2,1)S(1)}, bf16[4,160,640]{2,1,0:T(8,128)(2,1)S(1)}, u32[]{:S(2)}, u32[]{:S(2)}) collective-permute-start(bf16[4,160,640]{2,1,0:T(8,128)(2,1)S(1)} %get-tuple-element.208.refs_9_), channel_id=1, source_target_pairs={{0,2},{2,0},{4,6},{6,4},{8,10},{10,8},{12,14},{14,12},{16,18},{18,... | collective-permute-start | bytes 2457608 | tf_op jit(solution)/shard_map/ppermute | solution.py:481
  138.1 37.2 %collective-permute-start.12 = (bf16[4,160,640]{2,1,0:T(8,128)(2,1)S(1)}, bf16[4,160,640]{2,1,0:T(8,128)(2,1)S(1)}, u32[]{:S(2)}, u32[]{:S(2)}) collective-permute-start(bf16[4,160,640]{2,1,0:T(8,128)(2,1)S(1)} %get-tuple-element.208.refs_9_), channel_id=1, source_target_pairs={{0,4},{2,6},{4,0},{6,2},{8,12},{10,14},{12,8},{14,10},{16,20},{18,... | collective-permute-start | bytes 2457608 | tf_op jit(solution)/shard_map/ppermute | solution.py:485
  138.3 36.9 %collective-permute-start.11 = (bf16[4,160,640]{2,1,0:T(8,128)(2,1)S(1)}, bf16[4,160,640]{2,1,0:T(8,128)(2,1)S(1)}, u32[]{:S(2)}, u32[]{:S(2)}) collective-permute-start(bf16[4,160,640]{2,1,0:T(8,128)(2,1)S(1)} %get-tuple-element.209.refs_6_), channel_id=1, source_target_pairs={{0,2},{2,0},{4,6},{6,4},{8,10},{10,8},{12,14},{14,12},{16,18},{18,... | collective-permute-start | bytes 2457608 | tf_op jit(solution)/shard_map/ppermute | solution.py:481
  140.3 35.7 %collective-permute-start.9 = (bf16[4,160,640]{2,1,0:T(8,128)(2,1)S(1)}, bf16[4,160,640]{2,1,0:T(8,128)(2,1)S(1)}, u32[]{:S(2)}, u32[]{:S(2)}) collective-permute-start(bf16[4,160,640]{2,1,0:T(8,128)(2,1)S(1)} %get-tuple-element.209.refs_6_), channel_id=1, source_target_pairs={{0,4},{2,6},{4,0},{6,2},{8,12},{10,14},{12,8},{14,10},{16,20},{18,... | collective-permute-start | bytes 2457608 | tf_op jit(solution)/shard_map/ppermute | solution.py:485
  148.8 28.1 %copy-start.1 = (bf16[2,512,1280]{2,1,0:T(8,128)(2,1)S(1)}, bf16[2,512,1280]{2,1,0:T(8,128)(2,1)}, u32[]{:S(2)}) copy-start(bf16[2,512,1280]{2,1,0:T(8,128)(2,1)} %cot_ref.1) | copy-start | bytes 7864324
  148.8 28.1 %copy-start.7 = (bf16[2,512,1280]{2,1,0:T(8,128)(2,1)S(1)}, bf16[2,512,1280]{2,1,0:T(8,128)(2,1)}, u32[]{:S(2)}) copy-start(bf16[2,512,1280]{2,1,0:T(8,128)(2,1)} %copy-done.6) | copy-start | bytes 7864324
  158.1 17.9 %copy-start.56 = (bf16[4,160,640]{2,1,0:T(8,128)(2,1)}, bf16[4,160,640]{2,1,0:T(8,128)(2,1)S(1)}, u32[]{:S(2)}) copy-start(bf16[4,160,640]{2,1,0:T(8,128)(2,1)S(1)} %collective-permute-done.10.refs_10_) | copy-start | bytes 2457604
  283.5 3.7 copy-start.24
  287.2 21.7 %collective-permute-start.13 = (bf16[2560,640]{1,0:T(8,128)(2,1)}, bf16[2560,640]{1,0:T(8,128)(2,1)}, u32[]{:S(2)}, u32[]{:S(2)}) collective-permute-start(bf16[2560,640]{1,0:T(8,128)(2,1)} %constant_dynamic-slice_fusion.8), channel_id=1, source_target_pairs={{0,1},{1,0},{2,3},{3,2},{4,5},{5,4},{6,7},{7,6},{8,9},{9,8},{10,11... | collective-permute-start | bytes 9830408 | tf_op jit(solution)/shard_map/ppermute | solution.py:284
  294.8 12.6 %copy-start.25 = (bf16[2560,1280]{1,0:T(8,128)(2,1)S(1)}, bf16[2560,1280]{1,0:T(8,128)(2,1)}, u32[]{:S(2)}) copy-start(bf16[2560,1280]{1,0:T(8,128)(2,1)} %copy-done.24) | copy-start | bytes 19660804
  306.8 3.4 copy-start.5
  311.7 38.2 %collective-permute-start.15 = (bf16[4,2,160,640]{3,2,0,1:T(8,128)(2,1)S(1)}, bf16[4,2,160,640]{3,2,0,1:T(8,128)(2,1)S(1)}, u32[]{:S(2)}, u32[]{:S(2)}) collective-permute-start(bf16[4,2,160,640]{3,2,0,1:T(8,128)(2,1)S(1)} %pad_maximum_fusion.9), channel_id=1, source_target_pairs={{0,4},{2,6},{4,0},{6,2},{8,12},{10,14},{12,8},{14,10},{16,20},{18,... | collective-permute-start | bytes 4915208 | tf_op jit(solution)/shard_map/ppermute | solution.py:485
  312.7 20.0 %slice-start.2 = ((s8[5242880]{0:T(1024)(128)(4,1)}), s8[4194304]{0:T(1024)(128)(4,1)S(1)}, s32[]{:S(2)}) async-start(s8[5242880]{0:T(1024)(128)(4,1)} %bitcast.162), calls=%async_computation.2 | async-start | bytes 8388608
  312.8 37.9 %collective-permute-start.14 = (bf16[4,2,160,640]{3,2,0,1:T(8,128)(2,1)S(1)}, bf16[4,2,160,640]{3,2,0,1:T(8,128)(2,1)S(1)}, u32[]{:S(2)}, u32[]{:S(2)}) collective-permute-start(bf16[4,2,160,640]{3,2,0,1:T(8,128)(2,1)S(1)} %pad_maximum_fusion.8), channel_id=1, source_target_pairs={{0,2},{2,0},{4,6},{6,4},{8,10},{10,8},{12,14},{14,12},{16,18},{18,... | collective-permute-start | bytes 4915208 | tf_op jit(solution)/shard_map/ppermute | solution.py:481
  314.1 18.6 %copy-start.11 = (bf16[2,1024,640]{2,1,0:T(8,128)(2,1)S(1)}, bf16[2,1024,640]{2,1,0:T(8,128)(2,1)}, u32[]{:S(2)}) copy-start(bf16[2,1024,640]{2,1,0:T(8,128)(2,1)} %copy-done.10) | copy-start | bytes 7864324
  314.1 18.6 %slice-start.3 = ((s8[5242880]{0:T(1024)(128)(4,1)}), s8[1048576]{0:T(1024)(128)(4,1)S(1)}, s32[]{:S(2)}) async-start(s8[5242880]{0:T(1024)(128)(4,1)} %bitcast.162), calls=%async_computation.3 | async-start | bytes 2097152
  332.6 3.9 copy-start.26
  336.5 11.8 %collective-permute-start.16 = (bf16[640,640]{1,0:T(8,128)(2,1)S(1)}, bf16[640,640]{1,0:T(8,128)(2,1)S(1)}, u32[]{:S(2)}, u32[]{:S(2)}) collective-permute-start(bf16[640,640]{1,0:T(8,128)(2,1)S(1)} %get-tuple-element.207), channel_id=1, source_target_pairs={{0,1},{1,0},{2,3},{3,2},{4,5},{5,4},{6,7},{7,6},{8,9},{9,8},{10,11... | collective-permute-start | bytes 2457608 | tf_op jit(solution)/shard_map/ppermute | solution.py:284
  336.5 3.5 copy-start.37
  355.9 5.1 copy-start.28
  355.9 40.3 %collective-permute-start.18 = (bf16[4,1,160,640]{3,2,0,1:T(8,128)(2,1)}, bf16[4,1,160,640]{3,2,0,1:T(8,128)(2,1)}, u32[]{:S(2)}, u32[]{:S(2)}) collective-permute-start(bf16[4,1,160,640]{3,2,0,1:T(8,128)(2,1)} %add_convert_fusion.4), channel_id=1, source_target_pairs={{0,2},{2,0},{4,6},{6,4},{8,10},{10,8},{12,14},{14,12},{16,18},{18,... | collective-permute-start | bytes 2457608 | tf_op jit(solution)/shard_map/ppermute | solution.py:481
  357.1 39.0 %collective-permute-start.17 = (bf16[4,1,160,640]{3,2,0,1:T(8,128)(2,1)}, bf16[4,1,160,640]{3,2,0,1:T(8,128)(2,1)}, u32[]{:S(2)}, u32[]{:S(2)}) collective-permute-start(bf16[4,1,160,640]{3,2,0,1:T(8,128)(2,1)} %add_convert_fusion.5), channel_id=1, source_target_pairs={{0,4},{2,6},{4,0},{6,2},{8,12},{10,14},{12,8},{14,10},{16,20},{18,... | collective-permute-start | bytes 2457608 | tf_op jit(solution)/shard_map/ppermute | solution.py:485
  361.0 3.6 copy-start.18
  362.5 69.1 %collective-permute-start.21 = (bf16[4,2,80,1664]{3,2,0,1:T(8,128)(2,1)}, bf16[4,2,80,1664]{3,2,0,1:T(8,128)(2,1)S(1)}, u32[]{:S(2)}, u32[]{:S(2)}) collective-permute-start(bf16[4,2,80,1664]{3,2,0,1:T(8,128)(2,1)} %pad_maximum_fusion.2), channel_id=1, source_target_pairs={{0,4},{2,6},{4,0},{6,2},{8,12},{10,14},{12,8},{14,10},{16,20},{18,... | collective-permute-start | bytes 6389768 | tf_op jit(solution)/shard_map/ppermute | solution.py:485
  363.7 67.9 %collective-permute-start.20 = (bf16[4,2,80,1536]{3,2,0,1:T(8,128)(2,1)}, bf16[4,2,80,1536]{3,2,0,1:T(8,128)(2,1)}, u32[]{:S(2)}, u32[]{:S(2)}) collective-permute-start(bf16[4,2,80,1536]{3,2,0,1:T(8,128)(2,1)} %copy_bitcast_fusion), channel_id=1, source_target_pairs={{0,2},{2,0},{4,6},{6,4},{8,10},{10,8},{12,14},{14,12},{16,18},{18,... | collective-permute-start | bytes 5898248 | tf_op jit(solution)/shard_map/ppermute | solution.py:481
  364.6 31.6 %copy-start.36 = (bf16[2,1,160,640]{3,2,0,1:T(8,128)(2,1)S(1)}, bf16[2,1,160,640]{3,2,0,1:T(8,128)(2,1)}, u32[]{:S(2)}) copy-start(bf16[2,1,160,640]{3,2,0,1:T(8,128)(2,1)} %get-tuple-element.194) | copy-start | bytes 1228804
  364.6 31.6 %copy-start.39 = (bf16[4,2,160,640]{3,2,0,1:T(8,128)(2,1)S(1)}, bf16[4,2,160,640]{3,2,0,1:T(8,128)(2,1)}, u32[]{:S(2)}) copy-start(bf16[4,2,160,640]{3,2,0,1:T(8,128)(2,1)} %copy-done.38) | copy-start | bytes 4915204
  364.6 31.6 %copy-start.44 = (bf16[2,1,160,640]{3,2,0,1:T(8,128)(2,1)S(1)}, bf16[2,1,160,640]{3,2,0,1:T(8,128)(2,1)}, u32[]{:S(2)}) copy-start(bf16[2,1,160,640]{3,2,0,1:T(8,128)(2,1)} %get-tuple-element.198) | copy-start | bytes 1228804
  398.0 37.4 %slice-start = ((s8[5242880]{0:T(1024)(128)(4,1)}), s8[4194304]{0:T(1024)(128)(4,1)S(1)}, s32[]{:S(2)}) async-start(s8[5242880]{0:T(1024)(128)(4,1)} %bitcast.137), calls=%async_computation | async-start | bytes 8388608
  399.7 30.7 %collective-permute-start.19 = (bf16[320,640]{1,0:T(8,128)(2,1)S(1)}, bf16[320,640]{1,0:T(8,128)(2,1)S(1)}, u32[]{:S(2)}, u32[]{:S(2)}) collective-permute-start(bf16[320,640]{1,0:T(8,128)(2,1)S(1)} %fusion.12), channel_id=1, source_target_pairs={{0,8},{2,10},{4,12},{6,14},{8,24},{10,26},{12,28},{14,30},{24,16},... | collective-permute-start | bytes 1228808 | tf_op jit(solution)/shard_map/ppermute | solution.py:493
  400.2 35.1 %slice-start.1 = ((s8[5242880]{0:T(1024)(128)(4,1)}), s8[1048576]{0:T(1024)(128)(4,1)S(1)}, s32[]{:S(2)}) async-start(s8[5242880]{0:T(1024)(128)(4,1)} %bitcast.137), calls=%async_computation.1 | async-start | bytes 2097152
  430.4 10.8 %copy-start.16 = (bf16[2,1024,640]{2,1,0:T(8,128)(2,1)}, bf16[2,1024,640]{2,1,0:T(8,128)(2,1)S(1)}, u32[]{:S(2)}) copy-start(bf16[2,1024,640]{2,1,0:T(8,128)(2,1)S(1)} %get-tuple-element.164) | copy-start | bytes 7864324
  430.4 3.2 copy-start.29
  430.5 4.9 copy-start.30
  430.5 16.0 %collective-permute-start.22 = (bf16[320,640]{1,0:T(8,128)(2,1)S(1)}, bf16[320,640]{1,0:T(8,128)(2,1)S(1)}, u32[]{:S(2)}, u32[]{:S(2)}) collective-permute-start(bf16[320,640]{1,0:T(8,128)(2,1)S(1)} %fusion.10), channel_id=1, source_target_pairs={{0,8},{2,10},{4,12},{6,14},{8,24},{10,26},{12,28},{14,30},{24,16},... | collective-permute-start | bytes 1228808 | tf_op jit(solution)/shard_map/ppermute | solution.py:493
  433.9 25.2 %collective-permute-start.25 = (bf16[4,1,80,1664]{3,2,0,1:T(8,128)(2,1)S(1)}, bf16[4,1,80,1664]{3,2,0,1:T(8,128)(2,1)S(1)}, u32[]{:S(2)}, u32[]{:S(2)}) collective-permute-start(bf16[4,1,80,1664]{3,2,0,1:T(8,128)(2,1)S(1)} %add_convert_fusion.1), channel_id=1, source_target_pairs={{0,2},{2,0},{4,6},{6,4},{8,10},{10,8},{12,14},{14,12},{16,18},{18,... | collective-permute-start | bytes 3194888 | tf_op jit(solution)/shard_map/ppermute | solution.py:481
  435.3 23.8 %collective-permute-start.24 = (bf16[4,1,80,1536]{3,2,0,1:T(8,128)(2,1)S(1)}, bf16[4,1,80,1536]{3,2,0,1:T(8,128)(2,1)S(1)}, u32[]{:S(2)}, u32[]{:S(2)}) collective-permute-start(bf16[4,1,80,1536]{3,2,0,1:T(8,128)(2,1)S(1)} %fusion.3), channel_id=1, source_target_pairs={{0,4},{2,6},{4,0},{6,2},{8,12},{10,14},{12,8},{14,10},{16,20},{18,... | collective-permute-start | bytes 2949128 | tf_op jit(solution)/shard_map/ppermute | solution.py:485
  441.1 10.1 %copy-start.31 = (bf16[2,1024,640]{2,1,0:T(8,128)(2,1)S(1)}, bf16[2,1024,640]{2,1,0:T(8,128)(2,1)}, u32[]{:S(2)}) copy-start(bf16[2,1024,640]{2,1,0:T(8,128)(2,1)} %get-tuple-element.166) | copy-start | bytes 7864324
  446.7 11.4 %collective-permute-start.23 = (bf16[320,640]{1,0:T(8,128)(2,1)S(1)}, bf16[320,640]{1,0:T(8,128)(2,1)S(1)}, u32[]{:S(2)}, u32[]{:S(2)}) collective-permute-start(bf16[320,640]{1,0:T(8,128)(2,1)S(1)} %fusion.9), channel_id=1, source_target_pairs={{0,8},{2,10},{4,12},{6,14},{8,24},{10,26},{12,28},{14,30},{24,16},... | collective-permute-start | bytes 1228808 | tf_op jit(solution)/shard_map/ppermute | solution.py:493
  462.8 70.2 %copy-start.9 = (bf16[1024,1280]{1,0:T(8,128)(2,1)S(1)}, bf16[1024,1280]{1,0:T(8,128)(2,1)}, u32[]{:S(2)}) copy-start(bf16[1024,1280]{1,0:T(8,128)(2,1)} %copy-done.8) | copy-start | bytes 7864324
  533.0 3.4 copy-start.27
  536.4 3.8 copy-start.49
  536.4 4.5 copy-start.48
  536.5 5.2 copy-start.47
  (26 other events, 46.9 us)

commit v6 on v5

--- a/solution.py
+++ b/solution.py
@@ -1584,6 +1584,7 @@
     mixed, down_steps[3], up_parts = tie((mixed, down_steps[3], up_parts))
     down_first, down_second = halves_z(natural_z(down_steps))
     down_came = swap_y(down_first), swap_x(down_second), swap_x(down_first), swap_y(down_second)
+    w_o_other = tie(w_o_other, down_first, down_second)
     w_o = jnp.where(
         first,
         jnp.concatenate([w_o_half, w_o_other], 1),
@@ -1602,11 +1603,11 @@
     residual = tokens_own + dot_low(mixed_own, w_o)
     unit_two, _ = norm_stats(residual)
     normed_two = (unit_two * gain_ffn).astype(jnp.bfloat16)
-    normed_two, down_came = tie((normed_two, down_came))
+    cot_other = tie(cot_other, mixed_own)
+    cot_all = jnp.concatenate([cot_own, cot_other.reshape(flat, width)], 0)
+    normed_two, cot_all, down_came = tie((normed_two, cot_all, down_came))
     first_y, second_x, first_x, second_y = down_came
     down_parts = (down_first, first_y, first_x, down_second, second_x, second_y)
-    cot_other = tie(cot_other, mixed_own)
-    cot_all = jnp.concatenate([cot_own, cot_other.reshape(flat, width)], 0)
     hidden_low, grad_pre, y_own, grad_two_own, normed_two_all, y_came, grad_two_came = feed_forward(
         normed_two, cot_all, up_parts, down_parts
     )

time: 548 us -> 542 us (0.989)
    ppermute x8, waiting for transfers between devices: 30 us -> 24.5 us  [swap_x(): return lax.ppermute(values, 'rows', [(row, row ^ 1) for row in range(16)])]
    unnamed x135 -> x129, local copies, waits for them, and re-layouts: 31.2 us -> 28.6 us
  transfers between devices with their start and end apart: 26 -> 26, of which waited for: 7 -> 9; matrix products, arithmetic and copies ran while one was open for 18% -> 19% of each run, Pallas kernels for 17% -> 17%
where the time goes in v6:
time: 542 us; the launch traced here: 536 us
  Pallas kernels  309 us (57%)
  matrix products  84 us (15%)
  local copies, waits for them, and re-layouts  53.3 us (10%)
  other arithmetic  32.4 us (6%)
  waiting for transfers between devices  32.3 us (6%)
  starting transfers between devices  24.1 us (4%)
    pallas_call x1, Pallas kernels, feed_forward(): pl.pallas_call(feed_forward_kernel, grid=(2 * tiles,), in_specs=[anywhere...  86.8 us
    pallas_call x3, Pallas kernels, attention_call(): pl.pallas_call(functools.partial(kernel, row, len(begun)), grid_spec=pltp...  81.8 us
    pallas_call x1, Pallas kernels, tail_call(): pl.pallas_call(tail_kernel, in_specs=[anywhere] * 4 + [here] * 3 + [anywh...  68 us
    pallas_call x1, Pallas kernels, head_call(): pl.pallas_call(head_kernel, in_specs=[anywhere, pl.BlockSpec(memory_space...  61.3 us
    dot_general x6, matrix products, outer_low(): jnp.einsum('tc,te->ce', left_side, right_side, preferred_element_type=jnp...  56.6 us
    unnamed x129, local copies, waits for them, and re-layouts  28.6 us
    ppermute x8, waiting for transfers between devices, swap_x(): return lax.ppermute(values, 'rows', [(row, row ^ 1) for row in range(16)])  24.5 us
    dot_general x3, matrix products, dot_low(): return jnp.dot(left_side, right_side, preferred_element_type=jnp.float32)  19.2 us
  transfers between devices with their start and end apart: 26, of which 9 were waited for; matrix products, arithmetic and copies ran while one was open for 19% of the time, Pallas kernels for 17%

profile of v6, /device:TPU:0, one launch (start us, length us, event | category | flops | bytes accessed | tf_op | source)
XLA Modules:
  0.0 536.3 jit_solution(11138883261311815555)
XLA Ops:
  2.4 1.7 copy-done
  4.2 1.7 copy-done.2
  6.9 61.3 %shard_map.186 = (bf16[2,1024,1280]{2,1,0:T(8,128)(2,1)S(1)}, bf16[2,512,1280]{2,1,0:T(8,128)(2,1)S(1)}, bf16[1280,2560]{1,0:T(8,128)(2,1)S(1)}, bf16[4,80,2560]{2,1,0:T(8,128)(2,1)S(1)}) custom-call(bf16[2,512,1280]{2,1,0:T(8,128)(2,1)S(1)} %copy-done.2, f32[1,1280]{1,0:T(1,128)S(1)} %reshape.421.gain_ref, bf16[2,512,1280]{2,1,0:T(8,128)(2,1)S(1)} %copy-done, ...), custom_call_target="tpu_custom_call" | custom-call | tf_op jit(solution)/shard_map/pallas_call | solution.py:1069
  68.3 1.5 copy-done.6
  69.8 1.6 slice_bitcast_fusion
  71.3 1.8 collective-permute-start.3
  75.4 8.6 %convolution_convert_fusion.2 = bf16[2048,1280]{1,0:T(8,128)(2,1)} fusion(bf16[2048,1280]{1,0:T(8,128)(2,1)S(1)} %bitcast.134, bf16[1280,2560]{1,0:T(8,128)(2,1)S(1)} %get-tuple-element.99.weights_ref), kind=kOutput, calls=%fused_computation.2 | convolution fusion | flops 6713507840 | bytes 13762560 | tf_op jit(solution)/shard_map/dot_general | solution.py:1445
  84.5 5.0 collective-permute-done.3
  89.5 1.4 pad_maximum_fusion.5.refs_4_
  90.9 2.2 pad_maximum_fusion.4.refs_2_
  93.2 1.6 collective-permute-start.6
  96.0 7.0 %convolution_convert_fusion.8 = bf16[2048,640]{1,0:T(8,128)(2,1)} fusion(bf16[2048,1280]{1,0:T(8,128)(2,1)S(1)} %bitcast.135, bf16[1280,2560]{1,0:T(8,128)(2,1)} %copy-done.4), kind=kOutput, calls=%fused_computation.14 | convolution fusion | flops 3356753920 | bytes 9502720 | tf_op jit(solution)/shard_map/dot_general | solution.py:1445
  102.9 3.2 collective-permute-done.4
  106.6 21.4 %shard_map.187 = bf16[2,1024,640]{2,1,0:T(8,128)(2,1)S(1)} custom-call(s32[2,8]{1,0:T(2,128)S(1)} %get-tuple-element.195.start_ref, s32[2,8]{1,0:T(2,128)S(1)} %get-tuple-element.194.count_ref, s32[2,1024,128]{2,1,0:T(8,128)S(1)} %broadcast_in_dim.4.column_ref, s32[2,8,1024]{2,1,0:T(8,128)S(1)} %lt.204.line_ref, bf16[2,1024,1280]{2,1,0:T(8,128)(2,1)} %bitcast.164, ...), custom_call_target="tpu_custom_call" | custom-call | flops 16106127360 | bytes 10485760 | tf_op jit(solution)/shard_map/pallas_call | solution.py:433
  130.2 1.4 pad_maximum_fusion.6
  134.5 2.0 collective-permute-start.11
  137.0 3.1 maximum_select_fusion
  140.1 1.3 constant_dynamic-slice_fusion.10
  143.2 3.7 fusion.22
  146.9 2.9 pad_maximum_fusion.refs_1_
  150.7 2.2 multiply_convert_fusion.refs_0_
  154.1 17.2 %collective-permute-done.11.refs_8_ = bf16[4,160,640]{2,1,0:T(8,128)(2,1)} collective-permute-done((bf16[4,160,640]{2,1,0:T(8,128)(2,1)}, bf16[4,160,640]{2,1,0:T(8,128)(2,1)}, u32[]{:S(2)}, u32[]{:S(2)}) %collective-permute-start.11) | collective-permute-done | bytes 819232 | tf_op jit(solution)/shard_map/ppermute | solution.py:481
  172.3 86.8 %shard_map.188 = (bf16[2048,2560]{1,0:T(8,128)(2,1)}, bf16[2048,2560]{1,0:T(8,128)(2,1)}, bf16[1024,1280]{1,0:T(8,128)(2,1)}, bf16[1024,1280]{1,0:T(8,128)(2,1)}...) custom-call(bf16[1024,1280]{1,0:T(8,128)(2,1)} %multiply_convert_fusion.refs_0_, ...), custom_call_target="tpu_custom_call" | custom-call | flops 53687091200 | bytes 55050240 | tf_op jit(solution)/shard_map/pallas_call | solution.py:775
  259.1 17.9 %convolution_convert_fusion.1 = bf16[2560,1280]{1,0:T(8,128)(2,1)S(1)} fusion(bf16[2048,2560]{1,0:T(8,128)(2,1)} %get-tuple-element.132, bf16[2048,1280]{1,0:T(8,128)(2,1)} %pad_maximum_fusion.refs_1_), kind=kOutput, calls=%fused_computation.1 | convolution fusion | flops 13425049600 | bytes 22282240 | tf_op jit(solution)/shard_map/tc,te->ce/dot_general | solution.py:1449
  277.0 2.2 constant_dynamic-slice_fusion.8
  279.2 1.5 copy-done.26
  281.3 1.7 copy-done.12
  283.1 1.7 copy-done.13
  284.8 1.7 copy-done.14
  286.5 1.7 copy-done.15
  288.3 10.5 %shard_map.189 = (bf16[1024,1280]{1,0:T(8,128)(2,1)S(1)}, f32[1024,1280]{1,0:T(8,128)S(1)}, f32[8,1280]{1,0:T(8,128)S(1)}, bf16[2,1024,1280]{2,1,0:T(8,128)(2,1)}) custom-call(f32[1024,1280]{1,0:T(8,128)} %copy-done.25, bf16[1024,1280]{1,0:T(8,128)(2,1)S(1)} %bitcast.126, bf16[1024,1280]{1,0:T(8,128)(2,1)S(1)} %copy-done.12, ...), custom_call_target="tpu_custom_call" | custom-call | tf_op jit(solution)/shard_map/pallas_call | solution.py:881
  298.8 1.5 copy-done.8
  301.0 1.6 dynamic-slice_bitcast_fusion.5
  302.6 1.3 copy_bitcast_fusion.3
  304.0 1.3 copy_bitcast_fusion.5
  306.3 1.6 collective-permute-start.14
  307.8 18.5 %convolution_convert_fusion = bf16[1280,2560]{1,0:T(8,128)(2,1)S(1)} fusion(bf16[2048,1280]{1,0:T(8,128)(2,1)} %get-tuple-element.136, bf16[2048,2560]{1,0:T(8,128)(2,1)} %get-tuple-element.142), kind=kOutput, calls=%fused_computation | convolution fusion | flops 13425049600 | bytes 22282240 | tf_op jit(solution)/shard_map/tc,te->ce/dot_general | solution.py:1449
  326.4 3.6 convolution_convert_fusion.6
  331.4 2.4 dynamic-slice_bitcast_fusion.4
  333.8 8.3 %convolution_convert_fusion.7 = bf16[2048,640]{1,0:T(8,128)(2,1)} fusion(bf16[2048,1280]{1,0:T(8,128)(2,1)} %bitcast.160, bf16[640,1280]{1,0:T(8,128)(2,1)S(1)} %copy-done.39), kind=kOutput, calls=%fused_computation.13 | convolution fusion | flops 3356753920 | bytes 9502720 | tf_op jit(solution)/shard_map/te,de->td/dot_general | solution.py:30
  344.1 1.3 add_convert_fusion.4
  346.7 2.5 copy_bitcast_fusion.1
  349.2 1.5 collective-permute-start.18
  351.3 3.1 copy_bitcast_fusion
  354.4 1.5 pad_maximum_fusion.2
  355.9 1.5 collective-permute-start.21
  358.0 29.0 %shard_map.190 = (bf16[2,1024,640]{2,1,0:T(8,128)(2,1)S(1)}, bf16[2,1024,640]{2,1,0:T(8,128)(2,1)}, bf16[2,1024,640]{2,1,0:T(8,128)(2,1)}) custom-call(s32[2,4]{1,0:T(2,128)S(1)} %get-tuple-element.193.start_ref, s32[2,4]{1,0:T(2,128)S(1)} %get-tuple-element.192.count_ref, s32[2,1024,128]{2,1,0:T(8,128)S(1)} %copy-done.18, s32[2,8,1024]{2,1,0:T(8,128)S(1)} %copy-done.21, ...), custom_call_target="tpu_custom_call" | custom-call | flops 10737418240 | bytes 9175040 | tf_op jit(solution)/shard_map/pallas_call | solution.py:433
  387.1 1.6 fusion.8
  388.9 1.6 fusion.7
  390.5 3.7 collective-permute-start.19
  394.2 31.4 %shard_map.191 = (bf16[2,1024,640]{2,1,0:T(8,128)(2,1)S(1)}, bf16[2,1024,640]{2,1,0:T(8,128)(2,1)}, bf16[2,1024,640]{2,1,0:T(8,128)(2,1)}) custom-call(s32[2,4]{1,0:T(2,128)S(1)} %get-tuple-element.193.start_ref, s32[2,4]{1,0:T(2,128)S(1)} %get-tuple-element.192.count_ref, ...), custom_call_target="tpu_custom_call", output_to_operand_aliasing={{0}: (8, {}), {1}: (9, {}), {2}: (10, {})} | custom-call | flops 10737418240 | bytes 9175040 | tf_op jit(solution)/shard_map/pallas_call | solution.py:433
  425.9 2.8 fusion.3
  430.0 5.7 %convolution_convert_fusion.4.key_ref = bf16[1280,640]{1,0:T(8,128)(2,1)} fusion(bf16[2048,1280]{1,0:T(8,128)(2,1)S(1)} %bitcast.138, bf16[2048,640]{1,0:T(8,128)(2,1)S(1)} %bitcast.154), kind=kOutput, calls=%fused_computation.10 | convolution fusion | flops 3356262400 | bytes 9502720 | tf_op jit(solution)/shard_map/tc,te->ce/dot_general | solution.py:1449
  435.7 5.4 %convolution_convert_fusion.5.query_ref = bf16[1280,640]{1,0:T(8,128)(2,1)} fusion(bf16[2048,1280]{1,0:T(8,128)(2,1)S(1)} %bitcast.139, bf16[2048,640]{1,0:T(8,128)(2,1)S(1)} %bitcast.132), kind=kOutput, calls=%fused_computation.11 | convolution fusion | flops 3356262400 | bytes 9502720 | tf_op jit(solution)/shard_map/tc,te->ce/dot_general | solution.py:1449
  441.2 1.9 collective-permute-start.23
  443.1 5.5 %convolution_convert_fusion.3.value_ref = bf16[1280,640]{1,0:T(8,128)(2,1)} fusion(bf16[2048,1280]{1,0:T(8,128)(2,1)S(1)} %bitcast.140, bf16[2048,640]{1,0:T(8,128)(2,1)S(1)} %bitcast.156), kind=kOutput, calls=%fused_computation.9 | convolution fusion | flops 3356262400 | bytes 9502720 | tf_op jit(solution)/shard_map/tc,te->ce/dot_general | solution.py:1449
  448.6 3.1 collective-permute-done.23
  453.4 1.9 fusion.6
  455.7 1.4 pad_maximum_fusion.3.hidden_ref
  457.1 68.0 %shard_map.192 = (f32[1024,1280]{1,0:T(8,128)}, f32[80,640]{1,0:T(8,128)}, f32[80,640]{1,0:T(8,128)}, f32[80,640]{1,0:T(8,128)}, f32[8,1280]{1,0:T(8,128)}, /*index=5*/f32[80,2560]{1,0:T(8,128)}, f32[80,640]{1,0:T(8,128)}) custom-call(bf16[2048,640]{1,0:T(8,128)(2,1)} %bitcast.133, bf16[2048,640]{1,0:T(8,128)(2,1)} %bitcast.153, ...), custom_call_target="tpu_custom_call" | custom-call | tf_op jit(solution)/shard_map/pallas_call | solution.py:1383
  525.1 1.5 slice_reduce_fusion
  526.6 1.5 copy.75
  528.1 1.9 copy-done.29
  530.1 2.4 copy.76
  (196 shorter events, 33.3 us)
Async XLA Ops:
  1.3 66.9 %copy-start.22 = (f32[1,1280]{1,0:T(1,128)}, f32[1,1280]{1,0:T(1,128)S(1)}, u32[]{:S(2)}) copy-start(f32[1,1280]{1,0:T(1,128)S(1)} %reshape.421.gain_ref) | copy-start | bytes 15364
  69.7 5.7 %copy-start.4 = (bf16[1280,2560]{1,0:T(8,128)(2,1)}, bf16[1280,2560]{1,0:T(8,128)(2,1)S(1)}, u32[]{:S(2)}) copy-start(bf16[1280,2560]{1,0:T(8,128)(2,1)S(1)} %get-tuple-element.99.weights_ref) | copy-start | bytes 19660804
  69.8 5.7 %copy-start.23 = (bf16[2,1024,1280]{2,1,0:T(8,128)(2,1)}, bf16[2,1024,1280]{2,1,0:T(8,128)(2,1)S(1)}, u32[]{:S(2)}) copy-start(bf16[2,1024,1280]{2,1,0:T(8,128)(2,1)S(1)} %get-tuple-element.98) | copy-start | bytes 15728644
  71.3 18.1 %collective-permute-start.3 = (bf16[4,80,1280]{2,1,0:T(8,128)(2,1)}, bf16[4,80,1280]{2,1,0:T(8,128)(2,1)}, u32[]{:S(2)}, u32[]{:S(2)}) collective-permute-start(bf16[4,80,1280]{2,1,0:T(8,128)(2,1)} %get-tuple-element.220), channel_id=1, source_target_pairs={{0,2},{2,0},{4,6},{6,4},{8,10},{10,8},{12,14},{14,12},{16,18},{18,... | collective-permute-start | bytes 2457608 | tf_op jit(solution)/shard_map/ppermute | solution.py:481
  73.1 17.8 %collective-permute-start.2 = (bf16[4,80,1280]{2,1,0:T(8,128)(2,1)}, bf16[4,80,1280]{2,1,0:T(8,128)(2,1)}, u32[]{:S(2)}, u32[]{:S(2)}) collective-permute-start(bf16[4,80,1280]{2,1,0:T(8,128)(2,1)} %get-tuple-element.221), channel_id=1, source_target_pairs={{0,4},{2,6},{4,0},{6,2},{8,12},{10,14},{12,8},{14,10},{16,20},{18,... | collective-permute-start | bytes 2457608 | tf_op jit(solution)/shard_map/ppermute | solution.py:485
  74.4 18.8 %collective-permute-start = (bf16[1280,640]{1,0:T(8,128)(2,1)S(1)}, bf16[1280,640]{1,0:T(8,128)(2,1)}, u32[]{:S(2)}, u32[]{:S(2)}) collective-permute-start(bf16[1280,640]{1,0:T(8,128)(2,1)S(1)} %slice.48), channel_id=1, source_target_pairs={{0,1},{1,0},{2,3},{3,2},{4,5},{5,4},{6,7},{7,6},{8,9},{9,8},{10,11... | collective-permute-start | bytes 4915208 | tf_op jit(solution)/shard_map/ppermute | solution.py:284
  74.5 18.7 %collective-permute-start.1 = (bf16[320,640]{1,0:T(8,128)(2,1)}, bf16[320,640]{1,0:T(8,128)(2,1)}, u32[]{:S(2)}, u32[]{:S(2)}) collective-permute-start(bf16[320,640]{1,0:T(8,128)(2,1)} %param.20), channel_id=1, source_target_pairs={{0,8},{2,10},{4,12},{6,14},{8,24},{10,26},{12,28},{14,30},{24,16},... | collective-permute-start | bytes 1228808 | tf_op jit(solution)/shard_map/ppermute | solution.py:493
  75.4 8.6 %copy-start.53 = (s32[2,1024]{1,0:T(2,128)S(1)}, s32[2,1024]{1,0:T(2,128)}, u32[]{:S(2)}) copy-start(s32[2,1024]{1,0:T(2,128)} %param.12) | copy-start | bytes 24580
  89.5 6.5 %copy-start.24 = (bf16[2,1024,1280]{2,1,0:T(8,128)(2,1)S(1)}, bf16[2,1024,1280]{2,1,0:T(8,128)(2,1)}, u32[]{:S(2)}) copy-start(bf16[2,1024,1280]{2,1,0:T(8,128)(2,1)} %copy-done.23) | copy-start | bytes 15728644
  90.9 12.0 %copy-start.35 = (bf16[2,4,80,1280]{3,2,1,0:T(8,128)(2,1)}, bf16[2,4,80,1280]{3,2,1,0:T(8,128)(2,1)S(1)}, u32[]{:S(2)}) copy-start(bf16[2,4,80,1280]{3,2,1,0:T(8,128)(2,1)S(1)} %pad_maximum_fusion.5.refs_4_) | copy-start | bytes 4915204
  93.1 9.8 %copy-start.36 = (bf16[2,4,80,1280]{3,2,1,0:T(8,128)(2,1)}, bf16[2,4,80,1280]{3,2,1,0:T(8,128)(2,1)S(1)}, u32[]{:S(2)}) copy-start(bf16[2,4,80,1280]{3,2,1,0:T(8,128)(2,1)S(1)} %pad_maximum_fusion.4.refs_2_) | copy-start | bytes 4915204
  93.2 34.9 %collective-permute-start.6 = (bf16[2,4,80,1280]{3,2,1,0:T(8,128)(2,1)S(1)}, bf16[2,4,80,1280]{3,2,1,0:T(8,128)(2,1)S(1)}, u32[]{:S(2)}, u32[]{:S(2)}) collective-permute-start(bf16[2,4,80,1280]{3,2,1,0:T(8,128)(2,1)S(1)} %pad_maximum_fusion.4.refs_2_), channel_id=1, source_target_pairs={{0,2},{2,0},{4,6},{6,4},{8,10},{10,8},{12,14},{14,12},{16,18},{18,... | collective-permute-start | bytes 4915208 | tf_op jit(solution)/shard_map/ppermute | solution.py:481
  94.7 33.9 %collective-permute-start.7 = (bf16[2,4,80,1280]{3,2,1,0:T(8,128)(2,1)S(1)}, bf16[2,4,80,1280]{3,2,1,0:T(8,128)(2,1)S(1)}, u32[]{:S(2)}, u32[]{:S(2)}) collective-permute-start(bf16[2,4,80,1280]{3,2,1,0:T(8,128)(2,1)S(1)} %pad_maximum_fusion.5.refs_4_), channel_id=1, source_target_pairs={{0,4},{2,6},{4,0},{6,2},{8,12},{10,14},{12,8},{14,10},{16,20},{18,... | collective-permute-start | bytes 4915208 | tf_op jit(solution)/shard_map/ppermute | solution.py:485
  95.3 10.8 %collective-permute-start.4 = (bf16[320,640]{1,0:T(8,128)(2,1)}, bf16[320,640]{1,0:T(8,128)(2,1)S(1)}, u32[]{:S(2)}, u32[]{:S(2)}) collective-permute-start(bf16[320,640]{1,0:T(8,128)(2,1)} %collective-permute-done.1), channel_id=1, source_target_pairs={{0,8},{2,10},{4,12},{6,14},{8,24},{10,26},{12,28},{14,30},{24,16},... | collective-permute-start | bytes 1228808 | tf_op jit(solution)/shard_map/ppermute | solution.py:493
  106.1 22.0 %collective-permute-start.5 = (bf16[320,640]{1,0:T(8,128)(2,1)S(1)}, bf16[320,640]{1,0:T(8,128)(2,1)S(1)}, u32[]{:S(2)}, u32[]{:S(2)}) collective-permute-start(bf16[320,640]{1,0:T(8,128)(2,1)S(1)} %collective-permute-done.4), channel_id=1, source_target_pairs={{0,8},{2,10},{4,12},{6,14},{8,24},{10,26},{12,28},{14,30},{24,16},... | collective-permute-start | bytes 1228808 | tf_op jit(solution)/shard_map/ppermute | solution.py:493
  106.6 21.5 %copy-start.17 = (s32[2,1024,128]{2,1,0:T(8,128)}, s32[2,1024,128]{2,1,0:T(8,128)S(1)}, u32[]{:S(2)}) copy-start(s32[2,1024,128]{2,1,0:T(8,128)S(1)} %broadcast_in_dim.4.column_ref) | copy-start | bytes 3145732
  106.6 21.5 %copy-start.20 = (s32[2,8,1024]{2,1,0:T(8,128)}, s32[2,8,1024]{2,1,0:T(8,128)S(1)}, u32[]{:S(2)}) copy-start(s32[2,8,1024]{2,1,0:T(8,128)S(1)} %lt.204.line_ref) | copy-start | bytes 196612
  128.6 4.4 copy-start.56
  130.2 11.3 %collective-permute-start.8 = (bf16[2,512,640]{2,1,0:T(8,128)(2,1)S(1)}, bf16[2,512,640]{2,1,0:T(8,128)(2,1)S(1)}, u32[]{:S(2)}, u32[]{:S(2)}) collective-permute-start(bf16[2,512,640]{2,1,0:T(8,128)(2,1)S(1)} %get-tuple-element.207), channel_id=1, source_target_pairs={{0,1},{1,0},{2,3},{3,2},{4,5},{5,4},{6,7},{7,6},{8,9},{9,8},{10,11... | collective-permute-start | bytes 3932168 | tf_op jit(solution)/shard_map/ppermute | solution.py:284
  133.0 7.1 %copy-start.47 = (bf16[4,160,640]{2,1,0:T(8,128)(2,1)}, bf16[4,160,640]{2,1,0:T(8,128)(2,1)S(1)}, u32[]{:S(2)}) copy-start(bf16[4,160,640]{2,1,0:T(8,128)(2,1)S(1)} %get-tuple-element.212.refs_9_) | copy-start | bytes 2457604
  133.0 21.1 %collective-permute-start.10 = (bf16[4,160,640]{2,1,0:T(8,128)(2,1)S(1)}, bf16[4,160,640]{2,1,0:T(8,128)(2,1)}, u32[]{:S(2)}, u32[]{:S(2)}) collective-permute-start(bf16[4,160,640]{2,1,0:T(8,128)(2,1)S(1)} %get-tuple-element.212.refs_9_), channel_id=1, source_target_pairs={{0,2},{2,0},{4,6},{6,4},{8,10},{10,8},{12,14},{14,12},{16,18},{18,... | collective-permute-start | bytes 2457608 | tf_op jit(solution)/shard_map/ppermute | solution.py:481
  134.3 37.0 %collective-permute-start.12 = (bf16[4,160,640]{2,1,0:T(8,128)(2,1)S(1)}, bf16[4,160,640]{2,1,0:T(8,128)(2,1)}, u32[]{:S(2)}, u32[]{:S(2)}) collective-permute-start(bf16[4,160,640]{2,1,0:T(8,128)(2,1)S(1)} %get-tuple-element.212.refs_9_), channel_id=1, source_target_pairs={{0,4},{2,6},{4,0},{6,2},{8,12},{10,14},{12,8},{14,10},{16,20},{18,... | collective-permute-start | bytes 2457608 | tf_op jit(solution)/shard_map/ppermute | solution.py:485
  134.5 36.8 %collective-permute-start.11 = (bf16[4,160,640]{2,1,0:T(8,128)(2,1)}, bf16[4,160,640]{2,1,0:T(8,128)(2,1)}, u32[]{:S(2)}, u32[]{:S(2)}) collective-permute-start(bf16[4,160,640]{2,1,0:T(8,128)(2,1)} %get-tuple-element.213.refs_6_), channel_id=1, source_target_pairs={{0,2},{2,0},{4,6},{6,4},{8,10},{10,8},{12,14},{14,12},{16,18},{18,... | collective-permute-start | bytes 2457608 | tf_op jit(solution)/shard_map/ppermute | solution.py:481
  136.5 35.8 %collective-permute-start.9 = (bf16[4,160,640]{2,1,0:T(8,128)(2,1)}, bf16[4,160,640]{2,1,0:T(8,128)(2,1)}, u32[]{:S(2)}, u32[]{:S(2)}) collective-permute-start(bf16[4,160,640]{2,1,0:T(8,128)(2,1)} %get-tuple-element.213.refs_6_), channel_id=1, source_target_pairs={{0,4},{2,6},{4,0},{6,2},{8,12},{10,14},{12,8},{14,10},{16,20},{18,... | collective-permute-start | bytes 2457608 | tf_op jit(solution)/shard_map/ppermute | solution.py:485
  143.2 3.7 copy-start.1
  143.2 3.7 copy-start.7
  146.9 3.9 copy-start.25
  277.0 3.7 copy-start.26
  280.7 21.9 %collective-permute-start.13 = (bf16[2560,640]{1,0:T(8,128)(2,1)}, bf16[2560,640]{1,0:T(8,128)(2,1)}, u32[]{:S(2)}, u32[]{:S(2)}) collective-permute-start(bf16[2560,640]{1,0:T(8,128)(2,1)} %constant_dynamic-slice_fusion.8), channel_id=1, source_target_pairs={{0,1},{1,0},{2,3},{3,2},{4,5},{5,4},{6,7},{7,6},{8,9},{9,8},{10,11... | collective-permute-start | bytes 9830408 | tf_op jit(solution)/shard_map/ppermute | solution.py:284
  288.3 12.7 %copy-start.27 = (bf16[2560,1280]{1,0:T(8,128)(2,1)S(1)}, bf16[2560,1280]{1,0:T(8,128)(2,1)}, u32[]{:S(2)}) copy-start(bf16[2560,1280]{1,0:T(8,128)(2,1)} %copy-done.26) | copy-start | bytes 19660804
  300.4 3.6 copy-start.5
  305.5 38.2 %collective-permute-start.15 = (bf16[4,2,160,640]{3,2,0,1:T(8,128)(2,1)S(1)}, bf16[4,2,160,640]{3,2,0,1:T(8,128)(2,1)S(1)}, u32[]{:S(2)}, u32[]{:S(2)}) collective-permute-start(bf16[4,2,160,640]{3,2,0,1:T(8,128)(2,1)S(1)} %pad_maximum_fusion.9), channel_id=1, source_target_pairs={{0,4},{2,6},{4,0},{6,2},{8,12},{10,14},{12,8},{14,10},{16,20},{18,... | collective-permute-start | bytes 4915208 | tf_op jit(solution)/shard_map/ppermute | solution.py:485
  306.1 20.3 %slice-start.2 = ((s8[5242880]{0:T(1024)(128)(4,1)}), s8[4194304]{0:T(1024)(128)(4,1)S(1)}, s32[]{:S(2)}) async-start(s8[5242880]{0:T(1024)(128)(4,1)} %bitcast.161), calls=%async_computation.2 | async-start | bytes 8388608
  306.3 37.9 %collective-permute-start.14 = (bf16[4,2,160,640]{3,2,0,1:T(8,128)(2,1)S(1)}, bf16[4,2,160,640]{3,2,0,1:T(8,128)(2,1)S(1)}, u32[]{:S(2)}, u32[]{:S(2)}) collective-permute-start(bf16[4,2,160,640]{3,2,0,1:T(8,128)(2,1)S(1)} %pad_maximum_fusion.8), channel_id=1, source_target_pairs={{0,2},{2,0},{4,6},{6,4},{8,10},{10,8},{12,14},{14,12},{16,18},{18,... | collective-permute-start | bytes 4915208 | tf_op jit(solution)/shard_map/ppermute | solution.py:481
  307.8 18.6 %copy-start.11 = (bf16[2,1024,640]{2,1,0:T(8,128)(2,1)S(1)}, bf16[2,1024,640]{2,1,0:T(8,128)(2,1)}, u32[]{:S(2)}) copy-start(bf16[2,1024,640]{2,1,0:T(8,128)(2,1)} %copy-done.10) | copy-start | bytes 7864324
  307.8 18.6 %slice-start.3 = ((s8[5242880]{0:T(1024)(128)(4,1)}), s8[1048576]{0:T(1024)(128)(4,1)S(1)}, s32[]{:S(2)}) async-start(s8[5242880]{0:T(1024)(128)(4,1)} %bitcast.161), calls=%async_computation.3 | async-start | bytes 2097152
  326.4 3.9 copy-start.28
  330.2 11.9 %collective-permute-start.16 = (bf16[640,640]{1,0:T(8,128)(2,1)S(1)}, bf16[640,640]{1,0:T(8,128)(2,1)S(1)}, u32[]{:S(2)}, u32[]{:S(2)}) collective-permute-start(bf16[640,640]{1,0:T(8,128)(2,1)S(1)} %get-tuple-element.211), channel_id=1, source_target_pairs={{0,1},{1,0},{2,3},{3,2},{4,5},{5,4},{6,7},{7,6},{8,9},{9,8},{10,11... | collective-permute-start | bytes 2457608 | tf_op jit(solution)/shard_map/ppermute | solution.py:284
  330.3 3.5 copy-start.39
  349.2 5.2 copy-start.30
  349.2 37.8 %collective-permute-start.18 = (bf16[4,1,160,640]{3,2,0,1:T(8,128)(2,1)}, bf16[4,1,160,640]{3,2,0,1:T(8,128)(2,1)}, u32[]{:S(2)}, u32[]{:S(2)}) collective-permute-start(bf16[4,1,160,640]{3,2,0,1:T(8,128)(2,1)} %add_convert_fusion.4), channel_id=1, source_target_pairs={{0,2},{2,0},{4,6},{6,4},{8,10},{10,8},{12,14},{14,12},{16,18},{18,... | collective-permute-start | bytes 2457608 | tf_op jit(solution)/shard_map/ppermute | solution.py:481
  350.7 36.3 %collective-permute-start.17 = (bf16[4,1,160,640]{3,2,0,1:T(8,128)(2,1)}, bf16[4,1,160,640]{3,2,0,1:T(8,128)(2,1)}, u32[]{:S(2)}, u32[]{:S(2)}) collective-permute-start(bf16[4,1,160,640]{3,2,0,1:T(8,128)(2,1)} %add_convert_fusion.5), channel_id=1, source_target_pairs={{0,4},{2,6},{4,0},{6,2},{8,12},{10,14},{12,8},{14,10},{16,20},{18,... | collective-permute-start | bytes 2457608 | tf_op jit(solution)/shard_map/ppermute | solution.py:485
  354.4 3.6 copy-start.18
  354.4 3.6 copy-start.21
  355.9 69.9 %collective-permute-start.21 = (bf16[4,2,80,1664]{3,2,0,1:T(8,128)(2,1)}, bf16[4,2,80,1664]{3,2,0,1:T(8,128)(2,1)S(1)}, u32[]{:S(2)}, u32[]{:S(2)}) collective-permute-start(bf16[4,2,80,1664]{3,2,0,1:T(8,128)(2,1)} %pad_maximum_fusion.2), channel_id=1, source_target_pairs={{0,4},{2,6},{4,0},{6,2},{8,12},{10,14},{12,8},{14,10},{16,20},{18,... | collective-permute-start | bytes 6389768 | tf_op jit(solution)/shard_map/ppermute | solution.py:485
  357.4 68.5 %collective-permute-start.20 = (bf16[4,2,80,1536]{3,2,0,1:T(8,128)(2,1)}, bf16[4,2,80,1536]{3,2,0,1:T(8,128)(2,1)}, u32[]{:S(2)}, u32[]{:S(2)}) collective-permute-start(bf16[4,2,80,1536]{3,2,0,1:T(8,128)(2,1)} %copy_bitcast_fusion), channel_id=1, source_target_pairs={{0,2},{2,0},{4,6},{6,4},{8,10},{10,8},{12,14},{14,12},{16,18},{18,... | collective-permute-start | bytes 5898248 | tf_op jit(solution)/shard_map/ppermute | solution.py:481
  358.0 29.1 %copy-start.38 = (bf16[2,1,160,640]{3,2,0,1:T(8,128)(2,1)S(1)}, bf16[2,1,160,640]{3,2,0,1:T(8,128)(2,1)}, u32[]{:S(2)}) copy-start(bf16[2,1,160,640]{3,2,0,1:T(8,128)(2,1)} %get-tuple-element.198) | copy-start | bytes 1228804
  358.0 29.1 %copy-start.41 = (bf16[4,2,160,640]{3,2,0,1:T(8,128)(2,1)S(1)}, bf16[4,2,160,640]{3,2,0,1:T(8,128)(2,1)}, u32[]{:S(2)}) copy-start(bf16[4,2,160,640]{3,2,0,1:T(8,128)(2,1)} %copy-done.40) | copy-start | bytes 4915204
  358.0 29.1 %copy-start.46 = (bf16[2,1,160,640]{3,2,0,1:T(8,128)(2,1)S(1)}, bf16[2,1,160,640]{3,2,0,1:T(8,128)(2,1)}, u32[]{:S(2)}) copy-start(bf16[2,1,160,640]{3,2,0,1:T(8,128)(2,1)} %get-tuple-element.202) | copy-start | bytes 1228804
  388.9 41.1 %slice-start = ((s8[5242880]{0:T(1024)(128)(4,1)}), s8[4194304]{0:T(1024)(128)(4,1)S(1)}, s32[]{:S(2)}) async-start(s8[5242880]{0:T(1024)(128)(4,1)} %bitcast.136), calls=%async_computation | async-start | bytes 8388608
  390.5 35.1 %collective-permute-start.19 = (bf16[320,640]{1,0:T(8,128)(2,1)S(1)}, bf16[320,640]{1,0:T(8,128)(2,1)S(1)}, u32[]{:S(2)}, u32[]{:S(2)}) collective-permute-start(bf16[320,640]{1,0:T(8,128)(2,1)S(1)} %fusion.12), channel_id=1, source_target_pairs={{0,8},{2,10},{4,12},{6,14},{8,24},{10,26},{12,28},{14,30},{24,16},... | collective-permute-start | bytes 1228808 | tf_op jit(solution)/shard_map/ppermute | solution.py:493
  394.2 35.8 %slice-start.1 = ((s8[5242880]{0:T(1024)(128)(4,1)}), s8[1048576]{0:T(1024)(128)(4,1)S(1)}, s32[]{:S(2)}) async-start(s8[5242880]{0:T(1024)(128)(4,1)} %bitcast.136), calls=%async_computation.1 | async-start | bytes 2097152
  425.6 10.1 %copy-start.16 = (bf16[2,1024,640]{2,1,0:T(8,128)(2,1)}, bf16[2,1024,640]{2,1,0:T(8,128)(2,1)S(1)}, u32[]{:S(2)}) copy-start(bf16[2,1024,640]{2,1,0:T(8,128)(2,1)S(1)} %get-tuple-element.168) | copy-start | bytes 7864324
  425.8 4.2 copy-start.32
  425.8 15.3 %collective-permute-start.22 = (bf16[320,640]{1,0:T(8,128)(2,1)S(1)}, bf16[320,640]{1,0:T(8,128)(2,1)S(1)}, u32[]{:S(2)}, u32[]{:S(2)}) collective-permute-start(bf16[320,640]{1,0:T(8,128)(2,1)S(1)} %fusion.10), channel_id=1, source_target_pairs={{0,8},{2,10},{4,12},{6,14},{8,24},{10,26},{12,28},{14,30},{24,16},... | collective-permute-start | bytes 1228808 | tf_op jit(solution)/shard_map/ppermute | solution.py:493
  428.9 24.4 %collective-permute-start.25 = (bf16[4,1,80,1664]{3,2,0,1:T(8,128)(2,1)S(1)}, bf16[4,1,80,1664]{3,2,0,1:T(8,128)(2,1)S(1)}, u32[]{:S(2)}, u32[]{:S(2)}) collective-permute-start(bf16[4,1,80,1664]{3,2,0,1:T(8,128)(2,1)S(1)} %add_convert_fusion.1), channel_id=1, source_target_pairs={{0,2},{2,0},{4,6},{6,4},{8,10},{10,8},{12,14},{14,12},{16,18},{18,... | collective-permute-start | bytes 3194888 | tf_op jit(solution)/shard_map/ppermute | solution.py:481
  429.1 23.6 %collective-permute-start.24 = (bf16[4,1,80,1536]{3,2,0,1:T(8,128)(2,1)S(1)}, bf16[4,1,80,1536]{3,2,0,1:T(8,128)(2,1)S(1)}, u32[]{:S(2)}, u32[]{:S(2)}) collective-permute-start(bf16[4,1,80,1536]{3,2,0,1:T(8,128)(2,1)S(1)} %fusion.3), channel_id=1, source_target_pairs={{0,4},{2,6},{4,0},{6,2},{8,12},{10,14},{12,8},{14,10},{16,20},{18,... | collective-permute-start | bytes 2949128 | tf_op jit(solution)/shard_map/ppermute | solution.py:485
  435.7 7.4 %copy-start.33 = (bf16[2,1024,640]{2,1,0:T(8,128)(2,1)S(1)}, bf16[2,1024,640]{2,1,0:T(8,128)(2,1)}, u32[]{:S(2)}) copy-start(bf16[2,1024,640]{2,1,0:T(8,128)(2,1)} %get-tuple-element.170) | copy-start | bytes 7864324
  441.2 10.5 %collective-permute-start.23 = (bf16[320,640]{1,0:T(8,128)(2,1)S(1)}, bf16[320,640]{1,0:T(8,128)(2,1)S(1)}, u32[]{:S(2)}, u32[]{:S(2)}) collective-permute-start(bf16[320,640]{1,0:T(8,128)(2,1)S(1)} %fusion.9), channel_id=1, source_target_pairs={{0,8},{2,10},{4,12},{6,14},{8,24},{10,26},{12,28},{14,30},{24,16},... | collective-permute-start | bytes 1228808 | tf_op jit(solution)/shard_map/ppermute | solution.py:493
  457.1 69.5 %copy-start.9 = (bf16[1024,1280]{1,0:T(8,128)(2,1)S(1)}, bf16[1024,1280]{1,0:T(8,128)(2,1)}, u32[]{:S(2)}) copy-start(bf16[1024,1280]{1,0:T(8,128)(2,1)} %copy-done.8) | copy-start | bytes 7864324
  526.6 3.4 copy-start.29
  530.0 3.8 copy-start.50
  530.0 4.5 copy-start.49
  530.0 5.2 copy-start.48
  (23 other events, 43.3 us)

commit v7 on v6

--- a/solution.py
+++ b/solution.py
@@ -914,7 +914,7 @@
     return (3 * zed + 2) % 5
 
 
-NORM_TILE = 64
+NORM_TILE = 128
 
 
 def head_kernel(

time: 542 us -> 543 us (level)
  transfers between devices with their start and end apart: 26 -> 26, of which waited for: 9 -> 7; matrix products, arithmetic and copies ran while one was open for 19% -> 19% of each run, Pallas kernels for 17% -> 18%
where the time goes in v7:
time: 543 us; the launch traced here: 539 us
  Pallas kernels  311 us (57%)
  matrix products  84 us (15%)
  local copies, waits for them, and re-layouts  53.7 us (10%)
  waiting for transfers between devices  33 us (6%)
  other arithmetic  32.4 us (6%)
  starting transfers between devices  23.3 us (4%)
    pallas_call x1, Pallas kernels, feed_forward(): pl.pallas_call(feed_forward_kernel, grid=(2 * tiles,), in_specs=[anywhere...  86.6 us
    pallas_call x3, Pallas kernels, attention_call(): pl.pallas_call(functools.partial(kernel, row, len(begun)), grid_spec=pltp...  84.5 us
    pallas_call x1, Pallas kernels, tail_call(): pl.pallas_call(tail_kernel, in_specs=[anywhere] * 4 + [here] * 3 + [anywh...  68.5 us
    pallas_call x1, Pallas kernels, head_call(): pl.pallas_call(head_kernel, in_specs=[anywhere, pl.BlockSpec(memory_space...  61.3 us
    dot_general x6, matrix products, outer_low(): jnp.einsum('tc,te->ce', left_side, right_side, preferred_element_type=jnp...  56.6 us
    unnamed x129, local copies, waits for them, and re-layouts  29 us
    ppermute x8, waiting for transfers between devices, swap_x(): return lax.ppermute(values, 'rows', [(row, row ^ 1) for row in range(16)])  24.3 us
    dot_general x3, matrix products, dot_low(): return jnp.dot(left_side, right_side, preferred_element_type=jnp.float32)  19.2 us
  transfers between devices with their start and end apart: 26, of which 7 were waited for; matrix products, arithmetic and copies ran while one was open for 19% of the time, Pallas kernels for 18%

profile of v7, /device:TPU:0, one launch (start us, length us, event | category | flops | bytes accessed | tf_op | source)
XLA Modules:
  0.0 539.5 jit_solution(5505455169485264133)
XLA Ops:
  2.4 1.7 copy-done
  4.2 1.7 copy-done.2
  6.9 61.3 %shard_map.186 = (bf16[2,1024,1280]{2,1,0:T(8,128)(2,1)S(1)}, bf16[2,512,1280]{2,1,0:T(8,128)(2,1)S(1)}, bf16[1280,2560]{1,0:T(8,128)(2,1)S(1)}, bf16[4,80,2560]{2,1,0:T(8,128)(2,1)S(1)}) custom-call(bf16[2,512,1280]{2,1,0:T(8,128)(2,1)S(1)} %copy-done.2, f32[1,1280]{1,0:T(1,128)S(1)} %reshape.421.gain_ref, bf16[2,512,1280]{2,1,0:T(8,128)(2,1)S(1)} %copy-done, ...), custom_call_target="tpu_custom_call" | custom-call | tf_op jit(solution)/shard_map/pallas_call | solution.py:1069
  68.3 1.5 copy-done.6
  69.8 1.6 slice_bitcast_fusion
  71.3 1.8 collective-permute-start.3
  75.4 8.6 %convolution_convert_fusion.2 = bf16[2048,1280]{1,0:T(8,128)(2,1)} fusion(bf16[2048,1280]{1,0:T(8,128)(2,1)S(1)} %bitcast.134, bf16[1280,2560]{1,0:T(8,128)(2,1)S(1)} %get-tuple-element.99.weights_ref), kind=kOutput, calls=%fused_computation.2 | convolution fusion | flops 6713507840 | bytes 13762560 | tf_op jit(solution)/shard_map/dot_general | solution.py:1445
  84.5 5.0 collective-permute-done.3
  89.5 1.4 pad_maximum_fusion.5.refs_4_
  90.9 2.2 pad_maximum_fusion.4.refs_2_
  93.2 1.6 collective-permute-start.6
  96.0 7.0 %convolution_convert_fusion.8 = bf16[2048,640]{1,0:T(8,128)(2,1)} fusion(bf16[2048,1280]{1,0:T(8,128)(2,1)S(1)} %bitcast.135, bf16[1280,2560]{1,0:T(8,128)(2,1)} %copy-done.4), kind=kOutput, calls=%fused_computation.14 | convolution fusion | flops 3356753920 | bytes 9502720 | tf_op jit(solution)/shard_map/dot_general | solution.py:1445
  102.9 3.2 collective-permute-done.4
  106.6 22.3 %shard_map.187 = bf16[2,1024,640]{2,1,0:T(8,128)(2,1)S(1)} custom-call(s32[2,8]{1,0:T(2,128)S(1)} %get-tuple-element.195.start_ref, s32[2,8]{1,0:T(2,128)S(1)} %get-tuple-element.194.count_ref, s32[2,1024,128]{2,1,0:T(8,128)S(1)} %broadcast_in_dim.4.column_ref, s32[2,8,1024]{2,1,0:T(8,128)S(1)} %lt.204.line_ref, bf16[2,1024,1280]{2,1,0:T(8,128)(2,1)} %bitcast.164, ...), custom_call_target="tpu_custom_call" | custom-call | flops 16106127360 | bytes 10485760 | tf_op jit(solution)/shard_map/pallas_call | solution.py:433
  131.0 1.4 pad_maximum_fusion.6
  135.9 2.0 collective-permute-start.9
  137.9 3.1 maximum_select_fusion
  141.0 1.3 constant_dynamic-slice_fusion.10
  144.1 3.7 fusion.22
  147.8 2.9 pad_maximum_fusion.refs_1_
  151.6 2.2 multiply_convert_fusion.refs_0_
  153.8 1.2 collective-permute-done.10.refs_10_
  155.0 17.2 %collective-permute-done.11.refs_8_ = bf16[4,160,640]{2,1,0:T(8,128)(2,1)} collective-permute-done((bf16[4,160,640]{2,1,0:T(8,128)(2,1)}, bf16[4,160,640]{2,1,0:T(8,128)(2,1)}, u32[]{:S(2)}, u32[]{:S(2)}) %collective-permute-start.11) | collective-permute-done | bytes 819232 | tf_op jit(solution)/shard_map/ppermute | solution.py:481
  172.8 86.6 %shard_map.188 = (bf16[2048,2560]{1,0:T(8,128)(2,1)}, bf16[2048,2560]{1,0:T(8,128)(2,1)}, bf16[1024,1280]{1,0:T(8,128)(2,1)}, bf16[1024,1280]{1,0:T(8,128)(2,1)}...) custom-call(bf16[1024,1280]{1,0:T(8,128)(2,1)} %multiply_convert_fusion.refs_0_, ...), custom_call_target="tpu_custom_call" | custom-call | flops 53687091200 | bytes 55050240 | tf_op jit(solution)/shard_map/pallas_call | solution.py:775
  259.4 17.9 %convolution_convert_fusion.1 = bf16[2560,1280]{1,0:T(8,128)(2,1)S(1)} fusion(bf16[2048,2560]{1,0:T(8,128)(2,1)} %get-tuple-element.132, bf16[2048,1280]{1,0:T(8,128)(2,1)} %pad_maximum_fusion.refs_1_), kind=kOutput, calls=%fused_computation.1 | convolution fusion | flops 13425049600 | bytes 22282240 | tf_op jit(solution)/shard_map/tc,te->ce/dot_general | solution.py:1449
  277.3 2.2 constant_dynamic-slice_fusion.8
  279.5 1.5 copy-done.26
  281.6 1.7 copy-done.12
  283.3 1.7 copy-done.13
  285.0 1.7 copy-done.14
  286.8 1.7 copy-done.15
  288.5 10.5 %shard_map.189 = (bf16[1024,1280]{1,0:T(8,128)(2,1)S(1)}, f32[1024,1280]{1,0:T(8,128)S(1)}, f32[8,1280]{1,0:T(8,128)S(1)}, bf16[2,1024,1280]{2,1,0:T(8,128)(2,1)}) custom-call(f32[1024,1280]{1,0:T(8,128)} %copy-done.25, bf16[1024,1280]{1,0:T(8,128)(2,1)S(1)} %bitcast.126, bf16[1024,1280]{1,0:T(8,128)(2,1)S(1)} %copy-done.12, ...), custom_call_target="tpu_custom_call" | custom-call | tf_op jit(solution)/shard_map/pallas_call | solution.py:881
  299.1 1.5 copy-done.8
  301.3 1.6 dynamic-slice_bitcast_fusion.5
  302.9 1.3 copy_bitcast_fusion.3
  304.2 1.3 copy_bitcast_fusion.5
  305.7 1.2 collective-permute-start.15
  308.1 18.5 %convolution_convert_fusion = bf16[1280,2560]{1,0:T(8,128)(2,1)S(1)} fusion(bf16[2048,1280]{1,0:T(8,128)(2,1)} %get-tuple-element.136, bf16[2048,2560]{1,0:T(8,128)(2,1)} %get-tuple-element.142), kind=kOutput, calls=%fused_computation | convolution fusion | flops 13425049600 | bytes 22282240 | tf_op jit(solution)/shard_map/tc,te->ce/dot_general | solution.py:1449
  326.7 3.6 convolution_convert_fusion.6
  331.7 2.4 dynamic-slice_bitcast_fusion.4
  334.2 8.3 %convolution_convert_fusion.7 = bf16[2048,640]{1,0:T(8,128)(2,1)} fusion(bf16[2048,1280]{1,0:T(8,128)(2,1)} %bitcast.160, bf16[640,1280]{1,0:T(8,128)(2,1)S(1)} %copy-done.39), kind=kOutput, calls=%fused_computation.13 | convolution fusion | flops 3356753920 | bytes 9502720 | tf_op jit(solution)/shard_map/te,de->td/dot_general | solution.py:30
  345.0 1.3 add_convert_fusion.4
  347.5 2.5 copy_bitcast_fusion.1
  351.0 1.1 collective-permute-start.17
  352.1 3.1 copy_bitcast_fusion
  355.2 1.5 pad_maximum_fusion.2
  357.7 1.2 collective-permute-start.20
  358.8 32.1 %shard_map.190 = (bf16[2,1024,640]{2,1,0:T(8,128)(2,1)S(1)}, bf16[2,1024,640]{2,1,0:T(8,128)(2,1)}, bf16[2,1024,640]{2,1,0:T(8,128)(2,1)}) custom-call(s32[2,4]{1,0:T(2,128)S(1)} %get-tuple-element.193.start_ref, s32[2,4]{1,0:T(2,128)S(1)} %get-tuple-element.192.count_ref, s32[2,1024,128]{2,1,0:T(8,128)S(1)} %copy-done.18, s32[2,8,1024]{2,1,0:T(8,128)S(1)} %copy-done.21, ...), custom_call_target="tpu_custom_call" | custom-call | flops 10737418240 | bytes 9175040 | tf_op jit(solution)/shard_map/pallas_call | solution.py:433
  391.0 1.6 fusion.8
  392.8 1.6 fusion.7
  394.6 30.0 %shard_map.191 = (bf16[2,1024,640]{2,1,0:T(8,128)(2,1)S(1)}, bf16[2,1024,640]{2,1,0:T(8,128)(2,1)}, bf16[2,1024,640]{2,1,0:T(8,128)(2,1)}) custom-call(s32[2,4]{1,0:T(2,128)S(1)} %get-tuple-element.193.start_ref, s32[2,4]{1,0:T(2,128)S(1)} %get-tuple-element.192.count_ref, ...), custom_call_target="tpu_custom_call", output_to_operand_aliasing={{0}: (8, {}), {1}: (9, {}), {2}: (10, {})} | custom-call | flops 10737418240 | bytes 9175040 | tf_op jit(solution)/shard_map/pallas_call | solution.py:433
  424.8 2.8 fusion.3
  427.9 4.3 collective-permute-start.25
  433.2 5.5 %convolution_convert_fusion.4.key_ref = bf16[1280,640]{1,0:T(8,128)(2,1)} fusion(bf16[2048,1280]{1,0:T(8,128)(2,1)S(1)} %bitcast.138, bf16[2048,640]{1,0:T(8,128)(2,1)S(1)} %bitcast.154), kind=kOutput, calls=%fused_computation.10 | convolution fusion | flops 3356262400 | bytes 9502720 | tf_op jit(solution)/shard_map/tc,te->ce/dot_general | solution.py:1449
  438.6 5.4 %convolution_convert_fusion.5.query_ref = bf16[1280,640]{1,0:T(8,128)(2,1)} fusion(bf16[2048,1280]{1,0:T(8,128)(2,1)S(1)} %bitcast.139, bf16[2048,640]{1,0:T(8,128)(2,1)S(1)} %bitcast.132), kind=kOutput, calls=%fused_computation.11 | convolution fusion | flops 3356262400 | bytes 9502720 | tf_op jit(solution)/shard_map/tc,te->ce/dot_general | solution.py:1449
  444.5 5.7 %convolution_convert_fusion.3.value_ref = bf16[1280,640]{1,0:T(8,128)(2,1)} fusion(bf16[2048,1280]{1,0:T(8,128)(2,1)S(1)} %bitcast.140, bf16[2048,640]{1,0:T(8,128)(2,1)S(1)} %bitcast.156), kind=kOutput, calls=%fused_computation.9 | convolution fusion | flops 3356262400 | bytes 9502720 | tf_op jit(solution)/shard_map/tc,te->ce/dot_general | solution.py:1449
  450.2 4.8 collective-permute-done.23
  456.0 1.9 fusion.6
  458.4 1.4 pad_maximum_fusion.3.hidden_ref
  459.8 68.5 %shard_map.192 = (f32[1024,1280]{1,0:T(8,128)}, f32[80,640]{1,0:T(8,128)}, f32[80,640]{1,0:T(8,128)}, f32[80,640]{1,0:T(8,128)}, f32[8,1280]{1,0:T(8,128)}, /*index=5*/f32[80,2560]{1,0:T(8,128)}, f32[80,640]{1,0:T(8,128)}) custom-call(bf16[2048,640]{1,0:T(8,128)(2,1)} %bitcast.133, bf16[2048,640]{1,0:T(8,128)(2,1)} %bitcast.153, ...), custom_call_target="tpu_custom_call" | custom-call | tf_op jit(solution)/shard_map/pallas_call | solution.py:1383
  528.3 1.5 slice_reduce_fusion
  529.8 1.5 copy.75
  531.2 1.9 copy-done.29
  533.2 2.4 copy.76
  (196 shorter events, 33.0 us)
Async XLA Ops:
  1.3 66.9 %copy-start.22 = (f32[1,1280]{1,0:T(1,128)}, f32[1,1280]{1,0:T(1,128)S(1)}, u32[]{:S(2)}) copy-start(f32[1,1280]{1,0:T(1,128)S(1)} %reshape.421.gain_ref) | copy-start | bytes 15364
  69.7 5.7 %copy-start.4 = (bf16[1280,2560]{1,0:T(8,128)(2,1)}, bf16[1280,2560]{1,0:T(8,128)(2,1)S(1)}, u32[]{:S(2)}) copy-start(bf16[1280,2560]{1,0:T(8,128)(2,1)S(1)} %get-tuple-element.99.weights_ref) | copy-start | bytes 19660804
  69.8 5.7 %copy-start.23 = (bf16[2,1024,1280]{2,1,0:T(8,128)(2,1)}, bf16[2,1024,1280]{2,1,0:T(8,128)(2,1)S(1)}, u32[]{:S(2)}) copy-start(bf16[2,1024,1280]{2,1,0:T(8,128)(2,1)S(1)} %get-tuple-element.98) | copy-start | bytes 15728644
  71.3 18.1 %collective-permute-start.3 = (bf16[4,80,1280]{2,1,0:T(8,128)(2,1)}, bf16[4,80,1280]{2,1,0:T(8,128)(2,1)}, u32[]{:S(2)}, u32[]{:S(2)}) collective-permute-start(bf16[4,80,1280]{2,1,0:T(8,128)(2,1)} %get-tuple-element.220), channel_id=1, source_target_pairs={{0,2},{2,0},{4,6},{6,4},{8,10},{10,8},{12,14},{14,12},{16,18},{18,... | collective-permute-start | bytes 2457608 | tf_op jit(solution)/shard_map/ppermute | solution.py:481
  73.1 17.8 %collective-permute-start.2 = (bf16[4,80,1280]{2,1,0:T(8,128)(2,1)}, bf16[4,80,1280]{2,1,0:T(8,128)(2,1)}, u32[]{:S(2)}, u32[]{:S(2)}) collective-permute-start(bf16[4,80,1280]{2,1,0:T(8,128)(2,1)} %get-tuple-element.221), channel_id=1, source_target_pairs={{0,4},{2,6},{4,0},{6,2},{8,12},{10,14},{12,8},{14,10},{16,20},{18,... | collective-permute-start | bytes 2457608 | tf_op jit(solution)/shard_map/ppermute | solution.py:485
  74.4 18.8 %collective-permute-start = (bf16[1280,640]{1,0:T(8,128)(2,1)S(1)}, bf16[1280,640]{1,0:T(8,128)(2,1)}, u32[]{:S(2)}, u32[]{:S(2)}) collective-permute-start(bf16[1280,640]{1,0:T(8,128)(2,1)S(1)} %slice.48), channel_id=1, source_target_pairs={{0,1},{1,0},{2,3},{3,2},{4,5},{5,4},{6,7},{7,6},{8,9},{9,8},{10,11... | collective-permute-start | bytes 4915208 | tf_op jit(solution)/shard_map/ppermute | solution.py:284
  74.5 18.7 %collective-permute-start.1 = (bf16[320,640]{1,0:T(8,128)(2,1)}, bf16[320,640]{1,0:T(8,128)(2,1)}, u32[]{:S(2)}, u32[]{:S(2)}) collective-permute-start(bf16[320,640]{1,0:T(8,128)(2,1)} %param.20), channel_id=1, source_target_pairs={{0,8},{2,10},{4,12},{6,14},{8,24},{10,26},{12,28},{14,30},{24,16},... | collective-permute-start | bytes 1228808 | tf_op jit(solution)/shard_map/ppermute | solution.py:493
  75.4 8.6 %copy-start.53 = (s32[2,1024]{1,0:T(2,128)S(1)}, s32[2,1024]{1,0:T(2,128)}, u32[]{:S(2)}) copy-start(s32[2,1024]{1,0:T(2,128)} %param.12) | copy-start | bytes 24580
  89.5 6.5 %copy-start.24 = (bf16[2,1024,1280]{2,1,0:T(8,128)(2,1)S(1)}, bf16[2,1024,1280]{2,1,0:T(8,128)(2,1)}, u32[]{:S(2)}) copy-start(bf16[2,1024,1280]{2,1,0:T(8,128)(2,1)} %copy-done.23) | copy-start | bytes 15728644
  90.9 12.0 %copy-start.35 = (bf16[2,4,80,1280]{3,2,1,0:T(8,128)(2,1)}, bf16[2,4,80,1280]{3,2,1,0:T(8,128)(2,1)S(1)}, u32[]{:S(2)}) copy-start(bf16[2,4,80,1280]{3,2,1,0:T(8,128)(2,1)S(1)} %pad_maximum_fusion.5.refs_4_) | copy-start | bytes 4915204
  93.1 9.8 %copy-start.36 = (bf16[2,4,80,1280]{3,2,1,0:T(8,128)(2,1)}, bf16[2,4,80,1280]{3,2,1,0:T(8,128)(2,1)S(1)}, u32[]{:S(2)}) copy-start(bf16[2,4,80,1280]{3,2,1,0:T(8,128)(2,1)S(1)} %pad_maximum_fusion.4.refs_2_) | copy-start | bytes 4915204
  93.2 35.8 %collective-permute-start.6 = (bf16[2,4,80,1280]{3,2,1,0:T(8,128)(2,1)S(1)}, bf16[2,4,80,1280]{3,2,1,0:T(8,128)(2,1)S(1)}, u32[]{:S(2)}, u32[]{:S(2)}) collective-permute-start(bf16[2,4,80,1280]{3,2,1,0:T(8,128)(2,1)S(1)} %pad_maximum_fusion.4.refs_2_), channel_id=1, source_target_pairs={{0,2},{2,0},{4,6},{6,4},{8,10},{10,8},{12,14},{14,12},{16,18},{18,... | collective-permute-start | bytes 4915208 | tf_op jit(solution)/shard_map/ppermute | solution.py:481
  94.7 34.3 %collective-permute-start.7 = (bf16[2,4,80,1280]{3,2,1,0:T(8,128)(2,1)S(1)}, bf16[2,4,80,1280]{3,2,1,0:T(8,128)(2,1)S(1)}, u32[]{:S(2)}, u32[]{:S(2)}) collective-permute-start(bf16[2,4,80,1280]{3,2,1,0:T(8,128)(2,1)S(1)} %pad_maximum_fusion.5.refs_4_), channel_id=1, source_target_pairs={{0,4},{2,6},{4,0},{6,2},{8,12},{10,14},{12,8},{14,10},{16,20},{18,... | collective-permute-start | bytes 4915208 | tf_op jit(solution)/shard_map/ppermute | solution.py:485
  95.3 10.8 %collective-permute-start.4 = (bf16[320,640]{1,0:T(8,128)(2,1)}, bf16[320,640]{1,0:T(8,128)(2,1)S(1)}, u32[]{:S(2)}, u32[]{:S(2)}) collective-permute-start(bf16[320,640]{1,0:T(8,128)(2,1)} %collective-permute-done.1), channel_id=1, source_target_pairs={{0,8},{2,10},{4,12},{6,14},{8,24},{10,26},{12,28},{14,30},{24,16},... | collective-permute-start | bytes 1228808 | tf_op jit(solution)/shard_map/ppermute | solution.py:493
  106.1 22.9 %collective-permute-start.5 = (bf16[320,640]{1,0:T(8,128)(2,1)S(1)}, bf16[320,640]{1,0:T(8,128)(2,1)S(1)}, u32[]{:S(2)}, u32[]{:S(2)}) collective-permute-start(bf16[320,640]{1,0:T(8,128)(2,1)S(1)} %collective-permute-done.4), channel_id=1, source_target_pairs={{0,8},{2,10},{4,12},{6,14},{8,24},{10,26},{12,28},{14,30},{24,16},... | collective-permute-start | bytes 1228808 | tf_op jit(solution)/shard_map/ppermute | solution.py:493
  106.6 22.4 %copy-start.17 = (s32[2,1024,128]{2,1,0:T(8,128)}, s32[2,1024,128]{2,1,0:T(8,128)S(1)}, u32[]{:S(2)}) copy-start(s32[2,1024,128]{2,1,0:T(8,128)S(1)} %broadcast_in_dim.4.column_ref) | copy-start | bytes 3145732
  106.6 22.4 %copy-start.20 = (s32[2,8,1024]{2,1,0:T(8,128)}, s32[2,8,1024]{2,1,0:T(8,128)S(1)}, u32[]{:S(2)}) copy-start(s32[2,8,1024]{2,1,0:T(8,128)S(1)} %lt.204.line_ref) | copy-start | bytes 196612
  129.0 4.8 copy-start.56
  131.0 11.3 %collective-permute-start.8 = (bf16[2,512,640]{2,1,0:T(8,128)(2,1)S(1)}, bf16[2,512,640]{2,1,0:T(8,128)(2,1)S(1)}, u32[]{:S(2)}, u32[]{:S(2)}) collective-permute-start(bf16[2,512,640]{2,1,0:T(8,128)(2,1)S(1)} %get-tuple-element.207), channel_id=1, source_target_pairs={{0,1},{1,0},{2,3},{3,2},{4,5},{5,4},{6,7},{7,6},{8,9},{9,8},{10,11... | collective-permute-start | bytes 3932168 | tf_op jit(solution)/shard_map/ppermute | solution.py:284
  133.9 7.1 %copy-start.47 = (bf16[4,160,640]{2,1,0:T(8,128)(2,1)}, bf16[4,160,640]{2,1,0:T(8,128)(2,1)S(1)}, u32[]{:S(2)}) copy-start(bf16[4,160,640]{2,1,0:T(8,128)(2,1)S(1)} %get-tuple-element.212.refs_9_) | copy-start | bytes 2457604
  133.9 21.1 %collective-permute-start.10 = (bf16[4,160,640]{2,1,0:T(8,128)(2,1)S(1)}, bf16[4,160,640]{2,1,0:T(8,128)(2,1)}, u32[]{:S(2)}, u32[]{:S(2)}) collective-permute-start(bf16[4,160,640]{2,1,0:T(8,128)(2,1)S(1)} %get-tuple-element.212.refs_9_), channel_id=1, source_target_pairs={{0,2},{2,0},{4,6},{6,4},{8,10},{10,8},{12,14},{14,12},{16,18},{18,... | collective-permute-start | bytes 2457608 | tf_op jit(solution)/shard_map/ppermute | solution.py:481
  134.7 37.4 %collective-permute-start.12 = (bf16[4,160,640]{2,1,0:T(8,128)(2,1)S(1)}, bf16[4,160,640]{2,1,0:T(8,128)(2,1)}, u32[]{:S(2)}, u32[]{:S(2)}) collective-permute-start(bf16[4,160,640]{2,1,0:T(8,128)(2,1)S(1)} %get-tuple-element.212.refs_9_), channel_id=1, source_target_pairs={{0,4},{2,6},{4,0},{6,2},{8,12},{10,14},{12,8},{14,10},{16,20},{18,... | collective-permute-start | bytes 2457608 | tf_op jit(solution)/shard_map/ppermute | solution.py:485
  135.9 36.3 %collective-permute-start.11 = (bf16[4,160,640]{2,1,0:T(8,128)(2,1)}, bf16[4,160,640]{2,1,0:T(8,128)(2,1)}, u32[]{:S(2)}, u32[]{:S(2)}) collective-permute-start(bf16[4,160,640]{2,1,0:T(8,128)(2,1)} %get-tuple-element.213.refs_6_), channel_id=1, source_target_pairs={{0,2},{2,0},{4,6},{6,4},{8,10},{10,8},{12,14},{14,12},{16,18},{18,... | collective-permute-start | bytes 2457608 | tf_op jit(solution)/shard_map/ppermute | solution.py:481
  135.9 36.8 %collective-permute-start.9 = (bf16[4,160,640]{2,1,0:T(8,128)(2,1)}, bf16[4,160,640]{2,1,0:T(8,128)(2,1)}, u32[]{:S(2)}, u32[]{:S(2)}) collective-permute-start(bf16[4,160,640]{2,1,0:T(8,128)(2,1)} %get-tuple-element.213.refs_6_), channel_id=1, source_target_pairs={{0,4},{2,6},{4,0},{6,2},{8,12},{10,14},{12,8},{14,10},{16,20},{18,... | collective-permute-start | bytes 2457608 | tf_op jit(solution)/shard_map/ppermute | solution.py:485
  144.1 3.7 copy-start.1
  144.1 3.7 copy-start.7
  147.7 3.9 copy-start.25
  277.3 3.7 copy-start.26
  280.9 21.9 %collective-permute-start.13 = (bf16[2560,640]{1,0:T(8,128)(2,1)}, bf16[2560,640]{1,0:T(8,128)(2,1)}, u32[]{:S(2)}, u32[]{:S(2)}) collective-permute-start(bf16[2560,640]{1,0:T(8,128)(2,1)} %constant_dynamic-slice_fusion.8), channel_id=1, source_target_pairs={{0,1},{1,0},{2,3},{3,2},{4,5},{5,4},{6,7},{7,6},{8,9},{9,8},{10,11... | collective-permute-start | bytes 9830408 | tf_op jit(solution)/shard_map/ppermute | solution.py:284
  288.5 12.7 %copy-start.27 = (bf16[2560,1280]{1,0:T(8,128)(2,1)S(1)}, bf16[2560,1280]{1,0:T(8,128)(2,1)}, u32[]{:S(2)}) copy-start(bf16[2560,1280]{1,0:T(8,128)(2,1)} %copy-done.26) | copy-start | bytes 19660804
  300.6 3.6 copy-start.5
  305.7 38.3 %collective-permute-start.15 = (bf16[4,2,160,640]{3,2,0,1:T(8,128)(2,1)S(1)}, bf16[4,2,160,640]{3,2,0,1:T(8,128)(2,1)S(1)}, u32[]{:S(2)}, u32[]{:S(2)}) collective-permute-start(bf16[4,2,160,640]{3,2,0,1:T(8,128)(2,1)S(1)} %pad_maximum_fusion.9), channel_id=1, source_target_pairs={{0,4},{2,6},{4,0},{6,2},{8,12},{10,14},{12,8},{14,10},{16,20},{18,... | collective-permute-start | bytes 4915208 | tf_op jit(solution)/shard_map/ppermute | solution.py:485
  307.0 19.7 %slice-start.2 = ((s8[5242880]{0:T(1024)(128)(4,1)}), s8[4194304]{0:T(1024)(128)(4,1)S(1)}, s32[]{:S(2)}) async-start(s8[5242880]{0:T(1024)(128)(4,1)} %bitcast.161), calls=%async_computation.2 | async-start | bytes 8388608
  307.1 37.9 %collective-permute-start.14 = (bf16[4,2,160,640]{3,2,0,1:T(8,128)(2,1)S(1)}, bf16[4,2,160,640]{3,2,0,1:T(8,128)(2,1)S(1)}, u32[]{:S(2)}, u32[]{:S(2)}) collective-permute-start(bf16[4,2,160,640]{3,2,0,1:T(8,128)(2,1)S(1)} %pad_maximum_fusion.8), channel_id=1, source_target_pairs={{0,2},{2,0},{4,6},{6,4},{8,10},{10,8},{12,14},{14,12},{16,18},{18,... | collective-permute-start | bytes 4915208 | tf_op jit(solution)/shard_map/ppermute | solution.py:481
  308.1 18.6 %copy-start.11 = (bf16[2,1024,640]{2,1,0:T(8,128)(2,1)S(1)}, bf16[2,1024,640]{2,1,0:T(8,128)(2,1)}, u32[]{:S(2)}) copy-start(bf16[2,1024,640]{2,1,0:T(8,128)(2,1)} %copy-done.10) | copy-start | bytes 7864324
  308.1 18.6 %slice-start.3 = ((s8[5242880]{0:T(1024)(128)(4,1)}), s8[1048576]{0:T(1024)(128)(4,1)S(1)}, s32[]{:S(2)}) async-start(s8[5242880]{0:T(1024)(128)(4,1)} %bitcast.161), calls=%async_computation.3 | async-start | bytes 2097152
  326.6 4.0 copy-start.28
  330.5 12.0 %collective-permute-start.16 = (bf16[640,640]{1,0:T(8,128)(2,1)S(1)}, bf16[640,640]{1,0:T(8,128)(2,1)S(1)}, u32[]{:S(2)}, u32[]{:S(2)}) collective-permute-start(bf16[640,640]{1,0:T(8,128)(2,1)S(1)} %get-tuple-element.211), channel_id=1, source_target_pairs={{0,1},{1,0},{2,3},{3,2},{4,5},{5,4},{6,7},{7,6},{8,9},{9,8},{10,11... | collective-permute-start | bytes 2457608 | tf_op jit(solution)/shard_map/ppermute | solution.py:284
  330.7 3.5 copy-start.39
  350.0 5.2 copy-start.30
  350.1 40.9 %collective-permute-start.18 = (bf16[4,1,160,640]{3,2,0,1:T(8,128)(2,1)}, bf16[4,1,160,640]{3,2,0,1:T(8,128)(2,1)}, u32[]{:S(2)}, u32[]{:S(2)}) collective-permute-start(bf16[4,1,160,640]{3,2,0,1:T(8,128)(2,1)} %add_convert_fusion.4), channel_id=1, source_target_pairs={{0,2},{2,0},{4,6},{6,4},{8,10},{10,8},{12,14},{14,12},{16,18},{18,... | collective-permute-start | bytes 2457608 | tf_op jit(solution)/shard_map/ppermute | solution.py:481
  351.0 40.0 %collective-permute-start.17 = (bf16[4,1,160,640]{3,2,0,1:T(8,128)(2,1)}, bf16[4,1,160,640]{3,2,0,1:T(8,128)(2,1)}, u32[]{:S(2)}, u32[]{:S(2)}) collective-permute-start(bf16[4,1,160,640]{3,2,0,1:T(8,128)(2,1)} %add_convert_fusion.5), channel_id=1, source_target_pairs={{0,4},{2,6},{4,0},{6,2},{8,12},{10,14},{12,8},{14,10},{16,20},{18,... | collective-permute-start | bytes 2457608 | tf_op jit(solution)/shard_map/ppermute | solution.py:485
  355.2 3.6 copy-start.18
  355.2 3.6 copy-start.21
  356.8 68.1 %collective-permute-start.21 = (bf16[4,2,80,1664]{3,2,0,1:T(8,128)(2,1)}, bf16[4,2,80,1664]{3,2,0,1:T(8,128)(2,1)S(1)}, u32[]{:S(2)}, u32[]{:S(2)}) collective-permute-start(bf16[4,2,80,1664]{3,2,0,1:T(8,128)(2,1)} %pad_maximum_fusion.2), channel_id=1, source_target_pairs={{0,4},{2,6},{4,0},{6,2},{8,12},{10,14},{12,8},{14,10},{16,20},{18,... | collective-permute-start | bytes 6389768 | tf_op jit(solution)/shard_map/ppermute | solution.py:485
  357.7 67.2 %collective-permute-start.20 = (bf16[4,2,80,1536]{3,2,0,1:T(8,128)(2,1)}, bf16[4,2,80,1536]{3,2,0,1:T(8,128)(2,1)}, u32[]{:S(2)}, u32[]{:S(2)}) collective-permute-start(bf16[4,2,80,1536]{3,2,0,1:T(8,128)(2,1)} %copy_bitcast_fusion), channel_id=1, source_target_pairs={{0,2},{2,0},{4,6},{6,4},{8,10},{10,8},{12,14},{14,12},{16,18},{18,... | collective-permute-start | bytes 5898248 | tf_op jit(solution)/shard_map/ppermute | solution.py:481
  358.8 32.2 %copy-start.38 = (bf16[2,1,160,640]{3,2,0,1:T(8,128)(2,1)S(1)}, bf16[2,1,160,640]{3,2,0,1:T(8,128)(2,1)}, u32[]{:S(2)}) copy-start(bf16[2,1,160,640]{3,2,0,1:T(8,128)(2,1)} %get-tuple-element.198) | copy-start | bytes 1228804
  358.8 32.2 %copy-start.41 = (bf16[4,2,160,640]{3,2,0,1:T(8,128)(2,1)S(1)}, bf16[4,2,160,640]{3,2,0,1:T(8,128)(2,1)}, u32[]{:S(2)}) copy-start(bf16[4,2,160,640]{3,2,0,1:T(8,128)(2,1)} %copy-done.40) | copy-start | bytes 4915204
  358.8 32.2 %copy-start.46 = (bf16[2,1,160,640]{3,2,0,1:T(8,128)(2,1)S(1)}, bf16[2,1,160,640]{3,2,0,1:T(8,128)(2,1)}, u32[]{:S(2)}) copy-start(bf16[2,1,160,640]{3,2,0,1:T(8,128)(2,1)} %get-tuple-element.202) | copy-start | bytes 1228804
  392.8 40.3 %slice-start = ((s8[5242880]{0:T(1024)(128)(4,1)}), s8[4194304]{0:T(1024)(128)(4,1)S(1)}, s32[]{:S(2)}) async-start(s8[5242880]{0:T(1024)(128)(4,1)} %bitcast.136), calls=%async_computation | async-start | bytes 8388608
  394.5 30.1 %collective-permute-start.19 = (bf16[320,640]{1,0:T(8,128)(2,1)S(1)}, bf16[320,640]{1,0:T(8,128)(2,1)S(1)}, u32[]{:S(2)}, u32[]{:S(2)}) collective-permute-start(bf16[320,640]{1,0:T(8,128)(2,1)S(1)} %fusion.12), channel_id=1, source_target_pairs={{0,8},{2,10},{4,12},{6,14},{8,24},{10,26},{12,28},{14,30},{24,16},... | collective-permute-start | bytes 1228808 | tf_op jit(solution)/shard_map/ppermute | solution.py:493
  394.6 38.6 %slice-start.1 = ((s8[5242880]{0:T(1024)(128)(4,1)}), s8[1048576]{0:T(1024)(128)(4,1)S(1)}, s32[]{:S(2)}) async-start(s8[5242880]{0:T(1024)(128)(4,1)} %bitcast.136), calls=%async_computation.1 | async-start | bytes 2097152
  424.6 14.0 %copy-start.16 = (bf16[2,1024,640]{2,1,0:T(8,128)(2,1)}, bf16[2,1024,640]{2,1,0:T(8,128)(2,1)S(1)}, u32[]{:S(2)}) copy-start(bf16[2,1024,640]{2,1,0:T(8,128)(2,1)S(1)} %get-tuple-element.168) | copy-start | bytes 7864324
  424.7 8.4 %copy-start.32 = (bf16[2,1024,640]{2,1,0:T(8,128)(2,1)S(1)}, bf16[2,1024,640]{2,1,0:T(8,128)(2,1)}, u32[]{:S(2)}) copy-start(bf16[2,1024,640]{2,1,0:T(8,128)(2,1)} %get-tuple-element.169) | copy-start | bytes 7864324
  424.8 19.3 %collective-permute-start.22 = (bf16[320,640]{1,0:T(8,128)(2,1)S(1)}, bf16[320,640]{1,0:T(8,128)(2,1)S(1)}, u32[]{:S(2)}, u32[]{:S(2)}) collective-permute-start(bf16[320,640]{1,0:T(8,128)(2,1)S(1)} %fusion.10), channel_id=1, source_target_pairs={{0,8},{2,10},{4,12},{6,14},{8,24},{10,26},{12,28},{14,30},{24,16},... | collective-permute-start | bytes 1228808 | tf_op jit(solution)/shard_map/ppermute | solution.py:493
  427.9 28.1 %collective-permute-start.25 = (bf16[4,1,80,1664]{3,2,0,1:T(8,128)(2,1)S(1)}, bf16[4,1,80,1664]{3,2,0,1:T(8,128)(2,1)S(1)}, u32[]{:S(2)}, u32[]{:S(2)}) collective-permute-start(bf16[4,1,80,1664]{3,2,0,1:T(8,128)(2,1)S(1)} %add_convert_fusion.1), channel_id=1, source_target_pairs={{0,2},{2,0},{4,6},{6,4},{8,10},{10,8},{12,14},{14,12},{16,18},{18,... | collective-permute-start | bytes 3194888 | tf_op jit(solution)/shard_map/ppermute | solution.py:481
  432.2 23.8 %collective-permute-start.24 = (bf16[4,1,80,1536]{3,2,0,1:T(8,128)(2,1)S(1)}, bf16[4,1,80,1536]{3,2,0,1:T(8,128)(2,1)S(1)}, u32[]{:S(2)}, u32[]{:S(2)}) collective-permute-start(bf16[4,1,80,1536]{3,2,0,1:T(8,128)(2,1)S(1)} %fusion.3), channel_id=1, source_target_pairs={{0,4},{2,6},{4,0},{6,2},{8,12},{10,14},{12,8},{14,10},{16,20},{18,... | collective-permute-start | bytes 2949128 | tf_op jit(solution)/shard_map/ppermute | solution.py:485
  438.6 5.9 %copy-start.33 = (bf16[2,1024,640]{2,1,0:T(8,128)(2,1)S(1)}, bf16[2,1024,640]{2,1,0:T(8,128)(2,1)}, u32[]{:S(2)}) copy-start(bf16[2,1024,640]{2,1,0:T(8,128)(2,1)} %get-tuple-element.170) | copy-start | bytes 7864324
  444.2 10.8 %collective-permute-start.23 = (bf16[320,640]{1,0:T(8,128)(2,1)S(1)}, bf16[320,640]{1,0:T(8,128)(2,1)S(1)}, u32[]{:S(2)}, u32[]{:S(2)}) collective-permute-start(bf16[320,640]{1,0:T(8,128)(2,1)S(1)} %fusion.9), channel_id=1, source_target_pairs={{0,8},{2,10},{4,12},{6,14},{8,24},{10,26},{12,28},{14,30},{24,16},... | collective-permute-start | bytes 1228808 | tf_op jit(solution)/shard_map/ppermute | solution.py:493
  459.8 70.0 %copy-start.9 = (bf16[1024,1280]{1,0:T(8,128)(2,1)S(1)}, bf16[1024,1280]{1,0:T(8,128)(2,1)}, u32[]{:S(2)}) copy-start(bf16[1024,1280]{1,0:T(8,128)(2,1)} %copy-done.8) | copy-start | bytes 7864324
  529.8 3.4 copy-start.29
  533.2 3.8 copy-start.50
  533.2 4.5 copy-start.49
  533.2 5.2 copy-start.48
  (23 other events, 43.2 us)
